TPU v7x, 32 devices: a whole 2x2x4 slice. The times are simulated.
32 devices in a mesh: narrow: 4 (over y, core), wide: 8 (over z, x).
Axes of the slice: x: 2, y: 2, z: 4, core: 2. Of those that a mesh axis runs over, the one named last changes fastest.
Arguments:
- points: float32 [2, 4096], P(None, ('narrow', 'wide')), may hold values from 0 to 1
- quad_weight: float32 [4096], P(('narrow', 'wide')), may hold values from 7.324219e-05 to 0.0007324219
- basis: float32 [4, 2, 4096, 128], P(None, None, ('narrow', 'wide')), may hold values from -6 to 6
- jacobi: float32 [2, 4096], P(None, ('narrow', 'wide')), may hold values from 0.5 to 2
- near_panel: int32 [256, 12], P(('narrow', 'wide')), may hold values from 0 to 255, as said below
- near_count: int32 [256], P(('narrow', 'wide')), may hold values from 2 to 12, as said below
- near_block: bfloat16 [256, 12, 32, 32], P(('narrow', 'wide')), may hold values from -0.875 to 0.875
- agg_index: int32 [2, 4096], P(None, ('narrow', 'wide')), may hold values from 0 to 47
- coarse_inverse: float32 [4, 384, 1536], P(None, 'wide', 'narrow'), may hold values from -0.1 to 0.5
Outputs:
- new_block: float32 [2, 4096, 128], P(None, ('narrow', 'wide'))
- hessenberg: float32 [4, 128, 128], replicated
- upper_factor: float32 [128, 128], replicated
Inputs may be any that keep to these rules, and one draw needn't show every extreme that they name: near_panel[p, 0] = p; every entry lies within 4 panels of p in panel order, and some entry lies exactly 4 panels away. `near_count`: slots at or beyond a panel's count are not used; some panel uses all 12.
All inputs are finite; a program needn't handle non-finite values.
Results may differ from a plain program's by a relative error of at most 0.0027.
The roundings to bfloat16 on the way count: a program that leaves them out, or rounds other values in their place, can miss the bound.
Values may be sent and summed in bfloat16 or wider, within the bound.
No kernel may reach another device: no remote copies, remote signals or barrier semaphores. Data moves between devices by JAX's collectives and lax.ppermute only.
A program may use at most 64 MiB of HBM per device.

v0:
```python
import math

import jax
import jax.numpy as jnp
from jax import lax
from jax.sharding import PartitionSpec as P

SPAN = 4


NU = 0.3
DELTA2 = 1e-05
ELASTIC = 40.0
HIGH = lax.Precision.HIGHEST


def extended(block, sides, width):
    for axis, dim in sides:
        count = lax.axis_size(axis)
        forward = [(i, i + 1) for i in range(count - 1)]
        backward = [(target, source) for source, target in forward]
        low = lax.ppermute(
            lax.slice_in_dim(block, block.shape[dim] - width, None, axis=dim), axis, forward
        )
        high = lax.ppermute(lax.slice_in_dim(block, 0, width, axis=dim), axis, backward)
        block = jnp.concatenate([low, block, high], axis=dim)
    return block


def far_kernel(targets, sources, weights):
    delta_x = targets[0][:, None] - sources[0][None, :]
    delta_y = targets[1][:, None] - sources[1][None, :]
    square_dist = delta_x * delta_x + delta_y * delta_y + DELTA2
    factor = ELASTIC * weights[None, :]
    log_part = -0.5 * (3.0 - 4.0 * NU) * jnp.log(square_dist)
    g_xx = factor * (log_part + delta_x * delta_x / square_dist)
    g_xy = factor * (delta_x * delta_y / square_dist)
    g_yy = factor * (log_part + delta_y * delta_y / square_dist)
    first_row = jnp.stack([g_xx, g_xy], axis=1)
    second_row = jnp.stack([g_xy, g_yy], axis=1)
    stacked = jnp.stack([first_row, second_row], axis=0)
    return stacked.reshape(2 * targets.shape[1], 2 * sources.shape[1]).astype(jnp.bfloat16)


def far_product(targets, sources, weights, fields):
    piece_len = sources.shape[1]
    row_count = targets.shape[1]
    rhs_count = fields.shape[2]
    block_size = math.gcd(piece_len, max(512, 524288 // row_count))
    block_count = piece_len // block_size

    def one_block(block_index, running):
        offset = block_index * block_size
        source_block = lax.dynamic_slice_in_dim(sources, offset, block_size, 1)
        weight_block = lax.dynamic_slice_in_dim(weights, offset, block_size, 0)
        field_block = lax.dynamic_slice_in_dim(fields, offset, block_size, 1)
        kernel_block = far_kernel(targets, source_block, weight_block)
        return running + jnp.dot(
            kernel_block,
            field_block.reshape(2 * block_size, rhs_count),
            preferred_element_type=jnp.float32,
        )

    initial = jnp.zeros((2 * row_count, rhs_count), jnp.float32)
    return lax.fori_loop(0, block_count, one_block, initial)


def make_fold(targets, source_all, shard_piece):
    return far_product(targets, source_all[0:2], source_all[2], shard_piece)


def body(
    points,
    quad_weight,
    basis,
    jacobi,
    near_panel,
    near_count,
    near_block,
    agg_index,
    coarse_inverse,
):
    block_total = basis.shape[0]
    point_count = basis.shape[2]
    rhs_count = basis.shape[3]
    coarse_count = coarse_inverse.shape[1]
    newest = basis[block_total - 1]
    member = (
        agg_index[:, :, None] == jnp.arange(coarse_count, dtype=jnp.int32)[None, None, :]
    ).astype(jnp.float32)
    coarse_rhs = jnp.einsum("apc,apr->cr", member, newest, precision=HIGH)
    coarse_part = jnp.einsum(
        "abc,cr->abr",
        coarse_inverse,
        lax.all_gather(coarse_rhs, "wide", axis=0, tiled=True),
        precision=HIGH,
    )
    coarse_sol = lax.psum_scatter(coarse_part, "narrow", scatter_dimension=0, tiled=True)[0]
    lifted = jnp.einsum("apc,cr->apr", member, coarse_sol, precision=HIGH)
    precond = (jacobi[:, :, None] * newest + lifted).astype(jnp.bfloat16)
    source_info = jnp.concatenate([points, quad_weight[None, :]], axis=0)
    targets = lax.all_gather(points, "narrow", axis=1, tiled=True)
    source_all = lax.all_gather(source_info, "wide", axis=1, tiled=True)
    far_part = make_fold(targets, source_all, lax.all_gather(precond, "wide", axis=1, tiled=True))
    far_local = lax.psum_scatter(
        far_part.reshape(2, targets.shape[1], rhs_count), "narrow", scatter_dimension=1, tiled=True
    )
    panels_dev = near_panel.shape[0]
    slot_total = near_panel.shape[1]
    nodes = near_block.shape[2] // 2
    padded = extended(precond, ((("narrow", "wide"), 1),), SPAN * nodes)
    panel_fields = padded.reshape(2, panels_dev + 2 * SPAN, nodes, rhs_count)
    local_index = near_panel - lax.axis_index(("narrow", "wide")) * panels_dev + SPAN
    gathered = panel_fields[:, local_index]
    slot_live = jnp.arange(slot_total, dtype=jnp.int32)[None, :] < near_count[:, None]
    gathered = jnp.where(slot_live[None, :, :, None, None], gathered, jnp.zeros((), gathered.dtype))
    gathered = jnp.transpose(gathered, (1, 2, 0, 3, 4)).reshape(
        panels_dev, slot_total, 2 * nodes, rhs_count
    )
    near_terms = jnp.einsum(
        "pkxy,pkyr->pxr", near_block, gathered, preferred_element_type=jnp.float32
    )
    near = jnp.transpose(near_terms.reshape(panels_dev, 2, nodes, rhs_count), (1, 0, 2, 3)).reshape(
        2, point_count, rhs_count
    )
    image = 0.5 * precond.astype(jnp.float32) + far_local + near
    weighted = basis * quad_weight[None, None, :, None]
    local_proj = jnp.einsum("jair,aiw->jrw", weighted, image, precision=HIGH)
    local_image = jnp.einsum(
        "air,aiw->rw", image * quad_weight[None, :, None], image, precision=HIGH
    )
    local_basis = jnp.einsum("jair,lais->jlrs", weighted, basis, precision=HIGH)
    hessenberg, image_gram, basis_gram = lax.psum(
        (local_proj, local_image, local_basis), ("narrow", "wide")
    )
    remainder = image - jnp.einsum("jair,jrw->aiw", basis, hessenberg, precision=HIGH)
    squared = jnp.einsum("jrw,jrv->wv", hessenberg, hessenberg, precision=HIGH)
    inner = jnp.einsum("jlrs,lsv->jrv", basis_gram, hessenberg, precision=HIGH)
    cross_term = jnp.einsum("jrw,jrv->wv", hessenberg, inner, precision=HIGH)
    gram_matrix = image_gram - 2.0 * squared + cross_term
    lower_factor = jnp.linalg.cholesky(gram_matrix)
    flat = remainder.reshape(2 * point_count, rhs_count)
    solved = jax.scipy.linalg.solve_triangular(lower_factor, flat.T, lower=True)
    new_block = solved.T.reshape(2, point_count, rhs_count)
    return (new_block, hessenberg, lower_factor.T)


def solution(mesh):
    in_specs = (
        P(None, ("narrow", "wide")),
        P(("narrow", "wide")),
        P(None, None, ("narrow", "wide"), None),
        P(None, ("narrow", "wide")),
        P(("narrow", "wide"), None),
        P(("narrow", "wide")),
        P(("narrow", "wide"), None, None, None),
        P(None, ("narrow", "wide")),
        P(None, "wide", "narrow"),
    )
    out_specs = (P(None, ("narrow", "wide"), None), P(), P())
    return jax.shard_map(body, mesh=mesh, in_specs=in_specs, out_specs=out_specs, check_vma=False)
```

profile of v0, /device:TPU:0, one launch (start us, length us, event | category | flops | bytes accessed | tf_op | source)
XLA Modules:
  0.0 327.3 jit_solution(1685941403485087284)
XLA Ops:
  7.2 0.0 copy-start
  7.2 0.0 reduce-scatter.3.cloned.1.call-start
  7.2 1.2 convolution_bitcast_fusion.8
  8.4 32.4 %all_gather.12 = f32[384,128]{1,0:T(8,128)S(1)} all-gather(f32[48,128]{1,0:T(8,128)S(1)} %convolution_bitcast_fusion.8), channel_id=1, replica_groups=mesh['narrow'=4,'wide'=8] {'wide'}, dimensions={0}, use_global_device_ids=true | all-gather | bytes 221184 | tf_op jit(solution)/shard_map/all_gather | solution.py:95
  40.8 2.0 convolution_bitcast_fusion.4
  42.8 0.0 reduce-scatter.3.cloned.1.call-update
  42.9 0.0 reduce-scatter.5.cloned.1.call-start
  42.9 5.3 %all_gather.14 = f32[2,512]{1,0:T(2,128)S(1)} all-gather(f32[2,128]{1,0:T(2,128)} %param.9), channel_id=1, replica_groups=mesh['narrow'=4,'wide'=8] {'narrow'}, dimensions={1}, use_global_device_ids=true | all-gather | bytes 5120 | tf_op jit(solution)/shard_map/all_gather | solution.py:102
  48.2 0.7 pad_maximum_fusion.3
  48.9 26.0 %all_gather.13 = f32[3,1024]{1,0:T(4,128)S(1)} all-gather(f32[3,128]{1,0:T(4,128)S(1)} %pad_maximum_fusion.3), channel_id=1, replica_groups=mesh['narrow'=4,'wide'=8] {'wide'}, dimensions={1}, use_global_device_ids=true | all-gather | bytes 13824 | tf_op jit(solution)/shard_map/all_gather | solution.py:103
  74.9 1.7 fusion.15
  76.6 1.7 pad_maximum_fusion
  78.3 4.0 %copy.34 = bf16[512,2,1024]{0,2,1:T(8,128)(2,1)} copy(bf16[512,2,1024]{2,0,1:T(8,128)(2,1)} %get-tuple-element.36) | data formatting | bytes 4194304 | tf_op jit(solution)/shard_map/while/body/eval_jaxpr/stack | solution.py:39
  82.3 3.9 %copy.36 = bf16[1,512,2048]{2,1,0:T(8,128)(2,1)} copy(bf16[1,512,2048]{1,2,0:T(8,128)(2,1)} %bitcast.116) | data formatting | bytes 4194304 | tf_op jit(solution)/shard_map/while/body/eval_jaxpr/stack | solution.py:41
  86.2 2.6 copy.35
  88.8 0.0 copy-start.7
  88.8 0.0 copy-start.9
  88.8 0.0 copy-start.1
  88.8 0.0 copy-start.8
  88.8 0.0 copy-start.3
  88.9 4.1 %copy.37 = bf16[1,512,2048]{2,1,0:T(8,128)(2,1)} copy(bf16[1,512,2048]{1,2,0:T(8,128)(2,1)} %bitcast.117) | data formatting | bytes 4194304 | tf_op jit(solution)/shard_map/while/body/eval_jaxpr/stack | solution.py:41
  93.0 0.0 copy-done.7
  93.0 0.0 copy-done.9
  93.0 0.1 iota_compare_fusion.5
  93.1 0.0 copy-done.1
  93.1 0.0 copy-done.6
  93.1 0.0 copy-done.8
  93.1 1.0 fusion.20
  94.1 31.3 %all_gather.15 = bf16[2,1024,128]{2,1,0:T(8,128)(2,1)S(1)} all-gather(bf16[2,128,128]{2,1,0:T(8,128)(2,1)S(1)} %fusion.20), channel_id=1, replica_groups=mesh['narrow'=4,'wide'=8] {'wide'}, dimensions={1}, use_global_device_ids=true | all-gather | bytes 589824 | tf_op jit(solution)/shard_map/all_gather | solution.py:104
  125.5 0.0 copy-done.3
  125.5 3.7 %fusion = f32[2,512,128]{2,1,0:T(8,128)} fusion(bf16[2048,128,1]{1,0,2:T(8,128)(2,1)S(1)} %bitcast.121, bf16[1,512,2048]{2,1,0:T(8,128)(2,1)} %copy.37, bf16[1,512,2048]{2,1,0:T(8,128)(2,1)S(1)} %copy-done.3), kind=kOutput, calls=%fused_computation.1 | convolution fusion | flops 538968064 | bytes 5242880 | tf_op jit(solution)/shard_map/while/body/eval_jaxpr/dot_general | solution.py:58
  129.2 0.0 reduce-scatter.5.cloned.1.call-update
  129.2 0.0 all-reduce.3.cloned.1.call-start
  129.2 0.0 copy-done.5
  129.2 2.1 convolution_bitcast_fusion
  131.3 0.1 reshape.519
  131.4 2.2 collective-permute-start
  133.7 1.5 collective-permute-start.1
  135.1 0.1 collective-permute-done
  135.2 4.2 %collective-permute-done.1 = bf16[2,64,128]{2,1,0:T(8,128)(2,1)S(1)} collective-permute-done((bf16[2,64,128]{2,1,0:T(8,128)(2,1)S(1)}, bf16[2,64,128]{2,1,0:T(8,128)(2,1)S(1)}, u32[]{:S(2)}, u32[]{:S(2)}) %collective-permute-start.1) | collective-permute-done | bytes 32800 | tf_op jit(solution)/shard_map/ppermute | solution.py:25
  139.5 0.7 gather_fusion
  140.2 0.2 broadcast_select_fusion
  140.4 0.0 copy-done
  140.4 0.5 fusion.48
  140.9 9.8 %reduce-scatter.5.cloned.1.call-done = f32[2,128,128]{2,1,0:T(8,128)} async-done(((f32[2,512,128]{2,1,0:T(8,128)}), f32[2,128,128]{2,1,0:T(8,128)}) %reduce-scatter.5.cloned.1.call-update) | async-done | bytes 131088 | tf_op jit(solution)/shard_map/reduce_scatter | solution.py:105
  150.7 0.9 bitcast_add_fusion
  151.7 1.8 convolution_bitcast_fusion.1
  153.4 1.1 convolution_bitcast_fusion.5
  154.5 0.0 all-reduce.3.cloned.1.call-update
  154.5 135.8 %all-reduce.3.cloned.1.call-done = (f32[4,128,128]{2,1,0:T(8,128)}, f32[128,128]{0,1:T(8,128)}, f32[4,4,128,128]{3,2,1,0:T(8,128)}) async-done(((f32[4,128,128]{2,1,0:T(8,128)}, f32[128,128]{0,1:T(8,128)}, f32[4,4,128,128]{3,2,1,0:T(8,128)}), (f32[4,128,128]{2,1,0:T(8,128)}, f32[128,128]{0,1:T(8,128)}, f32[4,4,128,128]{3,2,1,0:T(8,128)})) %all-reduce.3.cloned.1.call-update) | async-done | bytes 1376272 | tf_op jit(solution)/shard_map/psum | solution.py:133
  290.3 1.6 fusion.19
  291.9 2.2 convolution_bitcast_fusion.2
  294.2 0.0 copy-done.2
  294.2 0.0 copy-done.4
  294.2 0.6 fusion.23
  294.8 0.6 fusion.21
  295.4 0.1 copy.50
  295.5 11.7 %cholesky.16 = f32[128,128]{1,0:T(8,128)S(1)} custom-call(f32[128,128]{1,0:T(8,128)S(1)} %fusion.39), custom_call_target="Cholesky" | custom-call | tf_op jit(solution)/shard_map/jit(cholesky)/cholesky | solution.py:141
  307.3 0.6 compare_reduce_fusion
  307.9 0.7 fusion.41
  308.6 9.8 %custom-call.7 = f32[1,128,128]{1,2,0:T(8,128)S(1)} custom-call(f32[1,128,128]{2,1,0:T(8,128)S(1)} %get-tuple-element.39), custom_call_target="InvertDiagBlocksLowerTriangular" | custom-call | tf_op jit(solution)/shard_map/jit(_solve_triangular)/triangular_solve | solution.py:143
  318.4 0.7 copy.52
  319.1 0.9 fusion.37
  320.0 0.7 copy.79
  (14 shorter events, 0.1 us)
Async XLA Ops:
  7.2 133.2 %copy-start = (bf16[8,12,32,32]{3,2,1,0:T(8,128)(2,1)S(1)}, bf16[8,12,32,32]{3,2,1,0:T(8,128)(2,1)}, u32[]{:S(2)}) copy-start(bf16[8,12,32,32]{3,2,1,0:T(8,128)(2,1)} %param.15) | copy-start | bytes 589828
  7.2 85.9 %reduce-scatter.3.cloned.1.call-start = ((), (), s32[]{:S(2)}) async-start(), calls=%async_computation.2 | async-start | bytes 122880 | tf_op jit(solution)/shard_map/reduce_scatter | solution.py:98
  42.9 107.9 %reduce-scatter.5.cloned.1.call-start = ((), (), s32[]{:S(2)}) async-start(), calls=%async_computation.3 | async-start | bytes 655360 | tf_op jit(solution)/shard_map/reduce_scatter | solution.py:105
  88.8 4.2 %copy-start.7 = (s32[8,12]{1,0:T(8,128)S(1)}, s32[8,12]{1,0:T(8,128)}, u32[]{:S(2)}) copy-start(s32[8,12]{1,0:T(8,128)} %param.13) | copy-start | bytes 1156
  88.8 4.2 %copy-start.9 = (s32[8]{0:T(128)S(1)}, s32[8]{0:T(128)}, u32[]{:S(2)}) copy-start(s32[8]{0:T(128)} %param.14) | copy-start | bytes 100
  88.8 4.3 %copy-start.1 = (f32[4,2,128,128]{3,2,1,0:T(8,128)S(1)}, f32[4,2,128,128]{3,2,1,0:T(8,128)}, u32[]{:S(2)}) copy-start(f32[4,2,128,128]{3,2,1,0:T(8,128)} %param.11) | copy-start | bytes 1572868
  88.8 4.3 %copy-start.6 = (s32[2,128]{1,0:T(2,128)S(1)}, s32[2,128]{1,0:T(2,128)}, u32[]{:S(2)}) copy-start(s32[2,128]{1,0:T(2,128)} %param.16) | copy-start | bytes 3076
  88.8 4.3 %copy-start.8 = (f32[2,128]{1,0:T(2,128)S(1)}, f32[2,128]{1,0:T(2,128)}, u32[]{:S(2)}) copy-start(f32[2,128]{1,0:T(2,128)} %param.12) | copy-start | bytes 3076
  88.8 36.6 %copy-start.3 = (bf16[1,512,2048]{2,1,0:T(8,128)(2,1)S(1)}, bf16[1,512,2048]{2,1,0:T(8,128)(2,1)}, u32[]{:S(2)}) copy-start(bf16[1,512,2048]{2,1,0:T(8,128)(2,1)} %copy.36) | copy-start | bytes 6291460
  125.5 3.8 %copy-start.5 = (f32[128]{0:T(128)S(1)}, f32[128]{0:T(128)}, u32[]{:S(2)}) copy-start(f32[128]{0:T(128)} %param.10) | copy-start | bytes 1540
  129.2 161.1 %all-reduce.3.cloned.1.call-start = ((), (), s32[]{:S(2)}) async-start(), calls=%async_computation.4 | async-start | bytes 2752512 | tf_op jit(solution)/shard_map/psum | solution.py:133
  131.4 3.8 %collective-permute-start = (bf16[2,64,128]{2,1,0:T(8,128)(2,1)S(1)}, bf16[2,64,128]{2,1,0:T(8,128)(2,1)S(1)}, u32[]{:S(2)}, u32[]{:S(2)}) collective-permute-start(bf16[2,64,128]{2,1,0:T(8,128)(2,1)S(1)} %get-tuple-element.40), channel_id=1, source_target_pairs={{0,1},{1,2},{2,3},{3,4},{4,5},{5,6},{6,7},{7,8},{8,9},{9,10},{10,1... | collective-permute-start | bytes 98312 | tf_op jit(solution)/shard_map/ppermute | solution.py:22
  133.7 5.8 %collective-permute-start.1 = (bf16[2,64,128]{2,1,0:T(8,128)(2,1)S(1)}, bf16[2,64,128]{2,1,0:T(8,128)(2,1)S(1)}, u32[]{:S(2)}, u32[]{:S(2)}) collective-permute-start(bf16[2,64,128]{2,1,0:T(8,128)(2,1)S(1)} %get-tuple-element.41), channel_id=1, source_target_pairs={{1,0},{2,1},{3,2},{4,3},{5,4},{6,5},{7,6},{8,7},{9,8},{10,9},{11,1... | collective-permute-start | bytes 98312 | tf_op jit(solution)/shard_map/ppermute | solution.py:25
  290.3 3.9 %copy-start.2 = (f32[4,128,128]{2,1,0:T(8,128)S(1)}, f32[4,128,128]{2,1,0:T(8,128)}, u32[]{:S(2)}) copy-start(f32[4,128,128]{2,1,0:T(8,128)} %get-tuple-element.51) | copy-start | bytes 786436
  290.3 3.9 %copy-start.4 = (f32[128,128]{0,1:T(8,128)S(1)}, f32[128,128]{0,1:T(8,128)}, u32[]{:S(2)}) copy-start(f32[128,128]{0,1:T(8,128)} %get-tuple-element.34) | copy-start | bytes 196612
Sparse Core Ops, SparseCore 0:
  43.0 20.4 reduce-scatter.2
  129.3 21.3 reduce-scatter.4
  158.0 132.2 all-reduce.2
where the time goes:
time: 328 us; the launch traced here: 327 us
  waiting for transfers between devices  150 us (46%)
  blocking collectives  95 us (29%)
  other arithmetic  28.2 us (9%)
  matrix products  19.2 us (6%)
  local copies, waits for them, and re-layouts  17.1 us (5%)
  between operations  14 us (4%)
  starting transfers between devices  3.82 us (1%)
    psum x1, waiting for transfers between devices, body(): lax.psum((local_proj, local_image, local_basis), ('narrow', 'wide'))  136 us
    all_gather x1, blocking collectives, body(): lax.all_gather(coarse_rhs, 'wide', axis=0, tiled=True)  32.4 us
    all_gather x1, blocking collectives, body(): lax.all_gather(precond, 'wide', axis=1, tiled=True)  31.3 us
    all_gather x1, blocking collectives, body(): source_all = lax.all_gather(source_info, 'wide', axis=1, tiled=True)  26 us
    another operation x3, other arithmetic, body(): lower_factor = jnp.linalg.cholesky(gram_matrix)  12.4 us
    reduce_scatter x1, waiting for transfers between devices, body(): lax.psum_scatter(far_part.reshape(2, targets.shape[1], rhs_count), 'narro...  9.83 us
    another operation x1, other arithmetic, body(): solved = jax.scipy.linalg.solve_triangular(lower_factor, flat.T, lower=True)  9.81 us
    another operation x2, local copies, waits for them, and re-layouts, far_kernel(): stacked = jnp.stack([first_row, second_row], axis=0)  8.08 us
  transfers between devices with their start and end apart: 5, of which 4 were waited for; matrix products, arithmetic and copies ran while one was open for 7% of the time, Pallas kernels for 0%

commit v1 on v0

v1 whole, which is shorter than its diff:
```python
import math

import jax
import jax.numpy as jnp
from jax import lax
from jax.sharding import PartitionSpec as P

SPAN = 4


NU = 0.3
DELTA2 = 1e-05
ELASTIC = 40.0
HIGH = lax.Precision.HIGHEST
AXES = ("narrow", "wide")


def gather_all(block, axis):
    count = lax.axis_size(axis)
    return lax.all_to_all(
        jnp.broadcast_to(block[None], (count,) + block.shape), axis, 0, 0, tiled=True
    )


def sum_scatter(parts, axis):
    return jnp.sum(lax.all_to_all(parts, axis, 0, 0, tiled=True), axis=0)


def sum_all(block, axis):
    count = lax.axis_size(axis)
    if block.shape[0] % count:
        return lax.psum(block, axis)
    rows = block.shape[0] // count
    mine = sum_scatter(block.reshape((count, rows) + block.shape[1:]), axis)
    return gather_all(mine, axis).reshape(block.shape)


def extended(block, sides, width):
    for axis, dim in sides:
        count = lax.axis_size(axis)
        forward = [(i, i + 1) for i in range(count - 1)]
        backward = [(target, source) for source, target in forward]
        low = lax.ppermute(
            lax.slice_in_dim(block, block.shape[dim] - width, None, axis=dim), axis, forward
        )
        high = lax.ppermute(lax.slice_in_dim(block, 0, width, axis=dim), axis, backward)
        block = jnp.concatenate([low, block, high], axis=dim)
    return block


def far_kernel(targets, sources, weights):
    delta_x = targets[0][:, None] - sources[0][None, :]
    delta_y = targets[1][:, None] - sources[1][None, :]
    square_dist = delta_x * delta_x + delta_y * delta_y + DELTA2
    factor = ELASTIC * weights[None, :]
    log_part = -0.5 * (3.0 - 4.0 * NU) * jnp.log(square_dist)
    g_xx = factor * (log_part + delta_x * delta_x / square_dist)
    g_xy = factor * (delta_x * delta_y / square_dist)
    g_yy = factor * (log_part + delta_y * delta_y / square_dist)
    return (
        g_xx.astype(jnp.bfloat16),
        g_xy.astype(jnp.bfloat16),
        g_yy.astype(jnp.bfloat16),
    )


def dot32(left, right):
    return jnp.dot(left, right, preferred_element_type=jnp.float32)


def body(
    points,
    quad_weight,
    basis,
    jacobi,
    near_panel,
    near_count,
    near_block,
    agg_index,
    coarse_inverse,
):
    block_total = basis.shape[0]
    point_count = basis.shape[2]
    rhs_count = basis.shape[3]
    coarse_count = coarse_inverse.shape[1]
    narrow_count = lax.axis_size("narrow")
    wide_count = lax.axis_size("wide")
    newest = basis[block_total - 1]
    member = (
        agg_index[:, :, None] == jnp.arange(coarse_count, dtype=jnp.int32)[None, None, :]
    ).astype(jnp.float32)
    coarse_rhs = jnp.einsum("apc,apr->cr", member, newest, precision=HIGH)
    coarse_part = jnp.einsum(
        "abc,cr->abr",
        coarse_inverse,
        gather_all(coarse_rhs, "wide").reshape(wide_count * coarse_count, rhs_count),
        precision=HIGH,
    )
    row_groups = coarse_inverse.shape[0]
    coarse_sol = sum_scatter(
        coarse_part.reshape(narrow_count, row_groups * coarse_count // narrow_count, rhs_count),
        "narrow",
    )
    lifted = jnp.einsum("apc,cr->apr", member, coarse_sol, precision=HIGH)
    precond = (jacobi[:, :, None] * newest + lifted).astype(jnp.bfloat16)
    source_info = jnp.concatenate([points, quad_weight[None, :]], axis=0)
    targets = gather_all(points, "narrow")
    targets = jnp.transpose(targets, (1, 0, 2)).reshape(2, narrow_count * point_count)
    source_all = gather_all(source_info, "wide")
    source_all = jnp.transpose(source_all, (1, 0, 2)).reshape(3, wide_count * point_count)
    g_xx, g_xy, g_yy = far_kernel(targets, source_all[0:2], source_all[2])
    fields = gather_all(precond, "wide")
    f_x = fields[:, 0].reshape(wide_count * point_count, rhs_count)
    f_y = fields[:, 1].reshape(wide_count * point_count, rhs_count)
    far_x = dot32(g_xx, f_x) + dot32(g_xy, f_y)
    far_y = dot32(g_xy, f_x) + dot32(g_yy, f_y)
    shape = (narrow_count, point_count, rhs_count)
    far_local = sum_scatter(
        jnp.stack([far_x.reshape(shape), far_y.reshape(shape)], axis=1), "narrow"
    )
    panels_dev = near_panel.shape[0]
    slot_total = near_panel.shape[1]
    nodes = near_block.shape[2] // 2
    padded = extended(precond, ((AXES, 1),), SPAN * nodes)
    panel_fields = padded.reshape(2, panels_dev + 2 * SPAN, nodes, rhs_count)
    local_index = near_panel - lax.axis_index(AXES) * panels_dev + SPAN
    gathered = panel_fields[:, local_index]
    slot_live = jnp.arange(slot_total, dtype=jnp.int32)[None, :] < near_count[:, None]
    gathered = jnp.where(slot_live[None, :, :, None, None], gathered, jnp.zeros((), gathered.dtype))
    gathered = jnp.transpose(gathered, (1, 2, 0, 3, 4)).reshape(
        panels_dev, slot_total, 2 * nodes, rhs_count
    )
    near_terms = jnp.einsum(
        "pkxy,pkyr->pxr", near_block, gathered, preferred_element_type=jnp.float32
    )
    near = jnp.transpose(near_terms.reshape(panels_dev, 2, nodes, rhs_count), (1, 0, 2, 3)).reshape(
        2, point_count, rhs_count
    )
    image = 0.5 * precond.astype(jnp.float32) + far_local + near
    weighted = basis * quad_weight[None, None, :, None]
    local_proj = jnp.einsum("jair,aiw->jrw", weighted, image, precision=HIGH)
    hessenberg = sum_all(
        local_proj.reshape(block_total * rhs_count, rhs_count), AXES
    ).reshape(block_total, rhs_count, rhs_count)
    remainder = image - jnp.einsum("jair,jrw->aiw", basis, hessenberg, precision=HIGH)
    gram_matrix = sum_all(
        jnp.einsum(
            "air,aiw->rw", remainder * quad_weight[None, :, None], remainder, precision=HIGH
        ),
        AXES,
    )
    lower_factor = jnp.linalg.cholesky(gram_matrix)
    flat = remainder.reshape(2 * point_count, rhs_count)
    solved = jax.scipy.linalg.solve_triangular(lower_factor, flat.T, lower=True)
    new_block = solved.T.reshape(2, point_count, rhs_count)
    return (new_block, hessenberg, lower_factor.T)


def solution(mesh):
    in_specs = (
        P(None, ("narrow", "wide")),
        P(("narrow", "wide")),
        P(None, None, ("narrow", "wide"), None),
        P(None, ("narrow", "wide")),
        P(("narrow", "wide"), None),
        P(("narrow", "wide")),
        P(("narrow", "wide"), None, None, None),
        P(None, ("narrow", "wide")),
        P(None, "wide", "narrow"),
    )
    out_specs = (P(None, ("narrow", "wide"), None), P(), P())
    return jax.shard_map(body, mesh=mesh, in_specs=in_specs, out_specs=out_specs, check_vma=False)
```

time: 328 us -> 155 us (0.47)
  waiting for transfers between devices: 150 us -> 44.4 us
  blocking collectives: 95 us -> 35.7 us
  starting transfers between devices: 3.82 us -> 32.7 us
  between operations: 14 us -> 1.02 us
  local copies, waits for them, and re-layouts: 17.1 us -> 5.92 us
  matrix products: 19.2 us -> 10.1 us
  other arithmetic: 28.2 us -> 24.1 us
    psum x1 -> x0, waiting for transfers between devices: 136 us -> none  [body(): lax.psum((local_proj, local_image, local_basis), ('narrow', 'wide'))]
    all_gather x4 -> x0, blocking collectives: 95 us -> none  [the longest x1 32.4 us: body(): lax.all_gather(coarse_rhs, 'wide', axis=0, tiled=True)]
    all_to_all x0 -> x7, waiting for transfers between devices: none -> 42.8 us  [the longest x5 30.4 us: gather_all(): lax.all_to_all(jnp.broadcast_to(block[None], (count,) + block.shape), axi...]
    all_to_all x0 -> x3, blocking collectives: none -> 35.7 us  [the longest x2 22.9 us: sum_scatter(): return jnp.sum(lax.all_to_all(parts, axis, 0, 0, tiled=True), axis=0)]
    all_to_all x0 -> x7, starting transfers between devices: none -> 26.8 us  [the longest x5 20.1 us: gather_all(): lax.all_to_all(jnp.broadcast_to(block[None], (count,) + block.shape), axi...]
    another operation x4 -> x0, local copies, waits for them, and re-layouts: 14.6 us -> none  [the longest x2 8.08 us: far_kernel(): stacked = jnp.stack([first_row, second_row], axis=0)]
    reduce_scatter x2 -> x0, waiting for transfers between devices: 9.83 us -> none  [the longest x1 9.83 us: body(): lax.psum_scatter(far_part.reshape(2, targets.shape[1], rhs_count), 'narro...]
    dot_general x7 -> x6, matrix products: 12.3 us -> 5.59 us  [the longest x4 4.07 us: dot32(): return jnp.dot(left, right, preferred_element_type=jnp.float32)]
  transfers between devices with their start and end apart: 5 -> 9, of which waited for: 4 -> 9; matrix products, arithmetic and copies ran while one was open for 7% -> 1% of each run, Pallas kernels for 0% -> 0%
where the time goes in v1:
time: 155 us; the launch traced here: 154 us
  waiting for transfers between devices  44.4 us (29%)
  blocking collectives  35.7 us (23%)
  starting transfers between devices  32.7 us (21%)
  other arithmetic  24.1 us (16%)
  matrix products  10.1 us (7%)
  local copies, waits for them, and re-layouts  5.92 us (4%)
    all_to_all x5, waiting for transfers between devices, gather_all(): lax.all_to_all(jnp.broadcast_to(block[None], (count,) + block.shape), axi...  30.4 us
    all_to_all x2, blocking collectives, sum_scatter(): return jnp.sum(lax.all_to_all(parts, axis, 0, 0, tiled=True), axis=0)  22.9 us
    all_to_all x5, starting transfers between devices, gather_all(): lax.all_to_all(jnp.broadcast_to(block[None], (count,) + block.shape), axi...  20.1 us
    all_to_all x1, blocking collectives, gather_all(): lax.all_to_all(jnp.broadcast_to(block[None], (count,) + block.shape), axi...  12.8 us
    another operation x3, other arithmetic, body(): lower_factor = jnp.linalg.cholesky(gram_matrix)  12.4 us
    all_to_all x2, waiting for transfers between devices, sum_scatter(): return jnp.sum(lax.all_to_all(parts, axis, 0, 0, tiled=True), axis=0)  12.4 us
    another operation x1, other arithmetic, body(): solved = jax.scipy.linalg.solve_triangular(lower_factor, flat.T, lower=True)  9.81 us
    all_to_all x2, starting transfers between devices, sum_scatter(): return jnp.sum(lax.all_to_all(parts, axis, 0, 0, tiled=True), axis=0)  6.77 us
  transfers between devices with their start and end apart: 9, of which 9 were waited for; matrix products, arithmetic and copies ran while one was open for 1% of the time, Pallas kernels for 0%

profile of v1, /device:TPU:0, one launch (start us, length us, event | category | flops | bytes accessed | tf_op | source)
XLA Modules:
  0.0 153.9 jit_solution(13703386532502484983)
XLA Ops:
  0.6 0.0 copy-start
  0.6 0.0 copy-start.2
  0.7 0.0 copy-start.6
  0.7 0.0 copy-start.5
  0.7 0.0 copy-start.3
  0.7 1.2 convolution_bitcast_fusion.2
  1.9 0.0 copy-start.1
  1.9 0.0 copy-start.4
  1.9 0.0 copy-start.7
  1.9 0.7 broadcast_in_dim.25
  2.6 7.3 %all-to-all-start = ((f32[8,48,128]{2,1,0:T(8,128)}), f32[8,48,128]{2,1,0:T(8,128)S(1)}, u32[]{:S(2)}, u32[]{:S(2)}) async-start(f32[8,48,128]{2,1,0:T(8,128)} %broadcast_in_dim.25), calls=%async_computation | async-start | bytes 393216 | tf_op jit(solution)/shard_map/all_to_all | solution.py:20
  9.9 8.0 %all-to-all-done = f32[8,48,128]{2,1,0:T(8,128)S(1)} async-done(((f32[8,48,128]{2,1,0:T(8,128)}), f32[8,48,128]{2,1,0:T(8,128)S(1)}, u32[]{:S(2)}, u32[]{:S(2)}) %all-to-all-start) | async-done | bytes 196640 | tf_op jit(solution)/shard_map/all_to_all | solution.py:20
  17.8 0.0 copy-done.2
  17.8 1.1 convolution_bitcast_fusion.1
  18.9 3.3 %all-to-all-start.1 = ((f32[4,48,128]{2,1,0:T(8,128)}), f32[4,48,128]{2,1,0:T(8,128)S(1)}, u32[]{:S(2)}, u32[]{:S(2)}) async-start(f32[4,48,128]{2,1,0:T(8,128)} %convolution_bitcast_fusion.1), calls=%async_computation.1 | async-start | bytes 196608 | tf_op jit(solution)/shard_map/all_to_all | solution.py:26
  22.2 4.2 %all-to-all-done.1 = f32[4,48,128]{2,1,0:T(8,128)S(1)} async-done(((f32[4,48,128]{2,1,0:T(8,128)}), f32[4,48,128]{2,1,0:T(8,128)S(1)}, u32[]{:S(2)}, u32[]{:S(2)}) %all-to-all-start.1) | async-done | bytes 98336 | tf_op jit(solution)/shard_map/all_to_all | solution.py:26
  26.4 0.6 broadcast_in_dim.32
  27.0 3.2 %all-to-all-start.3 = ((f32[4,2,128]{2,1,0:T(2,128)}), f32[4,2,128]{2,1,0:T(2,128)S(1)}, u32[]{:S(2)}, u32[]{:S(2)}) async-start(f32[4,2,128]{2,1,0:T(2,128)} %broadcast_in_dim.32), calls=%async_computation.3 | async-start | bytes 8192 | tf_op jit(solution)/shard_map/all_to_all | solution.py:20
  30.3 0.0 copy-done.3
  30.3 3.7 %all-to-all-done.3 = f32[4,2,128]{2,1,0:T(2,128)S(1)} async-done(((f32[4,2,128]{2,1,0:T(2,128)}), f32[4,2,128]{2,1,0:T(2,128)S(1)}, u32[]{:S(2)}, u32[]{:S(2)}) %all-to-all-start.3) | async-done | bytes 4128 | tf_op jit(solution)/shard_map/all_to_all | solution.py:20
  34.1 0.6 broadcast_in_dim.27
  34.7 3.3 %all-to-all-start.2 = ((f32[8,3,128]{2,1,0:T(4,128)}), f32[8,3,128]{2,1,0:T(4,128)S(1)}, u32[]{:S(2)}, u32[]{:S(2)}) async-start(f32[8,3,128]{2,1,0:T(4,128)} %broadcast_in_dim.27), calls=%async_computation.2 | async-start | bytes 32768 | tf_op jit(solution)/shard_map/all_to_all | solution.py:20
  38.0 0.0 copy-done.1
  38.0 0.0 copy-done.4
  38.0 0.0 copy-done.7
  38.0 0.3 fusion.16
  38.3 0.0 copy-start.8
  38.3 6.2 %all-to-all-done.2 = f32[8,3,128]{2,1,0:T(4,128)S(1)} async-done(((f32[8,3,128]{2,1,0:T(4,128)}), f32[8,3,128]{2,1,0:T(4,128)S(1)}, u32[]{:S(2)}, u32[]{:S(2)}) %all-to-all-start.2) | async-done | bytes 12320 | tf_op jit(solution)/shard_map/all_to_all | solution.py:20
  44.5 0.9 broadcast_in_dim.33
  45.4 3.5 %all-to-all-start.4 = ((bf16[8,2,128,128]{3,2,1,0:T(8,128)(2,1)}), bf16[8,2,128,128]{3,2,1,0:T(8,128)(2,1)S(1)}, u32[]{:S(2)}, u32[]{:S(2)}) async-start(bf16[8,2,128,128]{3,2,1,0:T(8,128)(2,1)} %broadcast_in_dim.33), calls=%async_computation.4 | async-start | bytes 1048576 | tf_op jit(solution)/shard_map/all_to_all | solution.py:20
  48.9 0.1 iota_compare_fusion.5
  49.0 0.1 reshape.104
  49.1 1.3 collective-permute-start.1
  50.4 4.5 %collective-permute-start = (bf16[2,64,128]{2,1,0:T(8,128)(2,1)S(1)}, bf16[2,64,128]{2,1,0:T(8,128)(2,1)S(1)}, u32[]{:S(2)}, u32[]{:S(2)}) collective-permute-start(bf16[2,64,128]{2,1,0:T(8,128)(2,1)S(1)} %get-tuple-element.16), channel_id=1, source_target_pairs={{0,1},{1,2},{2,3},{3,4},{4,5},{5,6},{6,7},{7,8},{8,9},{9,10},{10,1... | collective-permute-start | bytes 98312 | tf_op jit(solution)/shard_map/ppermute | solution.py:43
  55.0 0.1 collective-permute-done.1
  55.0 1.5 collective-permute-done
  56.6 0.7 gather_fusion
  57.3 5.5 %all-to-all-done.4 = bf16[8,2,128,128]{3,2,1,0:T(8,128)(2,1)S(1)} async-done(((bf16[8,2,128,128]{3,2,1,0:T(8,128)(2,1)}), bf16[8,2,128,128]{3,2,1,0:T(8,128)(2,1)S(1)}, u32[]{:S(2)}, u32[]{:S(2)}) %all-to-all-start.4) | async-done | bytes 524320 | tf_op jit(solution)/shard_map/all_to_all | solution.py:20
  62.9 0.9 fusion.26
  63.8 1.1 fusion.24
  64.9 1.1 convolution_add_fusion
  66.0 0.9 convolution_add_fusion.1
  67.0 0.9 pad_maximum_fusion
  67.8 3.5 %all-to-all-start.5 = ((f32[4,2,128,128]{3,2,1,0:T(8,128)}), f32[4,2,128,128]{3,2,1,0:T(8,128)S(1)}, u32[]{:S(2)}, u32[]{:S(2)}) async-start(f32[4,2,128,128]{3,2,1,0:T(8,128)} %pad_maximum_fusion), calls=%async_computation.5 | async-start | bytes 1048576 | tf_op jit(solution)/shard_map/all_to_all | solution.py:26
  71.3 0.2 broadcast_select_fusion
  71.5 0.5 fusion.54
  72.0 8.1 %all-to-all-done.5 = f32[4,2,128,128]{3,2,1,0:T(8,128)S(1)} async-done(((f32[4,2,128,128]{3,2,1,0:T(8,128)}), f32[4,2,128,128]{3,2,1,0:T(8,128)S(1)}, u32[]{:S(2)}, u32[]{:S(2)}) %all-to-all-start.5) | async-done | bytes 524320 | tf_op jit(solution)/shard_map/all_to_all | solution.py:26
  80.2 1.1 fusion.29
  81.2 13.4 %all_to_all.50 = f32[32,16,128]{2,1,0:T(8,128)S(1)} all-to-all(f32[32,16,128]{2,1,0:T(8,128)S(1)} %bitcast.99), channel_id=1, replica_groups=mesh['narrow'=4,'wide'=8] {'narrow','wide'}, dimensions={0} | all-to-all | bytes 524288 | tf_op jit(solution)/shard_map/all_to_all | solution.py:26
  94.7 12.8 %all_to_all.51 = f32[32,16,128]{2,1,0:T(8,128)S(1)} all-to-all(f32[32,16,128]{2,1,0:T(8,128)S(1)} %broadcast_in_dim.37), channel_id=1, replica_groups=mesh['narrow'=4,'wide'=8] {'narrow','wide'}, dimensions={0} | all-to-all | bytes 524288 | tf_op jit(solution)/shard_map/all_to_all | solution.py:20
  107.5 0.6 fusion.15
  108.1 0.5 fusion.32
  108.6 9.4 %all_to_all.52 = f32[32,4,128]{2,1,0:T(4,128)S(1)} all-to-all(f32[32,4,128]{2,1,0:T(4,128)S(1)} %bitcast.104), channel_id=1, replica_groups=mesh['narrow'=4,'wide'=8] {'narrow','wide'}, dimensions={0} | all-to-all | bytes 131072 | tf_op jit(solution)/shard_map/all_to_all | solution.py:26
  118.1 0.6 broadcast_in_dim.38
  118.7 2.8 %all-to-all-start.9 = ((f32[32,4,128]{2,1,0:T(4,128)}), f32[32,4,128]{2,1,0:T(4,128)S(1)}, u32[]{:S(2)}, u32[]{:S(2)}) async-start(f32[32,4,128]{2,1,0:T(4,128)} %broadcast_in_dim.38), calls=%async_computation.9 | async-start | bytes 131072 | tf_op jit(solution)/shard_map/all_to_all | solution.py:20
  121.5 7.1 %all-to-all-done.9 = f32[32,4,128]{2,1,0:T(4,128)S(1)} async-done(((f32[32,4,128]{2,1,0:T(4,128)}), f32[32,4,128]{2,1,0:T(4,128)S(1)}, u32[]{:S(2)}, u32[]{:S(2)}) %all-to-all-start.9) | async-done | bytes 65568 | tf_op jit(solution)/shard_map/all_to_all | solution.py:20
  128.6 0.1 copy.38
  128.7 11.7 %cholesky.16 = f32[128,128]{1,0:T(8,128)S(1)} custom-call(f32[128,128]{1,0:T(8,128)S(1)} %fusion.39), custom_call_target="Cholesky" | custom-call | tf_op jit(solution)/shard_map/jit(cholesky)/cholesky | solution.py:152
  140.4 0.6 compare_reduce_fusion
  141.1 0.7 fusion.41
  141.7 9.8 %custom-call.7 = f32[1,128,128]{1,2,0:T(8,128)S(1)} custom-call(f32[1,128,128]{2,1,0:T(8,128)S(1)} %get-tuple-element.15), custom_call_target="InvertDiagBlocksLowerTriangular" | custom-call | tf_op jit(solution)/shard_map/jit(_solve_triangular)/triangular_solve | solution.py:154
  151.5 0.9 fusion.37
  152.5 0.7 copy.40
  153.2 0.7 copy.52
  (21 shorter events, 0.3 us)
Async XLA Ops:
  0.6 70.8 %copy-start = (bf16[8,12,32,32]{3,2,1,0:T(8,128)(2,1)S(1)}, bf16[8,12,32,32]{3,2,1,0:T(8,128)(2,1)}, u32[]{:S(2)}) copy-start(bf16[8,12,32,32]{3,2,1,0:T(8,128)(2,1)} %param.15) | copy-start | bytes 589828
  0.6 17.2 %copy-start.2 = (f32[4,48,384]{2,1,0:T(8,128)S(1)}, f32[4,48,384]{2,1,0:T(8,128)}, u32[]{:S(2)}) copy-start(f32[4,48,384]{2,1,0:T(8,128)} %param.17) | copy-start | bytes 884740
  0.7 21.5 %copy-start.6 = (s32[8,12]{1,0:T(8,128)S(1)}, s32[8,12]{1,0:T(8,128)}, u32[]{:S(2)}) copy-start(s32[8,12]{1,0:T(8,128)} %param.13) | copy-start | bytes 1156
  0.7 25.8 %copy-start.5 = (f32[2,128]{1,0:T(2,128)S(1)}, f32[2,128]{1,0:T(2,128)}, u32[]{:S(2)}) copy-start(f32[2,128]{1,0:T(2,128)} %param.9) | copy-start | bytes 3076
  0.7 29.6 %copy-start.3 = (f32[128]{0:T(128)S(1)}, f32[128]{0:T(128)}, u32[]{:S(2)}) copy-start(f32[128]{0:T(128)} %param.10) | copy-start | bytes 1540
  1.9 36.1 %copy-start.1 = (f32[4,2,128,128]{3,2,1,0:T(8,128)S(1)}, f32[4,2,128,128]{3,2,1,0:T(8,128)}, u32[]{:S(2)}) copy-start(f32[4,2,128,128]{3,2,1,0:T(8,128)} %param.11) | copy-start | bytes 1572868
  1.9 36.1 %copy-start.4 = (s32[2,128]{1,0:T(2,128)S(1)}, s32[2,128]{1,0:T(2,128)}, u32[]{:S(2)}) copy-start(s32[2,128]{1,0:T(2,128)} %param.16) | copy-start | bytes 3076
  1.9 36.1 %copy-start.7 = (f32[2,128]{1,0:T(2,128)S(1)}, f32[2,128]{1,0:T(2,128)}, u32[]{:S(2)}) copy-start(f32[2,128]{1,0:T(2,128)} %param.12) | copy-start | bytes 3076
  2.6 15.2 %all-to-all-start = ((f32[8,48,128]{2,1,0:T(8,128)}), f32[8,48,128]{2,1,0:T(8,128)S(1)}, u32[]{:S(2)}, u32[]{:S(2)}) async-start(f32[8,48,128]{2,1,0:T(8,128)} %broadcast_in_dim.25), calls=%async_computation | async-start | bytes 393216 | tf_op jit(solution)/shard_map/all_to_all | solution.py:20
  18.9 7.6 %all-to-all-start.1 = ((f32[4,48,128]{2,1,0:T(8,128)}), f32[4,48,128]{2,1,0:T(8,128)S(1)}, u32[]{:S(2)}, u32[]{:S(2)}) async-start(f32[4,48,128]{2,1,0:T(8,128)} %convolution_bitcast_fusion.1), calls=%async_computation.1 | async-start | bytes 196608 | tf_op jit(solution)/shard_map/all_to_all | solution.py:26
  27.0 7.0 %all-to-all-start.3 = ((f32[4,2,128]{2,1,0:T(2,128)}), f32[4,2,128]{2,1,0:T(2,128)S(1)}, u32[]{:S(2)}, u32[]{:S(2)}) async-start(f32[4,2,128]{2,1,0:T(2,128)} %broadcast_in_dim.32), calls=%async_computation.3 | async-start | bytes 8192 | tf_op jit(solution)/shard_map/all_to_all | solution.py:20
  34.7 9.9 %all-to-all-start.2 = ((f32[8,3,128]{2,1,0:T(4,128)}), f32[8,3,128]{2,1,0:T(4,128)S(1)}, u32[]{:S(2)}, u32[]{:S(2)}) async-start(f32[8,3,128]{2,1,0:T(4,128)} %broadcast_in_dim.27), calls=%async_computation.2 | async-start | bytes 32768 | tf_op jit(solution)/shard_map/all_to_all | solution.py:20
  38.3 10.6 %copy-start.8 = (s32[8]{0:T(128)S(1)}, s32[8]{0:T(128)}, u32[]{:S(2)}) copy-start(s32[8]{0:T(128)} %param.14) | copy-start | bytes 100
  45.4 17.4 %all-to-all-start.4 = ((bf16[8,2,128,128]{3,2,1,0:T(8,128)(2,1)}), bf16[8,2,128,128]{3,2,1,0:T(8,128)(2,1)S(1)}, u32[]{:S(2)}, u32[]{:S(2)}) async-start(bf16[8,2,128,128]{3,2,1,0:T(8,128)(2,1)} %broadcast_in_dim.33), calls=%async_computation.4 | async-start | bytes 1048576 | tf_op jit(solution)/shard_map/all_to_all | solution.py:20
  49.1 5.9 %collective-permute-start.1 = (bf16[2,64,128]{2,1,0:T(8,128)(2,1)S(1)}, bf16[2,64,128]{2,1,0:T(8,128)(2,1)S(1)}, u32[]{:S(2)}, u32[]{:S(2)}) collective-permute-start(bf16[2,64,128]{2,1,0:T(8,128)(2,1)S(1)} %get-tuple-element.17), channel_id=1, source_target_pairs={{1,0},{2,1},{3,2},{4,3},{5,4},{6,5},{7,6},{8,7},{9,8},{10,9},{11,1... | collective-permute-start | bytes 98312 | tf_op jit(solution)/shard_map/ppermute | solution.py:46
  50.4 6.1 %collective-permute-start = (bf16[2,64,128]{2,1,0:T(8,128)(2,1)S(1)}, bf16[2,64,128]{2,1,0:T(8,128)(2,1)S(1)}, u32[]{:S(2)}, u32[]{:S(2)}) collective-permute-start(bf16[2,64,128]{2,1,0:T(8,128)(2,1)S(1)} %get-tuple-element.16), channel_id=1, source_target_pairs={{0,1},{1,2},{2,3},{3,4},{4,5},{5,6},{6,7},{7,8},{8,9},{9,10},{10,1... | collective-permute-start | bytes 98312 | tf_op jit(solution)/shard_map/ppermute | solution.py:43
  67.8 12.3 %all-to-all-start.5 = ((f32[4,2,128,128]{3,2,1,0:T(8,128)}), f32[4,2,128,128]{3,2,1,0:T(8,128)S(1)}, u32[]{:S(2)}, u32[]{:S(2)}) async-start(f32[4,2,128,128]{3,2,1,0:T(8,128)} %pad_maximum_fusion), calls=%async_computation.5 | async-start | bytes 1048576 | tf_op jit(solution)/shard_map/all_to_all | solution.py:26
  118.7 9.9 %all-to-all-start.9 = ((f32[32,4,128]{2,1,0:T(4,128)}), f32[32,4,128]{2,1,0:T(4,128)S(1)}, u32[]{:S(2)}, u32[]{:S(2)}) async-start(f32[32,4,128]{2,1,0:T(4,128)} %broadcast_in_dim.38), calls=%async_computation.9 | async-start | bytes 131072 | tf_op jit(solution)/shard_map/all_to_all | solution.py:20

commit v2 on v1

--- a/solution.py
+++ b/solution.py
@@ -3,6 +3,8 @@
 import jax
 import jax.numpy as jnp
 from jax import lax
+from jax.experimental import pallas as pl
+from jax.experimental.pallas import tpu as pltpu
 from jax.sharding import PartitionSpec as P
 
 SPAN = 4
@@ -35,17 +37,22 @@
     return gather_all(mine, axis).reshape(block.shape)
 
 
-def extended(block, sides, width):
-    for axis, dim in sides:
-        count = lax.axis_size(axis)
-        forward = [(i, i + 1) for i in range(count - 1)]
-        backward = [(target, source) for source, target in forward]
-        low = lax.ppermute(
-            lax.slice_in_dim(block, block.shape[dim] - width, None, axis=dim), axis, forward
-        )
-        high = lax.ppermute(lax.slice_in_dim(block, 0, width, axis=dim), axis, backward)
-        block = jnp.concatenate([low, block, high], axis=dim)
-    return block
+def halo_fields(precond, fields, width):
+    narrow_count = lax.axis_size("narrow")
+    wide_count = lax.axis_size("wide")
+    wide_index = lax.axis_index("wide")
+    pairs = []
+    for group in range(narrow_count - 1):
+        left = group * wide_count + wide_count - 1
+        pairs += [(left, left + 1), (left + 1, left)]
+    first = precond[:, :width]
+    last = precond[:, precond.shape[1] - width :]
+    crossed = lax.ppermute(jnp.where(wide_index == 0, first, last), AXES, pairs)
+    before = lax.dynamic_index_in_dim(fields, jnp.maximum(wide_index - 1, 0), 0, False)
+    after = lax.dynamic_index_in_dim(fields, jnp.minimum(wide_index + 1, wide_count - 1), 0, False)
+    low = jnp.where(wide_index == 0, crossed, before[:, before.shape[1] - width :])
+    high = jnp.where(wide_index == wide_count - 1, crossed, after[:, :width])
+    return jnp.concatenate([low, precond, high], axis=1)
 
 
 def far_kernel(targets, sources, weights):
@@ -62,6 +69,96 @@
         g_xy.astype(jnp.bfloat16),
         g_yy.astype(jnp.bfloat16),
     )
+
+
+ROWS = 8
+
+
+def factor_kernel(gram_ref, remainder_ref, upper_ref, new_ref, work_ref, inverse_ref):
+    order = gram_ref.shape[0]
+    tile = (ROWS, order)
+    lane = lax.broadcasted_iota(jnp.int32, tile, 1)
+    row = lax.broadcasted_iota(jnp.int32, tile, 0)
+    work_ref[...] = gram_ref[...]
+    for block in range(order // ROWS):
+        start = block * ROWS
+        inverse_ref[start : start + ROWS, :] = jnp.where(lane == row + start, 1.0, 0.0)
+    for block in range(order // ROWS):
+        start = block * ROWS
+        own = work_ref[start : start + ROWS, :]
+        own_inverse = inverse_ref[start : start + ROWS, :]
+        columns = [
+            jnp.broadcast_to(own[:, start + m : start + m + 1], tile) for m in range(ROWS)
+        ]
+        entry = {
+            (j, m): jnp.broadcast_to(columns[m][j : j + 1, :], tile)
+            for m in range(ROWS)
+            for j in range(m, ROWS)
+        }
+        scale = []
+        for m in range(ROWS):
+            scale.append(lax.rsqrt(entry[m, m]))
+            for j in range(m + 1, ROWS):
+                entry[j, m] = entry[j, m] * scale[m]
+            for n in range(m + 1, ROWS):
+                for j in range(n, ROWS):
+                    entry[j, n] = entry[j, n] - entry[j, m] * entry[n, m]
+        solved = []
+        solved_inverse = []
+        for m in range(ROWS):
+            upper_row = jnp.broadcast_to(own[m : m + 1, :], tile)
+            inverse_row = jnp.broadcast_to(own_inverse[m : m + 1, :], tile)
+            for j in range(m):
+                upper_row = upper_row - entry[m, j] * solved[j]
+                inverse_row = inverse_row - entry[m, j] * solved_inverse[j]
+            upper_row = upper_row * scale[m]
+            inverse_row = inverse_row * scale[m]
+            solved.append(upper_row)
+            solved_inverse.append(inverse_row)
+        upper_rows = solved[ROWS - 1]
+        inverse_rows = solved_inverse[ROWS - 1]
+        for m in range(ROWS - 1):
+            upper_rows = jnp.where(row == m, solved[m], upper_rows)
+            inverse_rows = jnp.where(row == m, solved_inverse[m], inverse_rows)
+        upper_ref[start : start + ROWS, :] = jnp.where(lane >= row + start, upper_rows, 0.0)
+        inverse_ref[start : start + ROWS, :] = inverse_rows
+        for later in range(block + 1, order // ROWS):
+            first = later * ROWS
+            target = work_ref[first : first + ROWS, :]
+            target_inverse = inverse_ref[first : first + ROWS, :]
+            multiplier = []
+            for m in range(ROWS):
+                value = jnp.broadcast_to(target[:, start + m : start + m + 1], tile)
+                for j in range(m):
+                    value = value - multiplier[j] * entry[m, j]
+                multiplier.append(value * scale[m])
+            for m in range(ROWS):
+                target = target - multiplier[m] * solved[m]
+                target_inverse = target_inverse - multiplier[m] * solved_inverse[m]
+            work_ref[first : first + ROWS, :] = target
+            inverse_ref[first : first + ROWS, :] = target_inverse
+    new_ref[...] = lax.dot_general(
+        remainder_ref[...],
+        inverse_ref[...],
+        (((1,), (1,)), ((), ())),
+        precision=HIGH,
+        preferred_element_type=jnp.float32,
+    )
+
+
+def factor_and_solve(gram_matrix, remainder):
+    order = gram_matrix.shape[0]
+    return pl.pallas_call(
+        factor_kernel,
+        out_shape=(
+            jax.ShapeDtypeStruct(gram_matrix.shape, jnp.float32),
+            jax.ShapeDtypeStruct(remainder.shape, jnp.float32),
+        ),
+        scratch_shapes=[
+            pltpu.VMEM((order, order), jnp.float32),
+            pltpu.VMEM((order, order), jnp.float32),
+        ],
+    )(gram_matrix, remainder)
 
 
 def dot32(left, right):
@@ -90,24 +187,27 @@
         agg_index[:, :, None] == jnp.arange(coarse_count, dtype=jnp.int32)[None, None, :]
     ).astype(jnp.float32)
     coarse_rhs = jnp.einsum("apc,apr->cr", member, newest, precision=HIGH)
+    source_info = jnp.concatenate([points, quad_weight[None, :]], axis=0)
+    from_wide = gather_all(jnp.concatenate([coarse_rhs, source_info], axis=0), "wide")
     coarse_part = jnp.einsum(
         "abc,cr->abr",
         coarse_inverse,
-        gather_all(coarse_rhs, "wide").reshape(wide_count * coarse_count, rhs_count),
+        from_wide[:, :coarse_count].reshape(wide_count * coarse_count, rhs_count),
         precision=HIGH,
     )
-    row_groups = coarse_inverse.shape[0]
-    coarse_sol = sum_scatter(
-        coarse_part.reshape(narrow_count, row_groups * coarse_count // narrow_count, rhs_count),
-        "narrow",
-    )
+    to_narrow = jnp.concatenate(
+        [coarse_part, jnp.broadcast_to(points[None], (narrow_count,) + points.shape)], axis=1
+    )
+    from_narrow = lax.all_to_all(to_narrow, "narrow", 0, 0, tiled=True)
+    coarse_sol = jnp.sum(from_narrow[:, :coarse_count], axis=0)
     lifted = jnp.einsum("apc,cr->apr", member, coarse_sol, precision=HIGH)
     precond = (jacobi[:, :, None] * newest + lifted).astype(jnp.bfloat16)
-    source_info = jnp.concatenate([points, quad_weight[None, :]], axis=0)
-    targets = gather_all(points, "narrow")
-    targets = jnp.transpose(targets, (1, 0, 2)).reshape(2, narrow_count * point_count)
-    source_all = gather_all(source_info, "wide")
-    source_all = jnp.transpose(source_all, (1, 0, 2)).reshape(3, wide_count * point_count)
+    targets = jnp.transpose(from_narrow[:, coarse_count:], (1, 0, 2)).reshape(
+        2, narrow_count * point_count
+    )
+    source_all = jnp.transpose(from_wide[:, coarse_count:], (1, 0, 2)).reshape(
+        3, wide_count * point_count
+    )
     g_xx, g_xy, g_yy = far_kernel(targets, source_all[0:2], source_all[2])
     fields = gather_all(precond, "wide")
     f_x = fields[:, 0].reshape(wide_count * point_count, rhs_count)
@@ -121,7 +221,7 @@
     panels_dev = near_panel.shape[0]
     slot_total = near_panel.shape[1]
     nodes = near_block.shape[2] // 2
-    padded = extended(precond, ((AXES, 1),), SPAN * nodes)
+    padded = halo_fields(precond, fields, SPAN * nodes)
     panel_fields = padded.reshape(2, panels_dev + 2 * SPAN, nodes, rhs_count)
     local_index = near_panel - lax.axis_index(AXES) * panels_dev + SPAN
     gathered = panel_fields[:, local_index]
@@ -149,11 +249,10 @@
         ),
         AXES,
     )
-    lower_factor = jnp.linalg.cholesky(gram_matrix)
-    flat = remainder.reshape(2 * point_count, rhs_count)
-    solved = jax.scipy.linalg.solve_triangular(lower_factor, flat.T, lower=True)
-    new_block = solved.T.reshape(2, point_count, rhs_count)
-    return (new_block, hessenberg, lower_factor.T)
+    upper_factor, new_block = factor_and_solve(
+        gram_matrix, remainder.reshape(2 * point_count, rhs_count)
+    )
+    return (new_block.reshape(2, point_count, rhs_count), hessenberg, upper_factor)
 
 
 def solution(mesh):

time: 155 us -> 121 us (0.78)
  other arithmetic: 24.1 us -> 2.64 us
  starting transfers between devices: 32.7 us -> 21.1 us
  Pallas kernels: 0 us -> 6.25 us
  waiting for transfers between devices: 44.4 us -> 40.7 us
  matrix products: 10.1 us -> 8.53 us
    another operation x4 -> x0, other arithmetic: 22.2 us -> none  [the longest x3 12.4 us: body(): lower_factor = jnp.linalg.cholesky(gram_matrix)]
    all_to_all x5 -> x3, starting transfers between devices: 20.1 us -> 13.6 us  [gather_all(): lax.all_to_all(jnp.broadcast_to(block[None], (count,) + block.shape), axi...]
    pallas_call x0 -> x1, Pallas kernels: none -> 6.25 us  [factor_and_solve(): pl.pallas_call(factor_kernel, out_shape=(jax.ShapeDtypeStruct(gram_matrix...]
    ppermute x2 -> x1, starting transfers between devices: 5.84 us -> 0.66 us  [halo_fields(): crossed = lax.ppermute(jnp.where(wide_index == 0, first, last), AXES, pairs)]
    all_to_all x2 -> x1, waiting for transfers between devices: 12.4 us -> 7.3 us  [sum_scatter(): return jnp.sum(lax.all_to_all(parts, axis, 0, 0, tiled=True), axis=0)]
    all_to_all x0 -> x1, waiting for transfers between devices: none -> 4.41 us  [body(): from_narrow = lax.all_to_all(to_narrow, 'narrow', 0, 0, tiled=True)]
    all_to_all x0 -> x1, starting transfers between devices: none -> 3.32 us  [body(): from_narrow = lax.all_to_all(to_narrow, 'narrow', 0, 0, tiled=True)]
    all_to_all x2 -> x1, starting transfers between devices: 6.77 us -> 3.47 us  [sum_scatter(): return jnp.sum(lax.all_to_all(parts, axis, 0, 0, tiled=True), axis=0)]
  transfers between devices with their start and end apart: 9 -> 6, of which waited for: 9 -> 5; matrix products, arithmetic and copies ran while one was open for 1% -> 5% of each run, Pallas kernels for 0% -> 0%
where the time goes in v2:
time: 121 us; the launch traced here: 120 us
  waiting for transfers between devices  40.7 us (34%)
  blocking collectives  35.4 us (29%)
  starting transfers between devices  21.1 us (17%)
  matrix products  8.53 us (7%)
  Pallas kernels  6.25 us (5%)
  local copies, waits for them, and re-layouts  4.57 us (4%)
  other arithmetic  2.64 us (2%)
    all_to_all x3, waiting for transfers between devices, gather_all(): lax.all_to_all(jnp.broadcast_to(block[None], (count,) + block.shape), axi...  28.9 us
    all_to_all x2, blocking collectives, sum_scatter(): return jnp.sum(lax.all_to_all(parts, axis, 0, 0, tiled=True), axis=0)  22.6 us
    all_to_all x3, starting transfers between devices, gather_all(): lax.all_to_all(jnp.broadcast_to(block[None], (count,) + block.shape), axi...  13.6 us
    all_to_all x1, blocking collectives, gather_all(): lax.all_to_all(jnp.broadcast_to(block[None], (count,) + block.shape), axi...  12.8 us
    all_to_all x1, waiting for transfers between devices, sum_scatter(): return jnp.sum(lax.all_to_all(parts, axis, 0, 0, tiled=True), axis=0)  7.3 us
    pallas_call x1, Pallas kernels, factor_and_solve(): pl.pallas_call(factor_kernel, out_shape=(jax.ShapeDtypeStruct(gram_matrix...  6.25 us
    all_to_all x1, waiting for transfers between devices, body(): from_narrow = lax.all_to_all(to_narrow, 'narrow', 0, 0, tiled=True)  4.41 us
    dot_general x4, matrix products, dot32(): return jnp.dot(left, right, preferred_element_type=jnp.float32)  4.07 us
  transfers between devices with their start and end apart: 6, of which 5 were waited for; matrix products, arithmetic and copies ran while one was open for 5% of the time, Pallas kernels for 0%

profile of v2, /device:TPU:0, one launch (start us, length us, event | category | flops | bytes accessed | tf_op | source)
XLA Modules:
  0.0 120.1 jit_solution(14618059051663859213)
XLA Ops:
  0.6 0.0 copy-start
  0.6 0.0 copy-start.8
  0.7 0.0 copy-start.10
  0.7 0.0 copy-start.3
  0.7 1.2 convolution_bitcast_fusion.2
  1.9 0.7 pad_maximum_fusion.3
  2.6 0.7 broadcast_in_dim.23
  3.3 0.0 copy-start.7
  3.3 7.4 %all-to-all-start = ((f32[8,51,128]{2,1,0:T(8,128)}), f32[8,51,128]{2,1,0:T(8,128)S(1)}, u32[]{:S(2)}, u32[]{:S(2)}) async-start(f32[8,51,128]{2,1,0:T(8,128)} %broadcast_in_dim.23), calls=%async_computation | async-start | bytes 458752 | tf_op jit(solution)/shard_map/all_to_all | solution.py:22
  10.7 0.0 copy-done.8
  10.7 0.0 copy-start.1
  10.7 0.0 copy-start.6
  10.7 0.0 copy-start.9
  10.7 0.1 reshape.97
  10.8 0.0 copy-done.10
  10.8 0.1 iota_compare_fusion.3
  10.9 8.2 %all-to-all-done = f32[8,51,128]{2,1,0:T(8,128)S(1)} async-done(((f32[8,51,128]{2,1,0:T(8,128)}), f32[8,51,128]{2,1,0:T(8,128)S(1)}, u32[]{:S(2)}, u32[]{:S(2)}) %all-to-all-start) | async-done | bytes 208928 | tf_op jit(solution)/shard_map/all_to_all | solution.py:22
  19.1 0.0 copy-done.3
  19.1 0.4 convolution_bitcast_fusion.1
  19.5 0.0 copy-done.7
  19.6 0.7 pad_maximum_fusion.2
  20.2 3.3 %all-to-all-start.1 = ((f32[4,50,128]{2,1,0:T(8,128)}), f32[4,50,128]{2,1,0:T(8,128)S(1)}, u32[]{:S(2)}, u32[]{:S(2)}) async-start(f32[4,50,128]{2,1,0:T(8,128)} %pad_maximum_fusion.2), calls=%async_computation.1 | async-start | bytes 229376 | tf_op jit(solution)/shard_map/all_to_all | solution.py:201
  23.6 4.4 %all-to-all-done.1 = f32[4,50,128]{2,1,0:T(8,128)S(1)} async-done(((f32[4,50,128]{2,1,0:T(8,128)}), f32[4,50,128]{2,1,0:T(8,128)S(1)}, u32[]{:S(2)}, u32[]{:S(2)}) %all-to-all-start.1) | async-done | bytes 102432 | tf_op jit(solution)/shard_map/all_to_all | solution.py:201
  28.0 0.0 copy-done.1
  28.0 0.0 copy-done.6
  28.0 0.0 copy-done.9
  28.0 0.3 fusion.16
  28.3 0.9 broadcast_in_dim.29
  29.2 3.5 %all-to-all-start.2 = ((bf16[8,2,128,128]{3,2,1,0:T(8,128)(2,1)}), bf16[8,2,128,128]{3,2,1,0:T(8,128)(2,1)S(1)}, u32[]{:S(2)}, u32[]{:S(2)}) async-start(bf16[8,2,128,128]{3,2,1,0:T(8,128)(2,1)} %broadcast_in_dim.29), calls=%async_computation.2 | async-start | bytes 1048576 | tf_op jit(solution)/shard_map/all_to_all | solution.py:22
  32.8 0.7 collective-permute-start
  33.5 13.6 %all-to-all-done.2 = bf16[8,2,128,128]{3,2,1,0:T(8,128)(2,1)S(1)} async-done(((bf16[8,2,128,128]{3,2,1,0:T(8,128)(2,1)}), bf16[8,2,128,128]{3,2,1,0:T(8,128)(2,1)S(1)}, u32[]{:S(2)}, u32[]{:S(2)}) %all-to-all-start.2) | async-done | bytes 524320 | tf_op jit(solution)/shard_map/all_to_all | solution.py:22
  47.1 0.9 fusion.26
  48.0 1.1 fusion.24
  49.1 0.9 convolution_add_fusion.1
  50.1 1.1 convolution_add_fusion
  51.2 0.8 pad_maximum_fusion
  52.1 3.5 %all-to-all-start.3 = ((f32[4,2,128,128]{3,2,1,0:T(8,128)}), f32[4,2,128,128]{3,2,1,0:T(8,128)S(1)}, u32[]{:S(2)}, u32[]{:S(2)}) async-start(f32[4,2,128,128]{3,2,1,0:T(8,128)} %pad_maximum_fusion), calls=%async_computation.3 | async-start | bytes 1048576 | tf_op jit(solution)/shard_map/all_to_all | solution.py:28
  55.6 0.0 collective-permute-done
  55.6 0.7 gather_fusion
  56.4 0.2 broadcast_select_fusion
  56.5 0.0 copy-done
  56.6 0.5 fusion.49
  57.0 0.0 copy-start.5
  57.0 7.3 %all-to-all-done.3 = f32[4,2,128,128]{3,2,1,0:T(8,128)S(1)} async-done(((f32[4,2,128,128]{3,2,1,0:T(8,128)}), f32[4,2,128,128]{3,2,1,0:T(8,128)S(1)}, u32[]{:S(2)}, u32[]{:S(2)}) %all-to-all-start.3) | async-done | bytes 524320 | tf_op jit(solution)/shard_map/all_to_all | solution.py:28
  64.4 0.0 copy-done.5
  64.4 1.1 fusion.29
  65.5 13.2 %all_to_all.40 = f32[32,16,128]{2,1,0:T(8,128)S(1)} all-to-all(f32[32,16,128]{2,1,0:T(8,128)S(1)} %bitcast.95), channel_id=1, replica_groups=mesh['narrow'=4,'wide'=8] {'narrow','wide'}, dimensions={0} | all-to-all | bytes 524288 | tf_op jit(solution)/shard_map/all_to_all | solution.py:28
  78.7 12.8 %all_to_all.41 = f32[32,16,128]{2,1,0:T(8,128)S(1)} all-to-all(f32[32,16,128]{2,1,0:T(8,128)S(1)} %broadcast_in_dim.33), channel_id=1, replica_groups=mesh['narrow'=4,'wide'=8] {'narrow','wide'}, dimensions={0} | all-to-all | bytes 524288 | tf_op jit(solution)/shard_map/all_to_all | solution.py:22
  91.5 0.6 fusion.15
  92.1 0.0 copy-start.2
  92.1 0.5 fusion.32
  92.6 9.4 %all_to_all.42 = f32[32,4,128]{2,1,0:T(4,128)S(1)} all-to-all(f32[32,4,128]{2,1,0:T(4,128)S(1)} %bitcast.99), channel_id=1, replica_groups=mesh['narrow'=4,'wide'=8] {'narrow','wide'}, dimensions={0} | all-to-all | bytes 131072 | tf_op jit(solution)/shard_map/all_to_all | solution.py:28
  102.1 0.6 broadcast_in_dim.34
  102.7 2.8 %all-to-all-start.7 = ((f32[32,4,128]{2,1,0:T(4,128)}), f32[32,4,128]{2,1,0:T(4,128)S(1)}, u32[]{:S(2)}, u32[]{:S(2)}) async-start(f32[32,4,128]{2,1,0:T(4,128)} %broadcast_in_dim.34), calls=%async_computation.7 | async-start | bytes 131072 | tf_op jit(solution)/shard_map/all_to_all | solution.py:22
  105.5 7.1 %all-to-all-done.7 = f32[32,4,128]{2,1,0:T(4,128)S(1)} async-done(((f32[32,4,128]{2,1,0:T(4,128)}), f32[32,4,128]{2,1,0:T(4,128)S(1)}, u32[]{:S(2)}, u32[]{:S(2)}) %all-to-all-start.7) | async-done | bytes 65568 | tf_op jit(solution)/shard_map/all_to_all | solution.py:22
  112.6 0.0 copy-start.4
  112.6 0.0 copy-done.2
  112.6 0.6 copy-done.4
  113.2 6.2 %shard_map.112 = (f32[128,128]{1,0:T(8,128)}, f32[256,128]{1,0:T(8,128)}) custom-call(f32[128,128]{1,0:T(8,128)} %bitcast.98, f32[256,128]{1,0:T(8,128)} %bitcast.94), custom_call_target="tpu_custom_call" | custom-call | tf_op jit(solution)/shard_map/pallas_call | solution.py:151
  119.4 0.7 copy.28
  (20 shorter events, 0.3 us)
Async XLA Ops:
  0.6 55.9 %copy-start = (bf16[8,12,32,32]{3,2,1,0:T(8,128)(2,1)S(1)}, bf16[8,12,32,32]{3,2,1,0:T(8,128)(2,1)}, u32[]{:S(2)}) copy-start(bf16[8,12,32,32]{3,2,1,0:T(8,128)(2,1)} %param.15) | copy-start | bytes 589828
  0.6 10.0 %copy-start.8 = (s32[8,12]{1,0:T(8,128)S(1)}, s32[8,12]{1,0:T(8,128)}, u32[]{:S(2)}) copy-start(s32[8,12]{1,0:T(8,128)} %param.13) | copy-start | bytes 1156
  0.7 10.1 %copy-start.10 = (s32[8]{0:T(128)S(1)}, s32[8]{0:T(128)}, u32[]{:S(2)}) copy-start(s32[8]{0:T(128)} %param.14) | copy-start | bytes 100
  0.7 18.5 %copy-start.3 = (f32[4,48,384]{2,1,0:T(8,128)S(1)}, f32[4,48,384]{2,1,0:T(8,128)}, u32[]{:S(2)}) copy-start(f32[4,48,384]{2,1,0:T(8,128)} %param.17) | copy-start | bytes 884740
  3.3 16.3 %copy-start.7 = (f32[2,128]{1,0:T(2,128)S(1)}, f32[2,128]{1,0:T(2,128)}, u32[]{:S(2)}) copy-start(f32[2,128]{1,0:T(2,128)} %param.9) | copy-start | bytes 3076
  3.3 15.8 %all-to-all-start = ((f32[8,51,128]{2,1,0:T(8,128)}), f32[8,51,128]{2,1,0:T(8,128)S(1)}, u32[]{:S(2)}, u32[]{:S(2)}) async-start(f32[8,51,128]{2,1,0:T(8,128)} %broadcast_in_dim.23), calls=%async_computation | async-start | bytes 458752 | tf_op jit(solution)/shard_map/all_to_all | solution.py:22
  10.7 17.3 %copy-start.1 = (f32[4,2,128,128]{3,2,1,0:T(8,128)S(1)}, f32[4,2,128,128]{3,2,1,0:T(8,128)}, u32[]{:S(2)}) copy-start(f32[4,2,128,128]{3,2,1,0:T(8,128)} %param.11) | copy-start | bytes 1572868
  10.7 17.3 %copy-start.6 = (s32[2,128]{1,0:T(2,128)S(1)}, s32[2,128]{1,0:T(2,128)}, u32[]{:S(2)}) copy-start(s32[2,128]{1,0:T(2,128)} %param.16) | copy-start | bytes 3076
  10.7 17.3 %copy-start.9 = (f32[2,128]{1,0:T(2,128)S(1)}, f32[2,128]{1,0:T(2,128)}, u32[]{:S(2)}) copy-start(f32[2,128]{1,0:T(2,128)} %param.12) | copy-start | bytes 3076
  20.2 7.7 %all-to-all-start.1 = ((f32[4,50,128]{2,1,0:T(8,128)}), f32[4,50,128]{2,1,0:T(8,128)S(1)}, u32[]{:S(2)}, u32[]{:S(2)}) async-start(f32[4,50,128]{2,1,0:T(8,128)} %pad_maximum_fusion.2), calls=%async_computation.1 | async-start | bytes 229376 | tf_op jit(solution)/shard_map/all_to_all | solution.py:201
  29.2 17.9 %all-to-all-start.2 = ((bf16[8,2,128,128]{3,2,1,0:T(8,128)(2,1)}), bf16[8,2,128,128]{3,2,1,0:T(8,128)(2,1)S(1)}, u32[]{:S(2)}, u32[]{:S(2)}) async-start(bf16[8,2,128,128]{3,2,1,0:T(8,128)(2,1)} %broadcast_in_dim.29), calls=%async_computation.2 | async-start | bytes 1048576 | tf_op jit(solution)/shard_map/all_to_all | solution.py:22
  32.8 22.8 %collective-permute-start = (bf16[2,64,128]{2,1,0:T(8,128)(2,1)S(1)}, bf16[2,64,128]{2,1,0:T(8,128)(2,1)S(1)}, u32[]{:S(2)}, u32[]{:S(2)}) collective-permute-start(bf16[2,64,128]{2,1,0:T(8,128)(2,1)S(1)} %slice_select_fusion.2), channel_id=1, source_target_pairs={{7,8},{8,7},{15,16},{16,15},{23,24},{24,23}} | collective-permute-start | bytes 98312 | tf_op jit(solution)/shard_map/ppermute | solution.py:50
  52.1 12.3 %all-to-all-start.3 = ((f32[4,2,128,128]{3,2,1,0:T(8,128)}), f32[4,2,128,128]{3,2,1,0:T(8,128)S(1)}, u32[]{:S(2)}, u32[]{:S(2)}) async-start(f32[4,2,128,128]{3,2,1,0:T(8,128)} %pad_maximum_fusion), calls=%async_computation.3 | async-start | bytes 1048576 | tf_op jit(solution)/shard_map/all_to_all | solution.py:28
  57.0 7.4 %copy-start.5 = (f32[128]{0:T(128)S(1)}, f32[128]{0:T(128)}, u32[]{:S(2)}) copy-start(f32[128]{0:T(128)} %param.10) | copy-start | bytes 1540
  92.1 20.5 %copy-start.2 = (f32[2,128,128]{2,1,0:T(8,128)}, f32[2,128,128]{2,1,0:T(8,128)S(1)}, u32[]{:S(2)}) copy-start(f32[2,128,128]{2,1,0:T(8,128)S(1)} %fusion.15) | copy-start | bytes 393220
  102.7 9.9 %all-to-all-start.7 = ((f32[32,4,128]{2,1,0:T(4,128)}), f32[32,4,128]{2,1,0:T(4,128)S(1)}, u32[]{:S(2)}, u32[]{:S(2)}) async-start(f32[32,4,128]{2,1,0:T(4,128)} %broadcast_in_dim.34), calls=%async_computation.7 | async-start | bytes 131072 | tf_op jit(solution)/shard_map/all_to_all | solution.py:22
  112.6 0.6 copy-start.4

commit v3 on v2

v3 whole, which is shorter than its diff:
```python
import jax
import jax.numpy as jnp
from jax import lax
from jax.experimental import pallas as pl
from jax.experimental.pallas import tpu as pltpu
from jax.sharding import PartitionSpec as P

SPAN = 4


NU = 0.3
DELTA2 = 1e-05
ELASTIC = 40.0
HIGH = lax.Precision.HIGHEST
AXES = ("narrow", "wide")
EXTRA = 8
ROWS = 8
SMEM = pl.BlockSpec(memory_space=pltpu.SMEM)
VMEM = pl.BlockSpec(memory_space=pltpu.VMEM)
PARAMS = pltpu.CompilerParams(vmem_limit_bytes=48 * 1024 * 1024)


def dot_rows(left, right, precision=HIGH):
    return lax.dot_general(
        left, right, (((1,), (0,)), ((), ())), precision=precision, preferred_element_type=jnp.float32
    )


def dot_first(left, right):
    return lax.dot_general(
        left, right, (((0,), (0,)), ((), ())), precision=HIGH, preferred_element_type=jnp.float32
    )


def as_column(row, width):
    return jnp.transpose(jnp.broadcast_to(row, (width, row.shape[1])))


def swap(block, axis, offset):
    count = lax.axis_size(axis)
    return lax.ppermute(block, axis, [(i, i ^ offset) for i in range(count)])


def gather_relative(block, axis):
    return [block] + [swap(block, axis, k) for k in range(1, lax.axis_size(axis))]


def gather_all(copies, axis):
    return lax.all_to_all(copies, axis, 0, 0, tiled=True)


def restrict_kernel(agg_ref, newest_ref, points_ref, weight_ref, pack_ref):
    coarse_count = pack_ref.shape[0] - EXTRA
    point_count = newest_ref.shape[1]
    ids = lax.broadcasted_iota(jnp.int32, (coarse_count, point_count), 0)
    total = None
    for a in range(2):
        member = jnp.where(ids == agg_ref[a : a + 1, :], 1.0, 0.0)
        term = dot_rows(member, newest_ref[a])
        total = term if total is None else total + term
    pack_ref[:coarse_count, :] = total
    pack_ref[coarse_count:, :] = jnp.concatenate(
        [points_ref[...], weight_ref[...], jnp.zeros((EXTRA - 3, point_count), jnp.float32)], axis=0
    )


def coarse_kernel(index_ref, inverse_ref, points_ref, *refs):
    wide_count = inverse_ref.shape[2] // inverse_ref.shape[1]
    narrow_count = inverse_ref.shape[0]
    coarse_count = inverse_ref.shape[1]
    packs = refs[:wide_count]
    outs = refs[wide_count : wide_count + narrow_count]
    rhs_ref = refs[wide_count + narrow_count]
    narrow_index = index_ref[0]
    wide_index = index_ref[1]
    for k in range(wide_count):
        first = pl.multiple_of((wide_index ^ k) * coarse_count, 8)
        rhs_ref[pl.ds(first, coarse_count), :] = packs[k][:coarse_count, :]
    tail = jnp.concatenate(
        [points_ref[...], jnp.zeros((EXTRA - 2, points_ref.shape[1]), jnp.float32)], axis=0
    )
    for k in range(narrow_count):
        outs[k][:coarse_count, :] = dot_rows(inverse_ref[narrow_index ^ k], rhs_ref[...])
        outs[k][coarse_count:, :] = tail


def precond_kernel(index_ref, agg_ref, jacobi_ref, newest_ref, *refs):
    parts = refs[:-2]
    precond_ref, edge_ref = refs[-2:]
    coarse_count = parts[0].shape[0] - EXTRA
    point_count = newest_ref.shape[1]
    rhs_count = newest_ref.shape[2]
    width = edge_ref.shape[1]
    coarse_sol = parts[0][:coarse_count, :]
    for part in parts[1:]:
        coarse_sol = coarse_sol + part[:coarse_count, :]
    ids = lax.broadcasted_iota(jnp.int32, (coarse_count, point_count), 0)
    for a in range(2):
        member = jnp.where(ids == agg_ref[a : a + 1, :], 1.0, 0.0)
        lifted = dot_first(member, coarse_sol)
        value = as_column(jacobi_ref[a : a + 1, :], rhs_count) * newest_ref[a] + lifted
        precond_ref[a] = value.astype(jnp.bfloat16)
    first = pl.multiple_of(jnp.where(index_ref[1] == 0, 0, point_count - width), 16)
    for a in range(2):
        edge_ref[a] = precond_ref[a, pl.ds(first, width), :]


def matrix_kernel(*refs):
    matrix_ref = refs[-1]
    point_count = refs[0].shape[1]
    source_count = matrix_ref.shape[3] // point_count
    sources = refs[:source_count]
    targets = refs[source_count:-1]
    coarse_count = sources[0].shape[0] - EXTRA
    for k in range(len(targets)):

        @pl.when(pl.program_id(0) == k)
        def _(k=k):
            target = targets[k][coarse_count:, :]
            target_x = as_column(target[0:1, :], point_count)
            target_y = as_column(target[1:2, :], point_count)
            for s in range(source_count):
                source = sources[s][coarse_count:, :]
                delta_x = target_x - source[0:1, :]
                delta_y = target_y - source[1:2, :]
                factor = ELASTIC * source[2:3, :]
                square_x = delta_x * delta_x
                square_y = delta_y * delta_y
                square_dist = square_x + square_y + DELTA2
                inverse = 1.0 / square_dist
                log_part = (-0.5 * (3.0 - 4.0 * NU)) * jnp.log(square_dist)
                lanes = slice(s * point_count, (s + 1) * point_count)
                matrix_ref[0, 0, :, lanes] = (factor * (log_part + square_x * inverse)).astype(
                    jnp.bfloat16
                )
                matrix_ref[0, 1, :, lanes] = (factor * (delta_x * delta_y * inverse)).astype(
                    jnp.bfloat16
                )
                matrix_ref[0, 2, :, lanes] = (factor * (log_part + square_y * inverse)).astype(
                    jnp.bfloat16
                )


def far_kernel(matrix_ref, *refs):
    keep_ref, send_ref, fields_ref = refs[-3:]
    fields = refs[:-3]
    point_count = fields[0].shape[1]
    step = pl.program_id(0)

    @pl.when(step == 0)
    def _():
        for s, field in enumerate(fields):
            for b in range(2):
                fields_ref[b, s * point_count : (s + 1) * point_count, :] = field[b]

    out_x = dot_rows(matrix_ref[0, 0], fields_ref[0], None) + dot_rows(
        matrix_ref[0, 1], fields_ref[1], None
    )
    out_y = dot_rows(matrix_ref[0, 1], fields_ref[0], None) + dot_rows(
        matrix_ref[0, 2], fields_ref[1], None
    )

    @pl.when(step % 2 == 0)
    def _():
        keep_ref[0, 0] = out_x
        keep_ref[0, 1] = out_y

    @pl.when(step % 2 == 1)
    def _():
        send_ref[0, 0] = out_x
        send_ref[0, 1] = out_y


def near_kernel(index_ref, panel_ref, count_ref, block_ref, crossed_ref, *refs):
    out_ref, line_ref, gathered_ref = refs[-3:]
    fields = refs[:-3]
    wide_count = len(fields)
    point_count = fields[0].shape[1]
    width = crossed_ref.shape[1]
    panels_dev, double_nodes, _ = block_ref.shape
    nodes = double_nodes // 2
    slot_total = panel_ref.shape[1]
    wide_index = index_ref[1]
    for b in range(2):
        line_ref[b, :width, :] = crossed_ref[b]
        line_ref[b, width + wide_count * point_count :, :] = crossed_ref[b]
        for k in range(wide_count):
            first = pl.multiple_of((wide_index ^ k) * point_count + width, 16)
            line_ref[b, pl.ds(first, point_count), :] = fields[k][b]
    group_start = index_ref[0] * (wide_count * panels_dev)
    lane = lax.broadcasted_iota(jnp.int32, block_ref.shape[1:], 1)
    for p in range(panels_dev):
        for k in range(slot_total):
            first = pl.multiple_of((panel_ref[p, k] - group_start) * nodes + width, 16)
            for b in range(2):
                row = (k * 2 + b) * nodes
                gathered_ref[p, row : row + nodes, :] = line_ref[b, pl.ds(first, nodes), :]
        blocks = jnp.where(
            lane < count_ref[p] * double_nodes, block_ref[p].astype(jnp.float32), 0.0
        ).astype(jnp.bfloat16)
        near = dot_rows(blocks, gathered_ref[p], None)
        for a in range(2):
            rows = slice(p * nodes, (p + 1) * nodes)
            own = fields[0][a, rows, :].astype(jnp.float32)
            out_ref[a, rows, :] = 0.5 * own + near[a * nodes : (a + 1) * nodes, :]


def project_kernel(weight_ref, basis_ref, base_ref, keep_ref, arrived_ref, image_ref, proj_ref):
    block_total, _, _, rhs_count = basis_ref.shape
    weight = as_column(weight_ref[...], rhs_count)
    weighted = []
    for a in range(2):
        image = base_ref[a] + keep_ref[0, a] + arrived_ref[0, a]
        image_ref[a] = image
        weighted.append(image * weight)
    for j in range(block_total):
        proj_ref[j] = dot_first(basis_ref[j, 0], weighted[0]) + dot_first(
            basis_ref[j, 1], weighted[1]
        )


def sum_kernel(parts_ref, out_ref):
    total = jnp.sum(parts_ref[...], axis=0)
    for k in range(out_ref.shape[0]):
        out_ref[k] = total


def remainder_kernel(weight_ref, basis_ref, image_ref, hess_ref, remainder_ref, gram_ref):
    block_total, _, _, rhs_count = basis_ref.shape
    weight = as_column(weight_ref[...], rhs_count)
    gram = None
    for a in range(2):
        value = image_ref[a]
        for j in range(block_total):
            value = value - dot_rows(basis_ref[j, a], hess_ref[j])
        remainder_ref[a] = value
        term = dot_first(value * weight, value)
        gram = term if gram is None else gram + term
    gram_ref[...] = gram


def factor_kernel(gram_ref, remainder_ref, upper_ref, new_ref, work_ref, inverse_ref):
    order = gram_ref.shape[0]
    tile = (ROWS, order)
    lane = lax.broadcasted_iota(jnp.int32, tile, 1)
    row = lax.broadcasted_iota(jnp.int32, tile, 0)
    work_ref[...] = gram_ref[...]
    for block in range(order // ROWS):
        start = block * ROWS
        inverse_ref[start : start + ROWS, :] = jnp.where(lane == row + start, 1.0, 0.0)
    for block in range(order // ROWS):
        start = block * ROWS
        own = work_ref[start : start + ROWS, :]
        own_inverse = inverse_ref[start : start + ROWS, :]
        columns = [
            jnp.broadcast_to(own[:, start + m : start + m + 1], tile) for m in range(ROWS)
        ]
        entry = {
            (j, m): jnp.broadcast_to(columns[m][j : j + 1, :], tile)
            for m in range(ROWS)
            for j in range(m, ROWS)
        }
        scale = []
        for m in range(ROWS):
            scale.append(lax.rsqrt(entry[m, m]))
            for j in range(m + 1, ROWS):
                entry[j, m] = entry[j, m] * scale[m]
            for n in range(m + 1, ROWS):
                for j in range(n, ROWS):
                    entry[j, n] = entry[j, n] - entry[j, m] * entry[n, m]
        solved = []
        solved_inverse = []
        for m in range(ROWS):
            upper_row = jnp.broadcast_to(own[m : m + 1, :], tile)
            inverse_row = jnp.broadcast_to(own_inverse[m : m + 1, :], tile)
            for j in range(m):
                upper_row = upper_row - entry[m, j] * solved[j]
                inverse_row = inverse_row - entry[m, j] * solved_inverse[j]
            upper_row = upper_row * scale[m]
            inverse_row = inverse_row * scale[m]
            solved.append(upper_row)
            solved_inverse.append(inverse_row)
        upper_rows = solved[ROWS - 1]
        inverse_rows = solved_inverse[ROWS - 1]
        for m in range(ROWS - 1):
            upper_rows = jnp.where(row == m, solved[m], upper_rows)
            inverse_rows = jnp.where(row == m, solved_inverse[m], inverse_rows)
        upper_ref[start : start + ROWS, :] = jnp.where(lane >= row + start, upper_rows, 0.0)
        inverse_ref[start : start + ROWS, :] = inverse_rows
        for later in range(block + 1, order // ROWS):
            first = later * ROWS
            target = work_ref[first : first + ROWS, :]
            target_inverse = inverse_ref[first : first + ROWS, :]
            multiplier = []
            for m in range(ROWS):
                value = jnp.broadcast_to(target[:, start + m : start + m + 1], tile)
                for j in range(m):
                    value = value - multiplier[j] * entry[m, j]
                multiplier.append(value * scale[m])
            for m in range(ROWS):
                target = target - multiplier[m] * solved[m]
                target_inverse = target_inverse - multiplier[m] * solved_inverse[m]
            work_ref[first : first + ROWS, :] = target
            inverse_ref[first : first + ROWS, :] = target_inverse
    new_ref[...] = lax.dot_general(
        remainder_ref[...],
        inverse_ref[...],
        (((1,), (1,)), ((), ())),
        precision=HIGH,
        preferred_element_type=jnp.float32,
    )


def factor_and_solve(gram_matrix, remainder):
    order = gram_matrix.shape[0]
    return pl.pallas_call(
        factor_kernel,
        out_shape=(
            jax.ShapeDtypeStruct(gram_matrix.shape, jnp.float32),
            jax.ShapeDtypeStruct(remainder.shape, jnp.float32),
        ),
        scratch_shapes=[
            pltpu.VMEM((order, order), jnp.float32),
            pltpu.VMEM((order, order), jnp.float32),
        ],
    )(gram_matrix, remainder)


def f32(*shape):
    return jax.ShapeDtypeStruct(shape, jnp.float32)


def b16(*shape):
    return jax.ShapeDtypeStruct(shape, jnp.bfloat16)


def call(kernel, out_shape, operands, scalars=0, scratch=()):
    many = isinstance(out_shape, (tuple, list))
    return pl.pallas_call(
        kernel,
        out_shape=out_shape,
        in_specs=[SMEM] * scalars + [VMEM] * (len(operands) - scalars),
        out_specs=[VMEM] * len(out_shape) if many else VMEM,
        scratch_shapes=list(scratch),
        compiler_params=PARAMS,
    )(*operands)


def sum_everywhere(block):
    count = lax.axis_size(AXES)
    if block.shape[0] % count:
        return lax.psum(block, AXES)
    parts = block.reshape((count, block.shape[0] // count) + block.shape[1:])
    parts = lax.all_to_all(parts, AXES, 0, 0, tiled=True)
    copies = call(sum_kernel, f32(*parts.shape), (parts,))
    return gather_all(copies, AXES).reshape(block.shape)


def body(
    points,
    quad_weight,
    basis,
    jacobi,
    near_panel,
    near_count,
    near_block,
    agg_index,
    coarse_inverse,
):
    block_total, _, point_count, rhs_count = basis.shape
    coarse_count = coarse_inverse.shape[1]
    narrow_count = lax.axis_size("narrow")
    wide_count = lax.axis_size("wide")
    panels_dev, slot_total = near_panel.shape
    nodes = near_block.shape[2] // 2
    width = SPAN * nodes
    pack_rows = coarse_count + EXTRA
    index = jnp.stack([lax.axis_index("narrow"), lax.axis_index("wide")]).astype(jnp.int32)
    newest = basis[block_total - 1]
    weight_row = quad_weight[None, :]

    pack = call(
        restrict_kernel, f32(pack_rows, point_count), (agg_index, newest, points, weight_row)
    )
    packs = gather_relative(pack, "wide")
    parts = call(
        coarse_kernel,
        [f32(pack_rows, rhs_count)] * narrow_count,
        (index, coarse_inverse, points, *packs),
        1,
        [pltpu.VMEM((wide_count * coarse_count, rhs_count), jnp.float32)],
    )
    arrived = [parts[0]] + [swap(parts[k], "narrow", k) for k in range(1, narrow_count)]
    precond, edge = call(
        precond_kernel,
        [b16(2, point_count, rhs_count), b16(2, width, rhs_count)],
        (index, agg_index, jacobi, newest, *arrived),
        1,
    )
    pairs = []
    for group in range(narrow_count - 1):
        left = group * wide_count + wide_count - 1
        pairs += [(left, left + 1), (left + 1, left)]
    fields = gather_relative(precond, "wide")
    crossed = lax.ppermute(edge, AXES, pairs)

    source_total = wide_count * point_count
    matrix = pl.pallas_call(
        matrix_kernel,
        out_shape=b16(narrow_count, 3, point_count, source_total),
        grid=(narrow_count,),
        in_specs=[VMEM] * (wide_count + narrow_count),
        out_specs=pl.BlockSpec((1, 3, point_count, source_total), lambda k: (k, 0, 0, 0)),
        compiler_params=PARAMS,
    )(*packs, *arrived)
    half = f32(narrow_count // 2, 2, point_count, rhs_count)
    half_spec = pl.BlockSpec((1, 2, point_count, rhs_count), lambda k: (k // 2, 0, 0, 0))
    keep, send = pl.pallas_call(
        far_kernel,
        out_shape=[half, half],
        grid=(narrow_count,),
        in_specs=[pl.BlockSpec((1, 3, point_count, source_total), lambda k: (k, 0, 0, 0))]
        + [VMEM] * wide_count,
        out_specs=[half_spec, half_spec],
        scratch_shapes=[pltpu.VMEM((2, source_total, rhs_count), jnp.bfloat16)],
        compiler_params=PARAMS,
    )(matrix, *fields)
    offset = 1
    got = swap(send, "narrow", offset)
    while keep.shape[0] > 1:
        offset *= 2
        send = keep[1::2] + got[1::2]
        keep = keep[0::2] + got[0::2]
        got = swap(send, "narrow", offset)
    near_rows = jnp.transpose(near_block, (0, 2, 1, 3)).reshape(
        panels_dev, 2 * nodes, slot_total * 2 * nodes
    )
    base = call(
        near_kernel,
        f32(2, point_count, rhs_count),
        (index, near_panel, near_count, near_rows, crossed, *fields),
        3,
        [
            pltpu.VMEM((2, 2 * width + source_total, rhs_count), jnp.bfloat16),
            pltpu.VMEM((panels_dev, slot_total * 2 * nodes, rhs_count), jnp.bfloat16),
        ],
    )
    image, local_proj = call(
        project_kernel,
        [f32(2, point_count, rhs_count), f32(block_total, rhs_count, rhs_count)],
        (weight_row, basis, base, keep, got),
    )
    hessenberg = sum_everywhere(local_proj.reshape(block_total * rhs_count, rhs_count)).reshape(
        block_total, rhs_count, rhs_count
    )
    remainder, local_gram = call(
        remainder_kernel,
        [f32(2, point_count, rhs_count), f32(rhs_count, rhs_count)],
        (weight_row, basis, image, hessenberg),
    )
    gram_matrix = sum_everywhere(local_gram)
    upper_factor, new_block = factor_and_solve(
        gram_matrix, remainder.reshape(2 * point_count, rhs_count)
    )
    return (new_block.reshape(2, point_count, rhs_count), hessenberg, upper_factor)


def solution(mesh):
    in_specs = (
        P(None, ("narrow", "wide")),
        P(("narrow", "wide")),
        P(None, None, ("narrow", "wide"), None),
        P(None, ("narrow", "wide")),
        P(("narrow", "wide"), None),
        P(("narrow", "wide")),
        P(("narrow", "wide"), None, None, None),
        P(None, ("narrow", "wide")),
        P(None, "wide", "narrow"),
    )
    out_specs = (P(None, ("narrow", "wide"), None), P(), P())
    return jax.shard_map(body, mesh=mesh, in_specs=in_specs, out_specs=out_specs, check_vma=False)
```

time: 121 us -> 117 us (0.967)
  waiting for transfers between devices: 40.7 us -> 14.8 us
  blocking collectives: 35.4 us -> 50.9 us
  Pallas kernels: 6.25 us -> 15 us
  matrix products: 8.53 us -> 0 us
  starting transfers between devices: 21.1 us -> 27.1 us
  local copies, waits for them, and re-layouts: 4.57 us -> 7.66 us
  other arithmetic: 2.64 us -> 0.1 us
    all_to_all x5 -> x0, waiting for transfers between devices: 40.7 us -> none  [the longest x3 28.9 us: gather_all(): lax.all_to_all(jnp.broadcast_to(block[None], (count,) + block.shape), axi...]
    ppermute x1 -> x20, starting transfers between devices: 0.66 us -> 27.1 us  [the longest x19 26.5 us: swap(): return lax.ppermute(block, axis, [(i, i ^ offset) for i in range(count)])]
    all_to_all x5 -> x0, starting transfers between devices: 20.4 us -> none  [the longest x3 13.6 us: gather_all(): lax.all_to_all(jnp.broadcast_to(block[None], (count,) + block.shape), axi...]
    all_to_all x3 -> x4, blocking collectives: 35.4 us -> 50.9 us  [the longest x2 28.5 us: sum_everywhere(): parts = lax.all_to_all(parts, AXES, 0, 0, tiled=True)]
    ppermute x1 -> x20, waiting for transfers between devices: 0.01 us -> 14.8 us  [the longest x19 14.8 us: swap(): return lax.ppermute(block, axis, [(i, i ^ offset) for i in range(count)])]
    pallas_call x0 -> x10, Pallas kernels: none -> 8.78 us  [the longest x8 5.06 us: call(): pl.pallas_call(kernel, out_shape=out_shape, in_specs=[SMEM] * scalars + [...]
    dot_general x11 -> x0, matrix products: 8.53 us -> none  [the longest x4 4.07 us: dot32(): return jnp.dot(left, right, preferred_element_type=jnp.float32)]
    unnamed x23 -> x27, local copies, waits for them, and re-layouts: 1.38 us -> 5.74 us
  transfers between devices with their start and end apart: 6 -> 20, of which waited for: 5 -> 8; matrix products, arithmetic and copies ran while one was open for 5% -> 1% of each run, Pallas kernels for 0% -> 3%
where the time goes in v3:
time: 117 us
  blocking collectives  50.9 us (44%)
  starting transfers between devices  27.1 us (23%)
  Pallas kernels  15 us (13%)
  waiting for transfers between devices  14.8 us (13%)
  local copies, waits for them, and re-layouts  7.66 us (7%)
    all_to_all x2, blocking collectives, sum_everywhere(): parts = lax.all_to_all(parts, AXES, 0, 0, tiled=True)  28.5 us
    ppermute x19, starting transfers between devices, swap(): return lax.ppermute(block, axis, [(i, i ^ offset) for i in range(count)])  26.5 us
    all_to_all x2, blocking collectives, gather_all(): return lax.all_to_all(copies, axis, 0, 0, tiled=True)  22.4 us
    ppermute x19, waiting for transfers between devices, swap(): return lax.ppermute(block, axis, [(i, i ^ offset) for i in range(count)])  14.8 us
    pallas_call x1, Pallas kernels, factor_and_solve(): pl.pallas_call(factor_kernel, out_shape=(jax.ShapeDtypeStruct(gram_matrix...  6.25 us
    unnamed x27, local copies, waits for them, and re-layouts  5.74 us
    pallas_call x8, Pallas kernels, call(): pl.pallas_call(kernel, out_shape=out_shape, in_specs=[SMEM] * scalars + [...  5.06 us
  transfers between devices with their start and end apart: 20, of which 8 were waited for; matrix products, arithmetic and copies ran while one was open for 1% of the time, Pallas kernels for 3%

profile of v3, /device:TPU:0, one launch (start us, length us, event | category | flops | bytes accessed | tf_op | source)
XLA Modules:
  0.0 116.6 jit_solution(7170818896077768487)
XLA Ops:
  0.6 0.9 slice_bitcast_fusion.newest_ref
  1.5 0.0 copy-start.3
  1.6 0.6 copy-done.3
  2.2 0.7 copy-done.6
  2.9 0.7 copy-done.8
  3.6 0.2 shard_map.112.refs_0_
  3.8 2.9 %collective-permute-start = (f32[56,128]{1,0:T(8,128)S(1)}, f32[56,128]{1,0:T(8,128)S(1)}, u32[]{:S(2)}, u32[]{:S(2)}) collective-permute-start(f32[56,128]{1,0:T(8,128)S(1)} %shard_map.112.refs_0_), channel_id=1, source_target_pairs={{0,1},{1,0},{2,3},{3,2},{4,5},{5,4},{6,7},{7,6},{8,9},{9,8},{10,11... | collective-permute-start | bytes 86024 | tf_op jit(solution)/shard_map/ppermute | solution.py:41
  6.7 1.6 %collective-permute-start.1 = (f32[56,128]{1,0:T(8,128)S(1)}, f32[56,128]{1,0:T(8,128)S(1)}, u32[]{:S(2)}, u32[]{:S(2)}) collective-permute-start(f32[56,128]{1,0:T(8,128)S(1)} %shard_map.112.refs_0_), channel_id=1, source_target_pairs={{0,2},{1,3},{2,0},{3,1},{4,6},{5,7},{6,4},{7,5},{8,10},{9,11},{10,... | collective-permute-start | bytes 86024 | tf_op jit(solution)/shard_map/ppermute | solution.py:41
  8.3 0.0 collective-permute-start.2
  8.3 3.0 %collective-permute-start.3 = (f32[56,128]{1,0:T(8,128)S(1)}, f32[56,128]{1,0:T(8,128)S(1)}, u32[]{:S(2)}, u32[]{:S(2)}) collective-permute-start(f32[56,128]{1,0:T(8,128)S(1)} %shard_map.112.refs_0_), channel_id=1, source_target_pairs={{0,4},{1,5},{2,6},{3,7},{4,0},{5,1},{6,2},{7,3},{8,12},{9,13},{10,... | collective-permute-start | bytes 86024 | tf_op jit(solution)/shard_map/ppermute | solution.py:41
  11.3 1.3 %collective-permute-start.4 = (f32[56,128]{1,0:T(8,128)S(1)}, f32[56,128]{1,0:T(8,128)S(1)}, u32[]{:S(2)}, u32[]{:S(2)}) collective-permute-start(f32[56,128]{1,0:T(8,128)S(1)} %shard_map.112.refs_0_), channel_id=1, source_target_pairs={{0,5},{1,4},{2,7},{3,6},{4,1},{5,0},{6,3},{7,2},{8,13},{9,12},{10,... | collective-permute-start | bytes 86024 | tf_op jit(solution)/shard_map/ppermute | solution.py:41
  12.6 0.0 collective-permute-done.refs_1_
  12.6 3.6 %collective-permute-start.5 = (f32[56,128]{1,0:T(8,128)S(1)}, f32[56,128]{1,0:T(8,128)S(1)}, u32[]{:S(2)}, u32[]{:S(2)}) collective-permute-start(f32[56,128]{1,0:T(8,128)S(1)} %shard_map.112.refs_0_), channel_id=1, source_target_pairs={{0,6},{1,7},{2,4},{3,5},{4,2},{5,3},{6,0},{7,1},{8,14},{9,15},{10,... | collective-permute-start | bytes 86024 | tf_op jit(solution)/shard_map/ppermute | solution.py:41
  16.2 0.0 collective-permute-done.1.refs_2_
  16.2 0.0 collective-permute-start.6
  16.2 0.1 pad_add_fusion.index_ref
  16.3 0.0 collective-permute-done.2.refs_3_
  16.3 0.0 collective-permute-done.3.refs_4_
  16.3 0.8 collective-permute-done.4.refs_5_
  17.2 1.2 %collective-permute-done.5.refs_6_ = f32[56,128]{1,0:T(8,128)S(1)} collective-permute-done((f32[56,128]{1,0:T(8,128)S(1)}, f32[56,128]{1,0:T(8,128)S(1)}, u32[]{:S(2)}, u32[]{:S(2)}) %collective-permute-start.5) | collective-permute-done | bytes 28704 | tf_op jit(solution)/shard_map/ppermute | solution.py:41
  18.3 4.4 %collective-permute-done.6.refs_7_ = f32[56,128]{1,0:T(8,128)S(1)} collective-permute-done((f32[56,128]{1,0:T(8,128)S(1)}, f32[56,128]{1,0:T(8,128)S(1)}, u32[]{:S(2)}, u32[]{:S(2)}) %collective-permute-start.6) | collective-permute-done | bytes 28704 | tf_op jit(solution)/shard_map/ppermute | solution.py:41
  22.8 1.0 copy-done.1
  23.7 0.7 copy-done.7
  24.4 1.1 shard_map.113
  25.5 0.1 collective-permute-start.7
  25.6 1.6 %collective-permute-start.8 = (f32[56,128]{1,0:T(8,128)S(1)}, f32[56,128]{1,0:T(8,128)S(1)}, u32[]{:S(2)}, u32[]{:S(2)}) collective-permute-start(f32[56,128]{1,0:T(8,128)S(1)} %get-tuple-element.19), channel_id=1, source_target_pairs={{0,16},{8,24},{16,0},{24,8},{1,17},{9,25},{17,1},{25,9},{2,18},{10... | collective-permute-start | bytes 86024 | tf_op jit(solution)/shard_map/ppermute | solution.py:41
  27.2 0.3 collective-permute-start.9
  27.5 2.1 %collective-permute-done.8.refs_2_.refs_10_ = f32[56,128]{1,0:T(8,128)S(1)} collective-permute-done((f32[56,128]{1,0:T(8,128)S(1)}, f32[56,128]{1,0:T(8,128)S(1)}, u32[]{:S(2)}, u32[]{:S(2)}) %collective-permute-start.8) | collective-permute-done | bytes 28704 | tf_op jit(solution)/shard_map/ppermute | solution.py:41
  29.5 0.9 collective-permute-done.9.refs_3_.refs_11_
  30.5 0.7 copy-done.9
  31.2 0.7 copy-done.10
  31.9 0.9 shard_map.114
  32.7 0.0 copy-start.12
  32.7 0.6 collective-permute-start.11
  33.3 3.0 %collective-permute-start.13 = (bf16[2,128,128]{2,1,0:T(8,128)(2,1)S(1)}, bf16[2,128,128]{2,1,0:T(8,128)(2,1)S(1)}, u32[]{:S(2)}, u32[]{:S(2)}) collective-permute-start(bf16[2,128,128]{2,1,0:T(8,128)(2,1)S(1)} %get-tuple-element.22.refs_0_), channel_id=1, source_target_pairs={{0,3},{1,2},{2,1},{3,0},{4,7},{5,6},{6,5},{7,4},{8,11},{9,10},{10,... | collective-permute-start | bytes 196616 | tf_op jit(solution)/shard_map/ppermute | solution.py:41
  36.3 0.0 collective-permute-start.14
  36.3 2.9 %collective-permute-start.15 = (bf16[2,128,128]{2,1,0:T(8,128)(2,1)S(1)}, bf16[2,128,128]{2,1,0:T(8,128)(2,1)S(1)}, u32[]{:S(2)}, u32[]{:S(2)}) collective-permute-start(bf16[2,128,128]{2,1,0:T(8,128)(2,1)S(1)} %get-tuple-element.22.refs_0_), channel_id=1, source_target_pairs={{0,5},{1,4},{2,7},{3,6},{4,1},{5,0},{6,3},{7,2},{8,13},{9,12},{10,... | collective-permute-start | bytes 196616 | tf_op jit(solution)/shard_map/ppermute | solution.py:41
  39.2 0.3 collective-permute-start.16
  39.5 4.4 %collective-permute-start.17 = (bf16[2,128,128]{2,1,0:T(8,128)(2,1)S(1)}, bf16[2,128,128]{2,1,0:T(8,128)(2,1)S(1)}, u32[]{:S(2)}, u32[]{:S(2)}) collective-permute-start(bf16[2,128,128]{2,1,0:T(8,128)(2,1)S(1)} %get-tuple-element.22.refs_0_), channel_id=1, source_target_pairs={{0,7},{1,6},{2,5},{3,4},{4,3},{5,2},{6,1},{7,0},{8,15},{9,14},{10,... | collective-permute-start | bytes 196616 | tf_op jit(solution)/shard_map/ppermute | solution.py:41
  44.0 1.9 %shard_map.116.matrix_ref = bf16[4,3,128,1024]{3,2,1,0:T(8,128)(2,1)S(1)} custom-call(f32[56,128]{1,0:T(8,128)S(1)} %shard_map.112.refs_0_, f32[56,128]{1,0:T(8,128)S(1)} %collective-permute-done.refs_1_, f32[56,128]{1,0:T(8,128)S(1)} %collective-permute-done.1.refs_2_, f32[56,128]{1,0:T(8,128)S(1)} %collective-permute-done.2.refs_3_, ...), custom_call_target="tpu_custom_call" | custom-call | tf_op jit(solution)/shard_map/pallas_call | solution.py:408
  45.9 0.0 copy-start.5
  45.9 0.0 copy-start.11
  45.9 1.8 %collective-permute-done.15.refs_5_ = bf16[2,128,128]{2,1,0:T(8,128)(2,1)S(1)} collective-permute-done((bf16[2,128,128]{2,1,0:T(8,128)(2,1)S(1)}, bf16[2,128,128]{2,1,0:T(8,128)(2,1)S(1)}, u32[]{:S(2)}, u32[]{:S(2)}) %collective-permute-start.15) | collective-permute-done | bytes 65568 | tf_op jit(solution)/shard_map/ppermute | solution.py:41
  47.7 1.8 %shard_map.117 = (f32[2,2,128,128]{3,2,1,0:T(8,128)S(1)}, f32[2,2,128,128]{3,2,1,0:T(8,128)S(1)}) custom-call(bf16[4,3,128,1024]{3,2,1,0:T(8,128)(2,1)S(1)} %shard_map.116.matrix_ref, bf16[2,128,128]{2,1,0:T(8,128)(2,1)S(1)} %get-tuple-element.22.refs_0_, bf16[2,128,128]{2,1,0:T(8,128)(2,1)S(1)} %collective-permute-done.11.refs_1_, ...), custom_call_target="tpu_custom_call" | custom-call | tf_op jit(solution)/shard_map/pallas_call | solution.py:418
  49.6 0.0 copy-start
  49.6 0.0 copy-start.4
  49.6 0.1 collective-permute-start.18
  49.7 1.5 %collective-permute-done.18 = f32[2,2,128,128]{3,2,1,0:T(8,128)S(1)} collective-permute-done((f32[2,2,128,128]{3,2,1,0:T(8,128)S(1)}, f32[2,2,128,128]{3,2,1,0:T(8,128)S(1)}, u32[]{:S(2)}, u32[]{:S(2)}) %collective-permute-start.18) | collective-permute-done | bytes 262176 | tf_op jit(solution)/shard_map/ppermute | solution.py:41
  51.2 0.8 collective-permute-start.19
  52.1 0.7 collective-permute-start.10
  52.7 0.3 copy.13
  53.1 0.7 reshape.21.block_ref
  53.8 1.0 shard_map.115.base_ref
  54.8 2.0 %collective-permute-done.19.arrived_ref = f32[1,2,128,128]{3,2,1,0:T(8,128)S(1)} collective-permute-done((f32[1,2,128,128]{3,2,1,0:T(8,128)S(1)}, f32[1,2,128,128]{3,2,1,0:T(8,128)S(1)}, u32[]{:S(2)}, u32[]{:S(2)}) %collective-permute-start.19) | collective-permute-done | bytes 131104 | tf_op jit(solution)/shard_map/ppermute | solution.py:41
  56.8 0.7 shard_map.118
  57.5 19.0 %all_to_all.20.parts_ref = f32[32,16,128]{2,1,0:T(8,128)S(1)} all-to-all(f32[32,16,128]{2,1,0:T(8,128)S(1)} %bitcast.14), channel_id=1, replica_groups=mesh['narrow'=4,'wide'=8] {'narrow','wide'}, dimensions={0} | all-to-all | bytes 524288 | tf_op jit(solution)/shard_map/all_to_all | solution.py:354
  76.6 0.1 shard_map.119
  76.6 12.8 %all_to_all.21 = f32[32,16,128]{2,1,0:T(8,128)S(1)} all-to-all(f32[32,16,128]{2,1,0:T(8,128)S(1)} %shard_map.119), channel_id=1, replica_groups=mesh['narrow'=4,'wide'=8] {'narrow','wide'}, dimensions={0} | all-to-all | bytes 524288 | tf_op jit(solution)/shard_map/all_to_all | solution.py:49
  89.4 1.0 shard_map.120
  90.5 0.0 copy-start.2
  90.5 9.4 %all_to_all.22.parts_ref = f32[32,4,128]{2,1,0:T(4,128)S(1)} all-to-all(f32[32,4,128]{2,1,0:T(4,128)S(1)} %bitcast.16), channel_id=1, replica_groups=mesh['narrow'=4,'wide'=8] {'narrow','wide'}, dimensions={0} | all-to-all | bytes 131072 | tf_op jit(solution)/shard_map/all_to_all | solution.py:354
  100.0 9.6 %all_to_all.23 = f32[32,4,128]{2,1,0:T(4,128)} all-to-all(f32[32,4,128]{2,1,0:T(4,128)S(1)} %shard_map.121), channel_id=1, replica_groups=mesh['narrow'=4,'wide'=8] {'narrow','wide'}, dimensions={0} | all-to-all | bytes 131072 | tf_op jit(solution)/shard_map/all_to_all | solution.py:49
  109.6 6.2 %shard_map.122 = (f32[128,128]{1,0:T(8,128)}, f32[256,128]{1,0:T(8,128)}) custom-call(f32[128,128]{1,0:T(8,128)} %bitcast.21, f32[256,128]{1,0:T(8,128)} %bitcast.15), custom_call_target="tpu_custom_call" | custom-call | tf_op jit(solution)/shard_map/pallas_call | solution.py:316
  115.9 0.7 copy.15
  (23 shorter events, 0.1 us)
Async XLA Ops:
  1.5 0.7 copy-start.3
  2.2 0.7 copy-start.6
  2.9 0.7 copy-start.8
  3.8 8.8 %collective-permute-start = (f32[56,128]{1,0:T(8,128)S(1)}, f32[56,128]{1,0:T(8,128)S(1)}, u32[]{:S(2)}, u32[]{:S(2)}) collective-permute-start(f32[56,128]{1,0:T(8,128)S(1)} %shard_map.112.refs_0_), channel_id=1, source_target_pairs={{0,1},{1,0},{2,3},{3,2},{4,5},{5,4},{6,7},{7,6},{8,9},{9,8},{10,11... | collective-permute-start | bytes 86024 | tf_op jit(solution)/shard_map/ppermute | solution.py:41
  6.7 9.5 %collective-permute-start.1 = (f32[56,128]{1,0:T(8,128)S(1)}, f32[56,128]{1,0:T(8,128)S(1)}, u32[]{:S(2)}, u32[]{:S(2)}) collective-permute-start(f32[56,128]{1,0:T(8,128)S(1)} %shard_map.112.refs_0_), channel_id=1, source_target_pairs={{0,2},{1,3},{2,0},{3,1},{4,6},{5,7},{6,4},{7,5},{8,10},{9,11},{10,... | collective-permute-start | bytes 86024 | tf_op jit(solution)/shard_map/ppermute | solution.py:41
  8.3 8.0 %collective-permute-start.2 = (f32[56,128]{1,0:T(8,128)S(1)}, f32[56,128]{1,0:T(8,128)S(1)}, u32[]{:S(2)}, u32[]{:S(2)}) collective-permute-start(f32[56,128]{1,0:T(8,128)S(1)} %shard_map.112.refs_0_), channel_id=1, source_target_pairs={{0,3},{1,2},{2,1},{3,0},{4,7},{5,6},{6,5},{7,4},{8,11},{9,10},{10,... | collective-permute-start | bytes 86024 | tf_op jit(solution)/shard_map/ppermute | solution.py:41
  8.3 8.0 %collective-permute-start.3 = (f32[56,128]{1,0:T(8,128)S(1)}, f32[56,128]{1,0:T(8,128)S(1)}, u32[]{:S(2)}, u32[]{:S(2)}) collective-permute-start(f32[56,128]{1,0:T(8,128)S(1)} %shard_map.112.refs_0_), channel_id=1, source_target_pairs={{0,4},{1,5},{2,6},{3,7},{4,0},{5,1},{6,2},{7,3},{8,12},{9,13},{10,... | collective-permute-start | bytes 86024 | tf_op jit(solution)/shard_map/ppermute | solution.py:41
  11.3 5.8 %collective-permute-start.4 = (f32[56,128]{1,0:T(8,128)S(1)}, f32[56,128]{1,0:T(8,128)S(1)}, u32[]{:S(2)}, u32[]{:S(2)}) collective-permute-start(f32[56,128]{1,0:T(8,128)S(1)} %shard_map.112.refs_0_), channel_id=1, source_target_pairs={{0,5},{1,4},{2,7},{3,6},{4,1},{5,0},{6,3},{7,2},{8,13},{9,12},{10,... | collective-permute-start | bytes 86024 | tf_op jit(solution)/shard_map/ppermute | solution.py:41
  12.6 5.8 %collective-permute-start.5 = (f32[56,128]{1,0:T(8,128)S(1)}, f32[56,128]{1,0:T(8,128)S(1)}, u32[]{:S(2)}, u32[]{:S(2)}) collective-permute-start(f32[56,128]{1,0:T(8,128)S(1)} %shard_map.112.refs_0_), channel_id=1, source_target_pairs={{0,6},{1,7},{2,4},{3,5},{4,2},{5,3},{6,0},{7,1},{8,14},{9,15},{10,... | collective-permute-start | bytes 86024 | tf_op jit(solution)/shard_map/ppermute | solution.py:41
  16.2 6.6 %collective-permute-start.6 = (f32[56,128]{1,0:T(8,128)S(1)}, f32[56,128]{1,0:T(8,128)S(1)}, u32[]{:S(2)}, u32[]{:S(2)}) collective-permute-start(f32[56,128]{1,0:T(8,128)S(1)} %shard_map.112.refs_0_), channel_id=1, source_target_pairs={{0,7},{1,6},{2,5},{3,4},{4,3},{5,2},{6,1},{7,0},{8,15},{9,14},{10,... | collective-permute-start | bytes 86024 | tf_op jit(solution)/shard_map/ppermute | solution.py:41
  22.8 1.0 copy-start.1
  23.7 0.7 copy-start.7
  25.5 1.9 %collective-permute-start.7 = (f32[56,128]{1,0:T(8,128)S(1)}, f32[56,128]{1,0:T(8,128)S(1)}, u32[]{:S(2)}, u32[]{:S(2)}) collective-permute-start(f32[56,128]{1,0:T(8,128)S(1)} %get-tuple-element.18), channel_id=1, source_target_pairs={{0,8},{8,0},{16,24},{24,16},{1,9},{9,1},{17,25},{25,17},{2,10},{10... | collective-permute-start | bytes 86024 | tf_op jit(solution)/shard_map/ppermute | solution.py:41
  25.6 3.9 %collective-permute-start.8 = (f32[56,128]{1,0:T(8,128)S(1)}, f32[56,128]{1,0:T(8,128)S(1)}, u32[]{:S(2)}, u32[]{:S(2)}) collective-permute-start(f32[56,128]{1,0:T(8,128)S(1)} %get-tuple-element.19), channel_id=1, source_target_pairs={{0,16},{8,24},{16,0},{24,8},{1,17},{9,25},{17,1},{25,9},{2,18},{10... | collective-permute-start | bytes 86024 | tf_op jit(solution)/shard_map/ppermute | solution.py:41
  27.2 3.3 %collective-permute-start.9 = (f32[56,128]{1,0:T(8,128)S(1)}, f32[56,128]{1,0:T(8,128)S(1)}, u32[]{:S(2)}, u32[]{:S(2)}) collective-permute-start(f32[56,128]{1,0:T(8,128)S(1)} %get-tuple-element.20), channel_id=1, source_target_pairs={{0,24},{8,16},{16,8},{24,0},{1,25},{9,17},{17,9},{25,1},{2,26},{10... | collective-permute-start | bytes 86024 | tf_op jit(solution)/shard_map/ppermute | solution.py:41
  30.5 0.7 copy-start.9
  31.2 0.7 copy-start.10
  32.7 20.0 %copy-start.12 = (bf16[8,12,32,32]{3,2,1,0:T(8,128)(2,1)S(1)}, bf16[8,12,32,32]{3,2,1,0:T(8,128)(2,1)}, u32[]{:S(2)}) copy-start(bf16[8,12,32,32]{3,2,1,0:T(8,128)(2,1)} %param.15) | copy-start | bytes 589828
  32.7 6.5 %collective-permute-start.11 = (bf16[2,128,128]{2,1,0:T(8,128)(2,1)S(1)}, bf16[2,128,128]{2,1,0:T(8,128)(2,1)S(1)}, u32[]{:S(2)}, u32[]{:S(2)}) collective-permute-start(bf16[2,128,128]{2,1,0:T(8,128)(2,1)S(1)} %get-tuple-element.22.refs_0_), channel_id=1, source_target_pairs={{0,1},{1,0},{2,3},{3,2},{4,5},{5,4},{6,7},{7,6},{8,9},{9,8},{10,11... | collective-permute-start | bytes 196616 | tf_op jit(solution)/shard_map/ppermute | solution.py:41
  33.3 6.2 %collective-permute-start.12 = (bf16[2,128,128]{2,1,0:T(8,128)(2,1)S(1)}, bf16[2,128,128]{2,1,0:T(8,128)(2,1)S(1)}, u32[]{:S(2)}, u32[]{:S(2)}) collective-permute-start(bf16[2,128,128]{2,1,0:T(8,128)(2,1)S(1)} %get-tuple-element.22.refs_0_), channel_id=1, source_target_pairs={{0,2},{1,3},{2,0},{3,1},{4,6},{5,7},{6,4},{7,5},{8,10},{9,11},{10,... | collective-permute-start | bytes 196616 | tf_op jit(solution)/shard_map/ppermute | solution.py:41
  33.3 12.5 %collective-permute-start.13 = (bf16[2,128,128]{2,1,0:T(8,128)(2,1)S(1)}, bf16[2,128,128]{2,1,0:T(8,128)(2,1)S(1)}, u32[]{:S(2)}, u32[]{:S(2)}) collective-permute-start(bf16[2,128,128]{2,1,0:T(8,128)(2,1)S(1)} %get-tuple-element.22.refs_0_), channel_id=1, source_target_pairs={{0,3},{1,2},{2,1},{3,0},{4,7},{5,6},{6,5},{7,4},{8,11},{9,10},{10,... | collective-permute-start | bytes 196616 | tf_op jit(solution)/shard_map/ppermute | solution.py:41
  36.3 9.6 %collective-permute-start.14 = (bf16[2,128,128]{2,1,0:T(8,128)(2,1)S(1)}, bf16[2,128,128]{2,1,0:T(8,128)(2,1)S(1)}, u32[]{:S(2)}, u32[]{:S(2)}) collective-permute-start(bf16[2,128,128]{2,1,0:T(8,128)(2,1)S(1)} %get-tuple-element.22.refs_0_), channel_id=1, source_target_pairs={{0,4},{1,5},{2,6},{3,7},{4,0},{5,1},{6,2},{7,3},{8,12},{9,13},{10,... | collective-permute-start | bytes 196616 | tf_op jit(solution)/shard_map/ppermute | solution.py:41
  36.3 11.4 %collective-permute-start.15 = (bf16[2,128,128]{2,1,0:T(8,128)(2,1)S(1)}, bf16[2,128,128]{2,1,0:T(8,128)(2,1)S(1)}, u32[]{:S(2)}, u32[]{:S(2)}) collective-permute-start(bf16[2,128,128]{2,1,0:T(8,128)(2,1)S(1)} %get-tuple-element.22.refs_0_), channel_id=1, source_target_pairs={{0,5},{1,4},{2,7},{3,6},{4,1},{5,0},{6,3},{7,2},{8,13},{9,12},{10,... | collective-permute-start | bytes 196616 | tf_op jit(solution)/shard_map/ppermute | solution.py:41
  39.2 8.5 %collective-permute-start.16 = (bf16[2,128,128]{2,1,0:T(8,128)(2,1)S(1)}, bf16[2,128,128]{2,1,0:T(8,128)(2,1)S(1)}, u32[]{:S(2)}, u32[]{:S(2)}) collective-permute-start(bf16[2,128,128]{2,1,0:T(8,128)(2,1)S(1)} %get-tuple-element.22.refs_0_), channel_id=1, source_target_pairs={{0,6},{1,7},{2,4},{3,5},{4,2},{5,3},{6,0},{7,1},{8,14},{9,15},{10,... | collective-permute-start | bytes 196616 | tf_op jit(solution)/shard_map/ppermute | solution.py:41
  39.5 8.2 %collective-permute-start.17 = (bf16[2,128,128]{2,1,0:T(8,128)(2,1)S(1)}, bf16[2,128,128]{2,1,0:T(8,128)(2,1)S(1)}, u32[]{:S(2)}, u32[]{:S(2)}) collective-permute-start(bf16[2,128,128]{2,1,0:T(8,128)(2,1)S(1)} %get-tuple-element.22.refs_0_), channel_id=1, source_target_pairs={{0,7},{1,6},{2,5},{3,4},{4,3},{5,2},{6,1},{7,0},{8,15},{9,14},{10,... | collective-permute-start | bytes 196616 | tf_op jit(solution)/shard_map/ppermute | solution.py:41
  45.9 7.9 %copy-start.5 = (s32[8,12]{1,0:T(8,128)S(1)}, s32[8,12]{1,0:T(8,128)}, u32[]{:S(2)}) copy-start(s32[8,12]{1,0:T(8,128)} %panel_ref.1) | copy-start | bytes 1156
  45.9 7.9 %copy-start.11 = (s32[8]{0:T(128)S(1)}, s32[8]{0:T(128)}, u32[]{:S(2)}) copy-start(s32[8]{0:T(128)} %count_ref.1) | copy-start | bytes 100
  49.6 7.3 %copy-start = (f32[4,2,128,128]{3,2,1,0:T(8,128)S(1)}, f32[4,2,128,128]{3,2,1,0:T(8,128)}, u32[]{:S(2)}) copy-start(f32[4,2,128,128]{3,2,1,0:T(8,128)} %basis_ref.3) | copy-start | bytes 1572868
  49.6 7.3 %copy-start.4 = (f32[128]{0:T(128)S(1)}, f32[128]{0:T(128)}, u32[]{:S(2)}) copy-start(f32[128]{0:T(128)} %param.10) | copy-start | bytes 1540
  49.6 1.6 %collective-permute-start.18 = (f32[2,2,128,128]{3,2,1,0:T(8,128)S(1)}, f32[2,2,128,128]{3,2,1,0:T(8,128)S(1)}, u32[]{:S(2)}, u32[]{:S(2)}) collective-permute-start(f32[2,2,128,128]{3,2,1,0:T(8,128)S(1)} %get-tuple-element.24), channel_id=1, source_target_pairs={{0,8},{8,0},{16,24},{24,16},{1,9},{9,1},{17,25},{25,17},{2,10},{10... | collective-permute-start | bytes 786440 | tf_op jit(solution)/shard_map/ppermute | solution.py:41
  51.2 5.6 %collective-permute-start.19 = (f32[1,2,128,128]{3,2,1,0:T(8,128)S(1)}, f32[1,2,128,128]{3,2,1,0:T(8,128)S(1)}, u32[]{:S(2)}, u32[]{:S(2)}) collective-permute-start(f32[1,2,128,128]{3,2,1,0:T(8,128)S(1)} %get-tuple-element.31), channel_id=1, source_target_pairs={{0,16},{8,24},{16,0},{24,8},{1,17},{9,25},{17,1},{25,9},{2,18},{10... | collective-permute-start | bytes 393224 | tf_op jit(solution)/shard_map/ppermute | solution.py:41
  52.1 1.7 %collective-permute-start.10 = (bf16[2,64,128]{2,1,0:T(8,128)(2,1)S(1)}, bf16[2,64,128]{2,1,0:T(8,128)(2,1)S(1)}, u32[]{:S(2)}, u32[]{:S(2)}) collective-permute-start(bf16[2,64,128]{2,1,0:T(8,128)(2,1)S(1)} %get-tuple-element.21), channel_id=1, source_target_pairs={{7,8},{8,7},{15,16},{16,15},{23,24},{24,23}} | collective-permute-start | bytes 98312 | tf_op jit(solution)/shard_map/ppermute | solution.py:405
  90.5 19.1 %copy-start.2 = (f32[2,128,128]{2,1,0:T(8,128)}, f32[2,128,128]{2,1,0:T(8,128)S(1)}, u32[]{:S(2)}) copy-start(f32[2,128,128]{2,1,0:T(8,128)S(1)} %get-tuple-element.28) | copy-start | bytes 393220

commit v4 on v3

v4 whole, which is shorter than its diff:
```python
import functools

import jax
import jax.numpy as jnp
from jax import lax
from jax.experimental import pallas as pl
from jax.experimental.pallas import tpu as pltpu
from jax.sharding import PartitionSpec as P

SPAN = 4


NU = 0.3
DELTA2 = 1e-05
ELASTIC = 40.0
HIGH = lax.Precision.HIGHEST
AXES = ("narrow", "wide")
EXTRA = 8
ROWS = 8
SMEM = pl.BlockSpec(memory_space=pltpu.SMEM)
VMEM = pl.BlockSpec(memory_space=pltpu.VMEM)
ANY = pl.BlockSpec(memory_space=pl.ANY)
PARAMS = pltpu.CompilerParams(vmem_limit_bytes=48 * 1024 * 1024)


def dot_rows(left, right, precision=HIGH):
    return lax.dot_general(
        left, right, (((1,), (0,)), ((), ())), precision=precision, preferred_element_type=jnp.float32
    )


def dot_first(left, right):
    return lax.dot_general(
        left, right, (((0,), (0,)), ((), ())), precision=HIGH, preferred_element_type=jnp.float32
    )


def as_column(row, width):
    return jnp.transpose(jnp.broadcast_to(row, (width, row.shape[1])))


def swap(block, axis, offset):
    count = lax.axis_size(axis)
    return lax.ppermute(block, axis, [(i, i ^ offset) for i in range(count)])


def offsets_of(count):
    return [1 << bit for bit in range(count.bit_length() - 1)]


def join_kernel(left_ref, right_ref, out_ref):
    half = left_ref.shape[0]
    out_ref[:half] = left_ref[...]
    out_ref[half:] = right_ref[...]


def join(left, right):
    shape = (2 * left.shape[0],) + left.shape[1:]
    return call(join_kernel, jax.ShapeDtypeStruct(shape, left.dtype), (left, right))


def add_kernel(left_ref, right_ref, out_ref):
    out_ref[...] = left_ref[...] + right_ref[...]


def add(left, right):
    return call(add_kernel, f32(*left.shape), (left, right))


def halve_kernel(kept_ref, got_ref, keep_ref, send_ref):
    for k in range(keep_ref.shape[0]):
        keep_ref[k] = kept_ref[2 * k] + got_ref[2 * k]
        send_ref[k] = kept_ref[2 * k + 1] + got_ref[2 * k + 1]


def halve(keep, got):
    half = f32(keep.shape[0] // 2, *keep.shape[1:])
    return call(halve_kernel, [half, half], (keep, got))


def gather_steps(held, steps):
    got = None
    for axis, offset in steps:
        if got is not None:
            held = join(held, got)
        got = swap(held, axis, offset)
    return held, got


def gather_order(offsets):
    order = [0]
    for offset in offsets:
        order = order + [k ^ offset for k in order]
    return order


def sum_steps(keep, send, halving, butterfly):
    for number, (axis, offset) in enumerate(halving):
        if number:
            keep, send = halve(keep, got)
        got = swap(send, axis, offset)
    total = add(keep, got)
    for axis, offset in butterfly:
        total = add(total, swap(total, axis, offset))
    return gather_steps(total, halving[::-1])


def members(agg_ref, a, coarse_count):
    ids = lax.broadcasted_iota(jnp.int32, (coarse_count, agg_ref.shape[1]), 0)
    return jnp.where(ids == agg_ref[a : a + 1, :], 1.0, 0.0)


def load_all(pairs, sems):
    copies = [
        pltpu.make_async_copy(source, target, sems.at[k])
        for k, (source, target) in enumerate(pairs)
    ]
    for copy in copies:
        copy.start()
    for copy in copies:
        copy.wait()


def restrict_kernel(
    agg_hbm, basis_hbm, points_hbm, weight_hbm, pack_ref, agg_ref, newest_ref, points_ref, weight_ref, sems
):
    coarse_count = pack_ref.shape[1] - EXTRA
    point_count = newest_ref.shape[1]
    load_all(
        [
            (basis_hbm.at[basis_hbm.shape[0] - 1], newest_ref),
            (agg_hbm, agg_ref),
            (points_hbm, points_ref),
            (weight_hbm, weight_ref),
        ],
        sems,
    )
    total = dot_rows(members(agg_ref, 0, coarse_count), newest_ref[0]) + dot_rows(
        members(agg_ref, 1, coarse_count), newest_ref[1]
    )
    pack_ref[0, :coarse_count, :] = total
    pack_ref[0, coarse_count:, :] = jnp.concatenate(
        [points_ref[...], weight_ref[...], jnp.zeros((EXTRA - 3, point_count), jnp.float32)], axis=0
    )


def prefetch_kernel(
    pack_hbm,
    agg_hbm,
    basis_hbm,
    jacobi_hbm,
    weight_hbm,
    inverse_hbm,
    inverse_ref,
    member_ref,
    smooth_ref,
    weight_out_ref,
    agg_ref,
    newest_ref,
    jacobi_ref,
    weight_ref,
    sems,
):
    coarse_count = member_ref.shape[1]
    rhs_count = newest_ref.shape[2]
    load_all(
        [
            (basis_hbm.at[basis_hbm.shape[0] - 1], newest_ref),
            (agg_hbm, agg_ref),
            (jacobi_hbm, jacobi_ref),
            (weight_hbm, weight_ref),
            (inverse_hbm, inverse_ref),
        ],
        sems,
    )
    for a in range(2):
        member_ref[a] = members(agg_ref, a, coarse_count)
        smooth_ref[a] = as_column(jacobi_ref[a : a + 1, :], rhs_count) * newest_ref[a]
    weight_out_ref[...] = as_column(weight_ref[...], rhs_count)


def coarse_kernel(order, index_ref, inverse_ref, held_ref, got_ref, keep_ref, send_ref, rhs_ref):
    narrow_count = inverse_ref.shape[0]
    coarse_count = inverse_ref.shape[1]
    half = held_ref.shape[0]
    narrow_index = index_ref[0]
    wide_index = index_ref[1]
    for k, offset in enumerate(order):
        first = pl.multiple_of((wide_index ^ offset) * coarse_count, 8)
        part = held_ref[k] if k < half else got_ref[k - half]
        rhs_ref[pl.ds(first, coarse_count), :] = part[:coarse_count, :]
    own = held_ref[0, coarse_count:, :]
    for k in range(narrow_count):
        out_ref = send_ref if k % 2 else keep_ref
        out_ref[k // 2, :coarse_count, :] = dot_rows(
            inverse_ref[narrow_index ^ k], rhs_ref[...]
        )
        out_ref[k // 2, coarse_count:, :] = own


def coarse_halve_kernel(pairs, kept_ref, got_ref, keep_ref, send_ref):
    coarse_count = kept_ref.shape[1] - EXTRA
    rows = 2 * pairs
    own = kept_ref[0, coarse_count : coarse_count + rows, :]
    other = got_ref[0, coarse_count : coarse_count + rows, :]
    tail = [own, other]
    if 2 * rows < EXTRA:
        tail.append(jnp.zeros((EXTRA - 2 * rows, own.shape[1]), jnp.float32))
    tail = jnp.concatenate(tail, axis=0)
    for k in range(keep_ref.shape[0]):
        for out_ref, source in ((keep_ref, 2 * k), (send_ref, 2 * k + 1)):
            out_ref[k, :coarse_count, :] = (
                kept_ref[source, :coarse_count, :] + got_ref[source, :coarse_count, :]
            )
            out_ref[k, coarse_count:, :] = tail


def precond_kernel(index_ref, member_ref, smooth_ref, keep_ref, got_ref, precond_ref, edge_ref):
    coarse_count = member_ref.shape[1]
    point_count = smooth_ref.shape[1]
    width = edge_ref.shape[1]
    coarse_sol = keep_ref[0, :coarse_count, :] + got_ref[0, :coarse_count, :]
    for a in range(2):
        value = smooth_ref[a] + dot_first(member_ref[a], coarse_sol)
        precond_ref[0, a] = value.astype(jnp.bfloat16)
    first = pl.multiple_of(jnp.where(index_ref[1] == 0, 0, point_count - width), 16)
    for a in range(2):
        edge_ref[a] = precond_ref[0, a, pl.ds(first, width), :]


def matrix_kernel(coarse_count, held_ref, got_ref, own_ref, other_ref, matrix_ref):
    half, _, point_count = held_ref.shape
    target_half = pl.num_programs(0) // 2
    step = pl.program_id(0)
    first = coarse_count + 2 * lax.rem(step, target_half)
    target = jnp.where(
        step < target_half,
        own_ref[0, pl.ds(first, 2), :],
        other_ref[0, pl.ds(first, 2), :],
    )
    target_x = as_column(target[0:1, :], point_count)
    target_y = as_column(target[1:2, :], point_count)
    for s in range(2 * half):
        part = held_ref[s] if s < half else got_ref[s - half]
        source = part[coarse_count:, :]
        delta_x = target_x - source[0:1, :]
        delta_y = target_y - source[1:2, :]
        factor = ELASTIC * source[2:3, :]
        square_x = delta_x * delta_x
        square_y = delta_y * delta_y
        square_dist = square_x + square_y + DELTA2
        inverse = 1.0 / square_dist
        log_part = (-0.5 * (3.0 - 4.0 * NU)) * jnp.log(square_dist)
        lanes = slice(s * point_count, (s + 1) * point_count)
        matrix_ref[0, 0, :, lanes] = (factor * (log_part + square_x * inverse)).astype(jnp.bfloat16)
        matrix_ref[0, 1, :, lanes] = (factor * (delta_x * delta_y * inverse)).astype(jnp.bfloat16)
        matrix_ref[0, 2, :, lanes] = (factor * (log_part + square_y * inverse)).astype(jnp.bfloat16)


def far_kernel(matrix_ref, held_ref, got_ref, keep_ref, send_ref, fields_ref):
    half, _, point_count, _ = held_ref.shape
    step = pl.program_id(0)

    @pl.when(step == 0)
    def _():
        for s in range(half):
            for b in range(2):
                fields_ref[b, s * point_count : (s + 1) * point_count, :] = held_ref[s, b]
                first = (half + s) * point_count
                fields_ref[b, first : first + point_count, :] = got_ref[s, b]

    out_x = dot_rows(matrix_ref[0, 0], fields_ref[0], None) + dot_rows(
        matrix_ref[0, 1], fields_ref[1], None
    )
    out_y = dot_rows(matrix_ref[0, 1], fields_ref[0], None) + dot_rows(
        matrix_ref[0, 2], fields_ref[1], None
    )

    @pl.when(step % 2 == 0)
    def _():
        keep_ref[0, 0] = out_x
        keep_ref[0, 1] = out_y

    @pl.when(step % 2 == 1)
    def _():
        send_ref[0, 0] = out_x
        send_ref[0, 1] = out_y


def near_kernel(
    order,
    index_ref,
    panel_ref,
    count_ref,
    block_ref,
    crossed_ref,
    held_ref,
    got_ref,
    out_ref,
    line_ref,
    gathered_ref,
):
    half, _, point_count, _ = held_ref.shape
    width = crossed_ref.shape[1]
    panels_dev, double_nodes, _ = block_ref.shape
    nodes = double_nodes // 2
    slot_total = panel_ref.shape[1]
    wide_index = index_ref[1]
    for b in range(2):
        line_ref[b, :width, :] = crossed_ref[b]
        line_ref[b, width + len(order) * point_count :, :] = crossed_ref[b]
        for k, offset in enumerate(order):
            first = pl.multiple_of((wide_index ^ offset) * point_count + width, 16)
            line_ref[b, pl.ds(first, point_count), :] = (
                held_ref[k, b] if k < half else got_ref[k - half, b]
            )
    group_start = index_ref[0] * (len(order) * panels_dev)
    lane = lax.broadcasted_iota(jnp.int32, block_ref.shape[1:], 1)
    for p in range(panels_dev):
        for k in range(slot_total):
            first = pl.multiple_of((panel_ref[p, k] - group_start) * nodes + width, 16)
            for b in range(2):
                row = (k * 2 + b) * nodes
                gathered_ref[p, row : row + nodes, :] = line_ref[b, pl.ds(first, nodes), :]
        blocks = jnp.where(
            lane < count_ref[p] * double_nodes, block_ref[p].astype(jnp.float32), 0.0
        ).astype(jnp.bfloat16)
        near = dot_rows(blocks, gathered_ref[p], None)
        for a in range(2):
            rows = slice(p * nodes, (p + 1) * nodes)
            own = held_ref[0, a, rows, :].astype(jnp.float32)
            out_ref[a, rows, :] = 0.5 * own + near[a * nodes : (a + 1) * nodes, :]


def spread(full_ref, keep_ref, send_ref, own):
    rows = keep_ref.shape[1]
    for k in range(2 * keep_ref.shape[0]):
        first = pl.multiple_of((own ^ k) * rows, 8)
        out_ref = send_ref if k % 2 else keep_ref
        out_ref[k // 2] = full_ref[pl.ds(first, rows), :]


def collect(order, held_ref, got_ref, full_ref, own):
    half, rows, _ = held_ref.shape
    for k, offset in enumerate(order):
        first = pl.multiple_of((own ^ offset) * rows, 8)
        full_ref[pl.ds(first, rows), :] = held_ref[k] if k < half else got_ref[k - half]


def own_part(index_ref, narrow_count, part_count):
    if part_count <= narrow_count:
        return index_ref[0] & (part_count - 1)
    return index_ref[0] + narrow_count * (index_ref[1] & (part_count // narrow_count - 1))


def project_kernel(
    narrow_count,
    index_ref,
    weight_ref,
    basis_ref,
    base_ref,
    kept_ref,
    arrived_ref,
    image_ref,
    keep_ref,
    send_ref,
    full_ref,
):
    block_total, _, _, rhs_count = basis_ref.shape
    weighted = []
    for a in range(2):
        image = base_ref[a] + kept_ref[0, a] + arrived_ref[0, a]
        image_ref[a] = image
        weighted.append(image * weight_ref[...])
    for j in range(block_total):
        full_ref[j * rhs_count : (j + 1) * rhs_count, :] = dot_first(
            basis_ref[j, 0], weighted[0]
        ) + dot_first(basis_ref[j, 1], weighted[1])
    spread(
        full_ref, keep_ref, send_ref, own_part(index_ref, narrow_count, 2 * keep_ref.shape[0])
    )


def remainder_kernel(
    order,
    narrow_count,
    index_ref,
    weight_ref,
    basis_ref,
    image_ref,
    held_ref,
    got_ref,
    hess_ref,
    remainder_ref,
    keep_ref,
    send_ref,
    gram_ref,
):
    block_total, _, point_count, rhs_count = basis_ref.shape
    collect(order, held_ref, got_ref, hess_ref, own_part(index_ref, narrow_count, len(order)))
    gram = None
    for a in range(2):
        value = image_ref[a]
        for j in range(block_total):
            value = value - dot_rows(
                basis_ref[j, a], hess_ref[j * rhs_count : (j + 1) * rhs_count, :]
            )
        remainder_ref[a * point_count : (a + 1) * point_count, :] = value
        term = dot_first(value * weight_ref[...], value)
        gram = term if gram is None else gram + term
    gram_ref[...] = gram
    spread(
        gram_ref, keep_ref, send_ref, own_part(index_ref, narrow_count, 2 * keep_ref.shape[0])
    )


def factor_kernel(
    gather,
    narrow_count,
    index_ref,
    held_ref,
    got_ref,
    remainder_ref,
    upper_ref,
    new_ref,
    work_ref,
    inverse_ref,
):
    order = remainder_ref.shape[1]
    tile = (ROWS, order)
    lane = lax.broadcasted_iota(jnp.int32, tile, 1)
    row = lax.broadcasted_iota(jnp.int32, tile, 0)
    collect(gather, held_ref, got_ref, work_ref, own_part(index_ref, narrow_count, len(gather)))
    for block in range(order // ROWS):
        start = block * ROWS
        inverse_ref[start : start + ROWS, :] = jnp.where(lane == row + start, 1.0, 0.0)
    for block in range(order // ROWS):
        start = block * ROWS
        own = work_ref[start : start + ROWS, :]
        own_inverse = inverse_ref[start : start + ROWS, :]
        columns = [
            jnp.broadcast_to(own[:, start + m : start + m + 1], tile) for m in range(ROWS)
        ]
        entry = {
            (j, m): jnp.broadcast_to(columns[m][j : j + 1, :], tile)
            for m in range(ROWS)
            for j in range(m, ROWS)
        }
        scale = []
        for m in range(ROWS):
            scale.append(lax.rsqrt(entry[m, m]))
            for j in range(m + 1, ROWS):
                entry[j, m] = entry[j, m] * scale[m]
            for n in range(m + 1, ROWS):
                for j in range(n, ROWS):
                    entry[j, n] = entry[j, n] - entry[j, m] * entry[n, m]
        solved = []
        solved_inverse = []
        for m in range(ROWS):
            upper_row = jnp.broadcast_to(own[m : m + 1, :], tile)
            inverse_row = jnp.broadcast_to(own_inverse[m : m + 1, :], tile)
            for j in range(m):
                upper_row = upper_row - entry[m, j] * solved[j]
                inverse_row = inverse_row - entry[m, j] * solved_inverse[j]
            upper_row = upper_row * scale[m]
            inverse_row = inverse_row * scale[m]
            solved.append(upper_row)
            solved_inverse.append(inverse_row)
        upper_rows = solved[ROWS - 1]
        inverse_rows = solved_inverse[ROWS - 1]
        for m in range(ROWS - 1):
            upper_rows = jnp.where(row == m, solved[m], upper_rows)
            inverse_rows = jnp.where(row == m, solved_inverse[m], inverse_rows)
        upper_ref[start : start + ROWS, :] = jnp.where(lane >= row + start, upper_rows, 0.0)
        inverse_ref[start : start + ROWS, :] = inverse_rows
        for later in range(block + 1, order // ROWS):
            first = later * ROWS
            target = work_ref[first : first + ROWS, :]
            target_inverse = inverse_ref[first : first + ROWS, :]
            multiplier = []
            for m in range(ROWS):
                value = jnp.broadcast_to(target[:, start + m : start + m + 1], tile)
                for j in range(m):
                    value = value - multiplier[j] * entry[m, j]
                multiplier.append(value * scale[m])
            for m in range(ROWS):
                target = target - multiplier[m] * solved[m]
                target_inverse = target_inverse - multiplier[m] * solved_inverse[m]
            work_ref[first : first + ROWS, :] = target
            inverse_ref[first : first + ROWS, :] = target_inverse
    new_ref[...] = lax.dot_general(
        remainder_ref[...],
        inverse_ref[...],
        (((1,), (1,)), ((), ())),
        precision=HIGH,
        preferred_element_type=jnp.float32,
    )


def f32(*shape):
    return jax.ShapeDtypeStruct(shape, jnp.float32)


def b16(*shape):
    return jax.ShapeDtypeStruct(shape, jnp.bfloat16)


def call(kernel, out_shape, operands, scalars=0, scratch=(), anywhere=False):
    many = isinstance(out_shape, (tuple, list))
    return pl.pallas_call(
        kernel,
        out_shape=out_shape,
        in_specs=[SMEM] * scalars + [ANY if anywhere else VMEM] * (len(operands) - scalars),
        out_specs=[VMEM] * len(out_shape) if many else VMEM,
        scratch_shapes=list(scratch),
        compiler_params=PARAMS,
    )(*operands)


def body(
    points,
    quad_weight,
    basis,
    jacobi,
    near_panel,
    near_count,
    near_block,
    agg_index,
    coarse_inverse,
):
    block_total, _, point_count, rhs_count = basis.shape
    coarse_count = coarse_inverse.shape[1]
    narrow_count = lax.axis_size("narrow")
    wide_count = lax.axis_size("wide")
    panels_dev, slot_total = near_panel.shape
    nodes = near_block.shape[2] // 2
    width = SPAN * nodes
    pack_rows = coarse_count + EXTRA
    source_total = wide_count * point_count
    index = jnp.stack([lax.axis_index("narrow"), lax.axis_index("wide")]).astype(jnp.int32)
    weight_row = quad_weight[None, :]
    narrow_steps = [("narrow", offset) for offset in offsets_of(narrow_count)]
    wide_steps = [("wide", offset) for offset in offsets_of(wide_count)]
    wide_order = gather_order([offset for _, offset in wide_steps[::-1]])
    pair_row = pltpu.VMEM((2, point_count), jnp.float32)
    one_row = pltpu.VMEM((1, point_count), jnp.float32)
    pair_index = pltpu.VMEM((2, point_count), jnp.int32)
    field = pltpu.VMEM((2, point_count, rhs_count), jnp.float32)

    pack = call(
        restrict_kernel,
        f32(1, pack_rows, point_count),
        (agg_index, basis, points, weight_row),
        0,
        [pair_index, field, pair_row, one_row, pltpu.SemaphoreType.DMA((4,))],
        True,
    )
    inverse, member, smooth, weight = call(
        prefetch_kernel,
        [
            f32(*coarse_inverse.shape),
            f32(2, coarse_count, point_count),
            f32(2, point_count, rhs_count),
            f32(point_count, rhs_count),
        ],
        (pack, agg_index, basis, jacobi, weight_row, coarse_inverse),
        0,
        [pair_index, field, pair_row, one_row, pltpu.SemaphoreType.DMA((5,))],
        True,
    )
    packs = gather_steps(pack, wide_steps[::-1])
    half = f32(narrow_count // 2, pack_rows, rhs_count)
    keep, send = call(
        functools.partial(coarse_kernel, wide_order),
        [half, half],
        (index, inverse, *packs),
        1,
        [pltpu.VMEM((wide_count * coarse_count, rhs_count), jnp.float32)],
    )
    got = swap(send, *narrow_steps[0])
    for number, (axis, offset) in enumerate(narrow_steps[1:]):
        half = f32(keep.shape[0] // 2, pack_rows, rhs_count)
        keep, send = call(
            functools.partial(coarse_halve_kernel, 1 << number), [half, half], (keep, got)
        )
        got = swap(send, axis, offset)
    precond, edge = call(
        precond_kernel,
        [b16(1, 2, point_count, rhs_count), b16(2, width, rhs_count)],
        (index, member, smooth, keep, got),
        1,
    )
    pairs = []
    for group in range(narrow_count - 1):
        left = group * wide_count + wide_count - 1
        pairs += [(left, left + 1), (left + 1, left)]
    fields = gather_steps(precond, wide_steps[::-1])
    crossed = lax.ppermute(edge, AXES, pairs)

    matrix_spec = pl.BlockSpec((1, 3, point_count, source_total), lambda k: (k, 0, 0, 0))
    matrix = pl.pallas_call(
        functools.partial(matrix_kernel, coarse_count),
        out_shape=b16(narrow_count, 3, point_count, source_total),
        grid=(narrow_count,),
        in_specs=[VMEM] * 4,
        out_specs=matrix_spec,
        compiler_params=PARAMS,
    )(*packs, keep, got)
    half = f32(narrow_count // 2, 2, point_count, rhs_count)
    half_spec = pl.BlockSpec((1, 2, point_count, rhs_count), lambda k: (k // 2, 0, 0, 0))
    keep, send = pl.pallas_call(
        far_kernel,
        out_shape=[half, half],
        grid=(narrow_count,),
        in_specs=[matrix_spec, VMEM, VMEM],
        out_specs=[half_spec, half_spec],
        scratch_shapes=[pltpu.VMEM((2, source_total, rhs_count), jnp.bfloat16)],
        compiler_params=PARAMS,
    )(matrix, *fields)
    got = swap(send, *narrow_steps[0])
    for axis, offset in narrow_steps[1:]:
        keep, send = halve(keep, got)
        got = swap(send, axis, offset)
    near_rows = jnp.transpose(near_block, (0, 2, 1, 3)).reshape(
        panels_dev, 2 * nodes, slot_total * 2 * nodes
    )
    base = call(
        functools.partial(near_kernel, wide_order),
        f32(2, point_count, rhs_count),
        (index, near_panel, near_count, near_rows, crossed, *fields),
        3,
        [
            pltpu.VMEM((2, 2 * width + source_total, rhs_count), jnp.bfloat16),
            pltpu.VMEM((panels_dev, slot_total * 2 * nodes, rhs_count), jnp.bfloat16),
        ],
    )

    hess_rows = block_total * rhs_count
    halving = narrow_steps + wide_steps[:1]
    butterfly = wide_steps[1:]
    hess_order = gather_order([1 << bit for bit in range(len(halving))][::-1])
    half = f32(len(hess_order) // 2, hess_rows // len(hess_order), rhs_count)
    image, keep, send = call(
        functools.partial(project_kernel, narrow_count),
        [f32(2, point_count, rhs_count), half, half],
        (index, weight, basis, base, keep, got),
        1,
        [pltpu.VMEM((hess_rows, rhs_count), jnp.float32)],
    )
    total = sum_steps(keep, send, halving, butterfly)
    gram_order = gather_order([1])
    half = f32(1, rhs_count // 2, rhs_count)
    hessenberg, remainder, keep, send = call(
        functools.partial(remainder_kernel, hess_order, narrow_count),
        [f32(hess_rows, rhs_count), f32(2 * point_count, rhs_count), half, half],
        (index, weight, basis, image, *total),
        1,
        [pltpu.VMEM((rhs_count, rhs_count), jnp.float32)],
    )
    total = sum_steps(keep, send, narrow_steps[:1], narrow_steps[1:] + wide_steps)
    upper_factor, new_block = call(
        functools.partial(factor_kernel, gram_order, narrow_count),
        [f32(rhs_count, rhs_count), f32(2 * point_count, rhs_count)],
        (index, *total, remainder),
        1,
        [pltpu.VMEM((rhs_count, rhs_count), jnp.float32)] * 2,
    )
    return (
        new_block.reshape(2, point_count, rhs_count),
        hessenberg.reshape(block_total, rhs_count, rhs_count),
        upper_factor,
    )


def solution(mesh):
    in_specs = (
        P(None, ("narrow", "wide")),
        P(("narrow", "wide")),
        P(None, None, ("narrow", "wide"), None),
        P(None, ("narrow", "wide")),
        P(("narrow", "wide"), None),
        P(("narrow", "wide")),
        P(("narrow", "wide"), None, None, None),
        P(None, ("narrow", "wide")),
        P(None, "wide", "narrow"),
    )
    out_specs = (P(None, ("narrow", "wide"), None), P(), P())
    return jax.shard_map(body, mesh=mesh, in_specs=in_specs, out_specs=out_specs, check_vma=False)
```

time: 117 us -> 115 us (0.983)
  blocking collectives: 50.9 us -> 0 us
  waiting for transfers between devices: 14.8 us -> 55.7 us
  starting transfers between devices: 27.1 us -> 33.4 us
  Pallas kernels: 15 us -> 16.7 us
    all_to_all x4 -> x0, blocking collectives: 50.9 us -> none  [the longest x2 28.5 us: sum_everywhere(): parts = lax.all_to_all(parts, AXES, 0, 0, tiled=True)]
    ppermute x19 -> x24, waiting for transfers between devices: 14.8 us -> 55.7 us  [swap(): return lax.ppermute(block, axis, [(i, i ^ offset) for i in range(count)])]
    pallas_call x8 -> x26, Pallas kernels: 5.06 us -> 13 us  [call(): pl.pallas_call(kernel, out_shape=out_shape, in_specs=[SMEM] * scalars + [...]
    pallas_call x2 -> x1, Pallas kernels: 8.15 us -> 1.86 us  [body(): pl.pallas_call(functools.partial(matrix_kernel, coarse_count), out_shape=...]
    ppermute x19 -> x24, starting transfers between devices: 26.5 us -> 32.8 us  [swap(): return lax.ppermute(block, axis, [(i, i ^ offset) for i in range(count)])]
    unnamed x27 -> x26, local copies, waits for them, and re-layouts: 5.74 us -> 7.09 us
  transfers between devices with their start and end apart: 20 -> 25, of which waited for: 8 -> 23; matrix products, arithmetic and copies ran while one was open for 1% -> 1% of each run, Pallas kernels for 3% -> 3%
where the time goes in v4:
time: 115 us
  waiting for transfers between devices  55.7 us (48%)
  starting transfers between devices  33.4 us (29%)
  Pallas kernels  16.7 us (15%)
  local copies, waits for them, and re-layouts  8.14 us (7%)
    ppermute x24, waiting for transfers between devices, swap(): return lax.ppermute(block, axis, [(i, i ^ offset) for i in range(count)])  55.7 us
    ppermute x24, starting transfers between devices, swap(): return lax.ppermute(block, axis, [(i, i ^ offset) for i in range(count)])  32.8 us
    pallas_call x26, Pallas kernels, call(): pl.pallas_call(kernel, out_shape=out_shape, in_specs=[SMEM] * scalars + [...  13 us
    unnamed x26, local copies, waits for them, and re-layouts  7.09 us
  transfers between devices with their start and end apart: 25, of which 23 were waited for; matrix products, arithmetic and copies ran while one was open for 1% of the time, Pallas kernels for 3%

profile of v4, /device:TPU:0, one launch (start us, length us, event | category | flops | bytes accessed | tf_op | source)
XLA Modules:
  0.0 114.9 jit_solution(1626137438840499670)
XLA Ops:
  0.6 1.0 copy-done
  1.7 0.7 copy-done.5
  2.4 0.7 copy-done.7
  3.0 0.7 copy-done.9
  3.7 0.4 shard_map.112.pack_hbm.left_ref
  4.1 4.1 %collective-permute-start = (f32[1,56,128]{2,1,0:T(8,128)S(1)}, f32[1,56,128]{2,1,0:T(8,128)S(1)}, u32[]{:S(2)}, u32[]{:S(2)}) collective-permute-start(f32[1,56,128]{2,1,0:T(8,128)S(1)} %shard_map.112.pack_hbm.left_ref), channel_id=1, source_target_pairs={{0,4},{1,5},{2,6},{3,7},{4,0},{5,1},{6,2},{7,3},{8,12},{9,13},{10,... | collective-permute-start | bytes 86024 | tf_op jit(solution)/shard_map/ppermute | solution.py:44
  8.2 1.9 %collective-permute-done.right_ref = f32[1,56,128]{2,1,0:T(8,128)S(1)} collective-permute-done((f32[1,56,128]{2,1,0:T(8,128)S(1)}, f32[1,56,128]{2,1,0:T(8,128)S(1)}, u32[]{:S(2)}, u32[]{:S(2)}) %collective-permute-start) | collective-permute-done | bytes 28704 | tf_op jit(solution)/shard_map/ppermute | solution.py:44
  10.1 1.9 %collective-permute-start.1 = (f32[2,56,128]{2,1,0:T(8,128)S(1)}, f32[2,56,128]{2,1,0:T(8,128)S(1)}, u32[]{:S(2)}, u32[]{:S(2)}) collective-permute-start(f32[2,56,128]{2,1,0:T(8,128)S(1)} %shard_map.114.left_ref), channel_id=1, source_target_pairs={{0,2},{1,3},{2,0},{3,1},{4,6},{5,7},{6,4},{7,5},{8,10},{9,11},{10,... | collective-permute-start | bytes 172040 | tf_op jit(solution)/shard_map/ppermute | solution.py:44
  12.0 2.3 %collective-permute-done.1.right_ref = f32[2,56,128]{2,1,0:T(8,128)S(1)} collective-permute-done((f32[2,56,128]{2,1,0:T(8,128)S(1)}, f32[2,56,128]{2,1,0:T(8,128)S(1)}, u32[]{:S(2)}, u32[]{:S(2)}) %collective-permute-start.1) | collective-permute-done | bytes 57376 | tf_op jit(solution)/shard_map/ppermute | solution.py:44
  14.3 2.1 %collective-permute-start.2 = (f32[4,56,128]{2,1,0:T(8,128)S(1)}, f32[4,56,128]{2,1,0:T(8,128)S(1)}, u32[]{:S(2)}, u32[]{:S(2)}) collective-permute-start(f32[4,56,128]{2,1,0:T(8,128)S(1)} %shard_map.115.held_ref), channel_id=1, source_target_pairs={{0,1},{1,0},{2,3},{3,2},{4,5},{5,4},{6,7},{7,6},{8,9},{9,8},{10,11... | collective-permute-start | bytes 344072 | tf_op jit(solution)/shard_map/ppermute | solution.py:44
  16.3 1.0 copy-done.1
  17.4 1.0 copy-done.3
  18.3 0.7 copy-done.6
  19.0 0.7 copy-done.8
  19.7 0.7 copy-done.10
  20.3 0.4 shard_map.113
  20.7 0.1 pad_add_fusion.index_ref
  20.8 1.1 shard_map.116
  22.0 1.2 %collective-permute-done.3.got_ref = f32[2,56,128]{2,1,0:T(8,128)S(1)} collective-permute-done((f32[2,56,128]{2,1,0:T(8,128)S(1)}, f32[2,56,128]{2,1,0:T(8,128)S(1)}, u32[]{:S(2)}, u32[]{:S(2)}) %collective-permute-start.3) | collective-permute-done | bytes 57376 | tf_op jit(solution)/shard_map/ppermute | solution.py:44
  23.3 1.6 %collective-permute-start.4 = (f32[1,56,128]{2,1,0:T(8,128)S(1)}, f32[1,56,128]{2,1,0:T(8,128)S(1)}, u32[]{:S(2)}, u32[]{:S(2)}) collective-permute-start(f32[1,56,128]{2,1,0:T(8,128)S(1)} %get-tuple-element.37), channel_id=1, source_target_pairs={{0,16},{8,24},{16,0},{24,8},{1,17},{9,25},{17,1},{25,9},{2,18},{10... | collective-permute-start | bytes 86024 | tf_op jit(solution)/shard_map/ppermute | solution.py:44
  24.8 2.4 %collective-permute-done.4.got_ref.other_ref = f32[1,56,128]{2,1,0:T(8,128)S(1)} collective-permute-done((f32[1,56,128]{2,1,0:T(8,128)S(1)}, f32[1,56,128]{2,1,0:T(8,128)S(1)}, u32[]{:S(2)}, u32[]{:S(2)}) %collective-permute-start.4) | collective-permute-done | bytes 28704 | tf_op jit(solution)/shard_map/ppermute | solution.py:44
  27.2 0.9 shard_map.118
  28.1 2.5 %collective-permute-start.6 = (bf16[1,2,128,128]{3,2,1,0:T(8,128)(2,1)S(1)}, bf16[1,2,128,128]{3,2,1,0:T(8,128)(2,1)S(1)}, u32[]{:S(2)}, u32[]{:S(2)}) collective-permute-start(bf16[1,2,128,128]{3,2,1,0:T(8,128)(2,1)S(1)} %get-tuple-element.39.left_ref), channel_id=1, source_target_pairs={{0,4},{1,5},{2,6},{3,7},{4,0},{5,1},{6,2},{7,3},{8,12},{9,13},{10,... | collective-permute-start | bytes 196616 | tf_op jit(solution)/shard_map/ppermute | solution.py:44
  30.5 2.7 %collective-permute-done.6.right_ref = bf16[1,2,128,128]{3,2,1,0:T(8,128)(2,1)S(1)} collective-permute-done((bf16[1,2,128,128]{3,2,1,0:T(8,128)(2,1)S(1)}, bf16[1,2,128,128]{3,2,1,0:T(8,128)(2,1)S(1)}, u32[]{:S(2)}, u32[]{:S(2)}) %collective-permute-start.6) | collective-permute-done | bytes 65568 | tf_op jit(solution)/shard_map/ppermute | solution.py:44
  33.3 1.5 %collective-permute-start.7 = (bf16[2,2,128,128]{3,2,1,0:T(8,128)(2,1)S(1)}, bf16[2,2,128,128]{3,2,1,0:T(8,128)(2,1)S(1)}, u32[]{:S(2)}, u32[]{:S(2)}) collective-permute-start(bf16[2,2,128,128]{3,2,1,0:T(8,128)(2,1)S(1)} %shard_map.119.left_ref), channel_id=1, source_target_pairs={{0,2},{1,3},{2,0},{3,1},{4,6},{5,7},{6,4},{7,5},{8,10},{9,11},{10,... | collective-permute-start | bytes 393224 | tf_op jit(solution)/shard_map/ppermute | solution.py:44
  34.8 3.6 %collective-permute-done.7.right_ref = bf16[2,2,128,128]{3,2,1,0:T(8,128)(2,1)S(1)} collective-permute-done((bf16[2,2,128,128]{3,2,1,0:T(8,128)(2,1)S(1)}, bf16[2,2,128,128]{3,2,1,0:T(8,128)(2,1)S(1)}, u32[]{:S(2)}, u32[]{:S(2)}) %collective-permute-start.7) | collective-permute-done | bytes 131104 | tf_op jit(solution)/shard_map/ppermute | solution.py:44
  38.4 0.4 collective-permute-start.8
  38.7 1.9 %shard_map.122.matrix_ref = bf16[4,3,128,1024]{3,2,1,0:T(8,128)(2,1)S(1)} custom-call(f32[4,56,128]{2,1,0:T(8,128)S(1)} %shard_map.115.held_ref, f32[4,56,128]{2,1,0:T(8,128)S(1)} %collective-permute-done.2.got_ref, f32[1,56,128]{2,1,0:T(8,128)S(1)} %get-tuple-element.36.keep_ref.own_ref, f32[1,56,128]{2,1,0:T(8,128)S(1)} %collective-permute-done.4.got_ref.other_ref), custom_call_target="tpu_custom_call" | custom-call | tf_op jit(solution)/shard_map/pallas_call | solution.py:601
  40.6 4.2 %collective-permute-done.8.got_ref = bf16[4,2,128,128]{3,2,1,0:T(8,128)(2,1)S(1)} collective-permute-done((bf16[4,2,128,128]{3,2,1,0:T(8,128)(2,1)S(1)}, bf16[4,2,128,128]{3,2,1,0:T(8,128)(2,1)S(1)}, u32[]{:S(2)}, u32[]{:S(2)}) %collective-permute-start.8) | collective-permute-done | bytes 262176 | tf_op jit(solution)/shard_map/ppermute | solution.py:44
  44.8 1.8 %shard_map.123 = (f32[2,2,128,128]{3,2,1,0:T(8,128)S(1)}, f32[2,2,128,128]{3,2,1,0:T(8,128)S(1)}) custom-call(bf16[4,3,128,1024]{3,2,1,0:T(8,128)(2,1)S(1)} %shard_map.122.matrix_ref, bf16[4,2,128,128]{3,2,1,0:T(8,128)(2,1)S(1)} %shard_map.120.held_ref, bf16[4,2,128,128]{3,2,1,0:T(8,128)(2,1)S(1)} %collective-permute-done.8.got_ref), custom_call_target="tpu_custom_call" | custom-call | tf_op jit(solution)/shard_map/pallas_call | solution.py:611
  46.7 1.5 %collective-permute-done.9.got_ref = f32[2,2,128,128]{3,2,1,0:T(8,128)S(1)} collective-permute-done((f32[2,2,128,128]{3,2,1,0:T(8,128)S(1)}, f32[2,2,128,128]{3,2,1,0:T(8,128)S(1)}, u32[]{:S(2)}, u32[]{:S(2)}) %collective-permute-start.9) | collective-permute-done | bytes 262176 | tf_op jit(solution)/shard_map/ppermute | solution.py:44
  48.3 1.6 %collective-permute-start.10 = (f32[1,2,128,128]{3,2,1,0:T(8,128)S(1)}, f32[1,2,128,128]{3,2,1,0:T(8,128)S(1)}, u32[]{:S(2)}, u32[]{:S(2)}) collective-permute-start(f32[1,2,128,128]{3,2,1,0:T(8,128)S(1)} %get-tuple-element.43), channel_id=1, source_target_pairs={{0,16},{8,24},{16,0},{24,8},{1,17},{9,25},{17,1},{25,9},{2,18},{10... | collective-permute-start | bytes 393224 | tf_op jit(solution)/shard_map/ppermute | solution.py:44
  49.9 0.7 collective-permute-start.5
  50.5 0.3 copy.13
  50.9 0.7 reshape.15.block_ref
  51.6 1.0 shard_map.121.base_ref
  52.7 1.2 %collective-permute-done.10.arrived_ref = f32[1,2,128,128]{3,2,1,0:T(8,128)S(1)} collective-permute-done((f32[1,2,128,128]{3,2,1,0:T(8,128)S(1)}, f32[1,2,128,128]{3,2,1,0:T(8,128)S(1)}, u32[]{:S(2)}, u32[]{:S(2)}) %collective-permute-start.10) | collective-permute-done | bytes 131104 | tf_op jit(solution)/shard_map/ppermute | solution.py:44
  53.9 1.2 %shard_map.125 = (f32[2,128,128]{2,1,0:T(8,128)S(1)}, f32[4,64,128]{2,1,0:T(8,128)S(1)}, f32[4,64,128]{2,1,0:T(8,128)S(1)}) custom-call(s32[2]{0:T(128)S(1)} %pad_add_fusion.index_ref, f32[128,128]{1,0:T(8,128)S(1)} %get-tuple-element.30.weight_ref, f32[4,2,128,128]{3,2,1,0:T(8,128)S(1)} %copy-done.2, f32[2,128,128]{2,1,0:T(8,128)S(1)} %shard_map.121.base_ref, ...), custom_call_target="tpu_custom_call" | custom-call | tf_op jit(solution)/shard_map/pallas_call | solution.py:510
  55.1 5.1 %collective-permute-start.11 = (f32[4,64,128]{2,1,0:T(8,128)S(1)}, f32[4,64,128]{2,1,0:T(8,128)S(1)}, u32[]{:S(2)}, u32[]{:S(2)}) collective-permute-start(f32[4,64,128]{2,1,0:T(8,128)S(1)} %get-tuple-element.46), channel_id=1, source_target_pairs={{0,8},{8,0},{16,24},{24,16},{1,9},{9,1},{17,25},{25,17},{2,10},{10... | collective-permute-start | bytes 393224 | tf_op jit(solution)/shard_map/ppermute | solution.py:44
  60.2 1.0 collective-permute-done.11.got_ref
  61.2 2.0 %collective-permute-start.12 = (f32[2,64,128]{2,1,0:T(8,128)S(1)}, f32[2,64,128]{2,1,0:T(8,128)S(1)}, u32[]{:S(2)}, u32[]{:S(2)}) collective-permute-start(f32[2,64,128]{2,1,0:T(8,128)S(1)} %get-tuple-element.48), channel_id=1, source_target_pairs={{0,16},{8,24},{16,0},{24,8},{1,17},{9,25},{17,1},{25,9},{2,18},{10... | collective-permute-start | bytes 196616 | tf_op jit(solution)/shard_map/ppermute | solution.py:44
  63.2 2.5 %collective-permute-done.12.got_ref = f32[2,64,128]{2,1,0:T(8,128)S(1)} collective-permute-done((f32[2,64,128]{2,1,0:T(8,128)S(1)}, f32[2,64,128]{2,1,0:T(8,128)S(1)}, u32[]{:S(2)}, u32[]{:S(2)}) %collective-permute-start.12) | collective-permute-done | bytes 65568 | tf_op jit(solution)/shard_map/ppermute | solution.py:44
  65.8 3.9 %collective-permute-done.13.right_ref = f32[1,64,128]{2,1,0:T(8,128)S(1)} collective-permute-done((f32[1,64,128]{2,1,0:T(8,128)S(1)}, f32[1,64,128]{2,1,0:T(8,128)S(1)}, u32[]{:S(2)}, u32[]{:S(2)}) %collective-permute-start.13) | collective-permute-done | bytes 32800 | tf_op jit(solution)/shard_map/ppermute | solution.py:44
  69.7 3.9 %collective-permute-done.14.right_ref = f32[1,64,128]{2,1,0:T(8,128)S(1)} collective-permute-done((f32[1,64,128]{2,1,0:T(8,128)S(1)}, f32[1,64,128]{2,1,0:T(8,128)S(1)}, u32[]{:S(2)}, u32[]{:S(2)}) %collective-permute-start.14) | collective-permute-done | bytes 32800 | tf_op jit(solution)/shard_map/ppermute | solution.py:44
  73.6 1.7 %collective-permute-start.15 = (f32[1,64,128]{2,1,0:T(8,128)S(1)}, f32[1,64,128]{2,1,0:T(8,128)S(1)}, u32[]{:S(2)}, u32[]{:S(2)}) collective-permute-start(f32[1,64,128]{2,1,0:T(8,128)S(1)} %shard_map.129.left_ref), channel_id=1, source_target_pairs={{0,4},{1,5},{2,6},{3,7},{4,0},{5,1},{6,2},{7,3},{8,12},{9,13},{10,... | collective-permute-start | bytes 98312 | tf_op jit(solution)/shard_map/ppermute | solution.py:44
  75.3 3.1 %collective-permute-done.15.right_ref = f32[1,64,128]{2,1,0:T(8,128)S(1)} collective-permute-done((f32[1,64,128]{2,1,0:T(8,128)S(1)}, f32[1,64,128]{2,1,0:T(8,128)S(1)}, u32[]{:S(2)}, u32[]{:S(2)}) %collective-permute-start.15) | collective-permute-done | bytes 32800 | tf_op jit(solution)/shard_map/ppermute | solution.py:44
  78.4 0.8 collective-permute-start.16
  79.2 3.1 %collective-permute-done.16.right_ref = f32[1,64,128]{2,1,0:T(8,128)S(1)} collective-permute-done((f32[1,64,128]{2,1,0:T(8,128)S(1)}, f32[1,64,128]{2,1,0:T(8,128)S(1)}, u32[]{:S(2)}, u32[]{:S(2)}) %collective-permute-start.16) | collective-permute-done | bytes 32800 | tf_op jit(solution)/shard_map/ppermute | solution.py:44
  82.3 1.8 %collective-permute-start.17 = (f32[2,64,128]{2,1,0:T(8,128)S(1)}, f32[2,64,128]{2,1,0:T(8,128)S(1)}, u32[]{:S(2)}, u32[]{:S(2)}) collective-permute-start(f32[2,64,128]{2,1,0:T(8,128)S(1)} %shard_map.131.left_ref), channel_id=1, source_target_pairs={{0,16},{8,24},{16,0},{24,8},{1,17},{9,25},{17,1},{25,9},{2,18},{10... | collective-permute-start | bytes 196616 | tf_op jit(solution)/shard_map/ppermute | solution.py:44
  84.1 2.5 %collective-permute-done.17.right_ref = f32[2,64,128]{2,1,0:T(8,128)S(1)} collective-permute-done((f32[2,64,128]{2,1,0:T(8,128)S(1)}, f32[2,64,128]{2,1,0:T(8,128)S(1)}, u32[]{:S(2)}, u32[]{:S(2)}) %collective-permute-start.17) | collective-permute-done | bytes 65568 | tf_op jit(solution)/shard_map/ppermute | solution.py:44
  86.7 1.3 %collective-permute-done.18.got_ref = f32[4,64,128]{2,1,0:T(8,128)S(1)} collective-permute-done((f32[4,64,128]{2,1,0:T(8,128)S(1)}, f32[4,64,128]{2,1,0:T(8,128)S(1)}, u32[]{:S(2)}, u32[]{:S(2)}) %collective-permute-start.18) | collective-permute-done | bytes 131104 | tf_op jit(solution)/shard_map/ppermute | solution.py:44
  88.0 1.9 %shard_map.133 = (f32[512,128]{1,0:T(8,128)}, f32[256,128]{1,0:T(8,128)S(1)}, f32[1,64,128]{2,1,0:T(8,128)S(1)}, f32[1,64,128]{2,1,0:T(8,128)S(1)}) custom-call(s32[2]{0:T(128)S(1)} %pad_add_fusion.index_ref, f32[128,128]{1,0:T(8,128)S(1)} %get-tuple-element.30.weight_ref, f32[4,2,128,128]{3,2,1,0:T(8,128)S(1)} %copy-done.2, ...), custom_call_target="tpu_custom_call" | custom-call | tf_op jit(solution)/shard_map/pallas_call | solution.py:510
  90.0 0.1 collective-permute-start.19
  90.1 1.1 collective-permute-done.19.right_ref
  91.2 1.8 %collective-permute-start.20 = (f32[1,64,128]{2,1,0:T(8,128)S(1)}, f32[1,64,128]{2,1,0:T(8,128)S(1)}, u32[]{:S(2)}, u32[]{:S(2)}) collective-permute-start(f32[1,64,128]{2,1,0:T(8,128)S(1)} %shard_map.134.left_ref), channel_id=1, source_target_pairs={{0,16},{8,24},{16,0},{24,8},{1,17},{9,25},{17,1},{25,9},{2,18},{10... | collective-permute-start | bytes 98312 | tf_op jit(solution)/shard_map/ppermute | solution.py:44
  93.0 2.1 %collective-permute-done.20.right_ref = f32[1,64,128]{2,1,0:T(8,128)S(1)} collective-permute-done((f32[1,64,128]{2,1,0:T(8,128)S(1)}, f32[1,64,128]{2,1,0:T(8,128)S(1)}, u32[]{:S(2)}, u32[]{:S(2)}) %collective-permute-start.20) | collective-permute-done | bytes 32800 | tf_op jit(solution)/shard_map/ppermute | solution.py:44
  95.1 0.8 collective-permute-start.21
  95.9 3.1 %collective-permute-done.21.right_ref = f32[1,64,128]{2,1,0:T(8,128)S(1)} collective-permute-done((f32[1,64,128]{2,1,0:T(8,128)S(1)}, f32[1,64,128]{2,1,0:T(8,128)S(1)}, u32[]{:S(2)}, u32[]{:S(2)}) %collective-permute-start.21) | collective-permute-done | bytes 32800 | tf_op jit(solution)/shard_map/ppermute | solution.py:44
  99.0 0.9 collective-permute-start.22
  99.9 3.0 %collective-permute-done.22.right_ref = f32[1,64,128]{2,1,0:T(8,128)S(1)} collective-permute-done((f32[1,64,128]{2,1,0:T(8,128)S(1)}, f32[1,64,128]{2,1,0:T(8,128)S(1)}, u32[]{:S(2)}, u32[]{:S(2)}) %collective-permute-start.22) | collective-permute-done | bytes 32800 | tf_op jit(solution)/shard_map/ppermute | solution.py:44
  103.0 1.8 %collective-permute-start.23 = (f32[1,64,128]{2,1,0:T(8,128)S(1)}, f32[1,64,128]{2,1,0:T(8,128)S(1)}, u32[]{:S(2)}, u32[]{:S(2)}) collective-permute-start(f32[1,64,128]{2,1,0:T(8,128)S(1)} %shard_map.137.left_ref), channel_id=1, source_target_pairs={{0,4},{1,5},{2,6},{3,7},{4,0},{5,1},{6,2},{7,3},{8,12},{9,13},{10,... | collective-permute-start | bytes 98312 | tf_op jit(solution)/shard_map/ppermute | solution.py:44
  104.8 3.0 %collective-permute-done.23.right_ref = f32[1,64,128]{2,1,0:T(8,128)S(1)} collective-permute-done((f32[1,64,128]{2,1,0:T(8,128)S(1)}, f32[1,64,128]{2,1,0:T(8,128)S(1)}, u32[]{:S(2)}, u32[]{:S(2)}) %collective-permute-start.23) | collective-permute-done | bytes 32800 | tf_op jit(solution)/shard_map/ppermute | solution.py:44
  107.8 1.2 %collective-permute-done.24.got_ref = f32[1,64,128]{2,1,0:T(8,128)S(1)} collective-permute-done((f32[1,64,128]{2,1,0:T(8,128)S(1)}, f32[1,64,128]{2,1,0:T(8,128)S(1)}, u32[]{:S(2)}, u32[]{:S(2)}) %collective-permute-start.24) | collective-permute-done | bytes 32800 | tf_op jit(solution)/shard_map/ppermute | solution.py:44
  109.0 5.9 %shard_map.139 = (f32[128,128]{1,0:T(8,128)}, f32[256,128]{1,0:T(8,128)}) custom-call(s32[2]{0:T(128)S(1)} %pad_add_fusion.index_ref, f32[1,64,128]{2,1,0:T(8,128)S(1)} %shard_map.138.held_ref, f32[1,64,128]{2,1,0:T(8,128)S(1)} %collective-permute-done.24.got_ref, f32[256,128]{1,0:T(8,128)S(1)} %get-tuple-element.53.remainder_ref), custom_call_target="tpu_custom_call" | custom-call | tf_op jit(solution)/shard_map/pallas_call | solution.py:510
  (43 shorter events, 0.5 us)
Async XLA Ops:
  0.6 1.0 copy-start
  1.7 0.7 copy-start.5
  2.4 0.7 copy-start.7
  3.0 0.7 copy-start.9
  4.1 6.0 %collective-permute-start = (f32[1,56,128]{2,1,0:T(8,128)S(1)}, f32[1,56,128]{2,1,0:T(8,128)S(1)}, u32[]{:S(2)}, u32[]{:S(2)}) collective-permute-start(f32[1,56,128]{2,1,0:T(8,128)S(1)} %shard_map.112.pack_hbm.left_ref), channel_id=1, source_target_pairs={{0,4},{1,5},{2,6},{3,7},{4,0},{5,1},{6,2},{7,3},{8,12},{9,13},{10,... | collective-permute-start | bytes 86024 | tf_op jit(solution)/shard_map/ppermute | solution.py:44
  10.1 4.2 %collective-permute-start.1 = (f32[2,56,128]{2,1,0:T(8,128)S(1)}, f32[2,56,128]{2,1,0:T(8,128)S(1)}, u32[]{:S(2)}, u32[]{:S(2)}) collective-permute-start(f32[2,56,128]{2,1,0:T(8,128)S(1)} %shard_map.114.left_ref), channel_id=1, source_target_pairs={{0,2},{1,3},{2,0},{3,1},{4,6},{5,7},{6,4},{7,5},{8,10},{9,11},{10,... | collective-permute-start | bytes 172040 | tf_op jit(solution)/shard_map/ppermute | solution.py:44
  14.3 6.6 %collective-permute-start.2 = (f32[4,56,128]{2,1,0:T(8,128)S(1)}, f32[4,56,128]{2,1,0:T(8,128)S(1)}, u32[]{:S(2)}, u32[]{:S(2)}) collective-permute-start(f32[4,56,128]{2,1,0:T(8,128)S(1)} %shard_map.115.held_ref), channel_id=1, source_target_pairs={{0,1},{1,0},{2,3},{3,2},{4,5},{5,4},{6,7},{7,6},{8,9},{9,8},{10,11... | collective-permute-start | bytes 344072 | tf_op jit(solution)/shard_map/ppermute | solution.py:44
  16.3 1.0 copy-start.1
  17.4 1.0 copy-start.3
  18.3 0.7 copy-start.6
  19.0 0.7 copy-start.8
  19.7 0.7 copy-start.10
  21.9 1.3 %collective-permute-start.3 = (f32[2,56,128]{2,1,0:T(8,128)S(1)}, f32[2,56,128]{2,1,0:T(8,128)S(1)}, u32[]{:S(2)}, u32[]{:S(2)}) collective-permute-start(f32[2,56,128]{2,1,0:T(8,128)S(1)} %get-tuple-element.35), channel_id=1, source_target_pairs={{0,8},{8,0},{16,24},{24,16},{1,9},{9,1},{17,25},{25,17},{2,10},{10... | collective-permute-start | bytes 172040 | tf_op jit(solution)/shard_map/ppermute | solution.py:44
  23.3 3.9 %collective-permute-start.4 = (f32[1,56,128]{2,1,0:T(8,128)S(1)}, f32[1,56,128]{2,1,0:T(8,128)S(1)}, u32[]{:S(2)}, u32[]{:S(2)}) collective-permute-start(f32[1,56,128]{2,1,0:T(8,128)S(1)} %get-tuple-element.37), channel_id=1, source_target_pairs={{0,16},{8,24},{16,0},{24,8},{1,17},{9,25},{17,1},{25,9},{2,18},{10... | collective-permute-start | bytes 86024 | tf_op jit(solution)/shard_map/ppermute | solution.py:44
  28.1 5.2 %collective-permute-start.6 = (bf16[1,2,128,128]{3,2,1,0:T(8,128)(2,1)S(1)}, bf16[1,2,128,128]{3,2,1,0:T(8,128)(2,1)S(1)}, u32[]{:S(2)}, u32[]{:S(2)}) collective-permute-start(bf16[1,2,128,128]{3,2,1,0:T(8,128)(2,1)S(1)} %get-tuple-element.39.left_ref), channel_id=1, source_target_pairs={{0,4},{1,5},{2,6},{3,7},{4,0},{5,1},{6,2},{7,3},{8,12},{9,13},{10,... | collective-permute-start | bytes 196616 | tf_op jit(solution)/shard_map/ppermute | solution.py:44
  33.3 5.0 %collective-permute-start.7 = (bf16[2,2,128,128]{3,2,1,0:T(8,128)(2,1)S(1)}, bf16[2,2,128,128]{3,2,1,0:T(8,128)(2,1)S(1)}, u32[]{:S(2)}, u32[]{:S(2)}) collective-permute-start(bf16[2,2,128,128]{3,2,1,0:T(8,128)(2,1)S(1)} %shard_map.119.left_ref), channel_id=1, source_target_pairs={{0,2},{1,3},{2,0},{3,1},{4,6},{5,7},{6,4},{7,5},{8,10},{9,11},{10,... | collective-permute-start | bytes 393224 | tf_op jit(solution)/shard_map/ppermute | solution.py:44
  38.4 12.2 %copy-start.12 = (bf16[8,12,32,32]{3,2,1,0:T(8,128)(2,1)S(1)}, bf16[8,12,32,32]{3,2,1,0:T(8,128)(2,1)}, u32[]{:S(2)}) copy-start(bf16[8,12,32,32]{3,2,1,0:T(8,128)(2,1)} %param.15) | copy-start | bytes 589828
  38.4 6.4 %collective-permute-start.8 = (bf16[4,2,128,128]{3,2,1,0:T(8,128)(2,1)S(1)}, bf16[4,2,128,128]{3,2,1,0:T(8,128)(2,1)S(1)}, u32[]{:S(2)}, u32[]{:S(2)}) collective-permute-start(bf16[4,2,128,128]{3,2,1,0:T(8,128)(2,1)S(1)} %shard_map.120.held_ref), channel_id=1, source_target_pairs={{0,1},{1,0},{2,3},{3,2},{4,5},{5,4},{6,7},{7,6},{8,9},{9,8},{10,11... | collective-permute-start | bytes 786440 | tf_op jit(solution)/shard_map/ppermute | solution.py:44
  40.6 11.0 %copy-start.4 = (s32[8,12]{1,0:T(8,128)S(1)}, s32[8,12]{1,0:T(8,128)}, u32[]{:S(2)}) copy-start(s32[8,12]{1,0:T(8,128)} %panel_ref.1) | copy-start | bytes 1156
  40.6 11.0 %copy-start.11 = (s32[8]{0:T(128)S(1)}, s32[8]{0:T(128)}, u32[]{:S(2)}) copy-start(s32[8]{0:T(128)} %count_ref.1) | copy-start | bytes 100
  46.6 7.3 %copy-start.2 = (f32[4,2,128,128]{3,2,1,0:T(8,128)S(1)}, f32[4,2,128,128]{3,2,1,0:T(8,128)}, u32[]{:S(2)}) copy-start(f32[4,2,128,128]{3,2,1,0:T(8,128)} %basis_ref.3) | copy-start | bytes 1572868
  46.7 1.6 %collective-permute-start.9 = (f32[2,2,128,128]{3,2,1,0:T(8,128)S(1)}, f32[2,2,128,128]{3,2,1,0:T(8,128)S(1)}, u32[]{:S(2)}, u32[]{:S(2)}) collective-permute-start(f32[2,2,128,128]{3,2,1,0:T(8,128)S(1)} %get-tuple-element.41), channel_id=1, source_target_pairs={{0,8},{8,0},{16,24},{24,16},{1,9},{9,1},{17,25},{25,17},{2,10},{10... | collective-permute-start | bytes 786440 | tf_op jit(solution)/shard_map/ppermute | solution.py:44
  48.3 5.6 %collective-permute-start.10 = (f32[1,2,128,128]{3,2,1,0:T(8,128)S(1)}, f32[1,2,128,128]{3,2,1,0:T(8,128)S(1)}, u32[]{:S(2)}, u32[]{:S(2)}) collective-permute-start(f32[1,2,128,128]{3,2,1,0:T(8,128)S(1)} %get-tuple-element.43), channel_id=1, source_target_pairs={{0,16},{8,24},{16,0},{24,8},{1,17},{9,25},{17,1},{25,9},{2,18},{10... | collective-permute-start | bytes 393224 | tf_op jit(solution)/shard_map/ppermute | solution.py:44
  49.9 1.7 %collective-permute-start.5 = (bf16[2,64,128]{2,1,0:T(8,128)(2,1)S(1)}, bf16[2,64,128]{2,1,0:T(8,128)(2,1)S(1)}, u32[]{:S(2)}, u32[]{:S(2)}) collective-permute-start(bf16[2,64,128]{2,1,0:T(8,128)(2,1)S(1)} %get-tuple-element.38), channel_id=1, source_target_pairs={{7,8},{8,7},{15,16},{16,15},{23,24},{24,23}} | collective-permute-start | bytes 98312 | tf_op jit(solution)/shard_map/ppermute | solution.py:598
  55.1 6.1 %collective-permute-start.11 = (f32[4,64,128]{2,1,0:T(8,128)S(1)}, f32[4,64,128]{2,1,0:T(8,128)S(1)}, u32[]{:S(2)}, u32[]{:S(2)}) collective-permute-start(f32[4,64,128]{2,1,0:T(8,128)S(1)} %get-tuple-element.46), channel_id=1, source_target_pairs={{0,8},{8,0},{16,24},{24,16},{1,9},{9,1},{17,25},{25,17},{2,10},{10... | collective-permute-start | bytes 393224 | tf_op jit(solution)/shard_map/ppermute | solution.py:44
  61.2 4.4 %collective-permute-start.12 = (f32[2,64,128]{2,1,0:T(8,128)S(1)}, f32[2,64,128]{2,1,0:T(8,128)S(1)}, u32[]{:S(2)}, u32[]{:S(2)}) collective-permute-start(f32[2,64,128]{2,1,0:T(8,128)S(1)} %get-tuple-element.48), channel_id=1, source_target_pairs={{0,16},{8,24},{16,0},{24,8},{1,17},{9,25},{17,1},{25,9},{2,18},{10... | collective-permute-start | bytes 196616 | tf_op jit(solution)/shard_map/ppermute | solution.py:44
  65.7 4.0 %collective-permute-start.13 = (f32[1,64,128]{2,1,0:T(8,128)S(1)}, f32[1,64,128]{2,1,0:T(8,128)S(1)}, u32[]{:S(2)}, u32[]{:S(2)}) collective-permute-start(f32[1,64,128]{2,1,0:T(8,128)S(1)} %get-tuple-element.50), channel_id=1, source_target_pairs={{0,1},{1,0},{2,3},{3,2},{4,5},{5,4},{6,7},{7,6},{8,9},{9,8},{10,11... | collective-permute-start | bytes 98312 | tf_op jit(solution)/shard_map/ppermute | solution.py:44
  69.7 3.9 %collective-permute-start.14 = (f32[1,64,128]{2,1,0:T(8,128)S(1)}, f32[1,64,128]{2,1,0:T(8,128)S(1)}, u32[]{:S(2)}, u32[]{:S(2)}) collective-permute-start(f32[1,64,128]{2,1,0:T(8,128)S(1)} %shard_map.128.left_ref), channel_id=1, source_target_pairs={{0,2},{1,3},{2,0},{3,1},{4,6},{5,7},{6,4},{7,5},{8,10},{9,11},{10,... | collective-permute-start | bytes 98312 | tf_op jit(solution)/shard_map/ppermute | solution.py:44
  73.6 4.8 %collective-permute-start.15 = (f32[1,64,128]{2,1,0:T(8,128)S(1)}, f32[1,64,128]{2,1,0:T(8,128)S(1)}, u32[]{:S(2)}, u32[]{:S(2)}) collective-permute-start(f32[1,64,128]{2,1,0:T(8,128)S(1)} %shard_map.129.left_ref), channel_id=1, source_target_pairs={{0,4},{1,5},{2,6},{3,7},{4,0},{5,1},{6,2},{7,3},{8,12},{9,13},{10,... | collective-permute-start | bytes 98312 | tf_op jit(solution)/shard_map/ppermute | solution.py:44
  78.4 3.9 %collective-permute-start.16 = (f32[1,64,128]{2,1,0:T(8,128)S(1)}, f32[1,64,128]{2,1,0:T(8,128)S(1)}, u32[]{:S(2)}, u32[]{:S(2)}) collective-permute-start(f32[1,64,128]{2,1,0:T(8,128)S(1)} %shard_map.130.left_ref), channel_id=1, source_target_pairs={{0,1},{1,0},{2,3},{3,2},{4,5},{5,4},{6,7},{7,6},{8,9},{9,8},{10,11... | collective-permute-start | bytes 98312 | tf_op jit(solution)/shard_map/ppermute | solution.py:44
  82.3 4.3 %collective-permute-start.17 = (f32[2,64,128]{2,1,0:T(8,128)S(1)}, f32[2,64,128]{2,1,0:T(8,128)S(1)}, u32[]{:S(2)}, u32[]{:S(2)}) collective-permute-start(f32[2,64,128]{2,1,0:T(8,128)S(1)} %shard_map.131.left_ref), channel_id=1, source_target_pairs={{0,16},{8,24},{16,0},{24,8},{1,17},{9,25},{17,1},{25,9},{2,18},{10... | collective-permute-start | bytes 196616 | tf_op jit(solution)/shard_map/ppermute | solution.py:44
  86.6 1.4 %collective-permute-start.18 = (f32[4,64,128]{2,1,0:T(8,128)S(1)}, f32[4,64,128]{2,1,0:T(8,128)S(1)}, u32[]{:S(2)}, u32[]{:S(2)}) collective-permute-start(f32[4,64,128]{2,1,0:T(8,128)S(1)} %shard_map.132.held_ref), channel_id=1, source_target_pairs={{0,8},{8,0},{16,24},{24,16},{1,9},{9,1},{17,25},{25,17},{2,10},{10... | collective-permute-start | bytes 393224 | tf_op jit(solution)/shard_map/ppermute | solution.py:44
  90.0 1.2 %collective-permute-start.19 = (f32[1,64,128]{2,1,0:T(8,128)S(1)}, f32[1,64,128]{2,1,0:T(8,128)S(1)}, u32[]{:S(2)}, u32[]{:S(2)}) collective-permute-start(f32[1,64,128]{2,1,0:T(8,128)S(1)} %get-tuple-element.52), channel_id=1, source_target_pairs={{0,8},{8,0},{16,24},{24,16},{1,9},{9,1},{17,25},{25,17},{2,10},{10... | collective-permute-start | bytes 98312 | tf_op jit(solution)/shard_map/ppermute | solution.py:44
  91.2 3.9 %collective-permute-start.20 = (f32[1,64,128]{2,1,0:T(8,128)S(1)}, f32[1,64,128]{2,1,0:T(8,128)S(1)}, u32[]{:S(2)}, u32[]{:S(2)}) collective-permute-start(f32[1,64,128]{2,1,0:T(8,128)S(1)} %shard_map.134.left_ref), channel_id=1, source_target_pairs={{0,16},{8,24},{16,0},{24,8},{1,17},{9,25},{17,1},{25,9},{2,18},{10... | collective-permute-start | bytes 98312 | tf_op jit(solution)/shard_map/ppermute | solution.py:44
  95.1 3.9 %collective-permute-start.21 = (f32[1,64,128]{2,1,0:T(8,128)S(1)}, f32[1,64,128]{2,1,0:T(8,128)S(1)}, u32[]{:S(2)}, u32[]{:S(2)}) collective-permute-start(f32[1,64,128]{2,1,0:T(8,128)S(1)} %shard_map.135.left_ref), channel_id=1, source_target_pairs={{0,1},{1,0},{2,3},{3,2},{4,5},{5,4},{6,7},{7,6},{8,9},{9,8},{10,11... | collective-permute-start | bytes 98312 | tf_op jit(solution)/shard_map/ppermute | solution.py:44
  99.0 3.9 %collective-permute-start.22 = (f32[1,64,128]{2,1,0:T(8,128)S(1)}, f32[1,64,128]{2,1,0:T(8,128)S(1)}, u32[]{:S(2)}, u32[]{:S(2)}) collective-permute-start(f32[1,64,128]{2,1,0:T(8,128)S(1)} %shard_map.136.left_ref), channel_id=1, source_target_pairs={{0,2},{1,3},{2,0},{3,1},{4,6},{5,7},{6,4},{7,5},{8,10},{9,11},{10,... | collective-permute-start | bytes 98312 | tf_op jit(solution)/shard_map/ppermute | solution.py:44
  103.0 4.8 %collective-permute-start.23 = (f32[1,64,128]{2,1,0:T(8,128)S(1)}, f32[1,64,128]{2,1,0:T(8,128)S(1)}, u32[]{:S(2)}, u32[]{:S(2)}) collective-permute-start(f32[1,64,128]{2,1,0:T(8,128)S(1)} %shard_map.137.left_ref), channel_id=1, source_target_pairs={{0,4},{1,5},{2,6},{3,7},{4,0},{5,1},{6,2},{7,3},{8,12},{9,13},{10,... | collective-permute-start | bytes 98312 | tf_op jit(solution)/shard_map/ppermute | solution.py:44
  107.8 1.2 %collective-permute-start.24 = (f32[1,64,128]{2,1,0:T(8,128)S(1)}, f32[1,64,128]{2,1,0:T(8,128)S(1)}, u32[]{:S(2)}, u32[]{:S(2)}) collective-permute-start(f32[1,64,128]{2,1,0:T(8,128)S(1)} %shard_map.138.held_ref), channel_id=1, source_target_pairs={{0,8},{8,0},{16,24},{24,16},{1,9},{9,1},{17,25},{25,17},{2,10},{10... | collective-permute-start | bytes 98312 | tf_op jit(solution)/shard_map/ppermute | solution.py:44

commit v5 on v4

v5 whole, which is shorter than its diff:
```python
import functools

import jax
import jax.numpy as jnp
from jax import lax
from jax.experimental import pallas as pl
from jax.experimental.pallas import tpu as pltpu
from jax.sharding import PartitionSpec as P

SPAN = 4


NU = 0.3
DELTA2 = 1e-05
ELASTIC = 40.0
HIGH = lax.Precision.HIGHEST
AXES = ("narrow", "wide")
EXTRA = 8
ROWS = 8
SMEM = pl.BlockSpec(memory_space=pltpu.SMEM)
VMEM = pl.BlockSpec(memory_space=pltpu.VMEM)
HBM = pl.BlockSpec(memory_space=pltpu.HBM)
PARAMS = pltpu.CompilerParams(vmem_limit_bytes=48 * 1024 * 1024)


def dot_rows(left, right, precision=HIGH):
    return lax.dot_general(
        left, right, (((1,), (0,)), ((), ())), precision=precision, preferred_element_type=jnp.float32
    )


def dot_first(left, right):
    return lax.dot_general(
        left, right, (((0,), (0,)), ((), ())), precision=HIGH, preferred_element_type=jnp.float32
    )


def as_column(row, width):
    return jnp.transpose(jnp.broadcast_to(row, (width, row.shape[1])))


def flip(block, mask):
    count = lax.axis_size(AXES)
    return lax.ppermute(block, AXES, [(i, i ^ mask) for i in range(count)])


def masks_of(count, scale=1):
    return [scale << bit for bit in range(count.bit_length() - 1)]


def in_pairs(masks):
    return [masks[k : k + 2] for k in range(0, len(masks), 2)]


def combined(group, number):
    mask = 0
    for bit, part in enumerate(group):
        if number >> bit & 1:
            mask ^= part
    return mask


def flip_each(parts, group):
    return [parts[0]] + [flip(parts[j], combined(group, j)) for j in range(1, 1 << len(group))]


def join_kernel(*refs):
    out_ref = refs[-1]
    size = refs[0].shape[0]
    for j, ref in enumerate(refs[:-1]):
        out_ref[j * size : (j + 1) * size] = ref[...]


def join(parts):
    shape = (len(parts) * parts[0].shape[0],) + parts[0].shape[1:]
    return call(join_kernel, jax.ShapeDtypeStruct(shape, parts[0].dtype), parts)


def gather_steps(held, groups):
    parts = [held]
    for group in groups:
        held = parts[0] if len(parts) == 1 else join(parts)
        parts = flip_each([held] * (1 << len(group)), group)
    return parts


def gather_order(groups):
    order = [0]
    for group in groups:
        order = [k ^ combined(group, j) for j in range(1 << len(group)) for k in order]
    return order


def total_of(values):
    while len(values) > 1:
        values = [values[k] + values[k + 1] for k in range(0, len(values), 2)]
    return values[0]


def sum_kernel(count, *refs):
    parts, outs = refs[:count], refs[count:]
    for k in range(outs[0].shape[0]):
        for j, out_ref in enumerate(outs):
            out_ref[k] = total_of([part[k * len(outs) + j] for part in parts])


def sum_parts(parts, ways):
    out = f32(parts[0].shape[0] // ways, *parts[0].shape[1:])
    return call(functools.partial(sum_kernel, len(parts)), [out] * ways, parts)


def scatter_steps(parts, groups):
    for number, group in enumerate(groups):
        if number:
            parts = sum_parts(parts, 1 << len(group))
        parts = flip_each(parts, group)
    return parts


def sum_steps(parts, halving, butterfly):
    (total,) = sum_parts(scatter_steps(parts, halving), 1)
    for group in butterfly:
        (total,) = sum_parts(flip_each([total] * (1 << len(group)), group), 1)
    return gather_steps(total, halving[::-1])


def part_groups(groups):
    bit, found = 0, []
    for group in groups:
        found.append([1 << (bit + k) for k in range(len(group))])
        bit += len(group)
    return found


def bits_of(index, masks):
    packed = 0
    for bit, mask in enumerate(masks):
        packed = packed + (lax.shift_right_logical(index, mask.bit_length() - 1) & 1) * (1 << bit)
    return packed


def members(agg_ref, a, coarse_count):
    ids = lax.broadcasted_iota(jnp.int32, (coarse_count, agg_ref.shape[1]), 0)
    return jnp.where(ids == agg_ref[a : a + 1, :], 1.0, 0.0)


def load_all(pairs, sems):
    copies = [
        pltpu.make_async_copy(source, target, sems.at[k])
        for k, (source, target) in enumerate(pairs)
    ]
    for copy in copies:
        copy.start()
    for copy in copies:
        copy.wait()


def restrict_kernel(
    agg_hbm, basis_hbm, points_hbm, weight_hbm, pack_ref, agg_ref, newest_ref, points_ref, weight_ref, sems
):
    coarse_count = pack_ref.shape[1] - EXTRA
    point_count = newest_ref.shape[1]
    load_all(
        [
            (basis_hbm.at[basis_hbm.shape[0] - 1], newest_ref),
            (agg_hbm, agg_ref),
            (points_hbm, points_ref),
            (weight_hbm, weight_ref),
        ],
        sems,
    )
    total = dot_rows(members(agg_ref, 0, coarse_count), newest_ref[0]) + dot_rows(
        members(agg_ref, 1, coarse_count), newest_ref[1]
    )
    pack_ref[0, :coarse_count, :] = total
    pack_ref[0, coarse_count:, :] = jnp.concatenate(
        [points_ref[...], weight_ref[...], jnp.zeros((EXTRA - 3, point_count), jnp.float32)], axis=0
    )


def prefetch_kernel(
    pack_hbm,
    agg_hbm,
    basis_hbm,
    jacobi_hbm,
    weight_hbm,
    inverse_hbm,
    inverse_ref,
    member_ref,
    smooth_ref,
    weight_out_ref,
    agg_ref,
    newest_ref,
    jacobi_ref,
    weight_ref,
    sems,
):
    coarse_count = member_ref.shape[1]
    rhs_count = newest_ref.shape[2]
    load_all(
        [
            (basis_hbm.at[basis_hbm.shape[0] - 1], newest_ref),
            (agg_hbm, agg_ref),
            (jacobi_hbm, jacobi_ref),
            (weight_hbm, weight_ref),
            (inverse_hbm, inverse_ref),
        ],
        sems,
    )
    for a in range(2):
        member_ref[a] = members(agg_ref, a, coarse_count)
        smooth_ref[a] = as_column(jacobi_ref[a : a + 1, :], rhs_count) * newest_ref[a]
    weight_out_ref[...] = as_column(weight_ref[...], rhs_count)


def part_at(parts, k):
    size = parts[0].shape[0]
    return parts[k // size], k % size


def coarse_kernel(order, ways, z_count, index_ref, inverse_ref, *refs):
    narrow_count, coarse_count, _ = inverse_ref.shape
    packs = refs[: len(refs) - ways - 3]
    outs = refs[len(packs) : len(packs) + ways]
    source_ref, target_ref, rhs_ref = refs[len(packs) + ways :]
    for k, offset in enumerate(order):
        first = pl.multiple_of((index_ref[1] ^ offset) * coarse_count, 8)
        ref, row = part_at(packs, k)
        rhs_ref[pl.ds(first, coarse_count), :] = ref[row, :coarse_count, :]
    for k in range(z_count):
        ref, row = part_at(packs, k)
        source_ref[k] = ref[row, coarse_count:, :]
    for k in range(target_ref.shape[0]):
        ref, row = part_at(packs, k * z_count)
        target_ref[k] = ref[row, coarse_count:, :]
    for k in range(narrow_count):
        outs[k % ways][k // ways] = dot_rows(inverse_ref[index_ref[0] ^ k], rhs_ref[...])


def precond_kernel(member_ref, smooth_ref, *refs):
    parts = refs[:-3]
    precond_ref, first_ref, last_ref = refs[-3:]
    point_count = smooth_ref.shape[1]
    width = first_ref.shape[1]
    coarse_sol = total_of([part[0] for part in parts])
    for a in range(2):
        value = (smooth_ref[a] + dot_first(member_ref[a], coarse_sol)).astype(jnp.bfloat16)
        precond_ref[0, a] = value
        first_ref[a] = value[:width]
        last_ref[a] = value[point_count - width :]


def matrix_kernel(source_parts, *refs):
    matrix_ref = refs[-1]
    sources = refs[:source_parts]
    targets = refs[source_parts:-1]
    point_count = sources[0].shape[2]
    size = targets[0].shape[0]
    step = pl.program_id(0)
    target = targets[0][lax.rem(step, size)]
    for j in range(1, len(targets)):
        target = jnp.where(step // size == j, targets[j][lax.rem(step, size)], target)
    target_x = as_column(target[0:1, :], point_count)
    target_y = as_column(target[1:2, :], point_count)
    for s in range(matrix_ref.shape[3] // point_count):
        ref, row = part_at(sources, s)
        source = ref[row]
        delta_x = target_x - source[0:1, :]
        delta_y = target_y - source[1:2, :]
        factor = ELASTIC * source[2:3, :]
        square_x = delta_x * delta_x
        square_y = delta_y * delta_y
        square_dist = square_x + square_y + DELTA2
        inverse = 1.0 / square_dist
        log_part = (-0.5 * (3.0 - 4.0 * NU)) * jnp.log(square_dist)
        lanes = slice(s * point_count, (s + 1) * point_count)
        matrix_ref[0, 0, :, lanes] = (factor * (log_part + square_x * inverse)).astype(jnp.bfloat16)
        matrix_ref[0, 1, :, lanes] = (factor * (delta_x * delta_y * inverse)).astype(jnp.bfloat16)
        matrix_ref[0, 2, :, lanes] = (factor * (log_part + square_y * inverse)).astype(jnp.bfloat16)


def far_kernel(ways, matrix_ref, *refs):
    fields = refs[: len(refs) - ways - 1]
    outs = refs[len(fields) : len(fields) + ways]
    fields_ref = refs[-1]
    point_count = fields[0].shape[2]
    step = pl.program_id(0)

    @pl.when(step == 0)
    def _():
        for s in range(fields_ref.shape[1] // point_count):
            ref, row = part_at(fields, s)
            for b in range(2):
                fields_ref[b, s * point_count : (s + 1) * point_count, :] = ref[row, b]

    out_x = dot_rows(matrix_ref[0, 0], fields_ref[0], None) + dot_rows(
        matrix_ref[0, 1], fields_ref[1], None
    )
    out_y = dot_rows(matrix_ref[0, 1], fields_ref[0], None) + dot_rows(
        matrix_ref[0, 2], fields_ref[1], None
    )
    for j, out_ref in enumerate(outs):

        @pl.when(lax.rem(step, ways) == j)
        def _(out_ref=out_ref):
            out_ref[step // ways, 0] = out_x
            out_ref[step // ways, 1] = out_y


def near_kernel(
    index_ref,
    panel_ref,
    count_ref,
    block_ref,
    low_ref,
    own_ref,
    high_ref,
    out_ref,
    line_ref,
    gathered_ref,
):
    point_count = own_ref.shape[2]
    width = low_ref.shape[1]
    panels_dev, double_nodes, _ = block_ref.shape
    nodes = double_nodes // 2
    slot_total = panel_ref.shape[1]
    for b in range(2):
        line_ref[b, :width, :] = low_ref[b]
        line_ref[b, width : width + point_count, :] = own_ref[0, b]
        line_ref[b, width + point_count :, :] = high_ref[b]
    first_panel = index_ref[2] * panels_dev
    lane = lax.broadcasted_iota(jnp.int32, block_ref.shape[1:], 1)
    for p in range(panels_dev):
        for k in range(slot_total):
            first = pl.multiple_of((panel_ref[p, k] - first_panel) * nodes + width, 16)
            for b in range(2):
                row = (k * 2 + b) * nodes
                gathered_ref[p, row : row + nodes, :] = line_ref[b, pl.ds(first, nodes), :]
        blocks = jnp.where(
            lane < count_ref[p] * double_nodes, block_ref[p].astype(jnp.float32), 0.0
        ).astype(jnp.bfloat16)
        near = dot_rows(blocks, gathered_ref[p], None)
        for a in range(2):
            rows = slice(p * nodes, (p + 1) * nodes)
            own = own_ref[0, a, rows, :].astype(jnp.float32)
            out_ref[a, rows, :] = 0.5 * own + near[a * nodes : (a + 1) * nodes, :]


def spread(full_ref, outs, own):
    rows = outs[0].shape[1]
    for k in range(len(outs) * outs[0].shape[0]):
        first = pl.multiple_of((own ^ k) * rows, 8)
        outs[k % len(outs)][k // len(outs)] = full_ref[pl.ds(first, rows), :]


def collect(order, parts, full_ref, own):
    rows = parts[0].shape[1]
    for k, offset in enumerate(order):
        first = pl.multiple_of((own ^ offset) * rows, 8)
        ref, row = part_at(parts, k)
        full_ref[pl.ds(first, rows), :] = ref[row]


def project_kernel(masks, ways, index_ref, weight_ref, basis_ref, base_ref, *refs):
    arrived = refs[: len(refs) - ways - 2]
    image_ref = refs[len(arrived)]
    outs = refs[len(arrived) + 1 : -1]
    full_ref = refs[-1]
    block_total, _, _, rhs_count = basis_ref.shape
    weighted = []
    for a in range(2):
        image = base_ref[a] + total_of([part[0, a] for part in arrived])
        image_ref[a] = image
        weighted.append(image * weight_ref[...])
    for j in range(block_total):
        full_ref[j * rhs_count : (j + 1) * rhs_count, :] = dot_first(
            basis_ref[j, 0], weighted[0]
        ) + dot_first(basis_ref[j, 1], weighted[1])
    spread(full_ref, outs, bits_of(index_ref[2], masks))


def remainder_kernel(
    order, masks, gram_masks, ways, index_ref, weight_ref, basis_ref, image_ref, *refs
):
    parts = refs[: len(refs) - ways - 3]
    hess_ref, remainder_ref = refs[len(parts) : len(parts) + 2]
    outs = refs[len(parts) + 2 : -1]
    gram_ref = refs[-1]
    block_total, _, point_count, rhs_count = basis_ref.shape
    collect(order, parts, hess_ref, bits_of(index_ref[2], masks))
    gram = None
    for a in range(2):
        value = image_ref[a]
        for j in range(block_total):
            value = value - dot_rows(
                basis_ref[j, a], hess_ref[j * rhs_count : (j + 1) * rhs_count, :]
            )
        remainder_ref[a * point_count : (a + 1) * point_count, :] = value
        term = dot_first(value * weight_ref[...], value)
        gram = term if gram is None else gram + term
    gram_ref[...] = gram
    spread(gram_ref, outs, bits_of(index_ref[2], gram_masks))


def factor_kernel(gather, masks, index_ref, remainder_ref, *refs):
    parts = refs[:-4]
    upper_ref, new_ref, work_ref, inverse_ref = refs[-4:]
    order = remainder_ref.shape[1]
    tile = (ROWS, order)
    lane = lax.broadcasted_iota(jnp.int32, tile, 1)
    row = lax.broadcasted_iota(jnp.int32, tile, 0)
    collect(gather, parts, work_ref, bits_of(index_ref[2], masks))
    for block in range(order // ROWS):
        start = block * ROWS
        inverse_ref[start : start + ROWS, :] = jnp.where(lane == row + start, 1.0, 0.0)
    for block in range(order // ROWS):
        start = block * ROWS
        own = work_ref[start : start + ROWS, :]
        own_inverse = inverse_ref[start : start + ROWS, :]
        columns = [
            jnp.broadcast_to(own[:, start + m : start + m + 1], tile) for m in range(ROWS)
        ]
        entry = {
            (j, m): jnp.broadcast_to(columns[m][j : j + 1, :], tile)
            for m in range(ROWS)
            for j in range(m, ROWS)
        }
        scale = []
        for m in range(ROWS):
            scale.append(lax.rsqrt(entry[m, m]))
            for j in range(m + 1, ROWS):
                entry[j, m] = entry[j, m] * scale[m]
            for n in range(m + 1, ROWS):
                for j in range(n, ROWS):
                    entry[j, n] = entry[j, n] - entry[j, m] * entry[n, m]
        solved = []
        solved_inverse = []
        for m in range(ROWS):
            upper_row = jnp.broadcast_to(own[m : m + 1, :], tile)
            inverse_row = jnp.broadcast_to(own_inverse[m : m + 1, :], tile)
            for j in range(m):
                upper_row = upper_row - entry[m, j] * solved[j]
                inverse_row = inverse_row - entry[m, j] * solved_inverse[j]
            upper_row = upper_row * scale[m]
            inverse_row = inverse_row * scale[m]
            solved.append(upper_row)
            solved_inverse.append(inverse_row)
        upper_rows = solved[ROWS - 1]
        inverse_rows = solved_inverse[ROWS - 1]
        for m in range(ROWS - 1):
            upper_rows = jnp.where(row == m, solved[m], upper_rows)
            inverse_rows = jnp.where(row == m, solved_inverse[m], inverse_rows)
        upper_ref[start : start + ROWS, :] = jnp.where(lane >= row + start, upper_rows, 0.0)
        inverse_ref[start : start + ROWS, :] = inverse_rows
        for later in range(block + 1, order // ROWS):
            first = later * ROWS
            target = work_ref[first : first + ROWS, :]
            target_inverse = inverse_ref[first : first + ROWS, :]
            multiplier = []
            for m in range(ROWS):
                value = jnp.broadcast_to(target[:, start + m : start + m + 1], tile)
                for j in range(m):
                    value = value - multiplier[j] * entry[m, j]
                multiplier.append(value * scale[m])
            for m in range(ROWS):
                target = target - multiplier[m] * solved[m]
                target_inverse = target_inverse - multiplier[m] * solved_inverse[m]
            work_ref[first : first + ROWS, :] = target
            inverse_ref[first : first + ROWS, :] = target_inverse
    new_ref[...] = lax.dot_general(
        remainder_ref[...],
        inverse_ref[...],
        (((1,), (1,)), ((), ())),
        precision=HIGH,
        preferred_element_type=jnp.float32,
    )


def f32(*shape):
    return jax.ShapeDtypeStruct(shape, jnp.float32)


def b16(*shape):
    return jax.ShapeDtypeStruct(shape, jnp.bfloat16)


def call(kernel, out_shape, operands, scalars=0, scratch=(), in_hbm=False):
    many = isinstance(out_shape, (tuple, list))
    return pl.pallas_call(
        kernel,
        out_shape=out_shape,
        in_specs=[SMEM] * scalars + [HBM if in_hbm else VMEM] * (len(operands) - scalars),
        out_specs=[VMEM] * len(out_shape) if many else VMEM,
        scratch_shapes=list(scratch),
        compiler_params=PARAMS,
    )(*operands)


def body(
    points,
    quad_weight,
    basis,
    jacobi,
    near_panel,
    near_count,
    near_block,
    agg_index,
    coarse_inverse,
):
    block_total, _, point_count, rhs_count = basis.shape
    coarse_count = coarse_inverse.shape[1]
    narrow_count = lax.axis_size("narrow")
    wide_count = lax.axis_size("wide")
    panels_dev, slot_total = near_panel.shape
    nodes = near_block.shape[2] // 2
    width = SPAN * nodes
    pack_rows = coarse_count + EXTRA
    index = jnp.stack(
        [lax.axis_index("narrow"), lax.axis_index("wide"), lax.axis_index(AXES)]
    ).astype(jnp.int32)
    weight_row = quad_weight[None, :]
    low, *high = masks_of(wide_count)
    core, *across = masks_of(narrow_count, wide_count)
    high_groups = in_pairs(high)
    plane_groups = in_pairs([low] + across)
    wide_groups = high_groups + [[low]]
    narrow_groups = [[core]] + in_pairs(across)
    source_groups = high_groups + [[core]]
    high_count = 1 << len(high)
    source_total = 2 * high_count * point_count
    target_count = narrow_count
    pair_row = pltpu.VMEM((2, point_count), jnp.float32)
    one_row = pltpu.VMEM((1, point_count), jnp.float32)
    pair_index = pltpu.VMEM((2, point_count), jnp.int32)
    field = pltpu.VMEM((2, point_count, rhs_count), jnp.float32)

    pack = call(
        restrict_kernel,
        f32(1, pack_rows, point_count),
        (agg_index, basis, points, weight_row),
        0,
        [pair_index, field, pair_row, one_row, pltpu.SemaphoreType.DMA((4,))],
        True,
    )
    inverse, member, smooth, weight = call(
        prefetch_kernel,
        [
            f32(*coarse_inverse.shape),
            f32(2, coarse_count, point_count),
            f32(2, point_count, rhs_count),
            f32(point_count, rhs_count),
        ],
        (pack, agg_index, basis, jacobi, weight_row, coarse_inverse),
        0,
        [pair_index, field, pair_row, one_row, pltpu.SemaphoreType.DMA((5,))],
        True,
    )
    packs = gather_steps(pack, wide_groups)
    coarse_outs = call(
        functools.partial(coarse_kernel, gather_order(wide_groups), 2, high_count),
        [f32(narrow_count // 2, coarse_count, rhs_count)] * 2
        + [f32(high_count, EXTRA, point_count), f32(2, EXTRA, point_count)],
        (index, inverse, *packs),
        1,
        [pltpu.VMEM((wide_count * coarse_count, rhs_count), jnp.float32)],
    )
    coarse_parts = scatter_steps(coarse_outs[:2], narrow_groups)
    sources = flip_each([coarse_outs[2]] * 2, [core])
    targets = gather_steps(coarse_outs[3], in_pairs(across))
    precond, first, last = call(
        precond_kernel,
        [b16(1, 2, point_count, rhs_count)] + [b16(2, width, rhs_count)] * 2,
        (member, smooth, *coarse_parts),
    )
    fields = gather_steps(precond, source_groups)
    forward = [(i, i + 1) for i in range(narrow_count * wide_count - 1)]
    before = lax.ppermute(last, AXES, forward)
    after = lax.ppermute(first, AXES, [(target, source) for source, target in forward])

    matrix_spec = pl.BlockSpec((1, 3, point_count, source_total), lambda k: (k, 0, 0, 0))
    matrix = pl.pallas_call(
        functools.partial(matrix_kernel, len(sources)),
        out_shape=b16(target_count, 3, point_count, source_total),
        grid=(target_count,),
        in_specs=[VMEM] * (len(sources) + len(targets)),
        out_specs=matrix_spec,
        compiler_params=PARAMS,
    )(*sources, *targets)
    ways = 1 << len(plane_groups[0])
    far_parts = pl.pallas_call(
        functools.partial(far_kernel, ways),
        out_shape=[f32(target_count // ways, 2, point_count, rhs_count)] * ways,
        grid=(target_count,),
        in_specs=[matrix_spec] + [VMEM] * len(fields),
        out_specs=[VMEM] * ways,
        scratch_shapes=[pltpu.VMEM((2, source_total, rhs_count), jnp.bfloat16)],
        compiler_params=PARAMS,
    )(matrix, *fields)
    far_parts = scatter_steps(far_parts, plane_groups)
    near_rows = jnp.transpose(near_block, (0, 2, 1, 3)).reshape(
        panels_dev, 2 * nodes, slot_total * 2 * nodes
    )
    base = call(
        near_kernel,
        f32(2, point_count, rhs_count),
        (index, near_panel, near_count, near_rows, before, precond, after),
        3,
        [
            pltpu.VMEM((2, 2 * width + point_count, rhs_count), jnp.bfloat16),
            pltpu.VMEM((panels_dev, slot_total * 2 * nodes, rhs_count), jnp.bfloat16),
        ],
    )

    hess_rows = block_total * rhs_count
    halving = [[core]] + plane_groups
    hess_masks = [core, low] + across
    image, *parts = call(
        functools.partial(project_kernel, hess_masks, 2),
        [f32(2, point_count, rhs_count)]
        + [f32(narrow_count, hess_rows // (2 * narrow_count), rhs_count)] * 2,
        (index, weight, basis, base, *far_parts),
        1,
        [pltpu.VMEM((hess_rows, rhs_count), jnp.float32)],
    )
    parts = sum_steps(parts, halving, high_groups)
    hessenberg, remainder, *gram_parts = call(
        functools.partial(
            remainder_kernel, gather_order(part_groups(halving)[::-1]), hess_masks, [core], 2
        ),
        [f32(hess_rows, rhs_count), f32(2 * point_count, rhs_count)]
        + [f32(1, rhs_count // 2, rhs_count)] * 2,
        (index, weight, basis, image, *parts),
        1,
        [pltpu.VMEM((rhs_count, rhs_count), jnp.float32)],
    )
    gram_parts = sum_steps(gram_parts, [[core]], plane_groups + high_groups)
    upper_factor, new_block = call(
        functools.partial(factor_kernel, gather_order([[1]]), [core]),
        [f32(rhs_count, rhs_count), f32(2 * point_count, rhs_count)],
        (index, remainder, *gram_parts),
        1,
        [pltpu.VMEM((rhs_count, rhs_count), jnp.float32)] * 2,
    )
    return (
        new_block.reshape(2, point_count, rhs_count),
        hessenberg.reshape(block_total, rhs_count, rhs_count),
        upper_factor,
    )


def solution(mesh):
    in_specs = (
        P(None, ("narrow", "wide")),
        P(("narrow", "wide")),
        P(None, None, ("narrow", "wide"), None),
        P(None, ("narrow", "wide")),
        P(("narrow", "wide"), None),
        P(("narrow", "wide")),
        P(("narrow", "wide"), None, None, None),
        P(None, ("narrow", "wide")),
        P(None, "wide", "narrow"),
    )
    out_specs = (P(None, ("narrow", "wide"), None), P(), P())
    return jax.shard_map(body, mesh=mesh, in_specs=in_specs, out_specs=out_specs, check_vma=False)
```

time: 115 us -> 109 us (0.948)
  waiting for transfers between devices: 55.7 us -> 37.7 us
  starting transfers between devices: 33.4 us -> 45.3 us
    ppermute x25 -> x36, waiting for transfers between devices: 55.7 us -> 37.7 us  [the longest x34 34.2 us: flip(): return lax.ppermute(block, AXES, [(i, i ^ mask) for i in range(count)])]
    ppermute x25 -> x36, starting transfers between devices: 33.4 us -> 45.3 us  [the longest x34 41.6 us: flip(): return lax.ppermute(block, AXES, [(i, i ^ mask) for i in range(count)])]
    pallas_call x26 -> x18, Pallas kernels: 13 us -> 12.4 us  [call(): pl.pallas_call(kernel, out_shape=out_shape, in_specs=[SMEM] * scalars + [...]
  transfers between devices with their start and end apart: 25 -> 36, of which waited for: 23 -> 24; matrix products, arithmetic and copies ran while one was open for 1% -> 1% of each run, Pallas kernels for 3% -> 3%
where the time goes in v5:
time: 109 us; the launch traced here: 108 us
  starting transfers between devices  45.3 us (42%)
  waiting for transfers between devices  37.7 us (35%)
  Pallas kernels  16.2 us (15%)
  local copies, waits for them, and re-layouts  8.13 us (7%)
    ppermute x34, starting transfers between devices, flip(): return lax.ppermute(block, AXES, [(i, i ^ mask) for i in range(count)])  41.6 us
    ppermute x34, waiting for transfers between devices, flip(): return lax.ppermute(block, AXES, [(i, i ^ mask) for i in range(count)])  34.2 us
    pallas_call x18, Pallas kernels, call(): pl.pallas_call(kernel, out_shape=out_shape, in_specs=[SMEM] * scalars + [...  12.4 us
    unnamed x26, local copies, waits for them, and re-layouts  7.08 us
    ppermute x1, waiting for transfers between devices, body(): lax.ppermute(first, AXES, [(target, source) for source, target in forward])  3.42 us
    ppermute x1, starting transfers between devices, body(): before = lax.ppermute(last, AXES, forward)  2.43 us
  transfers between devices with their start and end apart: 36, of which 24 were waited for; matrix products, arithmetic and copies ran while one was open for 1% of the time, Pallas kernels for 3%

profile of v5, /device:TPU:0, one launch (start us, length us, event | category | flops | bytes accessed | tf_op | source)
XLA Modules:
  0.0 108.3 jit_solution(162783638581035775)
XLA Ops:
  0.6 1.0 copy-done
  1.7 0.7 copy-done.5
  2.4 0.7 copy-done.7
  3.0 0.7 copy-done.9
  4.1 5.1 %collective-permute-start.2 = (f32[1,56,128]{2,1,0:T(8,128)S(1)}, f32[1,56,128]{2,1,0:T(8,128)S(1)}, u32[]{:S(2)}, u32[]{:S(2)}) collective-permute-start(f32[1,56,128]{2,1,0:T(8,128)S(1)} %shard_map.112.pack_hbm.refs_0_), channel_id=1, source_target_pairs={{0,6},{1,7},{2,4},{3,5},{4,2},{5,3},{6,0},{7,1},{8,14},{9,15},{10,... | collective-permute-start | bytes 86024 | tf_op jit(solution)/shard_map/ppermute | solution.py:44
  9.2 0.6 collective-permute-start
  9.9 1.2 %collective-permute-done.2.refs_3_ = f32[1,56,128]{2,1,0:T(8,128)S(1)} collective-permute-done((f32[1,56,128]{2,1,0:T(8,128)S(1)}, f32[1,56,128]{2,1,0:T(8,128)S(1)}, u32[]{:S(2)}, u32[]{:S(2)}) %collective-permute-start.2) | collective-permute-done | bytes 28704 | tf_op jit(solution)/shard_map/ppermute | solution.py:44
  11.1 2.9 %collective-permute-done.1.refs_2_ = f32[1,56,128]{2,1,0:T(8,128)S(1)} collective-permute-done((f32[1,56,128]{2,1,0:T(8,128)S(1)}, f32[1,56,128]{2,1,0:T(8,128)S(1)}, u32[]{:S(2)}, u32[]{:S(2)}) %collective-permute-start.1) | collective-permute-done | bytes 28704 | tf_op jit(solution)/shard_map/ppermute | solution.py:44
  14.0 1.6 %collective-permute-start.3 = (f32[4,56,128]{2,1,0:T(8,128)S(1)}, f32[4,56,128]{2,1,0:T(8,128)S(1)}, u32[]{:S(2)}, u32[]{:S(2)}) collective-permute-start(f32[4,56,128]{2,1,0:T(8,128)S(1)} %shard_map.114.refs_0_), channel_id=1, source_target_pairs={{0,1},{1,0},{2,3},{3,2},{4,5},{5,4},{6,7},{7,6},{8,9},{9,8},{10,11... | collective-permute-start | bytes 344072 | tf_op jit(solution)/shard_map/ppermute | solution.py:44
  15.6 1.0 copy-done.1
  16.6 1.0 copy-done.3
  17.6 0.7 copy-done.6
  18.3 0.7 copy-done.8
  18.9 0.7 copy-done.10
  20.1 1.1 %shard_map.115 = (f32[2,48,128]{2,1,0:T(8,128)S(1)}, f32[2,48,128]{2,1,0:T(8,128)S(1)}, f32[4,8,128]{2,1,0:T(8,128)S(1)}, f32[2,8,128]{2,1,0:T(8,128)S(1)}) custom-call(s32[3]{0:T(128)S(1)} %pad_add_fusion.index_ref, f32[4,48,384]{2,1,0:T(8,128)S(1)} %get-tuple-element.36.inverse_ref, f32[4,56,128]{2,1,0:T(8,128)S(1)} %shard_map.114.refs_0_, ...), custom_call_target="tpu_custom_call" | custom-call | tf_op jit(solution)/shard_map/pallas_call | solution.py:489
  21.3 1.2 %collective-permute-done.4.refs_1_ = f32[2,48,128]{2,1,0:T(8,128)S(1)} collective-permute-done((f32[2,48,128]{2,1,0:T(8,128)S(1)}, f32[2,48,128]{2,1,0:T(8,128)S(1)}, u32[]{:S(2)}, u32[]{:S(2)}) %collective-permute-start.4) | collective-permute-done | bytes 49184 | tf_op jit(solution)/shard_map/ppermute | solution.py:44
  22.5 1.6 %collective-permute-start.5 = (f32[1,48,128]{2,1,0:T(8,128)S(1)}, f32[1,48,128]{2,1,0:T(8,128)S(1)}, u32[]{:S(2)}, u32[]{:S(2)}) collective-permute-start(f32[1,48,128]{2,1,0:T(8,128)S(1)} %get-tuple-element.40), channel_id=1, source_target_pairs={{0,16},{1,17},{2,18},{3,19},{4,20},{5,21},{6,22},{7,23},{8,24},{9,... | collective-permute-start | bytes 73736 | tf_op jit(solution)/shard_map/ppermute | solution.py:44
  24.1 2.3 %collective-permute-done.5.refs_1_ = f32[1,48,128]{2,1,0:T(8,128)S(1)} collective-permute-done((f32[1,48,128]{2,1,0:T(8,128)S(1)}, f32[1,48,128]{2,1,0:T(8,128)S(1)}, u32[]{:S(2)}, u32[]{:S(2)}) %collective-permute-start.5) | collective-permute-done | bytes 24608 | tf_op jit(solution)/shard_map/ppermute | solution.py:44
  26.7 1.5 %collective-permute-start.12 = (bf16[1,2,128,128]{3,2,1,0:T(8,128)(2,1)S(1)}, bf16[1,2,128,128]{3,2,1,0:T(8,128)(2,1)S(1)}, u32[]{:S(2)}, u32[]{:S(2)}) collective-permute-start(bf16[1,2,128,128]{3,2,1,0:T(8,128)(2,1)S(1)} %get-tuple-element.42.own_ref.refs_0_), channel_id=1, source_target_pairs={{0,6},{1,7},{2,4},{3,5},{4,2},{5,3},{6,0},{7,1},{8,14},{9,15},{10,... | collective-permute-start | bytes 196616 | tf_op jit(solution)/shard_map/ppermute | solution.py:44
  28.2 0.6 collective-permute-start.11
  28.9 2.3 %collective-permute-start.10 = (bf16[1,2,128,128]{3,2,1,0:T(8,128)(2,1)S(1)}, bf16[1,2,128,128]{3,2,1,0:T(8,128)(2,1)S(1)}, u32[]{:S(2)}, u32[]{:S(2)}) collective-permute-start(bf16[1,2,128,128]{3,2,1,0:T(8,128)(2,1)S(1)} %get-tuple-element.42.own_ref.refs_0_), channel_id=1, source_target_pairs={{0,2},{1,3},{2,0},{3,1},{4,6},{5,7},{6,4},{7,5},{8,10},{9,11},{10,... | collective-permute-start | bytes 196616 | tf_op jit(solution)/shard_map/ppermute | solution.py:44
  31.1 2.1 %collective-permute-done.12.refs_3_ = bf16[1,2,128,128]{3,2,1,0:T(8,128)(2,1)S(1)} collective-permute-done((bf16[1,2,128,128]{3,2,1,0:T(8,128)(2,1)S(1)}, bf16[1,2,128,128]{3,2,1,0:T(8,128)(2,1)S(1)}, u32[]{:S(2)}, u32[]{:S(2)}) %collective-permute-start.12) | collective-permute-done | bytes 65568 | tf_op jit(solution)/shard_map/ppermute | solution.py:44
  33.2 1.8 %collective-permute-done.11.refs_2_ = bf16[1,2,128,128]{3,2,1,0:T(8,128)(2,1)S(1)} collective-permute-done((bf16[1,2,128,128]{3,2,1,0:T(8,128)(2,1)S(1)}, bf16[1,2,128,128]{3,2,1,0:T(8,128)(2,1)S(1)}, u32[]{:S(2)}, u32[]{:S(2)}) %collective-permute-start.11) | collective-permute-done | bytes 65568 | tf_op jit(solution)/shard_map/ppermute | solution.py:44
  35.6 1.5 %collective-permute-start.9 = (f32[2,8,128]{2,1,0:T(8,128)S(1)}, f32[2,8,128]{2,1,0:T(8,128)S(1)}, u32[]{:S(2)}, u32[]{:S(2)}) collective-permute-start(f32[2,8,128]{2,1,0:T(8,128)S(1)} %get-tuple-element.45.refs_2_), channel_id=1, source_target_pairs={{0,16},{1,17},{2,18},{3,19},{4,20},{5,21},{6,22},{7,23},{8,24},{9,... | collective-permute-start | bytes 24584 | tf_op jit(solution)/shard_map/ppermute | solution.py:44
  37.1 2.1 %collective-permute-done.9.refs_3_ = f32[2,8,128]{2,1,0:T(8,128)S(1)} collective-permute-done((f32[2,8,128]{2,1,0:T(8,128)S(1)}, f32[2,8,128]{2,1,0:T(8,128)S(1)}, u32[]{:S(2)}, u32[]{:S(2)}) %collective-permute-start.9) | collective-permute-done | bytes 8224 | tf_op jit(solution)/shard_map/ppermute | solution.py:44
  39.3 1.9 %shard_map.119.matrix_ref = bf16[4,3,128,1024]{3,2,1,0:T(8,128)(2,1)S(1)} custom-call(f32[4,8,128]{2,1,0:T(8,128)S(1)} %get-tuple-element.44.refs_0_, f32[4,8,128]{2,1,0:T(8,128)S(1)} %collective-permute-done.8.refs_1_, f32[2,8,128]{2,1,0:T(8,128)S(1)} %get-tuple-element.45.refs_2_, f32[2,8,128]{2,1,0:T(8,128)S(1)} %collective-permute-done.9.refs_3_), custom_call_target="tpu_custom_call" | custom-call | tf_op jit(solution)/shard_map/pallas_call | solution.py:581
  41.2 1.9 %shard_map.121 = (f32[1,2,128,128]{3,2,1,0:T(8,128)S(1)}, f32[1,2,128,128]{3,2,1,0:T(8,128)S(1)}, f32[1,2,128,128]{3,2,1,0:T(8,128)S(1)}, f32[1,2,128,128]{3,2,1,0:T(8,128)S(1)}) custom-call(bf16[4,3,128,1024]{3,2,1,0:T(8,128)(2,1)S(1)} %shard_map.119.matrix_ref, bf16[4,2,128,128]{3,2,1,0:T(8,128)(2,1)S(1)} %shard_map.120.refs_0_, ...), custom_call_target="tpu_custom_call" | custom-call | tf_op jit(solution)/shard_map/pallas_call | solution.py:590
  43.1 0.6 collective-permute-start.14
  43.7 1.5 %collective-permute-start.15 = (f32[1,2,128,128]{3,2,1,0:T(8,128)S(1)}, f32[1,2,128,128]{3,2,1,0:T(8,128)S(1)}, u32[]{:S(2)}, u32[]{:S(2)}) collective-permute-start(f32[1,2,128,128]{3,2,1,0:T(8,128)S(1)} %get-tuple-element.48), channel_id=1, source_target_pairs={{0,16},{1,17},{2,18},{3,19},{4,20},{5,21},{6,22},{7,23},{8,24},{9,... | collective-permute-start | bytes 393224 | tf_op jit(solution)/shard_map/ppermute | solution.py:44
  45.2 1.4 %collective-permute-start.16 = (f32[1,2,128,128]{3,2,1,0:T(8,128)S(1)}, f32[1,2,128,128]{3,2,1,0:T(8,128)S(1)}, u32[]{:S(2)}, u32[]{:S(2)}) collective-permute-start(f32[1,2,128,128]{3,2,1,0:T(8,128)S(1)} %get-tuple-element.49), channel_id=1, source_target_pairs={{0,17},{1,16},{2,19},{3,18},{4,21},{5,20},{6,23},{7,22},{8,25},{9,... | collective-permute-start | bytes 393224 | tf_op jit(solution)/shard_map/ppermute | solution.py:44
  46.7 2.4 %collective-permute-start.6 = (bf16[2,64,128]{2,1,0:T(8,128)(2,1)S(1)}, bf16[2,64,128]{2,1,0:T(8,128)(2,1)S(1)}, u32[]{:S(2)}, u32[]{:S(2)}) collective-permute-start(bf16[2,64,128]{2,1,0:T(8,128)(2,1)S(1)} %get-tuple-element.41), channel_id=1, source_target_pairs={{0,1},{1,2},{2,3},{3,4},{4,5},{5,6},{6,7},{7,8},{8,9},{9,10},{10,1... | collective-permute-start | bytes 98312 | tf_op jit(solution)/shard_map/ppermute | solution.py:577
  49.1 1.3 %collective-permute-start.7 = (bf16[2,64,128]{2,1,0:T(8,128)(2,1)S(1)}, bf16[2,64,128]{2,1,0:T(8,128)(2,1)S(1)}, u32[]{:S(2)}, u32[]{:S(2)}) collective-permute-start(bf16[2,64,128]{2,1,0:T(8,128)(2,1)S(1)} %get-tuple-element.43), channel_id=1, source_target_pairs={{1,0},{2,1},{3,2},{4,3},{5,4},{6,5},{7,6},{8,7},{9,8},{10,9},{11,1... | collective-permute-start | bytes 98312 | tf_op jit(solution)/shard_map/ppermute | solution.py:578
  50.8 0.7 reshape.15.block_ref
  51.5 3.4 %collective-permute-done.7.high_ref = bf16[2,64,128]{2,1,0:T(8,128)(2,1)S(1)} collective-permute-done((bf16[2,64,128]{2,1,0:T(8,128)(2,1)S(1)}, bf16[2,64,128]{2,1,0:T(8,128)(2,1)S(1)}, u32[]{:S(2)}, u32[]{:S(2)}) %collective-permute-start.7) | collective-permute-done | bytes 32800 | tf_op jit(solution)/shard_map/ppermute | solution.py:578
  54.9 1.0 shard_map.118.base_ref
  56.0 1.2 %shard_map.122 = (f32[2,128,128]{2,1,0:T(8,128)S(1)}, f32[4,64,128]{2,1,0:T(8,128)S(1)}, f32[4,64,128]{2,1,0:T(8,128)S(1)}) custom-call(s32[3]{0:T(128)S(1)} %pad_add_fusion.index_ref, f32[128,128]{1,0:T(8,128)S(1)} %get-tuple-element.33.weight_ref, f32[4,2,128,128]{3,2,1,0:T(8,128)S(1)} %copy-done.2, f32[2,128,128]{2,1,0:T(8,128)S(1)} %shard_map.118.base_ref, ...), custom_call_target="tpu_custom_call" | custom-call | tf_op jit(solution)/shard_map/pallas_call | solution.py:489
  57.3 1.3 %collective-permute-done.17.refs_1_ = f32[4,64,128]{2,1,0:T(8,128)S(1)} collective-permute-done((f32[4,64,128]{2,1,0:T(8,128)S(1)}, f32[4,64,128]{2,1,0:T(8,128)S(1)}, u32[]{:S(2)}, u32[]{:S(2)}) %collective-permute-start.17) | collective-permute-done | bytes 131104 | tf_op jit(solution)/shard_map/ppermute | solution.py:44
  58.6 2.3 %collective-permute-start.18 = (f32[1,64,128]{2,1,0:T(8,128)S(1)}, f32[1,64,128]{2,1,0:T(8,128)S(1)}, u32[]{:S(2)}, u32[]{:S(2)}) collective-permute-start(f32[1,64,128]{2,1,0:T(8,128)S(1)} %get-tuple-element.54), channel_id=1, source_target_pairs={{0,1},{1,0},{2,3},{3,2},{4,5},{5,4},{6,7},{7,6},{8,9},{9,8},{10,11... | collective-permute-start | bytes 98312 | tf_op jit(solution)/shard_map/ppermute | solution.py:44
  60.9 1.9 %collective-permute-start.19 = (f32[1,64,128]{2,1,0:T(8,128)S(1)}, f32[1,64,128]{2,1,0:T(8,128)S(1)}, u32[]{:S(2)}, u32[]{:S(2)}) collective-permute-start(f32[1,64,128]{2,1,0:T(8,128)S(1)} %get-tuple-element.55), channel_id=1, source_target_pairs={{0,16},{1,17},{2,18},{3,19},{4,20},{5,21},{6,22},{7,23},{8,24},{9,... | collective-permute-start | bytes 98312 | tf_op jit(solution)/shard_map/ppermute | solution.py:44
  62.8 1.4 %collective-permute-start.20 = (f32[1,64,128]{2,1,0:T(8,128)S(1)}, f32[1,64,128]{2,1,0:T(8,128)S(1)}, u32[]{:S(2)}, u32[]{:S(2)}) collective-permute-start(f32[1,64,128]{2,1,0:T(8,128)S(1)} %get-tuple-element.56), channel_id=1, source_target_pairs={{0,17},{1,16},{2,19},{3,18},{4,21},{5,20},{6,23},{7,22},{8,25},{9,... | collective-permute-start | bytes 98312 | tf_op jit(solution)/shard_map/ppermute | solution.py:44
  64.2 0.7 collective-permute-done.19.refs_2_
  64.8 2.8 %collective-permute-done.20.refs_3_ = f32[1,64,128]{2,1,0:T(8,128)S(1)} collective-permute-done((f32[1,64,128]{2,1,0:T(8,128)S(1)}, f32[1,64,128]{2,1,0:T(8,128)S(1)}, u32[]{:S(2)}, u32[]{:S(2)}) %collective-permute-start.20) | collective-permute-done | bytes 32800 | tf_op jit(solution)/shard_map/ppermute | solution.py:44
  67.6 4.5 %collective-permute-start.23 = (f32[1,64,128]{2,1,0:T(8,128)S(1)}, f32[1,64,128]{2,1,0:T(8,128)S(1)}, u32[]{:S(2)}, u32[]{:S(2)}) collective-permute-start(f32[1,64,128]{2,1,0:T(8,128)S(1)} %shard_map.124.refs_0_), channel_id=1, source_target_pairs={{0,6},{1,7},{2,4},{3,5},{4,2},{5,3},{6,0},{7,1},{8,14},{9,15},{10,... | collective-permute-start | bytes 98312 | tf_op jit(solution)/shard_map/ppermute | solution.py:44
  72.1 0.6 collective-permute-start.21
  72.7 1.3 %collective-permute-done.23.refs_3_ = f32[1,64,128]{2,1,0:T(8,128)S(1)} collective-permute-done((f32[1,64,128]{2,1,0:T(8,128)S(1)}, f32[1,64,128]{2,1,0:T(8,128)S(1)}, u32[]{:S(2)}, u32[]{:S(2)}) %collective-permute-start.23) | collective-permute-done | bytes 32800 | tf_op jit(solution)/shard_map/ppermute | solution.py:44
  74.0 2.8 %collective-permute-done.22.refs_2_ = f32[1,64,128]{2,1,0:T(8,128)S(1)} collective-permute-done((f32[1,64,128]{2,1,0:T(8,128)S(1)}, f32[1,64,128]{2,1,0:T(8,128)S(1)}, u32[]{:S(2)}, u32[]{:S(2)}) %collective-permute-start.22) | collective-permute-done | bytes 32800 | tf_op jit(solution)/shard_map/ppermute | solution.py:44
  76.9 1.6 %collective-permute-start.26 = (f32[1,64,128]{2,1,0:T(8,128)S(1)}, f32[1,64,128]{2,1,0:T(8,128)S(1)}, u32[]{:S(2)}, u32[]{:S(2)}) collective-permute-start(f32[1,64,128]{2,1,0:T(8,128)S(1)} %shard_map.125.refs_0_), channel_id=1, source_target_pairs={{0,17},{1,16},{2,19},{3,18},{4,21},{5,20},{6,23},{7,22},{8,25},{9,... | collective-permute-start | bytes 98312 | tf_op jit(solution)/shard_map/ppermute | solution.py:44
  79.1 1.4 %collective-permute-start.24 = (f32[1,64,128]{2,1,0:T(8,128)S(1)}, f32[1,64,128]{2,1,0:T(8,128)S(1)}, u32[]{:S(2)}, u32[]{:S(2)}) collective-permute-start(f32[1,64,128]{2,1,0:T(8,128)S(1)} %shard_map.125.refs_0_), channel_id=1, source_target_pairs={{0,1},{1,0},{2,3},{3,2},{4,5},{5,4},{6,7},{7,6},{8,9},{9,8},{10,11... | collective-permute-start | bytes 98312 | tf_op jit(solution)/shard_map/ppermute | solution.py:44
  80.5 1.3 %collective-permute-done.26.refs_3_ = f32[1,64,128]{2,1,0:T(8,128)S(1)} collective-permute-done((f32[1,64,128]{2,1,0:T(8,128)S(1)}, f32[1,64,128]{2,1,0:T(8,128)S(1)}, u32[]{:S(2)}, u32[]{:S(2)}) %collective-permute-start.26) | collective-permute-done | bytes 32800 | tf_op jit(solution)/shard_map/ppermute | solution.py:44
  81.8 0.6 collective-permute-done.25.refs_2_
  83.1 1.3 %collective-permute-done.27.refs_1_ = f32[4,64,128]{2,1,0:T(8,128)S(1)} collective-permute-done((f32[4,64,128]{2,1,0:T(8,128)S(1)}, f32[4,64,128]{2,1,0:T(8,128)S(1)}, u32[]{:S(2)}, u32[]{:S(2)}) %collective-permute-start.27) | collective-permute-done | bytes 131104 | tf_op jit(solution)/shard_map/ppermute | solution.py:44
  84.4 1.9 %shard_map.127 = (f32[512,128]{1,0:T(8,128)}, f32[256,128]{1,0:T(8,128)S(1)}, f32[1,64,128]{2,1,0:T(8,128)S(1)}, f32[1,64,128]{2,1,0:T(8,128)S(1)}) custom-call(s32[3]{0:T(128)S(1)} %pad_add_fusion.index_ref, f32[128,128]{1,0:T(8,128)S(1)} %get-tuple-element.33.weight_ref, f32[4,2,128,128]{3,2,1,0:T(8,128)S(1)} %copy-done.2, ...), custom_call_target="tpu_custom_call" | custom-call | tf_op jit(solution)/shard_map/pallas_call | solution.py:489
  86.5 1.1 collective-permute-done.28.refs_1_
  87.6 2.8 %collective-permute-start.31 = (f32[1,64,128]{2,1,0:T(8,128)S(1)}, f32[1,64,128]{2,1,0:T(8,128)S(1)}, u32[]{:S(2)}, u32[]{:S(2)}) collective-permute-start(f32[1,64,128]{2,1,0:T(8,128)S(1)} %shard_map.128.refs_0_), channel_id=1, source_target_pairs={{0,17},{1,16},{2,19},{3,18},{4,21},{5,20},{6,23},{7,22},{8,25},{9,... | collective-permute-start | bytes 98312 | tf_op jit(solution)/shard_map/ppermute | solution.py:44
  90.4 0.6 collective-permute-start.29
  91.1 1.3 %collective-permute-done.31.refs_3_ = f32[1,64,128]{2,1,0:T(8,128)S(1)} collective-permute-done((f32[1,64,128]{2,1,0:T(8,128)S(1)}, f32[1,64,128]{2,1,0:T(8,128)S(1)}, u32[]{:S(2)}, u32[]{:S(2)}) %collective-permute-start.31) | collective-permute-done | bytes 32800 | tf_op jit(solution)/shard_map/ppermute | solution.py:44
  92.4 1.9 %collective-permute-done.30.refs_2_ = f32[1,64,128]{2,1,0:T(8,128)S(1)} collective-permute-done((f32[1,64,128]{2,1,0:T(8,128)S(1)}, f32[1,64,128]{2,1,0:T(8,128)S(1)}, u32[]{:S(2)}, u32[]{:S(2)}) %collective-permute-start.30) | collective-permute-done | bytes 32800 | tf_op jit(solution)/shard_map/ppermute | solution.py:44
  94.4 1.5 %collective-permute-start.34 = (f32[1,64,128]{2,1,0:T(8,128)S(1)}, f32[1,64,128]{2,1,0:T(8,128)S(1)}, u32[]{:S(2)}, u32[]{:S(2)}) collective-permute-start(f32[1,64,128]{2,1,0:T(8,128)S(1)} %shard_map.129.refs_0_), channel_id=1, source_target_pairs={{0,6},{1,7},{2,4},{3,5},{4,2},{5,3},{6,0},{7,1},{8,14},{9,15},{10,... | collective-permute-start | bytes 98312 | tf_op jit(solution)/shard_map/ppermute | solution.py:44
  95.9 0.6 collective-permute-start.33
  96.5 2.3 %collective-permute-start.32 = (f32[1,64,128]{2,1,0:T(8,128)S(1)}, f32[1,64,128]{2,1,0:T(8,128)S(1)}, u32[]{:S(2)}, u32[]{:S(2)}) collective-permute-start(f32[1,64,128]{2,1,0:T(8,128)S(1)} %shard_map.129.refs_0_), channel_id=1, source_target_pairs={{0,2},{1,3},{2,0},{3,1},{4,6},{5,7},{6,4},{7,5},{8,10},{9,11},{10,... | collective-permute-start | bytes 98312 | tf_op jit(solution)/shard_map/ppermute | solution.py:44
  98.8 1.3 %collective-permute-done.34.refs_3_ = f32[1,64,128]{2,1,0:T(8,128)S(1)} collective-permute-done((f32[1,64,128]{2,1,0:T(8,128)S(1)}, f32[1,64,128]{2,1,0:T(8,128)S(1)}, u32[]{:S(2)}, u32[]{:S(2)}) %collective-permute-start.34) | collective-permute-done | bytes 32800 | tf_op jit(solution)/shard_map/ppermute | solution.py:44
  100.1 0.6 collective-permute-done.33.refs_2_
  101.1 1.2 %collective-permute-done.35.refs_1_ = f32[1,64,128]{2,1,0:T(8,128)S(1)} collective-permute-done((f32[1,64,128]{2,1,0:T(8,128)S(1)}, f32[1,64,128]{2,1,0:T(8,128)S(1)}, u32[]{:S(2)}, u32[]{:S(2)}) %collective-permute-start.35) | collective-permute-done | bytes 32800 | tf_op jit(solution)/shard_map/ppermute | solution.py:44
  102.3 5.9 %shard_map.131 = (f32[128,128]{1,0:T(8,128)}, f32[256,128]{1,0:T(8,128)}) custom-call(s32[3]{0:T(128)S(1)} %pad_add_fusion.index_ref, f32[256,128]{1,0:T(8,128)S(1)} %get-tuple-element.57.remainder_ref, f32[1,64,128]{2,1,0:T(8,128)S(1)} %shard_map.130.refs_0_, f32[1,64,128]{2,1,0:T(8,128)S(1)} %collective-permute-done.35.refs_1_), custom_call_target="tpu_custom_call" | custom-call | tf_op jit(solution)/shard_map/pallas_call | solution.py:489
  (57 shorter events, 4.2 us)
Async XLA Ops:
  0.6 1.0 copy-start
  1.7 0.7 copy-start.5
  2.4 0.7 copy-start.7
  3.0 0.7 copy-start.9
  4.1 7.0 %collective-permute-start.2 = (f32[1,56,128]{2,1,0:T(8,128)S(1)}, f32[1,56,128]{2,1,0:T(8,128)S(1)}, u32[]{:S(2)}, u32[]{:S(2)}) collective-permute-start(f32[1,56,128]{2,1,0:T(8,128)S(1)} %shard_map.112.pack_hbm.refs_0_), channel_id=1, source_target_pairs={{0,6},{1,7},{2,4},{3,5},{4,2},{5,3},{6,0},{7,1},{8,14},{9,15},{10,... | collective-permute-start | bytes 86024 | tf_op jit(solution)/shard_map/ppermute | solution.py:44
  9.2 4.8 %collective-permute-start.1 = (f32[1,56,128]{2,1,0:T(8,128)S(1)}, f32[1,56,128]{2,1,0:T(8,128)S(1)}, u32[]{:S(2)}, u32[]{:S(2)}) collective-permute-start(f32[1,56,128]{2,1,0:T(8,128)S(1)} %shard_map.112.pack_hbm.refs_0_), channel_id=1, source_target_pairs={{0,4},{1,5},{2,6},{3,7},{4,0},{5,1},{6,2},{7,3},{8,12},{9,13},{10,... | collective-permute-start | bytes 86024 | tf_op jit(solution)/shard_map/ppermute | solution.py:44
  9.2 4.8 %collective-permute-start = (f32[1,56,128]{2,1,0:T(8,128)S(1)}, f32[1,56,128]{2,1,0:T(8,128)S(1)}, u32[]{:S(2)}, u32[]{:S(2)}) collective-permute-start(f32[1,56,128]{2,1,0:T(8,128)S(1)} %shard_map.112.pack_hbm.refs_0_), channel_id=1, source_target_pairs={{0,2},{1,3},{2,0},{3,1},{4,6},{5,7},{6,4},{7,5},{8,10},{9,11},{10,... | collective-permute-start | bytes 86024 | tf_op jit(solution)/shard_map/ppermute | solution.py:44
  14.0 6.0 %collective-permute-start.3 = (f32[4,56,128]{2,1,0:T(8,128)S(1)}, f32[4,56,128]{2,1,0:T(8,128)S(1)}, u32[]{:S(2)}, u32[]{:S(2)}) collective-permute-start(f32[4,56,128]{2,1,0:T(8,128)S(1)} %shard_map.114.refs_0_), channel_id=1, source_target_pairs={{0,1},{1,0},{2,3},{3,2},{4,5},{5,4},{6,7},{7,6},{8,9},{9,8},{10,11... | collective-permute-start | bytes 344072 | tf_op jit(solution)/shard_map/ppermute | solution.py:44
  15.6 1.0 copy-start.1
  16.6 1.0 copy-start.3
  17.6 0.7 copy-start.6
  18.3 0.7 copy-start.8
  18.9 0.7 copy-start.10
  21.2 1.3 %collective-permute-start.4 = (f32[2,48,128]{2,1,0:T(8,128)S(1)}, f32[2,48,128]{2,1,0:T(8,128)S(1)}, u32[]{:S(2)}, u32[]{:S(2)}) collective-permute-start(f32[2,48,128]{2,1,0:T(8,128)S(1)} %get-tuple-element.38), channel_id=1, source_target_pairs={{0,8},{1,9},{2,10},{3,11},{4,12},{5,13},{6,14},{7,15},{8,0},{9,1},... | collective-permute-start | bytes 147464 | tf_op jit(solution)/shard_map/ppermute | solution.py:44
  22.5 3.9 %collective-permute-start.5 = (f32[1,48,128]{2,1,0:T(8,128)S(1)}, f32[1,48,128]{2,1,0:T(8,128)S(1)}, u32[]{:S(2)}, u32[]{:S(2)}) collective-permute-start(f32[1,48,128]{2,1,0:T(8,128)S(1)} %get-tuple-element.40), channel_id=1, source_target_pairs={{0,16},{1,17},{2,18},{3,19},{4,20},{5,21},{6,22},{7,23},{8,24},{9,... | collective-permute-start | bytes 73736 | tf_op jit(solution)/shard_map/ppermute | solution.py:44
  26.7 6.5 %collective-permute-start.12 = (bf16[1,2,128,128]{3,2,1,0:T(8,128)(2,1)S(1)}, bf16[1,2,128,128]{3,2,1,0:T(8,128)(2,1)S(1)}, u32[]{:S(2)}, u32[]{:S(2)}) collective-permute-start(bf16[1,2,128,128]{3,2,1,0:T(8,128)(2,1)S(1)} %get-tuple-element.42.own_ref.refs_0_), channel_id=1, source_target_pairs={{0,6},{1,7},{2,4},{3,5},{4,2},{5,3},{6,0},{7,1},{8,14},{9,15},{10,... | collective-permute-start | bytes 196616 | tf_op jit(solution)/shard_map/ppermute | solution.py:44
  28.2 6.8 %collective-permute-start.11 = (bf16[1,2,128,128]{3,2,1,0:T(8,128)(2,1)S(1)}, bf16[1,2,128,128]{3,2,1,0:T(8,128)(2,1)S(1)}, u32[]{:S(2)}, u32[]{:S(2)}) collective-permute-start(bf16[1,2,128,128]{3,2,1,0:T(8,128)(2,1)S(1)} %get-tuple-element.42.own_ref.refs_0_), channel_id=1, source_target_pairs={{0,4},{1,5},{2,6},{3,7},{4,0},{5,1},{6,2},{7,3},{8,12},{9,13},{10,... | collective-permute-start | bytes 196616 | tf_op jit(solution)/shard_map/ppermute | solution.py:44
  28.9 6.2 %collective-permute-start.10 = (bf16[1,2,128,128]{3,2,1,0:T(8,128)(2,1)S(1)}, bf16[1,2,128,128]{3,2,1,0:T(8,128)(2,1)S(1)}, u32[]{:S(2)}, u32[]{:S(2)}) collective-permute-start(bf16[1,2,128,128]{3,2,1,0:T(8,128)(2,1)S(1)} %get-tuple-element.42.own_ref.refs_0_), channel_id=1, source_target_pairs={{0,2},{1,3},{2,0},{3,1},{4,6},{5,7},{6,4},{7,5},{8,10},{9,11},{10,... | collective-permute-start | bytes 196616 | tf_op jit(solution)/shard_map/ppermute | solution.py:44
  35.0 6.2 %collective-permute-start.13 = (bf16[4,2,128,128]{3,2,1,0:T(8,128)(2,1)S(1)}, bf16[4,2,128,128]{3,2,1,0:T(8,128)(2,1)S(1)}, u32[]{:S(2)}, u32[]{:S(2)}) collective-permute-start(bf16[4,2,128,128]{3,2,1,0:T(8,128)(2,1)S(1)} %shard_map.120.refs_0_), channel_id=1, source_target_pairs={{0,8},{1,9},{2,10},{3,11},{4,12},{5,13},{6,14},{7,15},{8,0},{9,1},... | collective-permute-start | bytes 786440 | tf_op jit(solution)/shard_map/ppermute | solution.py:44
  35.1 4.2 %collective-permute-start.8 = (f32[4,8,128]{2,1,0:T(8,128)S(1)}, f32[4,8,128]{2,1,0:T(8,128)S(1)}, u32[]{:S(2)}, u32[]{:S(2)}) collective-permute-start(f32[4,8,128]{2,1,0:T(8,128)S(1)} %get-tuple-element.44.refs_0_), channel_id=1, source_target_pairs={{0,8},{1,9},{2,10},{3,11},{4,12},{5,13},{6,14},{7,15},{8,0},{9,1},... | collective-permute-start | bytes 49160 | tf_op jit(solution)/shard_map/ppermute | solution.py:44
  35.6 14.8 %copy-start.12 = (bf16[8,12,32,32]{3,2,1,0:T(8,128)(2,1)S(1)}, bf16[8,12,32,32]{3,2,1,0:T(8,128)(2,1)}, u32[]{:S(2)}) copy-start(bf16[8,12,32,32]{3,2,1,0:T(8,128)(2,1)} %param.15) | copy-start | bytes 589828
  35.6 3.7 %collective-permute-start.9 = (f32[2,8,128]{2,1,0:T(8,128)S(1)}, f32[2,8,128]{2,1,0:T(8,128)S(1)}, u32[]{:S(2)}, u32[]{:S(2)}) collective-permute-start(f32[2,8,128]{2,1,0:T(8,128)S(1)} %get-tuple-element.45.refs_2_), channel_id=1, source_target_pairs={{0,16},{1,17},{2,18},{3,19},{4,20},{5,21},{6,22},{7,23},{8,24},{9,... | collective-permute-start | bytes 24584 | tf_op jit(solution)/shard_map/ppermute | solution.py:44
  41.2 13.8 %copy-start.4 = (s32[8,12]{1,0:T(8,128)S(1)}, s32[8,12]{1,0:T(8,128)}, u32[]{:S(2)}) copy-start(s32[8,12]{1,0:T(8,128)} %panel_ref.1) | copy-start | bytes 1156
  41.2 13.7 %copy-start.11 = (s32[8]{0:T(128)S(1)}, s32[8]{0:T(128)}, u32[]{:S(2)}) copy-start(s32[8]{0:T(128)} %count_ref.1) | copy-start | bytes 100
  41.2 14.8 %copy-start.2 = (f32[4,2,128,128]{3,2,1,0:T(8,128)S(1)}, f32[4,2,128,128]{3,2,1,0:T(8,128)}, u32[]{:S(2)}) copy-start(f32[4,2,128,128]{3,2,1,0:T(8,128)} %basis_ref.3) | copy-start | bytes 1572868
  43.1 12.8 %collective-permute-start.14 = (f32[1,2,128,128]{3,2,1,0:T(8,128)S(1)}, f32[1,2,128,128]{3,2,1,0:T(8,128)S(1)}, u32[]{:S(2)}, u32[]{:S(2)}) collective-permute-start(f32[1,2,128,128]{3,2,1,0:T(8,128)S(1)} %get-tuple-element.47), channel_id=1, source_target_pairs={{0,1},{1,0},{2,3},{3,2},{4,5},{5,4},{6,7},{7,6},{8,9},{9,8},{10,11... | collective-permute-start | bytes 393224 | tf_op jit(solution)/shard_map/ppermute | solution.py:44
  43.7 12.2 %collective-permute-start.15 = (f32[1,2,128,128]{3,2,1,0:T(8,128)S(1)}, f32[1,2,128,128]{3,2,1,0:T(8,128)S(1)}, u32[]{:S(2)}, u32[]{:S(2)}) collective-permute-start(f32[1,2,128,128]{3,2,1,0:T(8,128)S(1)} %get-tuple-element.48), channel_id=1, source_target_pairs={{0,16},{1,17},{2,18},{3,19},{4,20},{5,21},{6,22},{7,23},{8,24},{9,... | collective-permute-start | bytes 393224 | tf_op jit(solution)/shard_map/ppermute | solution.py:44
  45.2 10.7 %collective-permute-start.16 = (f32[1,2,128,128]{3,2,1,0:T(8,128)S(1)}, f32[1,2,128,128]{3,2,1,0:T(8,128)S(1)}, u32[]{:S(2)}, u32[]{:S(2)}) collective-permute-start(f32[1,2,128,128]{3,2,1,0:T(8,128)S(1)} %get-tuple-element.49), channel_id=1, source_target_pairs={{0,17},{1,16},{2,19},{3,18},{4,21},{5,20},{6,23},{7,22},{8,25},{9,... | collective-permute-start | bytes 393224 | tf_op jit(solution)/shard_map/ppermute | solution.py:44
  46.7 4.8 %collective-permute-start.6 = (bf16[2,64,128]{2,1,0:T(8,128)(2,1)S(1)}, bf16[2,64,128]{2,1,0:T(8,128)(2,1)S(1)}, u32[]{:S(2)}, u32[]{:S(2)}) collective-permute-start(bf16[2,64,128]{2,1,0:T(8,128)(2,1)S(1)} %get-tuple-element.41), channel_id=1, source_target_pairs={{0,1},{1,2},{2,3},{3,4},{4,5},{5,6},{6,7},{7,8},{8,9},{9,10},{10,1... | collective-permute-start | bytes 98312 | tf_op jit(solution)/shard_map/ppermute | solution.py:577
  49.1 5.8 %collective-permute-start.7 = (bf16[2,64,128]{2,1,0:T(8,128)(2,1)S(1)}, bf16[2,64,128]{2,1,0:T(8,128)(2,1)S(1)}, u32[]{:S(2)}, u32[]{:S(2)}) collective-permute-start(bf16[2,64,128]{2,1,0:T(8,128)(2,1)S(1)} %get-tuple-element.43), channel_id=1, source_target_pairs={{1,0},{2,1},{3,2},{4,3},{5,4},{6,5},{7,6},{8,7},{9,8},{10,9},{11,1... | collective-permute-start | bytes 98312 | tf_op jit(solution)/shard_map/ppermute | solution.py:578
  57.2 1.4 %collective-permute-start.17 = (f32[4,64,128]{2,1,0:T(8,128)S(1)}, f32[4,64,128]{2,1,0:T(8,128)S(1)}, u32[]{:S(2)}, u32[]{:S(2)}) collective-permute-start(f32[4,64,128]{2,1,0:T(8,128)S(1)} %get-tuple-element.52), channel_id=1, source_target_pairs={{0,8},{1,9},{2,10},{3,11},{4,12},{5,13},{6,14},{7,15},{8,0},{9,1},... | collective-permute-start | bytes 393224 | tf_op jit(solution)/shard_map/ppermute | solution.py:44
  58.6 5.6 %collective-permute-start.18 = (f32[1,64,128]{2,1,0:T(8,128)S(1)}, f32[1,64,128]{2,1,0:T(8,128)S(1)}, u32[]{:S(2)}, u32[]{:S(2)}) collective-permute-start(f32[1,64,128]{2,1,0:T(8,128)S(1)} %get-tuple-element.54), channel_id=1, source_target_pairs={{0,1},{1,0},{2,3},{3,2},{4,5},{5,4},{6,7},{7,6},{8,9},{9,8},{10,11... | collective-permute-start | bytes 98312 | tf_op jit(solution)/shard_map/ppermute | solution.py:44
  60.9 3.9 %collective-permute-start.19 = (f32[1,64,128]{2,1,0:T(8,128)S(1)}, f32[1,64,128]{2,1,0:T(8,128)S(1)}, u32[]{:S(2)}, u32[]{:S(2)}) collective-permute-start(f32[1,64,128]{2,1,0:T(8,128)S(1)} %get-tuple-element.55), channel_id=1, source_target_pairs={{0,16},{1,17},{2,18},{3,19},{4,20},{5,21},{6,22},{7,23},{8,24},{9,... | collective-permute-start | bytes 98312 | tf_op jit(solution)/shard_map/ppermute | solution.py:44
  62.8 4.8 %collective-permute-start.20 = (f32[1,64,128]{2,1,0:T(8,128)S(1)}, f32[1,64,128]{2,1,0:T(8,128)S(1)}, u32[]{:S(2)}, u32[]{:S(2)}) collective-permute-start(f32[1,64,128]{2,1,0:T(8,128)S(1)} %get-tuple-element.56), channel_id=1, source_target_pairs={{0,17},{1,16},{2,19},{3,18},{4,21},{5,20},{6,23},{7,22},{8,25},{9,... | collective-permute-start | bytes 98312 | tf_op jit(solution)/shard_map/ppermute | solution.py:44
  67.6 6.4 %collective-permute-start.23 = (f32[1,64,128]{2,1,0:T(8,128)S(1)}, f32[1,64,128]{2,1,0:T(8,128)S(1)}, u32[]{:S(2)}, u32[]{:S(2)}) collective-permute-start(f32[1,64,128]{2,1,0:T(8,128)S(1)} %shard_map.124.refs_0_), channel_id=1, source_target_pairs={{0,6},{1,7},{2,4},{3,5},{4,2},{5,3},{6,0},{7,1},{8,14},{9,15},{10,... | collective-permute-start | bytes 98312 | tf_op jit(solution)/shard_map/ppermute | solution.py:44
  72.1 4.8 %collective-permute-start.22 = (f32[1,64,128]{2,1,0:T(8,128)S(1)}, f32[1,64,128]{2,1,0:T(8,128)S(1)}, u32[]{:S(2)}, u32[]{:S(2)}) collective-permute-start(f32[1,64,128]{2,1,0:T(8,128)S(1)} %shard_map.124.refs_0_), channel_id=1, source_target_pairs={{0,4},{1,5},{2,6},{3,7},{4,0},{5,1},{6,2},{7,3},{8,12},{9,13},{10,... | collective-permute-start | bytes 98312 | tf_op jit(solution)/shard_map/ppermute | solution.py:44
  72.1 4.8 %collective-permute-start.21 = (f32[1,64,128]{2,1,0:T(8,128)S(1)}, f32[1,64,128]{2,1,0:T(8,128)S(1)}, u32[]{:S(2)}, u32[]{:S(2)}) collective-permute-start(f32[1,64,128]{2,1,0:T(8,128)S(1)} %shard_map.124.refs_0_), channel_id=1, source_target_pairs={{0,2},{1,3},{2,0},{3,1},{4,6},{5,7},{6,4},{7,5},{8,10},{9,11},{10,... | collective-permute-start | bytes 98312 | tf_op jit(solution)/shard_map/ppermute | solution.py:44
  76.9 4.9 %collective-permute-start.26 = (f32[1,64,128]{2,1,0:T(8,128)S(1)}, f32[1,64,128]{2,1,0:T(8,128)S(1)}, u32[]{:S(2)}, u32[]{:S(2)}) collective-permute-start(f32[1,64,128]{2,1,0:T(8,128)S(1)} %shard_map.125.refs_0_), channel_id=1, source_target_pairs={{0,17},{1,16},{2,19},{3,18},{4,21},{5,20},{6,23},{7,22},{8,25},{9,... | collective-permute-start | bytes 98312 | tf_op jit(solution)/shard_map/ppermute | solution.py:44
  78.5 3.9 %collective-permute-start.25 = (f32[1,64,128]{2,1,0:T(8,128)S(1)}, f32[1,64,128]{2,1,0:T(8,128)S(1)}, u32[]{:S(2)}, u32[]{:S(2)}) collective-permute-start(f32[1,64,128]{2,1,0:T(8,128)S(1)} %shard_map.125.refs_0_), channel_id=1, source_target_pairs={{0,16},{1,17},{2,18},{3,19},{4,20},{5,21},{6,22},{7,23},{8,24},{9,... | collective-permute-start | bytes 98312 | tf_op jit(solution)/shard_map/ppermute | solution.py:44
  79.1 3.9 %collective-permute-start.24 = (f32[1,64,128]{2,1,0:T(8,128)S(1)}, f32[1,64,128]{2,1,0:T(8,128)S(1)}, u32[]{:S(2)}, u32[]{:S(2)}) collective-permute-start(f32[1,64,128]{2,1,0:T(8,128)S(1)} %shard_map.125.refs_0_), channel_id=1, source_target_pairs={{0,1},{1,0},{2,3},{3,2},{4,5},{5,4},{6,7},{7,6},{8,9},{9,8},{10,11... | collective-permute-start | bytes 98312 | tf_op jit(solution)/shard_map/ppermute | solution.py:44
  83.0 1.4 %collective-permute-start.27 = (f32[4,64,128]{2,1,0:T(8,128)S(1)}, f32[4,64,128]{2,1,0:T(8,128)S(1)}, u32[]{:S(2)}, u32[]{:S(2)}) collective-permute-start(f32[4,64,128]{2,1,0:T(8,128)S(1)} %shard_map.126.refs_0_), channel_id=1, source_target_pairs={{0,8},{1,9},{2,10},{3,11},{4,12},{5,13},{6,14},{7,15},{8,0},{9,1},... | collective-permute-start | bytes 393224 | tf_op jit(solution)/shard_map/ppermute | solution.py:44
  86.4 1.2 %collective-permute-start.28 = (f32[1,64,128]{2,1,0:T(8,128)S(1)}, f32[1,64,128]{2,1,0:T(8,128)S(1)}, u32[]{:S(2)}, u32[]{:S(2)}) collective-permute-start(f32[1,64,128]{2,1,0:T(8,128)S(1)} %get-tuple-element.59), channel_id=1, source_target_pairs={{0,8},{1,9},{2,10},{3,11},{4,12},{5,13},{6,14},{7,15},{8,0},{9,1},... | collective-permute-start | bytes 98312 | tf_op jit(solution)/shard_map/ppermute | solution.py:44
  87.6 4.8 %collective-permute-start.31 = (f32[1,64,128]{2,1,0:T(8,128)S(1)}, f32[1,64,128]{2,1,0:T(8,128)S(1)}, u32[]{:S(2)}, u32[]{:S(2)}) collective-permute-start(f32[1,64,128]{2,1,0:T(8,128)S(1)} %shard_map.128.refs_0_), channel_id=1, source_target_pairs={{0,17},{1,16},{2,19},{3,18},{4,21},{5,20},{6,23},{7,22},{8,25},{9,... | collective-permute-start | bytes 98312 | tf_op jit(solution)/shard_map/ppermute | solution.py:44
  90.4 3.9 %collective-permute-start.30 = (f32[1,64,128]{2,1,0:T(8,128)S(1)}, f32[1,64,128]{2,1,0:T(8,128)S(1)}, u32[]{:S(2)}, u32[]{:S(2)}) collective-permute-start(f32[1,64,128]{2,1,0:T(8,128)S(1)} %shard_map.128.refs_0_), channel_id=1, source_target_pairs={{0,16},{1,17},{2,18},{3,19},{4,20},{5,21},{6,22},{7,23},{8,24},{9,... | collective-permute-start | bytes 98312 | tf_op jit(solution)/shard_map/ppermute | solution.py:44
  90.4 3.9 %collective-permute-start.29 = (f32[1,64,128]{2,1,0:T(8,128)S(1)}, f32[1,64,128]{2,1,0:T(8,128)S(1)}, u32[]{:S(2)}, u32[]{:S(2)}) collective-permute-start(f32[1,64,128]{2,1,0:T(8,128)S(1)} %shard_map.128.refs_0_), channel_id=1, source_target_pairs={{0,1},{1,0},{2,3},{3,2},{4,5},{5,4},{6,7},{7,6},{8,9},{9,8},{10,11... | collective-permute-start | bytes 98312 | tf_op jit(solution)/shard_map/ppermute | solution.py:44
  94.4 5.8 %collective-permute-start.34 = (f32[1,64,128]{2,1,0:T(8,128)S(1)}, f32[1,64,128]{2,1,0:T(8,128)S(1)}, u32[]{:S(2)}, u32[]{:S(2)}) collective-permute-start(f32[1,64,128]{2,1,0:T(8,128)S(1)} %shard_map.129.refs_0_), channel_id=1, source_target_pairs={{0,6},{1,7},{2,4},{3,5},{4,2},{5,3},{6,0},{7,1},{8,14},{9,15},{10,... | collective-permute-start | bytes 98312 | tf_op jit(solution)/shard_map/ppermute | solution.py:44
  95.9 4.8 %collective-permute-start.33 = (f32[1,64,128]{2,1,0:T(8,128)S(1)}, f32[1,64,128]{2,1,0:T(8,128)S(1)}, u32[]{:S(2)}, u32[]{:S(2)}) collective-permute-start(f32[1,64,128]{2,1,0:T(8,128)S(1)} %shard_map.129.refs_0_), channel_id=1, source_target_pairs={{0,4},{1,5},{2,6},{3,7},{4,0},{5,1},{6,2},{7,3},{8,12},{9,13},{10,... | collective-permute-start | bytes 98312 | tf_op jit(solution)/shard_map/ppermute | solution.py:44
  96.5 4.5 %collective-permute-start.32 = (f32[1,64,128]{2,1,0:T(8,128)S(1)}, f32[1,64,128]{2,1,0:T(8,128)S(1)}, u32[]{:S(2)}, u32[]{:S(2)}) collective-permute-start(f32[1,64,128]{2,1,0:T(8,128)S(1)} %shard_map.129.refs_0_), channel_id=1, source_target_pairs={{0,2},{1,3},{2,0},{3,1},{4,6},{5,7},{6,4},{7,5},{8,10},{9,11},{10,... | collective-permute-start | bytes 98312 | tf_op jit(solution)/shard_map/ppermute | solution.py:44
  101.1 1.3 %collective-permute-start.35 = (f32[1,64,128]{2,1,0:T(8,128)S(1)}, f32[1,64,128]{2,1,0:T(8,128)S(1)}, u32[]{:S(2)}, u32[]{:S(2)}) collective-permute-start(f32[1,64,128]{2,1,0:T(8,128)S(1)} %shard_map.130.refs_0_), channel_id=1, source_target_pairs={{0,8},{1,9},{2,10},{3,11},{4,12},{5,13},{6,14},{7,15},{8,0},{9,1},... | collective-permute-start | bytes 98312 | tf_op jit(solution)/shard_map/ppermute | solution.py:44

commit v6 on v5

--- a/solution.py
+++ b/solution.py
@@ -13,25 +13,42 @@
 NU = 0.3
 DELTA2 = 1e-05
 ELASTIC = 40.0
-HIGH = lax.Precision.HIGHEST
 AXES = ("narrow", "wide")
 EXTRA = 8
 ROWS = 8
 SMEM = pl.BlockSpec(memory_space=pltpu.SMEM)
 VMEM = pl.BlockSpec(memory_space=pltpu.VMEM)
-HBM = pl.BlockSpec(memory_space=pltpu.HBM)
+ANY = pl.BlockSpec(memory_space=pl.ANY)
 PARAMS = pltpu.CompilerParams(vmem_limit_bytes=48 * 1024 * 1024)
 
 
-def dot_rows(left, right, precision=HIGH):
-    return lax.dot_general(
-        left, right, (((1,), (0,)), ((), ())), precision=precision, preferred_element_type=jnp.float32
+def split(value):
+    high = value.astype(jnp.bfloat16)
+    return high, (value - high.astype(jnp.float32)).astype(jnp.bfloat16)
+
+
+def dot16(left, right, contract=((1,), (0,))):
+    return lax.dot_general(left, right, (contract, ((), ())), preferred_element_type=jnp.float32)
+
+
+def dot_rows(left, right, contract=((1,), (0,))):
+    left_high, left_low = split(left)
+    right_high, right_low = split(right)
+    return dot16(left_high, right_high, contract) + (
+        dot16(left_high, right_low, contract) + dot16(left_low, right_high, contract)
     )
 
 
 def dot_first(left, right):
-    return lax.dot_general(
-        left, right, (((0,), (0,)), ((), ())), precision=HIGH, preferred_element_type=jnp.float32
+    return dot_rows(left, right, ((0,), (0,)))
+
+
+def pick(member, value, contract=((1,), (0,))):
+    member = member.astype(jnp.bfloat16)
+    high, low = split(value)
+    lowest = (value - high.astype(jnp.float32) - low.astype(jnp.float32)).astype(jnp.bfloat16)
+    return dot16(member, high, contract) + (
+        dot16(member, low, contract) + dot16(member, lowest, contract)
     )
 
 
@@ -169,7 +186,7 @@
         ],
         sems,
     )
-    total = dot_rows(members(agg_ref, 0, coarse_count), newest_ref[0]) + dot_rows(
+    total = pick(members(agg_ref, 0, coarse_count), newest_ref[0]) + pick(
         members(agg_ref, 1, coarse_count), newest_ref[1]
     )
     pack_ref[0, :coarse_count, :] = total
@@ -218,7 +235,7 @@
     return parts[k // size], k % size
 
 
-def coarse_kernel(order, ways, z_count, index_ref, inverse_ref, *refs):
+def coarse_kernel(order, ways, z_count, rows, index_ref, inverse_ref, near_ref, *refs):
     narrow_count, coarse_count, _ = inverse_ref.shape
     packs = refs[: len(refs) - ways - 3]
     outs = refs[len(packs) : len(packs) + ways]
@@ -233,37 +250,69 @@
     for k in range(target_ref.shape[0]):
         ref, row = part_at(packs, k * z_count)
         target_ref[k] = ref[row, coarse_count:, :]
+    left = jnp.concatenate(
+        [inverse_ref[index_ref[0] ^ k] for k in range(narrow_count)], axis=0
+    )
+    product = dot_rows(left, rhs_ref[...])
+    tail = jnp.concatenate([source_ref[k] for k in range(z_count)], axis=0)
+    each = z_count * EXTRA // (narrow_count // ways)
     for k in range(narrow_count):
-        outs[k % ways][k // ways] = dot_rows(inverse_ref[index_ref[0] ^ k], rhs_ref[...])
-
-
-def precond_kernel(member_ref, smooth_ref, *refs):
+        part = product[k * coarse_count : (k + 1) * coarse_count, :]
+        outs[k % ways][k // ways, :coarse_count, :] = part
+        first = (k // ways) * each
+        outs[k % ways][k // ways, coarse_count:, :] = tail[first : first + each, :]
+
+
+def coarse_sum_kernel(ways, kept_ref, got_ref, target_ref, *refs):
+    outs, source_ref = refs[:ways], refs[ways]
+    rows = target_ref.shape[0] * EXTRA
+    coarse_count = outs[0].shape[1] - rows
+    each = (kept_ref.shape[1] - coarse_count) // EXTRA
+    for k in range(kept_ref.shape[0]):
+        for j in range(each):
+            first = coarse_count + j * EXTRA
+            source_ref[k * each + j] = got_ref[k, first : first + EXTRA, :]
+    for k in range(outs[0].shape[0]):
+        for j in range(ways):
+            source = k * ways + j
+            outs[j][k, :coarse_count, :] = (
+                kept_ref[source, :coarse_count, :] + got_ref[source, :coarse_count, :]
+            )
+            for t in range(target_ref.shape[0]):
+                first = coarse_count + t * EXTRA
+                outs[j][k, first : first + EXTRA, :] = target_ref[t]
+
+
+def precond_kernel(index_ref, member_ref, smooth_ref, *refs):
     parts = refs[:-3]
-    precond_ref, first_ref, last_ref = refs[-3:]
+    precond_ref, pair_ref, next_ref = refs[-3:]
+    coarse_count = member_ref.shape[1]
     point_count = smooth_ref.shape[1]
-    width = first_ref.shape[1]
-    coarse_sol = total_of([part[0] for part in parts])
+    width = pair_ref.shape[1]
+    even = (index_ref[2] & 1) == 0
+    coarse_sol = total_of([part[0, :coarse_count, :] for part in parts])
     for a in range(2):
-        value = (smooth_ref[a] + dot_first(member_ref[a], coarse_sol)).astype(jnp.bfloat16)
-        precond_ref[0, a] = value
-        first_ref[a] = value[:width]
-        last_ref[a] = value[point_count - width :]
-
-
-def matrix_kernel(source_parts, *refs):
-    matrix_ref = refs[-1]
-    sources = refs[:source_parts]
-    targets = refs[source_parts:-1]
-    point_count = sources[0].shape[2]
-    size = targets[0].shape[0]
+        value = smooth_ref[a] + pick(member_ref[a], coarse_sol, ((0,), (0,)))
+        precond_ref[0, a] = value.astype(jnp.bfloat16)
+        first = value[:width]
+        last = value[point_count - width :]
+        pair_ref[a] = jnp.where(even, last, first).astype(jnp.bfloat16)
+        next_ref[a] = jnp.where(even, first, last).astype(jnp.bfloat16)
+
+
+def matrix_kernel(coarse_count, own_ref, other_ref, *refs):
+    targets, matrix_ref = refs[:-1], refs[-1]
+    point_count = own_ref.shape[2]
+    size = (targets[0].shape[1] - coarse_count) // EXTRA
     step = pl.program_id(0)
-    target = targets[0][lax.rem(step, size)]
+    first = pl.multiple_of(coarse_count + lax.rem(step, size) * EXTRA, EXTRA)
+    target = targets[0][0, pl.ds(first, EXTRA), :]
     for j in range(1, len(targets)):
-        target = jnp.where(step // size == j, targets[j][lax.rem(step, size)], target)
+        target = jnp.where(step // size == j, targets[j][0, pl.ds(first, EXTRA), :], target)
     target_x = as_column(target[0:1, :], point_count)
     target_y = as_column(target[1:2, :], point_count)
     for s in range(matrix_ref.shape[3] // point_count):
-        ref, row = part_at(sources, s)
+        ref, row = part_at((own_ref, other_ref), s)
         source = ref[row]
         delta_x = target_x - source[0:1, :]
         delta_y = target_y - source[1:2, :]
@@ -279,26 +328,24 @@
         matrix_ref[0, 2, :, lanes] = (factor * (log_part + square_y * inverse)).astype(jnp.bfloat16)
 
 
-def far_kernel(ways, matrix_ref, *refs):
+def far_kernel(ways, pair_hbm, next_hbm, matrix_ref, *refs):
     fields = refs[: len(refs) - ways - 1]
     outs = refs[len(fields) : len(fields) + ways]
     fields_ref = refs[-1]
-    point_count = fields[0].shape[2]
+    point_count, rhs_count = fields[0].shape[2:]
     step = pl.program_id(0)
 
     @pl.when(step == 0)
     def _():
-        for s in range(fields_ref.shape[1] // point_count):
+        for s in range(fields_ref.shape[0] // point_count):
             ref, row = part_at(fields, s)
             for b in range(2):
-                fields_ref[b, s * point_count : (s + 1) * point_count, :] = ref[row, b]
-
-    out_x = dot_rows(matrix_ref[0, 0], fields_ref[0], None) + dot_rows(
-        matrix_ref[0, 1], fields_ref[1], None
-    )
-    out_y = dot_rows(matrix_ref[0, 1], fields_ref[0], None) + dot_rows(
-        matrix_ref[0, 2], fields_ref[1], None
-    )
+                rows = slice(s * point_count, (s + 1) * point_count)
+                fields_ref[rows, b * rhs_count : (b + 1) * rhs_count] = ref[row, b]
+
+    mixed = dot16(matrix_ref[0, 1], fields_ref[...])
+    out_x = dot16(matrix_ref[0, 0], fields_ref[:, :rhs_count]) + mixed[:, rhs_count:]
+    out_y = dot16(matrix_ref[0, 2], fields_ref[:, rhs_count:]) + mixed[:, :rhs_count]
     for j, out_ref in enumerate(outs):
 
         @pl.when(lax.rem(step, ways) == j)
@@ -312,22 +359,27 @@
     panel_ref,
     count_ref,
     block_ref,
-    low_ref,
     own_ref,
-    high_ref,
+    pair_ref,
+    next_ref,
     out_ref,
     line_ref,
     gathered_ref,
 ):
     point_count = own_ref.shape[2]
-    width = low_ref.shape[1]
+    width = pair_ref.shape[1]
+    even = (index_ref[2] & 1) == 0
     panels_dev, double_nodes, _ = block_ref.shape
     nodes = double_nodes // 2
     slot_total = panel_ref.shape[1]
     for b in range(2):
-        line_ref[b, :width, :] = low_ref[b]
+        pair = pair_ref[b].astype(jnp.float32)
+        following = next_ref[b].astype(jnp.float32)
+        line_ref[b, :width, :] = jnp.where(even, following, pair).astype(jnp.bfloat16)
         line_ref[b, width : width + point_count, :] = own_ref[0, b]
-        line_ref[b, width + point_count :, :] = high_ref[b]
+        line_ref[b, width + point_count :, :] = jnp.where(even, pair, following).astype(
+            jnp.bfloat16
+        )
     first_panel = index_ref[2] * panels_dev
     lane = lax.broadcasted_iota(jnp.int32, block_ref.shape[1:], 1)
     for p in range(panels_dev):
@@ -339,7 +391,7 @@
         blocks = jnp.where(
             lane < count_ref[p] * double_nodes, block_ref[p].astype(jnp.float32), 0.0
         ).astype(jnp.bfloat16)
-        near = dot_rows(blocks, gathered_ref[p], None)
+        near = dot16(blocks, gathered_ref[p])
         for a in range(2):
             rows = slice(p * nodes, (p + 1) * nodes)
             own = own_ref[0, a, rows, :].astype(jnp.float32)
@@ -361,21 +413,27 @@
         full_ref[pl.ds(first, rows), :] = ref[row]
 
 
+def stacked(basis_ref):
+    return jnp.concatenate(
+        [
+            jnp.concatenate([basis_ref[j, a] for j in range(basis_ref.shape[0])], axis=1)
+            for a in range(2)
+        ],
+        axis=0,
+    )
+
+
 def project_kernel(masks, ways, index_ref, weight_ref, basis_ref, base_ref, *refs):
     arrived = refs[: len(refs) - ways - 2]
     image_ref = refs[len(arrived)]
     outs = refs[len(arrived) + 1 : -1]
     full_ref = refs[-1]
-    block_total, _, _, rhs_count = basis_ref.shape
     weighted = []
     for a in range(2):
         image = base_ref[a] + total_of([part[0, a] for part in arrived])
         image_ref[a] = image
         weighted.append(image * weight_ref[...])
-    for j in range(block_total):
-        full_ref[j * rhs_count : (j + 1) * rhs_count, :] = dot_first(
-            basis_ref[j, 0], weighted[0]
-        ) + dot_first(basis_ref[j, 1], weighted[1])
+    full_ref[...] = dot_first(stacked(basis_ref), jnp.concatenate(weighted, axis=0))
     spread(full_ref, outs, bits_of(index_ref[2], masks))
 
 
@@ -386,19 +444,12 @@
     hess_ref, remainder_ref = refs[len(parts) : len(parts) + 2]
     outs = refs[len(parts) + 2 : -1]
     gram_ref = refs[-1]
-    block_total, _, point_count, rhs_count = basis_ref.shape
     collect(order, parts, hess_ref, bits_of(index_ref[2], masks))
-    gram = None
-    for a in range(2):
-        value = image_ref[a]
-        for j in range(block_total):
-            value = value - dot_rows(
-                basis_ref[j, a], hess_ref[j * rhs_count : (j + 1) * rhs_count, :]
-            )
-        remainder_ref[a * point_count : (a + 1) * point_count, :] = value
-        term = dot_first(value * weight_ref[...], value)
-        gram = term if gram is None else gram + term
-    gram_ref[...] = gram
+    image = jnp.concatenate([image_ref[0], image_ref[1]], axis=0)
+    value = image - dot_rows(stacked(basis_ref), hess_ref[...])
+    remainder_ref[...] = value
+    weight = jnp.concatenate([weight_ref[...]] * 2, axis=0)
+    gram_ref[...] = dot_first(value * weight, value)
     spread(gram_ref, outs, bits_of(index_ref[2], gram_masks))
 
 
@@ -467,13 +518,7 @@
                 target_inverse = target_inverse - multiplier[m] * solved_inverse[m]
             work_ref[first : first + ROWS, :] = target
             inverse_ref[first : first + ROWS, :] = target_inverse
-    new_ref[...] = lax.dot_general(
-        remainder_ref[...],
-        inverse_ref[...],
-        (((1,), (1,)), ((), ())),
-        precision=HIGH,
-        preferred_element_type=jnp.float32,
-    )
+    new_ref[...] = dot_rows(remainder_ref[...], inverse_ref[...], ((1,), (1,)))
 
 
 def f32(*shape):
@@ -489,10 +534,10 @@
     return pl.pallas_call(
         kernel,
         out_shape=out_shape,
-        in_specs=[SMEM] * scalars + [HBM if in_hbm else VMEM] * (len(operands) - scalars),
+        in_specs=[SMEM] * scalars + [ANY if in_hbm else VMEM] * (len(operands) - scalars),
         out_specs=[VMEM] * len(out_shape) if many else VMEM,
         scratch_shapes=list(scratch),
-        compiler_params=PARAMS,
+        compiler_params=None if in_hbm else PARAMS,
     )(*operands)
 
 
@@ -555,55 +600,70 @@
         [pair_index, field, pair_row, one_row, pltpu.SemaphoreType.DMA((5,))],
         True,
     )
+    near_rows = jnp.transpose(near_block, (0, 2, 1, 3)).reshape(
+        panels_dev, 2 * nodes, slot_total * 2 * nodes
+    )
     packs = gather_steps(pack, wide_groups)
-    coarse_outs = call(
-        functools.partial(coarse_kernel, gather_order(wide_groups), 2, high_count),
-        [f32(narrow_count // 2, coarse_count, rhs_count)] * 2
+    source_rows = high_count * EXTRA // (narrow_count // 2)
+    target_rows = 2 * EXTRA
+    coarse_outs = pl.pallas_call(
+        functools.partial(
+            coarse_kernel, gather_order(wide_groups), 2, high_count, source_rows
+        ),
+        out_shape=[f32(narrow_count // 2, coarse_count + source_rows, rhs_count)] * 2
         + [f32(high_count, EXTRA, point_count), f32(2, EXTRA, point_count)],
-        (index, inverse, *packs),
-        1,
-        [pltpu.VMEM((wide_count * coarse_count, rhs_count), jnp.float32)],
-    )
-    coarse_parts = scatter_steps(coarse_outs[:2], narrow_groups)
-    sources = flip_each([coarse_outs[2]] * 2, [core])
-    targets = gather_steps(coarse_outs[3], in_pairs(across))
-    precond, first, last = call(
+        in_specs=[SMEM, VMEM, ANY] + [VMEM] * len(packs),
+        out_specs=[VMEM] * 4,
+        scratch_shapes=[pltpu.VMEM((wide_count * coarse_count, rhs_count), jnp.float32)],
+        compiler_params=PARAMS,
+    )(index, inverse, near_rows, *packs)
+    own_sources = coarse_outs[2]
+    kept, got = flip_each(coarse_outs[:2], [core])
+    groups = in_pairs(across)
+    ways = 1 << len(groups[0])
+    *coarse_parts, other_sources = call(
+        functools.partial(coarse_sum_kernel, ways),
+        [f32(narrow_count // 2 // ways, coarse_count + target_rows, rhs_count)] * ways
+        + [f32(high_count, EXTRA, point_count)],
+        (kept, got, coarse_outs[3]),
+    )
+    coarse_parts = scatter_steps(coarse_parts, groups)
+    precond, pair_edge, next_edge = call(
         precond_kernel,
         [b16(1, 2, point_count, rhs_count)] + [b16(2, width, rhs_count)] * 2,
-        (member, smooth, *coarse_parts),
+        (index, member, smooth, *coarse_parts),
+        1,
     )
     fields = gather_steps(precond, source_groups)
-    forward = [(i, i + 1) for i in range(narrow_count * wide_count - 1)]
-    before = lax.ppermute(last, AXES, forward)
-    after = lax.ppermute(first, AXES, [(target, source) for source, target in forward])
+    device_count = narrow_count * wide_count
+    pair_edge = flip(pair_edge, 1)
+    pairs = [(i, i + 1) for i in range(1, device_count - 1, 2)]
+    next_edge = lax.ppermute(next_edge, AXES, pairs + [(j, i) for i, j in pairs])
 
     matrix_spec = pl.BlockSpec((1, 3, point_count, source_total), lambda k: (k, 0, 0, 0))
     matrix = pl.pallas_call(
-        functools.partial(matrix_kernel, len(sources)),
+        functools.partial(matrix_kernel, coarse_count),
         out_shape=b16(target_count, 3, point_count, source_total),
         grid=(target_count,),
-        in_specs=[VMEM] * (len(sources) + len(targets)),
+        in_specs=[VMEM] * (2 + len(coarse_parts)),
         out_specs=matrix_spec,
         compiler_params=PARAMS,
-    )(*sources, *targets)
+    )(own_sources, other_sources, *coarse_parts)
     ways = 1 << len(plane_groups[0])
     far_parts = pl.pallas_call(
         functools.partial(far_kernel, ways),
         out_shape=[f32(target_count // ways, 2, point_count, rhs_count)] * ways,
         grid=(target_count,),
-        in_specs=[matrix_spec] + [VMEM] * len(fields),
+        in_specs=[ANY, ANY, matrix_spec] + [VMEM] * len(fields),
         out_specs=[VMEM] * ways,
-        scratch_shapes=[pltpu.VMEM((2, source_total, rhs_count), jnp.bfloat16)],
+        scratch_shapes=[pltpu.VMEM((source_total, 2 * rhs_count), jnp.bfloat16)],
         compiler_params=PARAMS,
-    )(matrix, *fields)
+    )(pair_edge, next_edge, matrix, *fields)
     far_parts = scatter_steps(far_parts, plane_groups)
-    near_rows = jnp.transpose(near_block, (0, 2, 1, 3)).reshape(
-        panels_dev, 2 * nodes, slot_total * 2 * nodes
-    )
     base = call(
         near_kernel,
         f32(2, point_count, rhs_count),
-        (index, near_panel, near_count, near_rows, before, precond, after),
+        (index, near_panel, near_count, near_rows, precond, pair_edge, next_edge),
         3,
         [
             pltpu.VMEM((2, 2 * width + point_count, rhs_count), jnp.bfloat16),

time: 109 us -> 105 us (0.963)
  local copies, waits for them, and re-layouts: 8.13 us -> 5.57 us
  Pallas kernels: 16.2 us -> 18.4 us
  starting transfers between devices: 45.3 us -> 43.3 us
  waiting for transfers between devices: 37.7 us -> 36.5 us
    unnamed x26 -> x16, local copies, waits for them, and re-layouts: 7.08 us -> 3.44 us
    ppermute x2 -> x1, waiting for transfers between devices: 3.42 us -> 0.01 us  [body(): lax.ppermute(next_edge, AXES, pairs + [(j, i) for i, j in pairs])]
    ppermute x2 -> x1, starting transfers between devices: 3.72 us -> 0.65 us  [body(): lax.ppermute(next_edge, AXES, pairs + [(j, i) for i, j in pairs])]
    ppermute x34 -> x33, waiting for transfers between devices: 34.2 us -> 36.5 us  [flip(): return lax.ppermute(block, AXES, [(i, i ^ mask) for i in range(count)])]
    pallas_call x18 -> x17, Pallas kernels: 12.4 us -> 14 us  [call(): pl.pallas_call(kernel, out_shape=out_shape, in_specs=[SMEM] * scalars + [...]
    transpose x1, local copies, waits for them, and re-layouts: 0.34 us -> 1.47 us  [body(): jnp.transpose(near_block, (0, 2, 1, 3))]
    ppermute x34 -> x33, starting transfers between devices: 41.6 us -> 42.6 us  [flip(): return lax.ppermute(block, AXES, [(i, i ^ mask) for i in range(count)])]
    pallas_call x1 -> x2, Pallas kernels: 1.88 us -> 2.73 us  [the longest x1 1.9 us: body(): pl.pallas_call(functools.partial(matrix_kernel, coarse_count), out_shape=...]
  transfers between devices with their start and end apart: 36 -> 34, of which waited for: 24 -> 26; matrix products, arithmetic and copies ran while one was open for 1% -> 2% of each run, Pallas kernels for 3% -> 5%
where the time goes in v6:
time: 105 us
  starting transfers between devices  43.3 us (41%)
  waiting for transfers between devices  36.5 us (35%)
  Pallas kernels  18.4 us (18%)
  local copies, waits for them, and re-layouts  5.57 us (5%)
    ppermute x33, starting transfers between devices, flip(): return lax.ppermute(block, AXES, [(i, i ^ mask) for i in range(count)])  42.6 us
    ppermute x33, waiting for transfers between devices, flip(): return lax.ppermute(block, AXES, [(i, i ^ mask) for i in range(count)])  36.5 us
    pallas_call x17, Pallas kernels, call(): pl.pallas_call(kernel, out_shape=out_shape, in_specs=[SMEM] * scalars + [...  14 us
    unnamed x16, local copies, waits for them, and re-layouts  3.44 us
  transfers between devices with their start and end apart: 34, of which 26 were waited for; matrix products, arithmetic and copies ran while one was open for 2% of the time, Pallas kernels for 5%

profile of v6, /device:TPU:0, one launch (start us, length us, event | category | flops | bytes accessed | tf_op | source)
XLA Modules:
  0.0 104.7 jit_solution(7122675751618722931)
XLA Ops:
  0.6 1.8 %shard_map.112.pack_hbm.refs_0_ = f32[1,56,128]{2,1,0:T(8,128)} custom-call(s32[2,128]{1,0:T(2,128)} %agg_hbm.3, f32[4,2,128,128]{3,2,1,0:T(8,128)} %basis_ref.3, f32[2,128]{1,0:T(2,128)} %points_hbm.1, f32[1,128]{1,0:T(1,128)} %bitcast.8), custom_call_target="tpu_custom_call" | custom-call | tf_op jit(solution)/shard_map/pallas_call | solution.py:534
  2.4 5.1 %collective-permute-start.2 = (f32[1,56,128]{2,1,0:T(8,128)}, f32[1,56,128]{2,1,0:T(8,128)S(1)}, u32[]{:S(2)}, u32[]{:S(2)}) collective-permute-start(f32[1,56,128]{2,1,0:T(8,128)} %shard_map.112.pack_hbm.refs_0_), channel_id=1, source_target_pairs={{0,6},{1,7},{2,4},{3,5},{4,2},{5,3},{6,0},{7,1},{8,14},{9,15},{10,... | collective-permute-start | bytes 86024 | tf_op jit(solution)/shard_map/ppermute | solution.py:61
  7.5 0.6 collective-permute-start
  8.1 1.4 %collective-permute-done.2.refs_3_ = f32[1,56,128]{2,1,0:T(8,128)S(1)} collective-permute-done((f32[1,56,128]{2,1,0:T(8,128)}, f32[1,56,128]{2,1,0:T(8,128)S(1)}, u32[]{:S(2)}, u32[]{:S(2)}) %collective-permute-start.2) | collective-permute-done | bytes 28704 | tf_op jit(solution)/shard_map/ppermute | solution.py:61
  9.6 2.9 %collective-permute-done.1.refs_2_ = f32[1,56,128]{2,1,0:T(8,128)S(1)} collective-permute-done((f32[1,56,128]{2,1,0:T(8,128)}, f32[1,56,128]{2,1,0:T(8,128)S(1)}, u32[]{:S(2)}, u32[]{:S(2)}) %collective-permute-start.1) | collective-permute-done | bytes 28704 | tf_op jit(solution)/shard_map/ppermute | solution.py:61
  12.5 0.7 copy-done.3
  13.2 1.6 %collective-permute-start.3 = (f32[4,56,128]{2,1,0:T(8,128)S(1)}, f32[4,56,128]{2,1,0:T(8,128)S(1)}, u32[]{:S(2)}, u32[]{:S(2)}) collective-permute-start(f32[4,56,128]{2,1,0:T(8,128)S(1)} %shard_map.114.refs_0_), channel_id=1, source_target_pairs={{0,1},{1,0},{2,3},{3,2},{4,5},{5,4},{6,7},{7,6},{8,9},{9,8},{10,11... | collective-permute-start | bytes 344072 | tf_op jit(solution)/shard_map/ppermute | solution.py:61
  14.8 1.5 %copy.13 = bf16[8,32,12,32]{3,2,1,0:T(8,128)(2,1)S(1)} copy(bf16[8,32,12,32]{3,1,2,0:T(8,128)(2,1)} %bitcast.7) | data formatting | bytes 393216 | tf_op jit(solution)/shard_map/transpose | solution.py:603
  16.3 0.7 reshape.15.near_ref.block_ref
  17.0 1.9 %shard_map.113 = (f32[4,48,384]{2,1,0:T(8,128)}, f32[2,48,128]{2,1,0:T(8,128)}, f32[2,128,128]{2,1,0:T(8,128)}, f32[128,128]{1,0:T(8,128)}) custom-call(f32[1,56,128]{2,1,0:T(8,128)} %shard_map.112.pack_hbm.refs_0_, s32[2,128]{1,0:T(2,128)} %agg_hbm.3, f32[4,2,128,128]{3,2,1,0:T(8,128)} %basis_ref.3, f32[2,128]{1,0:T(2,128)} %jacobi_hbm.1, ...), custom_call_target="tpu_custom_call" | custom-call | tf_op jit(solution)/shard_map/pallas_call | solution.py:534
  19.0 1.0 copy-done.1
  19.9 0.8 shard_map.115
  20.8 1.2 %collective-permute-done.4.got_ref = f32[2,64,128]{2,1,0:T(8,128)S(1)} collective-permute-done((f32[2,64,128]{2,1,0:T(8,128)S(1)}, f32[2,64,128]{2,1,0:T(8,128)S(1)}, u32[]{:S(2)}, u32[]{:S(2)}) %collective-permute-start.4) | collective-permute-done | bytes 65568 | tf_op jit(solution)/shard_map/ppermute | solution.py:61
  22.1 1.6 %collective-permute-start.5 = (f32[1,64,128]{2,1,0:T(8,128)S(1)}, f32[1,64,128]{2,1,0:T(8,128)S(1)}, u32[]{:S(2)}, u32[]{:S(2)}) collective-permute-start(f32[1,64,128]{2,1,0:T(8,128)S(1)} %get-tuple-element.42), channel_id=1, source_target_pairs={{0,16},{1,17},{2,18},{3,19},{4,20},{5,21},{6,22},{7,23},{8,24},{9,... | collective-permute-start | bytes 98312 | tf_op jit(solution)/shard_map/ppermute | solution.py:61
  23.7 2.4 %collective-permute-done.5.refs_1_ = f32[1,64,128]{2,1,0:T(8,128)S(1)} collective-permute-done((f32[1,64,128]{2,1,0:T(8,128)S(1)}, f32[1,64,128]{2,1,0:T(8,128)S(1)}, u32[]{:S(2)}, u32[]{:S(2)}) %collective-permute-start.5) | collective-permute-done | bytes 32800 | tf_op jit(solution)/shard_map/ppermute | solution.py:61
  26.1 0.9 copy-done.4
  27.0 0.8 copy-done.5
  27.8 0.8 shard_map.117
  28.6 1.6 %collective-permute-start.10 = (bf16[1,2,128,128]{3,2,1,0:T(8,128)(2,1)S(1)}, bf16[1,2,128,128]{3,2,1,0:T(8,128)(2,1)S(1)}, u32[]{:S(2)}, u32[]{:S(2)}) collective-permute-start(bf16[1,2,128,128]{3,2,1,0:T(8,128)(2,1)S(1)} %get-tuple-element.43.own_ref.refs_0_), channel_id=1, source_target_pairs={{0,6},{1,7},{2,4},{3,5},{4,2},{5,3},{6,0},{7,1},{8,14},{9,15},{10,... | collective-permute-start | bytes 196616 | tf_op jit(solution)/shard_map/ppermute | solution.py:61
  30.1 0.6 collective-permute-start.9
  30.7 2.3 %collective-permute-start.8 = (bf16[1,2,128,128]{3,2,1,0:T(8,128)(2,1)S(1)}, bf16[1,2,128,128]{3,2,1,0:T(8,128)(2,1)S(1)}, u32[]{:S(2)}, u32[]{:S(2)}) collective-permute-start(bf16[1,2,128,128]{3,2,1,0:T(8,128)(2,1)S(1)} %get-tuple-element.43.own_ref.refs_0_), channel_id=1, source_target_pairs={{0,2},{1,3},{2,0},{3,1},{4,6},{5,7},{6,4},{7,5},{8,10},{9,11},{10,... | collective-permute-start | bytes 196616 | tf_op jit(solution)/shard_map/ppermute | solution.py:61
  33.0 2.0 %collective-permute-done.10.refs_3_ = bf16[1,2,128,128]{3,2,1,0:T(8,128)(2,1)S(1)} collective-permute-done((bf16[1,2,128,128]{3,2,1,0:T(8,128)(2,1)S(1)}, bf16[1,2,128,128]{3,2,1,0:T(8,128)(2,1)S(1)}, u32[]{:S(2)}, u32[]{:S(2)}) %collective-permute-start.10) | collective-permute-done | bytes 65568 | tf_op jit(solution)/shard_map/ppermute | solution.py:61
  35.0 1.9 %collective-permute-done.9.refs_2_ = bf16[1,2,128,128]{3,2,1,0:T(8,128)(2,1)S(1)} collective-permute-done((bf16[1,2,128,128]{3,2,1,0:T(8,128)(2,1)S(1)}, bf16[1,2,128,128]{3,2,1,0:T(8,128)(2,1)S(1)}, u32[]{:S(2)}, u32[]{:S(2)}) %collective-permute-start.9) | collective-permute-done | bytes 65568 | tf_op jit(solution)/shard_map/ppermute | solution.py:61
  37.1 0.7 collective-permute-start.6
  37.8 0.7 collective-permute-start.7
  38.5 1.9 %shard_map.119.matrix_ref = bf16[4,3,128,1024]{3,2,1,0:T(8,128)(2,1)S(1)} custom-call(f32[4,8,128]{2,1,0:T(8,128)S(1)} %get-tuple-element.46.own_ref, f32[4,8,128]{2,1,0:T(8,128)S(1)} %get-tuple-element.47.other_ref, f32[1,64,128]{2,1,0:T(8,128)S(1)} %get-tuple-element.41.refs_0_, f32[1,64,128]{2,1,0:T(8,128)S(1)} %collective-permute-done.5.refs_1_), custom_call_target="tpu_custom_call" | custom-call | tf_op jit(solution)/shard_map/pallas_call | solution.py:644
  40.4 0.7 collective-permute-done.6.pair_ref.pair_hbm
  41.0 1.7 %shard_map.121 = (f32[1,2,128,128]{3,2,1,0:T(8,128)S(1)}, f32[1,2,128,128]{3,2,1,0:T(8,128)S(1)}, f32[1,2,128,128]{3,2,1,0:T(8,128)S(1)}, f32[1,2,128,128]{3,2,1,0:T(8,128)S(1)}) custom-call(bf16[2,64,128]{2,1,0:T(8,128)(2,1)S(1)} %collective-permute-done.6.pair_ref.pair_hbm, bf16[2,64,128]{2,1,0:T(8,128)(2,1)S(1)} %collective-permute-done.7.next_ref.next_hbm, ...), custom_call_target="tpu_custom_call" | custom-call | tf_op jit(solution)/shard_map/pallas_call | solution.py:653
  42.7 4.9 %collective-permute-start.12 = (f32[1,2,128,128]{3,2,1,0:T(8,128)S(1)}, f32[1,2,128,128]{3,2,1,0:T(8,128)S(1)}, u32[]{:S(2)}, u32[]{:S(2)}) collective-permute-start(f32[1,2,128,128]{3,2,1,0:T(8,128)S(1)} %get-tuple-element.49), channel_id=1, source_target_pairs={{0,1},{1,0},{2,3},{3,2},{4,5},{5,4},{6,7},{7,6},{8,9},{9,8},{10,11... | collective-permute-start | bytes 393224 | tf_op jit(solution)/shard_map/ppermute | solution.py:61
  47.6 2.3 %collective-permute-start.13 = (f32[1,2,128,128]{3,2,1,0:T(8,128)S(1)}, f32[1,2,128,128]{3,2,1,0:T(8,128)S(1)}, u32[]{:S(2)}, u32[]{:S(2)}) collective-permute-start(f32[1,2,128,128]{3,2,1,0:T(8,128)S(1)} %get-tuple-element.50), channel_id=1, source_target_pairs={{0,16},{1,17},{2,18},{3,19},{4,20},{5,21},{6,22},{7,23},{8,24},{9,... | collective-permute-start | bytes 393224 | tf_op jit(solution)/shard_map/ppermute | solution.py:61
  49.9 1.4 %collective-permute-start.14 = (f32[1,2,128,128]{3,2,1,0:T(8,128)S(1)}, f32[1,2,128,128]{3,2,1,0:T(8,128)S(1)}, u32[]{:S(2)}, u32[]{:S(2)}) collective-permute-start(f32[1,2,128,128]{3,2,1,0:T(8,128)S(1)} %get-tuple-element.51), channel_id=1, source_target_pairs={{0,17},{1,16},{2,19},{3,18},{4,21},{5,20},{6,23},{7,22},{8,25},{9,... | collective-permute-start | bytes 393224 | tf_op jit(solution)/shard_map/ppermute | solution.py:61
  51.3 1.0 shard_map.118.base_ref
  52.3 2.8 %collective-permute-done.13.refs_2_ = f32[1,2,128,128]{3,2,1,0:T(8,128)S(1)} collective-permute-done((f32[1,2,128,128]{3,2,1,0:T(8,128)S(1)}, f32[1,2,128,128]{3,2,1,0:T(8,128)S(1)}, u32[]{:S(2)}, u32[]{:S(2)}) %collective-permute-start.13) | collective-permute-done | bytes 131104 | tf_op jit(solution)/shard_map/ppermute | solution.py:61
  55.1 1.6 %collective-permute-done.14.refs_3_ = f32[1,2,128,128]{3,2,1,0:T(8,128)S(1)} collective-permute-done((f32[1,2,128,128]{3,2,1,0:T(8,128)S(1)}, f32[1,2,128,128]{3,2,1,0:T(8,128)S(1)}, u32[]{:S(2)}, u32[]{:S(2)}) %collective-permute-start.14) | collective-permute-done | bytes 131104 | tf_op jit(solution)/shard_map/ppermute | solution.py:61
  56.8 1.0 shard_map.122
  57.8 1.3 %collective-permute-done.15.refs_1_ = f32[4,64,128]{2,1,0:T(8,128)S(1)} collective-permute-done((f32[4,64,128]{2,1,0:T(8,128)S(1)}, f32[4,64,128]{2,1,0:T(8,128)S(1)}, u32[]{:S(2)}, u32[]{:S(2)}) %collective-permute-start.15) | collective-permute-done | bytes 131104 | tf_op jit(solution)/shard_map/ppermute | solution.py:61
  59.2 1.0 collective-permute-start.16
  60.2 1.3 %collective-permute-start.17 = (f32[1,64,128]{2,1,0:T(8,128)S(1)}, f32[1,64,128]{2,1,0:T(8,128)S(1)}, u32[]{:S(2)}, u32[]{:S(2)}) collective-permute-start(f32[1,64,128]{2,1,0:T(8,128)S(1)} %get-tuple-element.57), channel_id=1, source_target_pairs={{0,16},{1,17},{2,18},{3,19},{4,20},{5,21},{6,22},{7,23},{8,24},{9,... | collective-permute-start | bytes 98312 | tf_op jit(solution)/shard_map/ppermute | solution.py:61
  61.6 1.2 %collective-permute-start.18 = (f32[1,64,128]{2,1,0:T(8,128)S(1)}, f32[1,64,128]{2,1,0:T(8,128)S(1)}, u32[]{:S(2)}, u32[]{:S(2)}) collective-permute-start(f32[1,64,128]{2,1,0:T(8,128)S(1)} %get-tuple-element.58), channel_id=1, source_target_pairs={{0,17},{1,16},{2,19},{3,18},{4,21},{5,20},{6,23},{7,22},{8,25},{9,... | collective-permute-start | bytes 98312 | tf_op jit(solution)/shard_map/ppermute | solution.py:61
  63.2 1.0 collective-permute-done.17.refs_2_
  64.2 2.2 %collective-permute-done.18.refs_3_ = f32[1,64,128]{2,1,0:T(8,128)S(1)} collective-permute-done((f32[1,64,128]{2,1,0:T(8,128)S(1)}, f32[1,64,128]{2,1,0:T(8,128)S(1)}, u32[]{:S(2)}, u32[]{:S(2)}) %collective-permute-start.18) | collective-permute-done | bytes 32800 | tf_op jit(solution)/shard_map/ppermute | solution.py:61
  66.4 2.2 %collective-permute-start.21 = (f32[1,64,128]{2,1,0:T(8,128)S(1)}, f32[1,64,128]{2,1,0:T(8,128)S(1)}, u32[]{:S(2)}, u32[]{:S(2)}) collective-permute-start(f32[1,64,128]{2,1,0:T(8,128)S(1)} %shard_map.124.refs_0_), channel_id=1, source_target_pairs={{0,6},{1,7},{2,4},{3,5},{4,2},{5,3},{6,0},{7,1},{8,14},{9,15},{10,... | collective-permute-start | bytes 98312 | tf_op jit(solution)/shard_map/ppermute | solution.py:61
  68.6 2.3 %collective-permute-start.19 = (f32[1,64,128]{2,1,0:T(8,128)S(1)}, f32[1,64,128]{2,1,0:T(8,128)S(1)}, u32[]{:S(2)}, u32[]{:S(2)}) collective-permute-start(f32[1,64,128]{2,1,0:T(8,128)S(1)} %shard_map.124.refs_0_), channel_id=1, source_target_pairs={{0,2},{1,3},{2,0},{3,1},{4,6},{5,7},{6,4},{7,5},{8,10},{9,11},{10,... | collective-permute-start | bytes 98312 | tf_op jit(solution)/shard_map/ppermute | solution.py:61
  70.9 1.3 %collective-permute-done.21.refs_3_ = f32[1,64,128]{2,1,0:T(8,128)S(1)} collective-permute-done((f32[1,64,128]{2,1,0:T(8,128)S(1)}, f32[1,64,128]{2,1,0:T(8,128)S(1)}, u32[]{:S(2)}, u32[]{:S(2)}) %collective-permute-start.21) | collective-permute-done | bytes 32800 | tf_op jit(solution)/shard_map/ppermute | solution.py:61
  72.2 1.2 %collective-permute-done.20.refs_2_ = f32[1,64,128]{2,1,0:T(8,128)S(1)} collective-permute-done((f32[1,64,128]{2,1,0:T(8,128)S(1)}, f32[1,64,128]{2,1,0:T(8,128)S(1)}, u32[]{:S(2)}, u32[]{:S(2)}) %collective-permute-start.20) | collective-permute-done | bytes 32800 | tf_op jit(solution)/shard_map/ppermute | solution.py:61
  73.4 2.2 %collective-permute-start.24 = (f32[1,64,128]{2,1,0:T(8,128)S(1)}, f32[1,64,128]{2,1,0:T(8,128)S(1)}, u32[]{:S(2)}, u32[]{:S(2)}) collective-permute-start(f32[1,64,128]{2,1,0:T(8,128)S(1)} %shard_map.125.refs_0_), channel_id=1, source_target_pairs={{0,17},{1,16},{2,19},{3,18},{4,21},{5,20},{6,23},{7,22},{8,25},{9,... | collective-permute-start | bytes 98312 | tf_op jit(solution)/shard_map/ppermute | solution.py:61
  75.9 1.1 %collective-permute-start.22 = (f32[1,64,128]{2,1,0:T(8,128)S(1)}, f32[1,64,128]{2,1,0:T(8,128)S(1)}, u32[]{:S(2)}, u32[]{:S(2)}) collective-permute-start(f32[1,64,128]{2,1,0:T(8,128)S(1)} %shard_map.125.refs_0_), channel_id=1, source_target_pairs={{0,1},{1,0},{2,3},{3,2},{4,5},{5,4},{6,7},{7,6},{8,9},{9,8},{10,11... | collective-permute-start | bytes 98312 | tf_op jit(solution)/shard_map/ppermute | solution.py:61
  76.9 1.3 %collective-permute-done.24.refs_3_ = f32[1,64,128]{2,1,0:T(8,128)S(1)} collective-permute-done((f32[1,64,128]{2,1,0:T(8,128)S(1)}, f32[1,64,128]{2,1,0:T(8,128)S(1)}, u32[]{:S(2)}, u32[]{:S(2)}) %collective-permute-start.24) | collective-permute-done | bytes 32800 | tf_op jit(solution)/shard_map/ppermute | solution.py:61
  78.3 1.2 %collective-permute-done.23.refs_2_ = f32[1,64,128]{2,1,0:T(8,128)S(1)} collective-permute-done((f32[1,64,128]{2,1,0:T(8,128)S(1)}, f32[1,64,128]{2,1,0:T(8,128)S(1)}, u32[]{:S(2)}, u32[]{:S(2)}) %collective-permute-start.23) | collective-permute-done | bytes 32800 | tf_op jit(solution)/shard_map/ppermute | solution.py:61
  79.9 1.3 %collective-permute-done.25.refs_1_ = f32[4,64,128]{2,1,0:T(8,128)S(1)} collective-permute-done((f32[4,64,128]{2,1,0:T(8,128)S(1)}, f32[4,64,128]{2,1,0:T(8,128)S(1)}, u32[]{:S(2)}, u32[]{:S(2)}) %collective-permute-start.25) | collective-permute-done | bytes 131104 | tf_op jit(solution)/shard_map/ppermute | solution.py:61
  81.2 1.7 %shard_map.127 = (f32[512,128]{1,0:T(8,128)}, f32[256,128]{1,0:T(8,128)S(1)}, f32[1,64,128]{2,1,0:T(8,128)S(1)}, f32[1,64,128]{2,1,0:T(8,128)S(1)}) custom-call(s32[3]{0:T(128)S(1)} %pad_add_fusion.index_ref, f32[128,128]{1,0:T(8,128)S(1)} %copy-done.2, f32[4,2,128,128]{3,2,1,0:T(8,128)S(1)} %copy-done, f32[2,128,128]{2,1,0:T(8,128)S(1)} %get-tuple-element.52.image_ref, ...), custom_call_target="tpu_custom_call" | custom-call | tf_op jit(solution)/shard_map/pallas_call | solution.py:534
  83.0 1.1 %collective-permute-done.26.refs_1_ = f32[1,64,128]{2,1,0:T(8,128)S(1)} collective-permute-done((f32[1,64,128]{2,1,0:T(8,128)S(1)}, f32[1,64,128]{2,1,0:T(8,128)S(1)}, u32[]{:S(2)}, u32[]{:S(2)}) %collective-permute-start.26) | collective-permute-done | bytes 32800 | tf_op jit(solution)/shard_map/ppermute | solution.py:61
  84.1 1.2 %collective-permute-start.29 = (f32[1,64,128]{2,1,0:T(8,128)S(1)}, f32[1,64,128]{2,1,0:T(8,128)S(1)}, u32[]{:S(2)}, u32[]{:S(2)}) collective-permute-start(f32[1,64,128]{2,1,0:T(8,128)S(1)} %shard_map.128.refs_0_), channel_id=1, source_target_pairs={{0,17},{1,16},{2,19},{3,18},{4,21},{5,20},{6,23},{7,22},{8,25},{9,... | collective-permute-start | bytes 98312 | tf_op jit(solution)/shard_map/ppermute | solution.py:61
  85.3 1.3 %collective-permute-start.28 = (f32[1,64,128]{2,1,0:T(8,128)S(1)}, f32[1,64,128]{2,1,0:T(8,128)S(1)}, u32[]{:S(2)}, u32[]{:S(2)}) collective-permute-start(f32[1,64,128]{2,1,0:T(8,128)S(1)} %shard_map.128.refs_0_), channel_id=1, source_target_pairs={{0,16},{1,17},{2,18},{3,19},{4,20},{5,21},{6,22},{7,23},{8,24},{9,... | collective-permute-start | bytes 98312 | tf_op jit(solution)/shard_map/ppermute | solution.py:61
  86.6 0.9 collective-permute-start.27
  87.6 1.3 %collective-permute-done.29.refs_3_ = f32[1,64,128]{2,1,0:T(8,128)S(1)} collective-permute-done((f32[1,64,128]{2,1,0:T(8,128)S(1)}, f32[1,64,128]{2,1,0:T(8,128)S(1)}, u32[]{:S(2)}, u32[]{:S(2)}) %collective-permute-start.29) | collective-permute-done | bytes 32800 | tf_op jit(solution)/shard_map/ppermute | solution.py:61
  89.2 1.3 %collective-permute-done.27.refs_1_ = f32[1,64,128]{2,1,0:T(8,128)S(1)} collective-permute-done((f32[1,64,128]{2,1,0:T(8,128)S(1)}, f32[1,64,128]{2,1,0:T(8,128)S(1)}, u32[]{:S(2)}, u32[]{:S(2)}) %collective-permute-start.27) | collective-permute-done | bytes 32800 | tf_op jit(solution)/shard_map/ppermute | solution.py:61
  90.6 1.9 %collective-permute-start.32 = (f32[1,64,128]{2,1,0:T(8,128)S(1)}, f32[1,64,128]{2,1,0:T(8,128)S(1)}, u32[]{:S(2)}, u32[]{:S(2)}) collective-permute-start(f32[1,64,128]{2,1,0:T(8,128)S(1)} %shard_map.129.refs_0_), channel_id=1, source_target_pairs={{0,6},{1,7},{2,4},{3,5},{4,2},{5,3},{6,0},{7,1},{8,14},{9,15},{10,... | collective-permute-start | bytes 98312 | tf_op jit(solution)/shard_map/ppermute | solution.py:61
  92.4 1.0 collective-permute-start.31
  93.5 1.5 %collective-permute-start.30 = (f32[1,64,128]{2,1,0:T(8,128)S(1)}, f32[1,64,128]{2,1,0:T(8,128)S(1)}, u32[]{:S(2)}, u32[]{:S(2)}) collective-permute-start(f32[1,64,128]{2,1,0:T(8,128)S(1)} %shard_map.129.refs_0_), channel_id=1, source_target_pairs={{0,2},{1,3},{2,0},{3,1},{4,6},{5,7},{6,4},{7,5},{8,10},{9,11},{10,... | collective-permute-start | bytes 98312 | tf_op jit(solution)/shard_map/ppermute | solution.py:61
  95.0 1.3 %collective-permute-done.32.refs_3_ = f32[1,64,128]{2,1,0:T(8,128)S(1)} collective-permute-done((f32[1,64,128]{2,1,0:T(8,128)S(1)}, f32[1,64,128]{2,1,0:T(8,128)S(1)}, u32[]{:S(2)}, u32[]{:S(2)}) %collective-permute-start.32) | collective-permute-done | bytes 32800 | tf_op jit(solution)/shard_map/ppermute | solution.py:61
  96.3 1.3 %collective-permute-done.31.refs_2_ = f32[1,64,128]{2,1,0:T(8,128)S(1)} collective-permute-done((f32[1,64,128]{2,1,0:T(8,128)S(1)}, f32[1,64,128]{2,1,0:T(8,128)S(1)}, u32[]{:S(2)}, u32[]{:S(2)}) %collective-permute-start.31) | collective-permute-done | bytes 32800 | tf_op jit(solution)/shard_map/ppermute | solution.py:61
  97.7 1.2 %collective-permute-done.33.refs_1_ = f32[1,64,128]{2,1,0:T(8,128)S(1)} collective-permute-done((f32[1,64,128]{2,1,0:T(8,128)S(1)}, f32[1,64,128]{2,1,0:T(8,128)S(1)}, u32[]{:S(2)}, u32[]{:S(2)}) %collective-permute-start.33) | collective-permute-done | bytes 32800 | tf_op jit(solution)/shard_map/ppermute | solution.py:61
  98.9 5.8 %shard_map.131 = (f32[128,128]{1,0:T(8,128)}, f32[256,128]{1,0:T(8,128)}) custom-call(s32[3]{0:T(128)S(1)} %pad_add_fusion.index_ref, f32[256,128]{1,0:T(8,128)S(1)} %get-tuple-element.59.remainder_ref, f32[1,64,128]{2,1,0:T(8,128)S(1)} %shard_map.130.refs_0_, f32[1,64,128]{2,1,0:T(8,128)S(1)} %collective-permute-done.33.refs_1_), custom_call_target="tpu_custom_call" | custom-call | tf_op jit(solution)/shard_map/pallas_call | solution.py:534
  (43 shorter events, 2.1 us)
Async XLA Ops:
  2.4 7.2 %collective-permute-start.2 = (f32[1,56,128]{2,1,0:T(8,128)}, f32[1,56,128]{2,1,0:T(8,128)S(1)}, u32[]{:S(2)}, u32[]{:S(2)}) collective-permute-start(f32[1,56,128]{2,1,0:T(8,128)} %shard_map.112.pack_hbm.refs_0_), channel_id=1, source_target_pairs={{0,6},{1,7},{2,4},{3,5},{4,2},{5,3},{6,0},{7,1},{8,14},{9,15},{10,... | collective-permute-start | bytes 86024 | tf_op jit(solution)/shard_map/ppermute | solution.py:61
  7.5 5.0 %collective-permute-start.1 = (f32[1,56,128]{2,1,0:T(8,128)}, f32[1,56,128]{2,1,0:T(8,128)S(1)}, u32[]{:S(2)}, u32[]{:S(2)}) collective-permute-start(f32[1,56,128]{2,1,0:T(8,128)} %shard_map.112.pack_hbm.refs_0_), channel_id=1, source_target_pairs={{0,4},{1,5},{2,6},{3,7},{4,0},{5,1},{6,2},{7,3},{8,12},{9,13},{10,... | collective-permute-start | bytes 86024 | tf_op jit(solution)/shard_map/ppermute | solution.py:61
  7.5 5.0 %collective-permute-start = (f32[1,56,128]{2,1,0:T(8,128)}, f32[1,56,128]{2,1,0:T(8,128)S(1)}, u32[]{:S(2)}, u32[]{:S(2)}) collective-permute-start(f32[1,56,128]{2,1,0:T(8,128)} %shard_map.112.pack_hbm.refs_0_), channel_id=1, source_target_pairs={{0,2},{1,3},{2,0},{3,1},{4,6},{5,7},{6,4},{7,5},{8,10},{9,11},{10,... | collective-permute-start | bytes 86024 | tf_op jit(solution)/shard_map/ppermute | solution.py:61
  12.5 0.7 copy-start.3
  13.2 5.7 %collective-permute-start.3 = (f32[4,56,128]{2,1,0:T(8,128)S(1)}, f32[4,56,128]{2,1,0:T(8,128)S(1)}, u32[]{:S(2)}, u32[]{:S(2)}) collective-permute-start(f32[4,56,128]{2,1,0:T(8,128)S(1)} %shard_map.114.refs_0_), channel_id=1, source_target_pairs={{0,1},{1,0},{2,3},{3,2},{4,5},{5,4},{6,7},{7,6},{8,9},{9,8},{10,11... | collective-permute-start | bytes 344072 | tf_op jit(solution)/shard_map/ppermute | solution.py:61
  19.0 1.0 copy-start.1
  20.8 1.3 %collective-permute-start.4 = (f32[2,64,128]{2,1,0:T(8,128)S(1)}, f32[2,64,128]{2,1,0:T(8,128)S(1)}, u32[]{:S(2)}, u32[]{:S(2)}) collective-permute-start(f32[2,64,128]{2,1,0:T(8,128)S(1)} %get-tuple-element.39), channel_id=1, source_target_pairs={{0,8},{1,9},{2,10},{3,11},{4,12},{5,13},{6,14},{7,15},{8,0},{9,1},... | collective-permute-start | bytes 196616 | tf_op jit(solution)/shard_map/ppermute | solution.py:61
  22.1 4.0 %collective-permute-start.5 = (f32[1,64,128]{2,1,0:T(8,128)S(1)}, f32[1,64,128]{2,1,0:T(8,128)S(1)}, u32[]{:S(2)}, u32[]{:S(2)}) collective-permute-start(f32[1,64,128]{2,1,0:T(8,128)S(1)} %get-tuple-element.42), channel_id=1, source_target_pairs={{0,16},{1,17},{2,18},{3,19},{4,20},{5,21},{6,22},{7,23},{8,24},{9,... | collective-permute-start | bytes 98312 | tf_op jit(solution)/shard_map/ppermute | solution.py:61
  26.1 0.9 copy-start.4
  27.0 0.8 copy-start.5
  28.6 6.5 %collective-permute-start.10 = (bf16[1,2,128,128]{3,2,1,0:T(8,128)(2,1)S(1)}, bf16[1,2,128,128]{3,2,1,0:T(8,128)(2,1)S(1)}, u32[]{:S(2)}, u32[]{:S(2)}) collective-permute-start(bf16[1,2,128,128]{3,2,1,0:T(8,128)(2,1)S(1)} %get-tuple-element.43.own_ref.refs_0_), channel_id=1, source_target_pairs={{0,6},{1,7},{2,4},{3,5},{4,2},{5,3},{6,0},{7,1},{8,14},{9,15},{10,... | collective-permute-start | bytes 196616 | tf_op jit(solution)/shard_map/ppermute | solution.py:61
  30.1 6.8 %collective-permute-start.9 = (bf16[1,2,128,128]{3,2,1,0:T(8,128)(2,1)S(1)}, bf16[1,2,128,128]{3,2,1,0:T(8,128)(2,1)S(1)}, u32[]{:S(2)}, u32[]{:S(2)}) collective-permute-start(bf16[1,2,128,128]{3,2,1,0:T(8,128)(2,1)S(1)} %get-tuple-element.43.own_ref.refs_0_), channel_id=1, source_target_pairs={{0,4},{1,5},{2,6},{3,7},{4,0},{5,1},{6,2},{7,3},{8,12},{9,13},{10,... | collective-permute-start | bytes 196616 | tf_op jit(solution)/shard_map/ppermute | solution.py:61
  30.7 6.2 %collective-permute-start.8 = (bf16[1,2,128,128]{3,2,1,0:T(8,128)(2,1)S(1)}, bf16[1,2,128,128]{3,2,1,0:T(8,128)(2,1)S(1)}, u32[]{:S(2)}, u32[]{:S(2)}) collective-permute-start(bf16[1,2,128,128]{3,2,1,0:T(8,128)(2,1)S(1)} %get-tuple-element.43.own_ref.refs_0_), channel_id=1, source_target_pairs={{0,2},{1,3},{2,0},{3,1},{4,6},{5,7},{6,4},{7,5},{8,10},{9,11},{10,... | collective-permute-start | bytes 196616 | tf_op jit(solution)/shard_map/ppermute | solution.py:61
  37.0 4.1 %collective-permute-start.11 = (bf16[4,2,128,128]{3,2,1,0:T(8,128)(2,1)S(1)}, bf16[4,2,128,128]{3,2,1,0:T(8,128)(2,1)S(1)}, u32[]{:S(2)}, u32[]{:S(2)}) collective-permute-start(bf16[4,2,128,128]{3,2,1,0:T(8,128)(2,1)S(1)} %shard_map.120.refs_0_), channel_id=1, source_target_pairs={{0,8},{1,9},{2,10},{3,11},{4,12},{5,13},{6,14},{7,15},{8,0},{9,1},... | collective-permute-start | bytes 786440 | tf_op jit(solution)/shard_map/ppermute | solution.py:61
  37.1 4.0 %collective-permute-start.6 = (bf16[2,64,128]{2,1,0:T(8,128)(2,1)S(1)}, bf16[2,64,128]{2,1,0:T(8,128)(2,1)S(1)}, u32[]{:S(2)}, u32[]{:S(2)}) collective-permute-start(bf16[2,64,128]{2,1,0:T(8,128)(2,1)S(1)} %get-tuple-element.44), channel_id=1, source_target_pairs={{0,1},{1,0},{2,3},{3,2},{4,5},{5,4},{6,7},{7,6},{8,9},{9,8},{10,11... | collective-permute-start | bytes 98312 | tf_op jit(solution)/shard_map/ppermute | solution.py:61
  37.8 3.3 %collective-permute-start.7 = (bf16[2,64,128]{2,1,0:T(8,128)(2,1)S(1)}, bf16[2,64,128]{2,1,0:T(8,128)(2,1)S(1)}, u32[]{:S(2)}, u32[]{:S(2)}) collective-permute-start(bf16[2,64,128]{2,1,0:T(8,128)(2,1)S(1)} %get-tuple-element.45), channel_id=1, source_target_pairs={{1,2},{3,4},{5,6},{7,8},{9,10},{11,12},{13,14},{15,16},{17,18},{19... | collective-permute-start | bytes 98312 | tf_op jit(solution)/shard_map/ppermute | solution.py:641
  38.4 12.9 %copy-start.6 = (s32[8,12]{1,0:T(8,128)S(1)}, s32[8,12]{1,0:T(8,128)}, u32[]{:S(2)}) copy-start(s32[8,12]{1,0:T(8,128)} %panel_ref.1) | copy-start | bytes 1156
  38.4 12.9 %copy-start.7 = (s32[8]{0:T(128)S(1)}, s32[8]{0:T(128)}, u32[]{:S(2)}) copy-start(s32[8]{0:T(128)} %count_ref.1) | copy-start | bytes 100
  38.4 18.3 %copy-start = (f32[4,2,128,128]{3,2,1,0:T(8,128)S(1)}, f32[4,2,128,128]{3,2,1,0:T(8,128)}, u32[]{:S(2)}) copy-start(f32[4,2,128,128]{3,2,1,0:T(8,128)} %basis_ref.3) | copy-start | bytes 1572868
  38.4 18.3 %copy-start.2 = (f32[128,128]{1,0:T(8,128)S(1)}, f32[128,128]{1,0:T(8,128)}, u32[]{:S(2)}) copy-start(f32[128,128]{1,0:T(8,128)} %get-tuple-element.34.weight_ref) | copy-start | bytes 196612
  42.7 9.6 %collective-permute-start.12 = (f32[1,2,128,128]{3,2,1,0:T(8,128)S(1)}, f32[1,2,128,128]{3,2,1,0:T(8,128)S(1)}, u32[]{:S(2)}, u32[]{:S(2)}) collective-permute-start(f32[1,2,128,128]{3,2,1,0:T(8,128)S(1)} %get-tuple-element.49), channel_id=1, source_target_pairs={{0,1},{1,0},{2,3},{3,2},{4,5},{5,4},{6,7},{7,6},{8,9},{9,8},{10,11... | collective-permute-start | bytes 393224 | tf_op jit(solution)/shard_map/ppermute | solution.py:61
  47.6 7.5 %collective-permute-start.13 = (f32[1,2,128,128]{3,2,1,0:T(8,128)S(1)}, f32[1,2,128,128]{3,2,1,0:T(8,128)S(1)}, u32[]{:S(2)}, u32[]{:S(2)}) collective-permute-start(f32[1,2,128,128]{3,2,1,0:T(8,128)S(1)} %get-tuple-element.50), channel_id=1, source_target_pairs={{0,16},{1,17},{2,18},{3,19},{4,20},{5,21},{6,22},{7,23},{8,24},{9,... | collective-permute-start | bytes 393224 | tf_op jit(solution)/shard_map/ppermute | solution.py:61
  49.9 6.8 %collective-permute-start.14 = (f32[1,2,128,128]{3,2,1,0:T(8,128)S(1)}, f32[1,2,128,128]{3,2,1,0:T(8,128)S(1)}, u32[]{:S(2)}, u32[]{:S(2)}) collective-permute-start(f32[1,2,128,128]{3,2,1,0:T(8,128)S(1)} %get-tuple-element.51), channel_id=1, source_target_pairs={{0,17},{1,16},{2,19},{3,18},{4,21},{5,20},{6,23},{7,22},{8,25},{9,... | collective-permute-start | bytes 393224 | tf_op jit(solution)/shard_map/ppermute | solution.py:61
  57.8 1.4 %collective-permute-start.15 = (f32[4,64,128]{2,1,0:T(8,128)S(1)}, f32[4,64,128]{2,1,0:T(8,128)S(1)}, u32[]{:S(2)}, u32[]{:S(2)}) collective-permute-start(f32[4,64,128]{2,1,0:T(8,128)S(1)} %get-tuple-element.54), channel_id=1, source_target_pairs={{0,8},{1,9},{2,10},{3,11},{4,12},{5,13},{6,14},{7,15},{8,0},{9,1},... | collective-permute-start | bytes 393224 | tf_op jit(solution)/shard_map/ppermute | solution.py:61
  59.2 4.0 %collective-permute-start.16 = (f32[1,64,128]{2,1,0:T(8,128)S(1)}, f32[1,64,128]{2,1,0:T(8,128)S(1)}, u32[]{:S(2)}, u32[]{:S(2)}) collective-permute-start(f32[1,64,128]{2,1,0:T(8,128)S(1)} %get-tuple-element.56), channel_id=1, source_target_pairs={{0,1},{1,0},{2,3},{3,2},{4,5},{5,4},{6,7},{7,6},{8,9},{9,8},{10,11... | collective-permute-start | bytes 98312 | tf_op jit(solution)/shard_map/ppermute | solution.py:61
  60.2 3.9 %collective-permute-start.17 = (f32[1,64,128]{2,1,0:T(8,128)S(1)}, f32[1,64,128]{2,1,0:T(8,128)S(1)}, u32[]{:S(2)}, u32[]{:S(2)}) collective-permute-start(f32[1,64,128]{2,1,0:T(8,128)S(1)} %get-tuple-element.57), channel_id=1, source_target_pairs={{0,16},{1,17},{2,18},{3,19},{4,20},{5,21},{6,22},{7,23},{8,24},{9,... | collective-permute-start | bytes 98312 | tf_op jit(solution)/shard_map/ppermute | solution.py:61
  61.6 4.8 %collective-permute-start.18 = (f32[1,64,128]{2,1,0:T(8,128)S(1)}, f32[1,64,128]{2,1,0:T(8,128)S(1)}, u32[]{:S(2)}, u32[]{:S(2)}) collective-permute-start(f32[1,64,128]{2,1,0:T(8,128)S(1)} %get-tuple-element.58), channel_id=1, source_target_pairs={{0,17},{1,16},{2,19},{3,18},{4,21},{5,20},{6,23},{7,22},{8,25},{9,... | collective-permute-start | bytes 98312 | tf_op jit(solution)/shard_map/ppermute | solution.py:61
  66.4 5.8 %collective-permute-start.21 = (f32[1,64,128]{2,1,0:T(8,128)S(1)}, f32[1,64,128]{2,1,0:T(8,128)S(1)}, u32[]{:S(2)}, u32[]{:S(2)}) collective-permute-start(f32[1,64,128]{2,1,0:T(8,128)S(1)} %shard_map.124.refs_0_), channel_id=1, source_target_pairs={{0,6},{1,7},{2,4},{3,5},{4,2},{5,3},{6,0},{7,1},{8,14},{9,15},{10,... | collective-permute-start | bytes 98312 | tf_op jit(solution)/shard_map/ppermute | solution.py:61
  68.6 4.8 %collective-permute-start.20 = (f32[1,64,128]{2,1,0:T(8,128)S(1)}, f32[1,64,128]{2,1,0:T(8,128)S(1)}, u32[]{:S(2)}, u32[]{:S(2)}) collective-permute-start(f32[1,64,128]{2,1,0:T(8,128)S(1)} %shard_map.124.refs_0_), channel_id=1, source_target_pairs={{0,4},{1,5},{2,6},{3,7},{4,0},{5,1},{6,2},{7,3},{8,12},{9,13},{10,... | collective-permute-start | bytes 98312 | tf_op jit(solution)/shard_map/ppermute | solution.py:61
  68.6 4.8 %collective-permute-start.19 = (f32[1,64,128]{2,1,0:T(8,128)S(1)}, f32[1,64,128]{2,1,0:T(8,128)S(1)}, u32[]{:S(2)}, u32[]{:S(2)}) collective-permute-start(f32[1,64,128]{2,1,0:T(8,128)S(1)} %shard_map.124.refs_0_), channel_id=1, source_target_pairs={{0,2},{1,3},{2,0},{3,1},{4,6},{5,7},{6,4},{7,5},{8,10},{9,11},{10,... | collective-permute-start | bytes 98312 | tf_op jit(solution)/shard_map/ppermute | solution.py:61
  73.4 4.9 %collective-permute-start.24 = (f32[1,64,128]{2,1,0:T(8,128)S(1)}, f32[1,64,128]{2,1,0:T(8,128)S(1)}, u32[]{:S(2)}, u32[]{:S(2)}) collective-permute-start(f32[1,64,128]{2,1,0:T(8,128)S(1)} %shard_map.125.refs_0_), channel_id=1, source_target_pairs={{0,17},{1,16},{2,19},{3,18},{4,21},{5,20},{6,23},{7,22},{8,25},{9,... | collective-permute-start | bytes 98312 | tf_op jit(solution)/shard_map/ppermute | solution.py:61
  75.6 3.9 %collective-permute-start.23 = (f32[1,64,128]{2,1,0:T(8,128)S(1)}, f32[1,64,128]{2,1,0:T(8,128)S(1)}, u32[]{:S(2)}, u32[]{:S(2)}) collective-permute-start(f32[1,64,128]{2,1,0:T(8,128)S(1)} %shard_map.125.refs_0_), channel_id=1, source_target_pairs={{0,16},{1,17},{2,18},{3,19},{4,20},{5,21},{6,22},{7,23},{8,24},{9,... | collective-permute-start | bytes 98312 | tf_op jit(solution)/shard_map/ppermute | solution.py:61
  75.9 3.9 %collective-permute-start.22 = (f32[1,64,128]{2,1,0:T(8,128)S(1)}, f32[1,64,128]{2,1,0:T(8,128)S(1)}, u32[]{:S(2)}, u32[]{:S(2)}) collective-permute-start(f32[1,64,128]{2,1,0:T(8,128)S(1)} %shard_map.125.refs_0_), channel_id=1, source_target_pairs={{0,1},{1,0},{2,3},{3,2},{4,5},{5,4},{6,7},{7,6},{8,9},{9,8},{10,11... | collective-permute-start | bytes 98312 | tf_op jit(solution)/shard_map/ppermute | solution.py:61
  79.8 1.4 %collective-permute-start.25 = (f32[4,64,128]{2,1,0:T(8,128)S(1)}, f32[4,64,128]{2,1,0:T(8,128)S(1)}, u32[]{:S(2)}, u32[]{:S(2)}) collective-permute-start(f32[4,64,128]{2,1,0:T(8,128)S(1)} %shard_map.126.refs_0_), channel_id=1, source_target_pairs={{0,8},{1,9},{2,10},{3,11},{4,12},{5,13},{6,14},{7,15},{8,0},{9,1},... | collective-permute-start | bytes 393224 | tf_op jit(solution)/shard_map/ppermute | solution.py:61
  82.9 1.2 %collective-permute-start.26 = (f32[1,64,128]{2,1,0:T(8,128)S(1)}, f32[1,64,128]{2,1,0:T(8,128)S(1)}, u32[]{:S(2)}, u32[]{:S(2)}) collective-permute-start(f32[1,64,128]{2,1,0:T(8,128)S(1)} %get-tuple-element.61), channel_id=1, source_target_pairs={{0,8},{1,9},{2,10},{3,11},{4,12},{5,13},{6,14},{7,15},{8,0},{9,1},... | collective-permute-start | bytes 98312 | tf_op jit(solution)/shard_map/ppermute | solution.py:61
  84.1 4.8 %collective-permute-start.29 = (f32[1,64,128]{2,1,0:T(8,128)S(1)}, f32[1,64,128]{2,1,0:T(8,128)S(1)}, u32[]{:S(2)}, u32[]{:S(2)}) collective-permute-start(f32[1,64,128]{2,1,0:T(8,128)S(1)} %shard_map.128.refs_0_), channel_id=1, source_target_pairs={{0,17},{1,16},{2,19},{3,18},{4,21},{5,20},{6,23},{7,22},{8,25},{9,... | collective-permute-start | bytes 98312 | tf_op jit(solution)/shard_map/ppermute | solution.py:61
  85.3 3.9 %collective-permute-start.28 = (f32[1,64,128]{2,1,0:T(8,128)S(1)}, f32[1,64,128]{2,1,0:T(8,128)S(1)}, u32[]{:S(2)}, u32[]{:S(2)}) collective-permute-start(f32[1,64,128]{2,1,0:T(8,128)S(1)} %shard_map.128.refs_0_), channel_id=1, source_target_pairs={{0,16},{1,17},{2,18},{3,19},{4,20},{5,21},{6,22},{7,23},{8,24},{9,... | collective-permute-start | bytes 98312 | tf_op jit(solution)/shard_map/ppermute | solution.py:61
  86.6 3.9 %collective-permute-start.27 = (f32[1,64,128]{2,1,0:T(8,128)S(1)}, f32[1,64,128]{2,1,0:T(8,128)S(1)}, u32[]{:S(2)}, u32[]{:S(2)}) collective-permute-start(f32[1,64,128]{2,1,0:T(8,128)S(1)} %shard_map.128.refs_0_), channel_id=1, source_target_pairs={{0,1},{1,0},{2,3},{3,2},{4,5},{5,4},{6,7},{7,6},{8,9},{9,8},{10,11... | collective-permute-start | bytes 98312 | tf_op jit(solution)/shard_map/ppermute | solution.py:61
  90.6 5.8 %collective-permute-start.32 = (f32[1,64,128]{2,1,0:T(8,128)S(1)}, f32[1,64,128]{2,1,0:T(8,128)S(1)}, u32[]{:S(2)}, u32[]{:S(2)}) collective-permute-start(f32[1,64,128]{2,1,0:T(8,128)S(1)} %shard_map.129.refs_0_), channel_id=1, source_target_pairs={{0,6},{1,7},{2,4},{3,5},{4,2},{5,3},{6,0},{7,1},{8,14},{9,15},{10,... | collective-permute-start | bytes 98312 | tf_op jit(solution)/shard_map/ppermute | solution.py:61
  92.4 5.2 %collective-permute-start.31 = (f32[1,64,128]{2,1,0:T(8,128)S(1)}, f32[1,64,128]{2,1,0:T(8,128)S(1)}, u32[]{:S(2)}, u32[]{:S(2)}) collective-permute-start(f32[1,64,128]{2,1,0:T(8,128)S(1)} %shard_map.129.refs_0_), channel_id=1, source_target_pairs={{0,4},{1,5},{2,6},{3,7},{4,0},{5,1},{6,2},{7,3},{8,12},{9,13},{10,... | collective-permute-start | bytes 98312 | tf_op jit(solution)/shard_map/ppermute | solution.py:61
  93.5 4.1 %collective-permute-start.30 = (f32[1,64,128]{2,1,0:T(8,128)S(1)}, f32[1,64,128]{2,1,0:T(8,128)S(1)}, u32[]{:S(2)}, u32[]{:S(2)}) collective-permute-start(f32[1,64,128]{2,1,0:T(8,128)S(1)} %shard_map.129.refs_0_), channel_id=1, source_target_pairs={{0,2},{1,3},{2,0},{3,1},{4,6},{5,7},{6,4},{7,5},{8,10},{9,11},{10,... | collective-permute-start | bytes 98312 | tf_op jit(solution)/shard_map/ppermute | solution.py:61
  97.6 1.3 %collective-permute-start.33 = (f32[1,64,128]{2,1,0:T(8,128)S(1)}, f32[1,64,128]{2,1,0:T(8,128)S(1)}, u32[]{:S(2)}, u32[]{:S(2)}) collective-permute-start(f32[1,64,128]{2,1,0:T(8,128)S(1)} %shard_map.130.refs_0_), channel_id=1, source_target_pairs={{0,8},{1,9},{2,10},{3,11},{4,12},{5,13},{6,14},{7,15},{8,0},{9,1},... | collective-permute-start | bytes 98312 | tf_op jit(solution)/shard_map/ppermute | solution.py:61

commit v7 on v6

--- a/solution.py
+++ b/solution.py
@@ -81,22 +81,30 @@
     return [parts[0]] + [flip(parts[j], combined(group, j)) for j in range(1, 1 << len(group))]
 
 
-def join_kernel(*refs):
-    out_ref = refs[-1]
-    size = refs[0].shape[0]
-    for j, ref in enumerate(refs[:-1]):
+def join_kernel(count, *refs):
+    parts, out_ref = refs[-1 - count : -1], refs[-1]
+    size = parts[0].shape[0]
+    for j, ref in enumerate(parts):
         out_ref[j * size : (j + 1) * size] = ref[...]
 
 
-def join(parts):
+def join(parts, after=()):
     shape = (len(parts) * parts[0].shape[0],) + parts[0].shape[1:]
-    return call(join_kernel, jax.ShapeDtypeStruct(shape, parts[0].dtype), parts)
-
-
-def gather_steps(held, groups):
+    return pl.pallas_call(
+        functools.partial(join_kernel, len(parts)),
+        out_shape=jax.ShapeDtypeStruct(shape, parts[0].dtype),
+        in_specs=[ANY] * len(after) + [VMEM] * len(parts),
+        out_specs=VMEM,
+        compiler_params=PARAMS,
+    )(*after, *parts)
+
+
+def gather_steps(held, groups, after=()):
     parts = [held]
     for group in groups:
-        held = parts[0] if len(parts) == 1 else join(parts)
+        if len(parts) > 1:
+            held = join(parts, after)
+            after = ()
         parts = flip_each([held] * (1 << len(group)), group)
     return parts
 
@@ -206,17 +214,18 @@
     member_ref,
     smooth_ref,
     weight_out_ref,
+    half_ref,
     agg_ref,
-    newest_ref,
+    basis_ref,
     jacobi_ref,
     weight_ref,
     sems,
 ):
     coarse_count = member_ref.shape[1]
-    rhs_count = newest_ref.shape[2]
+    block_total, _, _, rhs_count = basis_ref.shape
     load_all(
         [
-            (basis_hbm.at[basis_hbm.shape[0] - 1], newest_ref),
+            (basis_hbm, basis_ref),
             (agg_hbm, agg_ref),
             (jacobi_hbm, jacobi_ref),
             (weight_hbm, weight_ref),
@@ -226,8 +235,20 @@
     )
     for a in range(2):
         member_ref[a] = members(agg_ref, a, coarse_count)
-        smooth_ref[a] = as_column(jacobi_ref[a : a + 1, :], rhs_count) * newest_ref[a]
-    weight_out_ref[...] = as_column(weight_ref[...], rhs_count)
+        smooth_ref[a] = (
+            as_column(jacobi_ref[a : a + 1, :], rhs_count) * basis_ref[block_total - 1, a]
+        )
+    weight = as_column(weight_ref[...], rhs_count)
+    weight_out_ref[...] = weight
+    right = stacked(basis_ref)
+    number = 0
+    for i in range(block_total):
+        left = jnp.concatenate([basis_ref[i, a] * weight for a in range(2)], axis=0)
+        row = dot_first(left, right[:, i * rhs_count :])
+        for j in range(i, block_total):
+            block = row[:, (j - i) * rhs_count : (j - i + 1) * rhs_count]
+            half_ref[number] = block * 0.5 if i == j else block
+            number += 1
 
 
 def part_at(parts, k):
@@ -235,7 +256,7 @@
     return parts[k // size], k % size
 
 
-def coarse_kernel(order, ways, z_count, rows, index_ref, inverse_ref, near_ref, *refs):
+def coarse_kernel(order, ways, z_count, index_ref, inverse_ref, *refs):
     narrow_count, coarse_count, _ = inverse_ref.shape
     packs = refs[: len(refs) - ways - 3]
     outs = refs[len(packs) : len(packs) + ways]
@@ -283,7 +304,7 @@
                 outs[j][k, first : first + EXTRA, :] = target_ref[t]
 
 
-def precond_kernel(index_ref, member_ref, smooth_ref, *refs):
+def precond_kernel(index_ref, member_ref, smooth_ref, near_ref, *refs):
     parts = refs[:-3]
     precond_ref, pair_ref, next_ref = refs[-3:]
     coarse_count = member_ref.shape[1]
@@ -433,34 +454,32 @@
         image = base_ref[a] + total_of([part[0, a] for part in arrived])
         image_ref[a] = image
         weighted.append(image * weight_ref[...])
-    full_ref[...] = dot_first(stacked(basis_ref), jnp.concatenate(weighted, axis=0))
+    image = jnp.concatenate([image_ref[0], image_ref[1]], axis=0)
+    left = jnp.concatenate([stacked(basis_ref), image], axis=1)
+    full_ref[...] = dot_first(left, jnp.concatenate(weighted, axis=0))
     spread(full_ref, outs, bits_of(index_ref[2], masks))
 
 
-def remainder_kernel(
-    order, masks, gram_masks, ways, index_ref, weight_ref, basis_ref, image_ref, *refs
-):
-    parts = refs[: len(refs) - ways - 3]
-    hess_ref, remainder_ref = refs[len(parts) : len(parts) + 2]
-    outs = refs[len(parts) + 2 : -1]
-    gram_ref = refs[-1]
-    collect(order, parts, hess_ref, bits_of(index_ref[2], masks))
-    image = jnp.concatenate([image_ref[0], image_ref[1]], axis=0)
-    value = image - dot_rows(stacked(basis_ref), hess_ref[...])
-    remainder_ref[...] = value
-    weight = jnp.concatenate([weight_ref[...]] * 2, axis=0)
-    gram_ref[...] = dot_first(value * weight, value)
-    spread(gram_ref, outs, bits_of(index_ref[2], gram_masks))
-
-
-def factor_kernel(gather, masks, index_ref, remainder_ref, *refs):
-    parts = refs[:-4]
-    upper_ref, new_ref, work_ref, inverse_ref = refs[-4:]
-    order = remainder_ref.shape[1]
+def factor_kernel(gather, masks, index_ref, basis_ref, image_ref, half_ref, *refs):
+    parts = refs[:-6]
+    hess_ref, upper_ref, new_ref, full_ref, work_ref, inverse_ref = refs[-6:]
+    block_total, _, _, order = basis_ref.shape
+    hess_rows = block_total * order
     tile = (ROWS, order)
     lane = lax.broadcasted_iota(jnp.int32, tile, 1)
     row = lax.broadcasted_iota(jnp.int32, tile, 0)
-    collect(gather, parts, work_ref, bits_of(index_ref[2], masks))
+    collect(gather, parts, full_ref, bits_of(index_ref[2], masks))
+    hessenberg = full_ref[:hess_rows, :]
+    hess_ref[...] = hessenberg
+    rows = []
+    number = 0
+    for i in range(block_total):
+        count = block_total - i
+        left = jnp.concatenate([half_ref[number + j] for j in range(count)], axis=1)
+        rows.append(dot_rows(left, full_ref[i * order : hess_rows, :]))
+        number += count
+    product = dot_first(hessenberg, jnp.concatenate(rows, axis=0) - hessenberg)
+    work_ref[...] = full_ref[hess_rows:, :] + (product + jnp.transpose(product))
     for block in range(order // ROWS):
         start = block * ROWS
         inverse_ref[start : start + ROWS, :] = jnp.where(lane == row + start, 1.0, 0.0)
@@ -518,7 +537,9 @@
                 target_inverse = target_inverse - multiplier[m] * solved_inverse[m]
             work_ref[first : first + ROWS, :] = target
             inverse_ref[first : first + ROWS, :] = target_inverse
-    new_ref[...] = dot_rows(remainder_ref[...], inverse_ref[...], ((1,), (1,)))
+    image = jnp.concatenate([image_ref[0], image_ref[1]], axis=0)
+    remainder = image - dot_rows(stacked(basis_ref), hessenberg)
+    new_ref[...] = dot_rows(remainder, inverse_ref[...], ((1,), (1,)))
 
 
 def f32(*shape):
@@ -529,15 +550,19 @@
     return jax.ShapeDtypeStruct(shape, jnp.bfloat16)
 
 
-def call(kernel, out_shape, operands, scalars=0, scratch=(), in_hbm=False):
+def call(kernel, out_shape, operands, scalars=0, scratch=(), in_hbm=0):
     many = isinstance(out_shape, (tuple, list))
+    free = len(operands) - in_hbm
+    operands = list(operands[:free]) + [
+        pltpu.with_memory_space_constraint(x, pltpu.HBM) for x in operands[free:]
+    ]
     return pl.pallas_call(
         kernel,
         out_shape=out_shape,
         in_specs=[SMEM] * scalars + [ANY if in_hbm else VMEM] * (len(operands) - scalars),
         out_specs=[VMEM] * len(out_shape) if many else VMEM,
         scratch_shapes=list(scratch),
-        compiler_params=None if in_hbm else PARAMS,
+        compiler_params=PARAMS,
     )(*operands)
 
 
@@ -585,38 +610,47 @@
         (agg_index, basis, points, weight_row),
         0,
         [pair_index, field, pair_row, one_row, pltpu.SemaphoreType.DMA((4,))],
-        True,
-    )
-    inverse, member, smooth, weight = call(
+        4,
+    )
+    half_blocks = block_total * (block_total + 1) // 2
+    inverse, member, smooth, weight, half_gram = call(
         prefetch_kernel,
         [
             f32(*coarse_inverse.shape),
             f32(2, coarse_count, point_count),
             f32(2, point_count, rhs_count),
             f32(point_count, rhs_count),
+            f32(half_blocks, rhs_count, rhs_count),
         ],
         (pack, agg_index, basis, jacobi, weight_row, coarse_inverse),
         0,
-        [pair_index, field, pair_row, one_row, pltpu.SemaphoreType.DMA((5,))],
-        True,
-    )
+        [
+            pair_index,
+            pltpu.VMEM(basis.shape, jnp.float32),
+            pair_row,
+            one_row,
+            pltpu.SemaphoreType.DMA((5,)),
+        ],
+        5,
+    )
+    half_gram = lax.psum(half_gram, AXES)
     near_rows = jnp.transpose(near_block, (0, 2, 1, 3)).reshape(
         panels_dev, 2 * nodes, slot_total * 2 * nodes
     )
-    packs = gather_steps(pack, wide_groups)
+    packs = gather_steps(pack, wide_groups, (weight,))
     source_rows = high_count * EXTRA // (narrow_count // 2)
     target_rows = 2 * EXTRA
     coarse_outs = pl.pallas_call(
         functools.partial(
-            coarse_kernel, gather_order(wide_groups), 2, high_count, source_rows
+            coarse_kernel, gather_order(wide_groups), 2, high_count
         ),
         out_shape=[f32(narrow_count // 2, coarse_count + source_rows, rhs_count)] * 2
         + [f32(high_count, EXTRA, point_count), f32(2, EXTRA, point_count)],
-        in_specs=[SMEM, VMEM, ANY] + [VMEM] * len(packs),
+        in_specs=[SMEM, VMEM] + [VMEM] * len(packs),
         out_specs=[VMEM] * 4,
         scratch_shapes=[pltpu.VMEM((wide_count * coarse_count, rhs_count), jnp.float32)],
         compiler_params=PARAMS,
-    )(index, inverse, near_rows, *packs)
+    )(index, inverse, *packs)
     own_sources = coarse_outs[2]
     kept, got = flip_each(coarse_outs[:2], [core])
     groups = in_pairs(across)
@@ -631,15 +665,9 @@
     precond, pair_edge, next_edge = call(
         precond_kernel,
         [b16(1, 2, point_count, rhs_count)] + [b16(2, width, rhs_count)] * 2,
-        (index, member, smooth, *coarse_parts),
+        (index, member, smooth, near_rows, *coarse_parts),
         1,
     )
-    fields = gather_steps(precond, source_groups)
-    device_count = narrow_count * wide_count
-    pair_edge = flip(pair_edge, 1)
-    pairs = [(i, i + 1) for i in range(1, device_count - 1, 2)]
-    next_edge = lax.ppermute(next_edge, AXES, pairs + [(j, i) for i, j in pairs])
-
     matrix_spec = pl.BlockSpec((1, 3, point_count, source_total), lambda k: (k, 0, 0, 0))
     matrix = pl.pallas_call(
         functools.partial(matrix_kernel, coarse_count),
@@ -649,6 +677,12 @@
         out_specs=matrix_spec,
         compiler_params=PARAMS,
     )(own_sources, other_sources, *coarse_parts)
+    fields = gather_steps(precond, source_groups, (matrix,))
+    device_count = narrow_count * wide_count
+    pair_edge = flip(pair_edge, 1)
+    pairs = [(i, i + 1) for i in range(1, device_count - 1, 2)]
+    next_edge = lax.ppermute(next_edge, AXES, pairs + [(j, i) for i, j in pairs])
+
     ways = 1 << len(plane_groups[0])
     far_parts = pl.pallas_call(
         functools.partial(far_kernel, ways),
@@ -672,34 +706,29 @@
     )
 
     hess_rows = block_total * rhs_count
+    sum_rows = hess_rows + rhs_count
     halving = [[core]] + plane_groups
-    hess_masks = [core, low] + across
+    masks = [core, low] + across
     image, *parts = call(
-        functools.partial(project_kernel, hess_masks, 2),
+        functools.partial(project_kernel, masks, 2),
         [f32(2, point_count, rhs_count)]
-        + [f32(narrow_count, hess_rows // (2 * narrow_count), rhs_count)] * 2,
+        + [f32(narrow_count, sum_rows // (2 * narrow_count), rhs_count)] * 2,
         (index, weight, basis, base, *far_parts),
         1,
-        [pltpu.VMEM((hess_rows, rhs_count), jnp.float32)],
+        [pltpu.VMEM((sum_rows, rhs_count), jnp.float32)],
     )
     parts = sum_steps(parts, halving, high_groups)
-    hessenberg, remainder, *gram_parts = call(
-        functools.partial(
-            remainder_kernel, gather_order(part_groups(halving)[::-1]), hess_masks, [core], 2
-        ),
-        [f32(hess_rows, rhs_count), f32(2 * point_count, rhs_count)]
-        + [f32(1, rhs_count // 2, rhs_count)] * 2,
-        (index, weight, basis, image, *parts),
+    hessenberg, upper_factor, new_block = call(
+        functools.partial(factor_kernel, gather_order(part_groups(halving)[::-1]), masks),
+        [
+            f32(hess_rows, rhs_count),
+            f32(rhs_count, rhs_count),
+            f32(2 * point_count, rhs_count),
+        ],
+        (index, basis, image, half_gram, *parts),
         1,
-        [pltpu.VMEM((rhs_count, rhs_count), jnp.float32)],
-    )
-    gram_parts = sum_steps(gram_parts, [[core]], plane_groups + high_groups)
-    upper_factor, new_block = call(
-        functools.partial(factor_kernel, gather_order([[1]]), [core]),
-        [f32(rhs_count, rhs_count), f32(2 * point_count, rhs_count)],
-        (index, remainder, *gram_parts),
-        1,
-        [pltpu.VMEM((rhs_count, rhs_count), jnp.float32)] * 2,
+        [pltpu.VMEM((sum_rows, rhs_count), jnp.float32)]
+        + [pltpu.VMEM((rhs_count, rhs_count), jnp.float32)] * 2,
     )
     return (
         new_block.reshape(2, point_count, rhs_count),

time: 105 us -> 204 us (1.94)
  waiting for transfers between devices: 36.5 us -> 132 us
  between operations: 0.87 us -> 14.2 us
  starting transfers between devices: 43.3 us -> 36.7 us
  local copies, waits for them, and re-layouts: 5.57 us -> 3.29 us
    psum x0 -> x1, waiting for transfers between devices: none -> 106 us  [body(): half_gram = lax.psum(half_gram, AXES)]
    ppermute x33 -> x25, waiting for transfers between devices: 36.5 us -> 25.4 us  [flip(): return lax.ppermute(block, AXES, [(i, i ^ mask) for i in range(count)])]
    ppermute x33 -> x25, starting transfers between devices: 42.6 us -> 36 us  [flip(): return lax.ppermute(block, AXES, [(i, i ^ mask) for i in range(count)])]
    unnamed x16 -> x8, local copies, waits for them, and re-layouts: 3.44 us -> 1.11 us
    pallas_call x17 -> x10, Pallas kernels: 14 us -> 13.4 us  [call(): pl.pallas_call(kernel, out_shape=out_shape, in_specs=[SMEM] * scalars + [...]
  transfers between devices with their start and end apart: 34 -> 27, of which waited for: 26 -> 19; matrix products, arithmetic and copies ran while one was open for 2% -> 1% of each run, Pallas kernels for 5% -> 3%
where the time goes in v7:
time: 204 us
  waiting for transfers between devices  132 us (65%)
  starting transfers between devices  36.7 us (18%)
  Pallas kernels  17.8 us (9%)
  between operations  14.2 us (7%)
  local copies, waits for them, and re-layouts  3.29 us (2%)
    psum x1, waiting for transfers between devices, body(): half_gram = lax.psum(half_gram, AXES)  106 us
    ppermute x25, starting transfers between devices, flip(): return lax.ppermute(block, AXES, [(i, i ^ mask) for i in range(count)])  36 us
    ppermute x25, waiting for transfers between devices, flip(): return lax.ppermute(block, AXES, [(i, i ^ mask) for i in range(count)])  25.4 us
    pallas_call x10, Pallas kernels, call(): pl.pallas_call(kernel, out_shape=out_shape, in_specs=[SMEM] * scalars + [...  13.4 us
  transfers between devices with their start and end apart: 27, of which 19 were waited for; matrix products, arithmetic and copies ran while one was open for 1% of the time, Pallas kernels for 3%

profile of v7, /device:TPU:0, one launch (start us, length us, event | category | flops | bytes accessed | tf_op | source)
XLA Modules:
  0.0 203.9 jit_solution(14724831598574908995)
XLA Ops:
  7.2 0.0 all-reduce.2.cloned.1.call-start
  7.2 1.2 shard_map.112.pack_hbm.refs_1_
  8.4 5.1 %collective-permute-start.2 = (f32[1,56,128]{2,1,0:T(8,128)S(1)}, f32[1,56,128]{2,1,0:T(8,128)S(1)}, u32[]{:S(2)}, u32[]{:S(2)}) collective-permute-start(f32[1,56,128]{2,1,0:T(8,128)S(1)} %shard_map.112.pack_hbm.refs_1_), channel_id=1, source_target_pairs={{0,6},{1,7},{2,4},{3,5},{4,2},{5,3},{6,0},{7,1},{8,14},{9,15},{10,... | collective-permute-start | bytes 86024 | tf_op jit(solution)/shard_map/ppermute | solution.py:61
  13.5 0.0 collective-permute-start.1
  13.5 0.6 collective-permute-start
  14.1 2.7 %shard_map.113 = (f32[4,48,384]{2,1,0:T(8,128)S(1)}, f32[2,48,128]{2,1,0:T(8,128)S(1)}, f32[2,128,128]{2,1,0:T(8,128)S(1)}, f32[128,128]{1,0:T(8,128)S(1)}, f32[10,128,128]{2,1,0:T(8,128)}) custom-call(f32[1,56,128]{2,1,0:T(8,128)S(1)} %shard_map.112.pack_hbm.refs_1_, s32[2,128]{1,0:T(2,128)} %agg_hbm.3, f32[4,2,128,128]{3,2,1,0:T(8,128)} %basis_ref.3, ...), custom_call_target="tpu_custom_call" | custom-call | tf_op jit(solution)/shard_map/pallas_call | solution.py:559
  16.8 1.4 collective-permute-done.1.refs_3_
  18.3 0.0 collective-permute-done.refs_2_
  18.3 1.6 collective-permute-start.3
  19.8 0.1 pad_add_fusion.index_ref
  19.9 3.2 %collective-permute-done.3.refs_1_ = f32[4,56,128]{2,1,0:T(8,128)S(1)} collective-permute-done((f32[4,56,128]{2,1,0:T(8,128)S(1)}, f32[4,56,128]{2,1,0:T(8,128)S(1)}, u32[]{:S(2)}, u32[]{:S(2)}) %collective-permute-start.3) | collective-permute-done | bytes 114720 | tf_op jit(solution)/shard_map/ppermute | solution.py:61
  23.1 0.8 shard_map.115
  24.0 0.1 collective-permute-start.4
  24.0 1.2 collective-permute-done.4.got_ref
  25.3 1.6 collective-permute-start.5
  26.9 1.5 copy.13
  28.4 0.7 reshape.15.near_ref.block_ref
  29.1 0.2 collective-permute-done.5.refs_1_
  29.3 0.8 shard_map.117
  30.1 2.4 %collective-permute-start.10 = (bf16[1,2,128,128]{3,2,1,0:T(8,128)(2,1)S(1)}, bf16[1,2,128,128]{3,2,1,0:T(8,128)(2,1)S(1)}, u32[]{:S(2)}, u32[]{:S(2)}) collective-permute-start(bf16[1,2,128,128]{3,2,1,0:T(8,128)(2,1)S(1)} %get-tuple-element.41.own_ref.refs_1_), channel_id=1, source_target_pairs={{0,6},{1,7},{2,4},{3,5},{4,2},{5,3},{6,0},{7,1},{8,14},{9,15},{10,... | collective-permute-start | bytes 196616 | tf_op jit(solution)/shard_map/ppermute | solution.py:61
  32.5 0.0 collective-permute-start.9
  32.5 2.0 %collective-permute-start.8 = (bf16[1,2,128,128]{3,2,1,0:T(8,128)(2,1)S(1)}, bf16[1,2,128,128]{3,2,1,0:T(8,128)(2,1)S(1)}, u32[]{:S(2)}, u32[]{:S(2)}) collective-permute-start(bf16[1,2,128,128]{3,2,1,0:T(8,128)(2,1)S(1)} %get-tuple-element.41.own_ref.refs_1_), channel_id=1, source_target_pairs={{0,2},{1,3},{2,0},{3,1},{4,6},{5,7},{6,4},{7,5},{8,10},{9,11},{10,... | collective-permute-start | bytes 196616 | tf_op jit(solution)/shard_map/ppermute | solution.py:61
  34.5 1.9 shard_map.119.refs_0_.matrix_ref
  36.4 0.0 copy-start.2
  36.4 0.0 copy-start.3
  36.4 0.0 copy-start
  36.4 0.1 collective-permute-done.10.refs_4_
  36.5 2.1 %collective-permute-done.9.refs_3_ = bf16[1,2,128,128]{3,2,1,0:T(8,128)(2,1)S(1)} collective-permute-done((bf16[1,2,128,128]{3,2,1,0:T(8,128)(2,1)S(1)}, bf16[1,2,128,128]{3,2,1,0:T(8,128)(2,1)S(1)}, u32[]{:S(2)}, u32[]{:S(2)}) %collective-permute-start.9) | collective-permute-done | bytes 65568 | tf_op jit(solution)/shard_map/ppermute | solution.py:61
  38.6 0.1 collective-permute-start.11
  38.7 1.5 collective-permute-start.6
  40.3 0.7 collective-permute-start.7
  40.9 1.8 collective-permute-done.6.pair_ref.pair_hbm
  42.7 1.7 shard_map.121
  44.4 4.9 %collective-permute-start.12 = (f32[1,2,128,128]{3,2,1,0:T(8,128)S(1)}, f32[1,2,128,128]{3,2,1,0:T(8,128)S(1)}, u32[]{:S(2)}, u32[]{:S(2)}) collective-permute-start(f32[1,2,128,128]{3,2,1,0:T(8,128)S(1)} %get-tuple-element.47), channel_id=1, source_target_pairs={{0,1},{1,0},{2,3},{3,2},{4,5},{5,4},{6,7},{7,6},{8,9},{9,8},{10,11... | collective-permute-start | bytes 393224 | tf_op jit(solution)/shard_map/ppermute | solution.py:61
  49.3 3.0 %collective-permute-start.13 = (f32[1,2,128,128]{3,2,1,0:T(8,128)S(1)}, f32[1,2,128,128]{3,2,1,0:T(8,128)S(1)}, u32[]{:S(2)}, u32[]{:S(2)}) collective-permute-start(f32[1,2,128,128]{3,2,1,0:T(8,128)S(1)} %get-tuple-element.48), channel_id=1, source_target_pairs={{0,16},{1,17},{2,18},{3,19},{4,20},{5,21},{6,22},{7,23},{8,24},{9,... | collective-permute-start | bytes 393224 | tf_op jit(solution)/shard_map/ppermute | solution.py:61
  52.3 1.4 collective-permute-start.14
  53.7 1.0 shard_map.118.base_ref
  54.7 2.6 %collective-permute-done.13.refs_2_ = f32[1,2,128,128]{3,2,1,0:T(8,128)S(1)} collective-permute-done((f32[1,2,128,128]{3,2,1,0:T(8,128)S(1)}, f32[1,2,128,128]{3,2,1,0:T(8,128)S(1)}, u32[]{:S(2)}, u32[]{:S(2)}) %collective-permute-start.13) | collective-permute-done | bytes 131104 | tf_op jit(solution)/shard_map/ppermute | solution.py:61
  57.3 1.8 collective-permute-done.14.refs_3_
  59.1 1.0 shard_map.122
  60.2 0.1 collective-permute-start.15
  60.3 0.0 all-reduce.2.cloned.1.call-update
  60.3 1.4 collective-permute-done.15.refs_1_
  61.7 1.0 collective-permute-start.16
  62.7 1.3 collective-permute-start.17
  64.0 1.2 collective-permute-start.18
  65.2 0.5 collective-permute-done.16.refs_1_
  65.7 1.0 collective-permute-done.17.refs_2_
  66.7 2.5 %collective-permute-done.18.refs_3_ = f32[1,80,128]{2,1,0:T(8,128)S(1)} collective-permute-done((f32[1,80,128]{2,1,0:T(8,128)S(1)}, f32[1,80,128]{2,1,0:T(8,128)S(1)}, u32[]{:S(2)}, u32[]{:S(2)}) %collective-permute-start.18) | collective-permute-done | bytes 40992 | tf_op jit(solution)/shard_map/ppermute | solution.py:61
  69.2 2.3 %collective-permute-start.21 = (f32[1,80,128]{2,1,0:T(8,128)S(1)}, f32[1,80,128]{2,1,0:T(8,128)S(1)}, u32[]{:S(2)}, u32[]{:S(2)}) collective-permute-start(f32[1,80,128]{2,1,0:T(8,128)S(1)} %shard_map.124.refs_0_), channel_id=1, source_target_pairs={{0,6},{1,7},{2,4},{3,5},{4,2},{5,3},{6,0},{7,1},{8,14},{9,15},{10,... | collective-permute-start | bytes 122888 | tf_op jit(solution)/shard_map/ppermute | solution.py:61
  71.5 0.0 collective-permute-start.20
  71.5 2.2 %collective-permute-start.19 = (f32[1,80,128]{2,1,0:T(8,128)S(1)}, f32[1,80,128]{2,1,0:T(8,128)S(1)}, u32[]{:S(2)}, u32[]{:S(2)}) collective-permute-start(f32[1,80,128]{2,1,0:T(8,128)S(1)} %shard_map.124.refs_0_), channel_id=1, source_target_pairs={{0,2},{1,3},{2,0},{3,1},{4,6},{5,7},{6,4},{7,5},{8,10},{9,11},{10,... | collective-permute-start | bytes 122888 | tf_op jit(solution)/shard_map/ppermute | solution.py:61
  73.7 1.7 collective-permute-done.21.refs_3_
  75.4 1.1 collective-permute-done.20.refs_2_
  76.6 2.0 collective-permute-start.24
  78.5 0.3 collective-permute-start.23
  78.8 1.3 collective-permute-start.22
  80.1 1.4 collective-permute-done.24.refs_3_
  81.5 1.0 collective-permute-done.23.refs_2_
  82.5 0.3 collective-permute-done.22.refs_1_
  82.8 0.1 collective-permute-start.25
  82.9 106.4 %all-reduce.2.cloned.1.call-done.half_ref = f32[10,128,128]{2,1,0:T(8,128)} async-done(((f32[10,128,128]{2,1,0:T(8,128)}), f32[10,128,128]{2,1,0:T(8,128)}) %all-reduce.2.cloned.1.call-update) | async-done | bytes 655376 | tf_op jit(solution)/shard_map/psum | solution.py:636
  189.3 1.1 copy-done.1
  190.3 6.7 %shard_map.127 = (f32[512,128]{1,0:T(8,128)}, f32[128,128]{1,0:T(8,128)}, f32[256,128]{1,0:T(8,128)}) custom-call(s32[3]{0:T(128)S(1)} %pad_add_fusion.index_ref, f32[4,2,128,128]{3,2,1,0:T(8,128)S(1)} %copy-done, f32[2,128,128]{2,1,0:T(8,128)S(1)} %get-tuple-element.50.image_ref, f32[10,128,128]{2,1,0:T(8,128)S(1)} %copy-done.1, ...), custom_call_target="tpu_custom_call" | custom-call | tf_op jit(solution)/shard_map/pallas_call | solution.py:559
  (18 shorter events, 0.1 us)
Async XLA Ops:
  7.2 182.1 %all-reduce.2.cloned.1.call-start = ((), (), s32[]{:S(2)}) async-start(), calls=%async_computation | async-start | bytes 1310720 | tf_op jit(solution)/shard_map/psum | solution.py:636
  8.4 8.4 %collective-permute-start.2 = (f32[1,56,128]{2,1,0:T(8,128)S(1)}, f32[1,56,128]{2,1,0:T(8,128)S(1)}, u32[]{:S(2)}, u32[]{:S(2)}) collective-permute-start(f32[1,56,128]{2,1,0:T(8,128)S(1)} %shard_map.112.pack_hbm.refs_1_), channel_id=1, source_target_pairs={{0,6},{1,7},{2,4},{3,5},{4,2},{5,3},{6,0},{7,1},{8,14},{9,15},{10,... | collective-permute-start | bytes 86024 | tf_op jit(solution)/shard_map/ppermute | solution.py:61
  13.5 4.8 %collective-permute-start.1 = (f32[1,56,128]{2,1,0:T(8,128)S(1)}, f32[1,56,128]{2,1,0:T(8,128)S(1)}, u32[]{:S(2)}, u32[]{:S(2)}) collective-permute-start(f32[1,56,128]{2,1,0:T(8,128)S(1)} %shard_map.112.pack_hbm.refs_1_), channel_id=1, source_target_pairs={{0,4},{1,5},{2,6},{3,7},{4,0},{5,1},{6,2},{7,3},{8,12},{9,13},{10,... | collective-permute-start | bytes 86024 | tf_op jit(solution)/shard_map/ppermute | solution.py:61
  13.5 4.8 %collective-permute-start = (f32[1,56,128]{2,1,0:T(8,128)S(1)}, f32[1,56,128]{2,1,0:T(8,128)S(1)}, u32[]{:S(2)}, u32[]{:S(2)}) collective-permute-start(f32[1,56,128]{2,1,0:T(8,128)S(1)} %shard_map.112.pack_hbm.refs_1_), channel_id=1, source_target_pairs={{0,2},{1,3},{2,0},{3,1},{4,6},{5,7},{6,4},{7,5},{8,10},{9,11},{10,... | collective-permute-start | bytes 86024 | tf_op jit(solution)/shard_map/ppermute | solution.py:61
  18.3 4.9 %collective-permute-start.3 = (f32[4,56,128]{2,1,0:T(8,128)S(1)}, f32[4,56,128]{2,1,0:T(8,128)S(1)}, u32[]{:S(2)}, u32[]{:S(2)}) collective-permute-start(f32[4,56,128]{2,1,0:T(8,128)S(1)} %shard_map.114.refs_0_), channel_id=1, source_target_pairs={{0,1},{1,0},{2,3},{3,2},{4,5},{5,4},{6,7},{7,6},{8,9},{9,8},{10,11... | collective-permute-start | bytes 344072 | tf_op jit(solution)/shard_map/ppermute | solution.py:61
  24.0 1.3 collective-permute-start.4
  25.3 4.0 %collective-permute-start.5 = (f32[1,64,128]{2,1,0:T(8,128)S(1)}, f32[1,64,128]{2,1,0:T(8,128)S(1)}, u32[]{:S(2)}, u32[]{:S(2)}) collective-permute-start(f32[1,64,128]{2,1,0:T(8,128)S(1)} %get-tuple-element.40), channel_id=1, source_target_pairs={{0,16},{1,17},{2,18},{3,19},{4,20},{5,21},{6,22},{7,23},{8,24},{9,... | collective-permute-start | bytes 98312 | tf_op jit(solution)/shard_map/ppermute | solution.py:61
  30.1 6.5 %collective-permute-start.10 = (bf16[1,2,128,128]{3,2,1,0:T(8,128)(2,1)S(1)}, bf16[1,2,128,128]{3,2,1,0:T(8,128)(2,1)S(1)}, u32[]{:S(2)}, u32[]{:S(2)}) collective-permute-start(bf16[1,2,128,128]{3,2,1,0:T(8,128)(2,1)S(1)} %get-tuple-element.41.own_ref.refs_1_), channel_id=1, source_target_pairs={{0,6},{1,7},{2,4},{3,5},{4,2},{5,3},{6,0},{7,1},{8,14},{9,15},{10,... | collective-permute-start | bytes 196616 | tf_op jit(solution)/shard_map/ppermute | solution.py:61
  32.5 6.2 %collective-permute-start.9 = (bf16[1,2,128,128]{3,2,1,0:T(8,128)(2,1)S(1)}, bf16[1,2,128,128]{3,2,1,0:T(8,128)(2,1)S(1)}, u32[]{:S(2)}, u32[]{:S(2)}) collective-permute-start(bf16[1,2,128,128]{3,2,1,0:T(8,128)(2,1)S(1)} %get-tuple-element.41.own_ref.refs_1_), channel_id=1, source_target_pairs={{0,4},{1,5},{2,6},{3,7},{4,0},{5,1},{6,2},{7,3},{8,12},{9,13},{10,... | collective-permute-start | bytes 196616 | tf_op jit(solution)/shard_map/ppermute | solution.py:61
  32.5 6.2 %collective-permute-start.8 = (bf16[1,2,128,128]{3,2,1,0:T(8,128)(2,1)S(1)}, bf16[1,2,128,128]{3,2,1,0:T(8,128)(2,1)S(1)}, u32[]{:S(2)}, u32[]{:S(2)}) collective-permute-start(bf16[1,2,128,128]{3,2,1,0:T(8,128)(2,1)S(1)} %get-tuple-element.41.own_ref.refs_1_), channel_id=1, source_target_pairs={{0,2},{1,3},{2,0},{3,1},{4,6},{5,7},{6,4},{7,5},{8,10},{9,11},{10,... | collective-permute-start | bytes 196616 | tf_op jit(solution)/shard_map/ppermute | solution.py:61
  36.4 17.3 %copy-start.2 = (s32[8,12]{1,0:T(8,128)S(1)}, s32[8,12]{1,0:T(8,128)}, u32[]{:S(2)}) copy-start(s32[8,12]{1,0:T(8,128)} %panel_ref.1) | copy-start | bytes 1156
  36.4 17.3 %copy-start.3 = (s32[8]{0:T(128)S(1)}, s32[8]{0:T(128)}, u32[]{:S(2)}) copy-start(s32[8]{0:T(128)} %count_ref.1) | copy-start | bytes 100
  36.4 22.7 %copy-start = (f32[4,2,128,128]{3,2,1,0:T(8,128)S(1)}, f32[4,2,128,128]{3,2,1,0:T(8,128)}, u32[]{:S(2)}) copy-start(f32[4,2,128,128]{3,2,1,0:T(8,128)} %basis_ref.3) | copy-start | bytes 1572868
  38.6 4.1 %collective-permute-start.11 = (bf16[4,2,128,128]{3,2,1,0:T(8,128)(2,1)S(1)}, bf16[4,2,128,128]{3,2,1,0:T(8,128)(2,1)S(1)}, u32[]{:S(2)}, u32[]{:S(2)}) collective-permute-start(bf16[4,2,128,128]{3,2,1,0:T(8,128)(2,1)S(1)} %shard_map.120.refs_0_), channel_id=1, source_target_pairs={{0,8},{1,9},{2,10},{3,11},{4,12},{5,13},{6,14},{7,15},{8,0},{9,1},... | collective-permute-start | bytes 786440 | tf_op jit(solution)/shard_map/ppermute | solution.py:61
  38.7 4.0 %collective-permute-start.6 = (bf16[2,64,128]{2,1,0:T(8,128)(2,1)S(1)}, bf16[2,64,128]{2,1,0:T(8,128)(2,1)S(1)}, u32[]{:S(2)}, u32[]{:S(2)}) collective-permute-start(bf16[2,64,128]{2,1,0:T(8,128)(2,1)S(1)} %get-tuple-element.42), channel_id=1, source_target_pairs={{0,1},{1,0},{2,3},{3,2},{4,5},{5,4},{6,7},{7,6},{8,9},{9,8},{10,11... | collective-permute-start | bytes 98312 | tf_op jit(solution)/shard_map/ppermute | solution.py:61
  40.3 2.4 %collective-permute-start.7 = (bf16[2,64,128]{2,1,0:T(8,128)(2,1)S(1)}, bf16[2,64,128]{2,1,0:T(8,128)(2,1)S(1)}, u32[]{:S(2)}, u32[]{:S(2)}) collective-permute-start(bf16[2,64,128]{2,1,0:T(8,128)(2,1)S(1)} %get-tuple-element.43), channel_id=1, source_target_pairs={{1,2},{3,4},{5,6},{7,8},{9,10},{11,12},{13,14},{15,16},{17,18},{19... | collective-permute-start | bytes 98312 | tf_op jit(solution)/shard_map/ppermute | solution.py:684
  44.4 10.3 %collective-permute-start.12 = (f32[1,2,128,128]{3,2,1,0:T(8,128)S(1)}, f32[1,2,128,128]{3,2,1,0:T(8,128)S(1)}, u32[]{:S(2)}, u32[]{:S(2)}) collective-permute-start(f32[1,2,128,128]{3,2,1,0:T(8,128)S(1)} %get-tuple-element.47), channel_id=1, source_target_pairs={{0,1},{1,0},{2,3},{3,2},{4,5},{5,4},{6,7},{7,6},{8,9},{9,8},{10,11... | collective-permute-start | bytes 393224 | tf_op jit(solution)/shard_map/ppermute | solution.py:61
  49.3 8.0 %collective-permute-start.13 = (f32[1,2,128,128]{3,2,1,0:T(8,128)S(1)}, f32[1,2,128,128]{3,2,1,0:T(8,128)S(1)}, u32[]{:S(2)}, u32[]{:S(2)}) collective-permute-start(f32[1,2,128,128]{3,2,1,0:T(8,128)S(1)} %get-tuple-element.48), channel_id=1, source_target_pairs={{0,16},{1,17},{2,18},{3,19},{4,20},{5,21},{6,22},{7,23},{8,24},{9,... | collective-permute-start | bytes 393224 | tf_op jit(solution)/shard_map/ppermute | solution.py:61
  52.3 6.8 %collective-permute-start.14 = (f32[1,2,128,128]{3,2,1,0:T(8,128)S(1)}, f32[1,2,128,128]{3,2,1,0:T(8,128)S(1)}, u32[]{:S(2)}, u32[]{:S(2)}) collective-permute-start(f32[1,2,128,128]{3,2,1,0:T(8,128)S(1)} %get-tuple-element.49), channel_id=1, source_target_pairs={{0,17},{1,16},{2,19},{3,18},{4,21},{5,20},{6,23},{7,22},{8,25},{9,... | collective-permute-start | bytes 393224 | tf_op jit(solution)/shard_map/ppermute | solution.py:61
  60.2 1.5 collective-permute-start.15
  61.7 4.1 %collective-permute-start.16 = (f32[1,80,128]{2,1,0:T(8,128)S(1)}, f32[1,80,128]{2,1,0:T(8,128)S(1)}, u32[]{:S(2)}, u32[]{:S(2)}) collective-permute-start(f32[1,80,128]{2,1,0:T(8,128)S(1)} %get-tuple-element.55), channel_id=1, source_target_pairs={{0,1},{1,0},{2,3},{3,2},{4,5},{5,4},{6,7},{7,6},{8,9},{9,8},{10,11... | collective-permute-start | bytes 122888 | tf_op jit(solution)/shard_map/ppermute | solution.py:61
  62.7 4.0 %collective-permute-start.17 = (f32[1,80,128]{2,1,0:T(8,128)S(1)}, f32[1,80,128]{2,1,0:T(8,128)S(1)}, u32[]{:S(2)}, u32[]{:S(2)}) collective-permute-start(f32[1,80,128]{2,1,0:T(8,128)S(1)} %get-tuple-element.56), channel_id=1, source_target_pairs={{0,16},{1,17},{2,18},{3,19},{4,20},{5,21},{6,22},{7,23},{8,24},{9,... | collective-permute-start | bytes 122888 | tf_op jit(solution)/shard_map/ppermute | solution.py:61
  64.0 5.2 %collective-permute-start.18 = (f32[1,80,128]{2,1,0:T(8,128)S(1)}, f32[1,80,128]{2,1,0:T(8,128)S(1)}, u32[]{:S(2)}, u32[]{:S(2)}) collective-permute-start(f32[1,80,128]{2,1,0:T(8,128)S(1)} %get-tuple-element.57), channel_id=1, source_target_pairs={{0,17},{1,16},{2,19},{3,18},{4,21},{5,20},{6,23},{7,22},{8,25},{9,... | collective-permute-start | bytes 122888 | tf_op jit(solution)/shard_map/ppermute | solution.py:61
  69.2 6.2 %collective-permute-start.21 = (f32[1,80,128]{2,1,0:T(8,128)S(1)}, f32[1,80,128]{2,1,0:T(8,128)S(1)}, u32[]{:S(2)}, u32[]{:S(2)}) collective-permute-start(f32[1,80,128]{2,1,0:T(8,128)S(1)} %shard_map.124.refs_0_), channel_id=1, source_target_pairs={{0,6},{1,7},{2,4},{3,5},{4,2},{5,3},{6,0},{7,1},{8,14},{9,15},{10,... | collective-permute-start | bytes 122888 | tf_op jit(solution)/shard_map/ppermute | solution.py:61
  71.5 5.0 %collective-permute-start.20 = (f32[1,80,128]{2,1,0:T(8,128)S(1)}, f32[1,80,128]{2,1,0:T(8,128)S(1)}, u32[]{:S(2)}, u32[]{:S(2)}) collective-permute-start(f32[1,80,128]{2,1,0:T(8,128)S(1)} %shard_map.124.refs_0_), channel_id=1, source_target_pairs={{0,4},{1,5},{2,6},{3,7},{4,0},{5,1},{6,2},{7,3},{8,12},{9,13},{10,... | collective-permute-start | bytes 122888 | tf_op jit(solution)/shard_map/ppermute | solution.py:61
  71.5 5.0 %collective-permute-start.19 = (f32[1,80,128]{2,1,0:T(8,128)S(1)}, f32[1,80,128]{2,1,0:T(8,128)S(1)}, u32[]{:S(2)}, u32[]{:S(2)}) collective-permute-start(f32[1,80,128]{2,1,0:T(8,128)S(1)} %shard_map.124.refs_0_), channel_id=1, source_target_pairs={{0,2},{1,3},{2,0},{3,1},{4,6},{5,7},{6,4},{7,5},{8,10},{9,11},{10,... | collective-permute-start | bytes 122888 | tf_op jit(solution)/shard_map/ppermute | solution.py:61
  76.6 5.0 %collective-permute-start.24 = (f32[1,80,128]{2,1,0:T(8,128)S(1)}, f32[1,80,128]{2,1,0:T(8,128)S(1)}, u32[]{:S(2)}, u32[]{:S(2)}) collective-permute-start(f32[1,80,128]{2,1,0:T(8,128)S(1)} %shard_map.125.refs_0_), channel_id=1, source_target_pairs={{0,17},{1,16},{2,19},{3,18},{4,21},{5,20},{6,23},{7,22},{8,25},{9,... | collective-permute-start | bytes 122888 | tf_op jit(solution)/shard_map/ppermute | solution.py:61
  78.5 4.0 %collective-permute-start.23 = (f32[1,80,128]{2,1,0:T(8,128)S(1)}, f32[1,80,128]{2,1,0:T(8,128)S(1)}, u32[]{:S(2)}, u32[]{:S(2)}) collective-permute-start(f32[1,80,128]{2,1,0:T(8,128)S(1)} %shard_map.125.refs_0_), channel_id=1, source_target_pairs={{0,16},{1,17},{2,18},{3,19},{4,20},{5,21},{6,22},{7,23},{8,24},{9,... | collective-permute-start | bytes 122888 | tf_op jit(solution)/shard_map/ppermute | solution.py:61
  78.8 4.0 %collective-permute-start.22 = (f32[1,80,128]{2,1,0:T(8,128)S(1)}, f32[1,80,128]{2,1,0:T(8,128)S(1)}, u32[]{:S(2)}, u32[]{:S(2)}) collective-permute-start(f32[1,80,128]{2,1,0:T(8,128)S(1)} %shard_map.125.refs_0_), channel_id=1, source_target_pairs={{0,1},{1,0},{2,3},{3,2},{4,5},{5,4},{6,7},{7,6},{8,9},{9,8},{10,11... | collective-permute-start | bytes 122888 | tf_op jit(solution)/shard_map/ppermute | solution.py:61
  82.8 106.4 %collective-permute-start.25 = (f32[4,80,128]{2,1,0:T(8,128)S(1)}, f32[4,80,128]{2,1,0:T(8,128)S(1)}, u32[]{:S(2)}, u32[]{:S(2)}) collective-permute-start(f32[4,80,128]{2,1,0:T(8,128)S(1)} %shard_map.126.refs_0_), channel_id=1, source_target_pairs={{0,8},{1,9},{2,10},{3,11},{4,12},{5,13},{6,14},{7,15},{8,0},{9,1},... | collective-permute-start | bytes 491528 | tf_op jit(solution)/shard_map/ppermute | solution.py:61
  189.3 1.1 copy-start.1
Sparse Core Ops, SparseCore 0:
  60.4 128.8 all-reduce.1

commit v8 on v7

--- a/solution.py
+++ b/solution.py
@@ -122,16 +122,22 @@
     return values[0]
 
 
-def sum_kernel(count, *refs):
-    parts, outs = refs[:count], refs[count:]
+def sum_kernel(count, skip, *refs):
+    parts, outs = refs[skip : skip + count], refs[skip + count :]
     for k in range(outs[0].shape[0]):
         for j, out_ref in enumerate(outs):
             out_ref[k] = total_of([part[k * len(outs) + j] for part in parts])
 
 
-def sum_parts(parts, ways):
+def sum_parts(parts, ways, after=()):
     out = f32(parts[0].shape[0] // ways, *parts[0].shape[1:])
-    return call(functools.partial(sum_kernel, len(parts)), [out] * ways, parts)
+    return pl.pallas_call(
+        functools.partial(sum_kernel, len(parts), len(after)),
+        out_shape=[out] * ways,
+        in_specs=[ANY] * len(after) + [VMEM] * len(parts),
+        out_specs=[VMEM] * ways,
+        compiler_params=PARAMS,
+    )(*after, *parts)
 
 
 def scatter_steps(parts, groups):
@@ -142,11 +148,22 @@
     return parts
 
 
-def sum_steps(parts, halving, butterfly):
-    (total,) = sum_parts(scatter_steps(parts, halving), 1)
-    for group in butterfly:
+def sum_butterfly(total, groups):
+    for group in groups:
         (total,) = sum_parts(flip_each([total] * (1 << len(group)), group), 1)
-    return gather_steps(total, halving[::-1])
+    return total
+
+
+def append_kernel(left_ref, right_ref, out_ref):
+    rows = left_ref.shape[1]
+    out_ref[:, :rows, :] = left_ref[...]
+    out_ref[:, rows:, :] = right_ref[...]
+
+
+def append(left, right):
+    count, rows, width = left.shape
+    shape = f32(count, rows + right.shape[1], width)
+    return call(append_kernel, shape, (left, right))
 
 
 def part_groups(groups):
@@ -204,6 +221,8 @@
 
 
 def prefetch_kernel(
+    masks,
+    index_ref,
     pack_hbm,
     agg_hbm,
     basis_hbm,
@@ -214,6 +233,8 @@
     member_ref,
     smooth_ref,
     weight_out_ref,
+    keep_ref,
+    send_ref,
     half_ref,
     agg_ref,
     basis_ref,
@@ -247,8 +268,10 @@
         row = dot_first(left, right[:, i * rhs_count :])
         for j in range(i, block_total):
             block = row[:, (j - i) * rhs_count : (j - i + 1) * rhs_count]
-            half_ref[number] = block * 0.5 if i == j else block
+            rows = slice(number * rhs_count, (number + 1) * rhs_count)
+            half_ref[rows, :] = block * 0.5 if i == j else block
             number += 1
+    spread(half_ref, (keep_ref, send_ref), bits_of(index_ref[2], masks))
 
 
 def part_at(parts, k):
@@ -426,12 +449,12 @@
         outs[k % len(outs)][k // len(outs)] = full_ref[pl.ds(first, rows), :]
 
 
-def collect(order, parts, full_ref, own):
-    rows = parts[0].shape[1]
+def collect(order, parts, full_ref, own, start):
+    rows = full_ref.shape[0] // len(order)
     for k, offset in enumerate(order):
         first = pl.multiple_of((own ^ offset) * rows, 8)
         ref, row = part_at(parts, k)
-        full_ref[pl.ds(first, rows), :] = ref[row]
+        full_ref[pl.ds(first, rows), :] = ref[row, start : start + rows, :]
 
 
 def stacked(basis_ref):
@@ -444,7 +467,7 @@
     )
 
 
-def project_kernel(masks, ways, index_ref, weight_ref, basis_ref, base_ref, *refs):
+def project_kernel(masks, ways, index_ref, half_hbm, weight_ref, basis_ref, base_ref, *refs):
     arrived = refs[: len(refs) - ways - 2]
     image_ref = refs[len(arrived)]
     outs = refs[len(arrived) + 1 : -1]
@@ -460,22 +483,30 @@
     spread(full_ref, outs, bits_of(index_ref[2], masks))
 
 
-def factor_kernel(gather, masks, index_ref, basis_ref, image_ref, half_ref, *refs):
-    parts = refs[:-6]
-    hess_ref, upper_ref, new_ref, full_ref, work_ref, inverse_ref = refs[-6:]
+def factor_kernel(gather, masks, index_ref, basis_ref, image_ref, *refs):
+    parts = refs[:-7]
+    hess_ref, upper_ref, new_ref, full_ref, half_ref, work_ref, inverse_ref = refs[-7:]
     block_total, _, _, order = basis_ref.shape
     hess_rows = block_total * order
     tile = (ROWS, order)
     lane = lax.broadcasted_iota(jnp.int32, tile, 1)
     row = lax.broadcasted_iota(jnp.int32, tile, 0)
-    collect(gather, parts, full_ref, bits_of(index_ref[2], masks))
+    own = bits_of(index_ref[2], masks)
+    collect(gather, parts, full_ref, own, 0)
+    collect(gather, parts, half_ref, own, full_ref.shape[0] // len(gather))
     hessenberg = full_ref[:hess_rows, :]
     hess_ref[...] = hessenberg
     rows = []
     number = 0
     for i in range(block_total):
         count = block_total - i
-        left = jnp.concatenate([half_ref[number + j] for j in range(count)], axis=1)
+        left = jnp.concatenate(
+            [
+                half_ref[(number + j) * order : (number + j + 1) * order, :]
+                for j in range(count)
+            ],
+            axis=1,
+        )
         rows.append(dot_rows(left, full_ref[i * order : hess_rows, :]))
         number += count
     product = dot_first(hessenberg, jnp.concatenate(rows, axis=0) - hessenberg)
@@ -612,19 +643,22 @@
         [pair_index, field, pair_row, one_row, pltpu.SemaphoreType.DMA((4,))],
         4,
     )
-    half_blocks = block_total * (block_total + 1) // 2
-    inverse, member, smooth, weight, half_gram = call(
-        prefetch_kernel,
+    half_rows = block_total * (block_total + 1) // 2 * rhs_count
+    halving = [[core]] + plane_groups
+    masks = [core, low] + across
+    inverse, member, smooth, weight, *half_parts = call(
+        functools.partial(prefetch_kernel, masks),
         [
             f32(*coarse_inverse.shape),
             f32(2, coarse_count, point_count),
             f32(2, point_count, rhs_count),
             f32(point_count, rhs_count),
-            f32(half_blocks, rhs_count, rhs_count),
-        ],
-        (pack, agg_index, basis, jacobi, weight_row, coarse_inverse),
-        0,
+        ]
+        + [f32(narrow_count, half_rows // (2 * narrow_count), rhs_count)] * 2,
+        (index, pack, agg_index, basis, jacobi, weight_row, coarse_inverse),
+        1,
         [
+            pltpu.VMEM((half_rows, rhs_count), jnp.float32),
             pair_index,
             pltpu.VMEM(basis.shape, jnp.float32),
             pair_row,
@@ -633,7 +667,7 @@
         ],
         5,
     )
-    half_gram = lax.psum(half_gram, AXES)
+    half_parts = flip_each(half_parts, [core])
     near_rows = jnp.transpose(near_block, (0, 2, 1, 3)).reshape(
         panels_dev, 2 * nodes, slot_total * 2 * nodes
     )
@@ -677,7 +711,10 @@
         out_specs=matrix_spec,
         compiler_params=PARAMS,
     )(own_sources, other_sources, *coarse_parts)
-    fields = gather_steps(precond, source_groups, (matrix,))
+    fields = flip_each([precond] * (1 << len(source_groups[0])), source_groups[0])
+    half_parts = sum_parts(half_parts, 1 << len(plane_groups[0]), fields[1:])
+    (half_total,) = sum_parts(scatter_steps(half_parts, plane_groups), 1)
+    fields = gather_steps(join(fields, (matrix,)), source_groups[1:])
     device_count = narrow_count * wide_count
     pair_edge = flip(pair_edge, 1)
     pairs = [(i, i + 1) for i in range(1, device_count - 1, 2)]
@@ -707,17 +744,19 @@
 
     hess_rows = block_total * rhs_count
     sum_rows = hess_rows + rhs_count
-    halving = [[core]] + plane_groups
-    masks = [core, low] + across
-    image, *parts = call(
+    half_total = sum_butterfly(half_total, high_groups)
+    image, *parts = pl.pallas_call(
         functools.partial(project_kernel, masks, 2),
-        [f32(2, point_count, rhs_count)]
+        out_shape=[f32(2, point_count, rhs_count)]
         + [f32(narrow_count, sum_rows // (2 * narrow_count), rhs_count)] * 2,
-        (index, weight, basis, base, *far_parts),
-        1,
-        [pltpu.VMEM((sum_rows, rhs_count), jnp.float32)],
-    )
-    parts = sum_steps(parts, halving, high_groups)
+        in_specs=[SMEM, ANY] + [VMEM] * (3 + len(far_parts)),
+        out_specs=[VMEM] * 3,
+        scratch_shapes=[pltpu.VMEM((sum_rows, rhs_count), jnp.float32)],
+        compiler_params=PARAMS,
+    )(index, half_total, weight, basis, base, *far_parts)
+    (total,) = sum_parts(scatter_steps(parts, halving), 1)
+    total = sum_butterfly(total, high_groups)
+    parts = gather_steps(append(total, half_total), halving[::-1])
     hessenberg, upper_factor, new_block = call(
         functools.partial(factor_kernel, gather_order(part_groups(halving)[::-1]), masks),
         [
@@ -725,9 +764,12 @@
             f32(rhs_count, rhs_count),
             f32(2 * point_count, rhs_count),
         ],
-        (index, basis, image, half_gram, *parts),
+        (index, basis, image, *parts),
         1,
-        [pltpu.VMEM((sum_rows, rhs_count), jnp.float32)]
+        [
+            pltpu.VMEM((sum_rows, rhs_count), jnp.float32),
+            pltpu.VMEM((half_rows, rhs_count), jnp.float32),
+        ]
         + [pltpu.VMEM((rhs_count, rhs_count), jnp.float32)] * 2,
     )
     return (

time: 204 us -> 90.6 us (0.44)
  waiting for transfers between devices: 132 us -> 27.6 us
  between operations: 14.2 us -> 0.89 us
  starting transfers between devices: 36.7 us -> 41.9 us
    psum x1 -> x0, waiting for transfers between devices: 106 us -> none  [body(): half_gram = lax.psum(half_gram, AXES)]
    ppermute x25 -> x32, starting transfers between devices: 36 us -> 41.3 us  [flip(): return lax.ppermute(block, AXES, [(i, i ^ mask) for i in range(count)])]
    ppermute x25 -> x32, waiting for transfers between devices: 25.4 us -> 27.5 us  [flip(): return lax.ppermute(block, AXES, [(i, i ^ mask) for i in range(count)])]
    pallas_call x10 -> x7, Pallas kernels: 13.4 us -> 12.1 us  [call(): pl.pallas_call(kernel, out_shape=out_shape, in_specs=[SMEM] * scalars + [...]
  transfers between devices with their start and end apart: 27 -> 33, of which waited for: 19 -> 19; matrix products, arithmetic and copies ran while one was open for 1% -> 2% of each run, Pallas kernels for 3% -> 10%
where the time goes in v8:
time: 90.6 us; the launch traced here: 90.4 us
  starting transfers between devices  41.9 us (46%)
  waiting for transfers between devices  27.6 us (30%)
  Pallas kernels  17.8 us (20%)
  local copies, waits for them, and re-layouts  2.2 us (2%)
    ppermute x32, starting transfers between devices, flip(): return lax.ppermute(block, AXES, [(i, i ^ mask) for i in range(count)])  41.3 us
    ppermute x32, waiting for transfers between devices, flip(): return lax.ppermute(block, AXES, [(i, i ^ mask) for i in range(count)])  27.5 us
    pallas_call x7, Pallas kernels, call(): pl.pallas_call(kernel, out_shape=out_shape, in_specs=[SMEM] * scalars + [...  12.1 us
    pallas_call x1, Pallas kernels, body(): pl.pallas_call(functools.partial(matrix_kernel, coarse_count), out_shape=...  1.88 us
  transfers between devices with their start and end apart: 33, of which 19 were waited for; matrix products, arithmetic and copies ran while one was open for 2% of the time, Pallas kernels for 10%

profile of v8, /device:TPU:0, one launch (start us, length us, event | category | flops | bytes accessed | tf_op | source)
XLA Modules:
  0.0 90.4 jit_solution(3239163523933131387)
XLA Ops:
  0.6 1.2 %shard_map.112.pack_hbm.refs_1_ = f32[1,56,128]{2,1,0:T(8,128)S(1)} custom-call(s32[2,128]{1,0:T(2,128)} %agg_hbm.3, f32[4,2,128,128]{3,2,1,0:T(8,128)} %basis_ref.3, f32[2,128]{1,0:T(2,128)} %points_hbm.1, f32[1,128]{1,0:T(1,128)} %bitcast.8), custom_call_target="tpu_custom_call" | custom-call | tf_op jit(solution)/shard_map/pallas_call | solution.py:590
  1.8 5.1 %collective-permute-start.2 = (f32[1,56,128]{2,1,0:T(8,128)S(1)}, f32[1,56,128]{2,1,0:T(8,128)S(1)}, u32[]{:S(2)}, u32[]{:S(2)}) collective-permute-start(f32[1,56,128]{2,1,0:T(8,128)S(1)} %shard_map.112.pack_hbm.refs_1_), channel_id=1, source_target_pairs={{0,6},{1,7},{2,4},{3,5},{4,2},{5,3},{6,0},{7,1},{8,14},{9,15},{10,... | collective-permute-start | bytes 86024 | tf_op jit(solution)/shard_map/ppermute | solution.py:61
  6.9 0.0 collective-permute-start.1
  6.9 0.6 collective-permute-start
  7.5 0.1 pad_add_fusion.index_ref
  7.6 2.4 %shard_map.113 = (f32[4,48,384]{2,1,0:T(8,128)S(1)}, f32[2,48,128]{2,1,0:T(8,128)S(1)}, f32[2,128,128]{2,1,0:T(8,128)S(1)}, f32[128,128]{1,0:T(8,128)S(1)}, f32[...) custom-call(s32[3]{0:T(128)S(1)} %pad_add_fusion.index_ref, f32[1,56,128]{2,1,0:T(8,128)S(1)} %shard_map.112.pack_hbm.refs_1_, ...), custom_call_target="tpu_custom_call" | custom-call | tf_op jit(solution)/shard_map/pallas_call | solution.py:590
  10.1 1.6 %collective-permute-done.1.refs_3_ = f32[1,56,128]{2,1,0:T(8,128)S(1)} collective-permute-done((f32[1,56,128]{2,1,0:T(8,128)S(1)}, f32[1,56,128]{2,1,0:T(8,128)S(1)}, u32[]{:S(2)}, u32[]{:S(2)}) %collective-permute-start.1) | collective-permute-done | bytes 28704 | tf_op jit(solution)/shard_map/ppermute | solution.py:61
  11.7 1.6 %collective-permute-start.3 = (f32[4,56,128]{2,1,0:T(8,128)S(1)}, f32[4,56,128]{2,1,0:T(8,128)S(1)}, u32[]{:S(2)}, u32[]{:S(2)}) collective-permute-start(f32[4,56,128]{2,1,0:T(8,128)S(1)} %shard_map.114.refs_0_), channel_id=1, source_target_pairs={{0,1},{1,0},{2,3},{3,2},{4,5},{5,4},{6,7},{7,6},{8,9},{9,8},{10,11... | collective-permute-start | bytes 344072 | tf_op jit(solution)/shard_map/ppermute | solution.py:61
  13.3 3.3 %collective-permute-done.3.refs_1_ = f32[4,56,128]{2,1,0:T(8,128)S(1)} collective-permute-done((f32[4,56,128]{2,1,0:T(8,128)S(1)}, f32[4,56,128]{2,1,0:T(8,128)S(1)}, u32[]{:S(2)}, u32[]{:S(2)}) %collective-permute-start.3) | collective-permute-done | bytes 114720 | tf_op jit(solution)/shard_map/ppermute | solution.py:61
  16.6 0.8 shard_map.115
  17.4 0.1 collective-permute-start.4
  17.5 1.2 %collective-permute-done.4.got_ref = f32[2,64,128]{2,1,0:T(8,128)S(1)} collective-permute-done((f32[2,64,128]{2,1,0:T(8,128)S(1)}, f32[2,64,128]{2,1,0:T(8,128)S(1)}, u32[]{:S(2)}, u32[]{:S(2)}) %collective-permute-start.4) | collective-permute-done | bytes 65568 | tf_op jit(solution)/shard_map/ppermute | solution.py:61
  18.7 1.6 %collective-permute-start.5 = (f32[1,64,128]{2,1,0:T(8,128)S(1)}, f32[1,64,128]{2,1,0:T(8,128)S(1)}, u32[]{:S(2)}, u32[]{:S(2)}) collective-permute-start(f32[1,64,128]{2,1,0:T(8,128)S(1)} %get-tuple-element.45), channel_id=1, source_target_pairs={{0,16},{1,17},{2,18},{3,19},{4,20},{5,21},{6,22},{7,23},{8,24},{9,... | collective-permute-start | bytes 98312 | tf_op jit(solution)/shard_map/ppermute | solution.py:61
  20.3 1.5 %copy.13 = bf16[8,32,12,32]{3,2,1,0:T(8,128)(2,1)S(1)} copy(bf16[8,32,12,32]{3,1,2,0:T(8,128)(2,1)} %bitcast.7) | data formatting | bytes 393216 | tf_op jit(solution)/shard_map/transpose | solution.py:671
  21.8 0.7 reshape.15.near_ref.block_ref
  22.5 0.2 collective-permute-done.5.refs_1_
  22.7 0.8 shard_map.117
  23.5 2.2 %collective-permute-start.8 = (bf16[1,2,128,128]{3,2,1,0:T(8,128)(2,1)S(1)}, bf16[1,2,128,128]{3,2,1,0:T(8,128)(2,1)S(1)}, u32[]{:S(2)}, u32[]{:S(2)}) collective-permute-start(bf16[1,2,128,128]{3,2,1,0:T(8,128)(2,1)S(1)} %get-tuple-element.46.own_ref.refs_1_), channel_id=1, source_target_pairs={{0,6},{1,7},{2,4},{3,5},{4,2},{5,3},{6,0},{7,1},{8,14},{9,15},{10,... | collective-permute-start | bytes 196616 | tf_op jit(solution)/shard_map/ppermute | solution.py:61
  25.7 2.2 %collective-permute-start.6 = (bf16[1,2,128,128]{3,2,1,0:T(8,128)(2,1)S(1)}, bf16[1,2,128,128]{3,2,1,0:T(8,128)(2,1)S(1)}, u32[]{:S(2)}, u32[]{:S(2)}) collective-permute-start(bf16[1,2,128,128]{3,2,1,0:T(8,128)(2,1)S(1)} %get-tuple-element.46.own_ref.refs_1_), channel_id=1, source_target_pairs={{0,2},{1,3},{2,0},{3,1},{4,6},{5,7},{6,4},{7,5},{8,10},{9,11},{10,... | collective-permute-start | bytes 196616 | tf_op jit(solution)/shard_map/ppermute | solution.py:61
  27.9 1.9 %shard_map.122.refs_0_.matrix_ref = bf16[4,3,128,1024]{3,2,1,0:T(8,128)(2,1)S(1)} custom-call(f32[4,8,128]{2,1,0:T(8,128)S(1)} %get-tuple-element.55.own_ref, f32[4,8,128]{2,1,0:T(8,128)S(1)} %get-tuple-element.56.other_ref, f32[1,64,128]{2,1,0:T(8,128)S(1)} %get-tuple-element.44.refs_0_, f32[1,64,128]{2,1,0:T(8,128)S(1)} %collective-permute-done.5.refs_1_), custom_call_target="tpu_custom_call" | custom-call | tf_op jit(solution)/shard_map/pallas_call | solution.py:706
  29.8 0.2 collective-permute-done.8.refs_2_.refs_4_
  30.0 2.0 %collective-permute-done.7.refs_1_.refs_3_ = bf16[1,2,128,128]{3,2,1,0:T(8,128)(2,1)S(1)} collective-permute-done((bf16[1,2,128,128]{3,2,1,0:T(8,128)(2,1)S(1)}, bf16[1,2,128,128]{3,2,1,0:T(8,128)(2,1)S(1)}, u32[]{:S(2)}, u32[]{:S(2)}) %collective-permute-start.7) | collective-permute-done | bytes 65568 | tf_op jit(solution)/shard_map/ppermute | solution.py:61
  32.1 0.0 copy-start.1
  32.1 0.0 copy-start.2
  32.1 0.0 copy-start
  32.1 0.1 collective-permute-start.18
  32.2 1.6 %collective-permute-start.10 = (f32[1,160,128]{2,1,0:T(8,128)S(1)}, f32[1,160,128]{2,1,0:T(8,128)S(1)}, u32[]{:S(2)}, u32[]{:S(2)}) collective-permute-start(f32[1,160,128]{2,1,0:T(8,128)S(1)} %get-tuple-element.50), channel_id=1, source_target_pairs={{0,1},{1,0},{2,3},{3,2},{4,5},{5,4},{6,7},{7,6},{8,9},{9,8},{10,11... | collective-permute-start | bytes 245768 | tf_op jit(solution)/shard_map/ppermute | solution.py:61
  33.8 1.3 %collective-permute-start.11 = (f32[1,160,128]{2,1,0:T(8,128)S(1)}, f32[1,160,128]{2,1,0:T(8,128)S(1)}, u32[]{:S(2)}, u32[]{:S(2)}) collective-permute-start(f32[1,160,128]{2,1,0:T(8,128)S(1)} %get-tuple-element.51), channel_id=1, source_target_pairs={{0,16},{1,17},{2,18},{3,19},{4,20},{5,21},{6,22},{7,23},{8,24},{9,... | collective-permute-start | bytes 245768 | tf_op jit(solution)/shard_map/ppermute | solution.py:61
  35.1 0.7 collective-permute-start.12
  35.8 1.5 %collective-permute-start.16 = (bf16[2,64,128]{2,1,0:T(8,128)(2,1)S(1)}, bf16[2,64,128]{2,1,0:T(8,128)(2,1)S(1)}, u32[]{:S(2)}, u32[]{:S(2)}) collective-permute-start(bf16[2,64,128]{2,1,0:T(8,128)(2,1)S(1)} %get-tuple-element.53), channel_id=1, source_target_pairs={{0,1},{1,0},{2,3},{3,2},{4,5},{5,4},{6,7},{7,6},{8,9},{9,8},{10,11... | collective-permute-start | bytes 98312 | tf_op jit(solution)/shard_map/ppermute | solution.py:61
  37.3 0.7 collective-permute-start.17
  38.0 0.4 collective-permute-done.11.refs_2_
  38.4 2.3 %collective-permute-done.12.refs_3_ = f32[1,160,128]{2,1,0:T(8,128)S(1)} collective-permute-done((f32[1,160,128]{2,1,0:T(8,128)S(1)}, f32[1,160,128]{2,1,0:T(8,128)S(1)}, u32[]{:S(2)}, u32[]{:S(2)}) %collective-permute-start.12) | collective-permute-done | bytes 81952 | tf_op jit(solution)/shard_map/ppermute | solution.py:61
  40.7 2.3 %collective-permute-start.15 = (f32[1,160,128]{2,1,0:T(8,128)S(1)}, f32[1,160,128]{2,1,0:T(8,128)S(1)}, u32[]{:S(2)}, u32[]{:S(2)}) collective-permute-start(f32[1,160,128]{2,1,0:T(8,128)S(1)} %shard_map.119.refs_0_), channel_id=1, source_target_pairs={{0,6},{1,7},{2,4},{3,5},{4,2},{5,3},{6,0},{7,1},{8,14},{9,15},{10,... | collective-permute-start | bytes 245768 | tf_op jit(solution)/shard_map/ppermute | solution.py:61
  42.9 1.7 %shard_map.124 = (f32[1,2,128,128]{3,2,1,0:T(8,128)S(1)}, f32[1,2,128,128]{3,2,1,0:T(8,128)S(1)}, f32[1,2,128,128]{3,2,1,0:T(8,128)S(1)}, f32[1,2,128,128]{3,2,1,0:T(8,128)S(1)}) custom-call(bf16[2,64,128]{2,1,0:T(8,128)(2,1)S(1)} %collective-permute-done.16.pair_ref.pair_hbm, bf16[2,64,128]{2,1,0:T(8,128)(2,1)S(1)} %collective-permute-done.17.next_ref.next_hbm, ...), custom_call_target="tpu_custom_call" | custom-call | tf_op jit(solution)/shard_map/pallas_call | solution.py:724
  44.7 2.7 %collective-permute-start.19 = (f32[1,2,128,128]{3,2,1,0:T(8,128)S(1)}, f32[1,2,128,128]{3,2,1,0:T(8,128)S(1)}, u32[]{:S(2)}, u32[]{:S(2)}) collective-permute-start(f32[1,2,128,128]{3,2,1,0:T(8,128)S(1)} %get-tuple-element.58), channel_id=1, source_target_pairs={{0,1},{1,0},{2,3},{3,2},{4,5},{5,4},{6,7},{7,6},{8,9},{9,8},{10,11... | collective-permute-start | bytes 393224 | tf_op jit(solution)/shard_map/ppermute | solution.py:61
  47.4 2.0 %collective-permute-start.20 = (f32[1,2,128,128]{3,2,1,0:T(8,128)S(1)}, f32[1,2,128,128]{3,2,1,0:T(8,128)S(1)}, u32[]{:S(2)}, u32[]{:S(2)}) collective-permute-start(f32[1,2,128,128]{3,2,1,0:T(8,128)S(1)} %get-tuple-element.59), channel_id=1, source_target_pairs={{0,16},{1,17},{2,18},{3,19},{4,20},{5,21},{6,22},{7,23},{8,24},{9,... | collective-permute-start | bytes 393224 | tf_op jit(solution)/shard_map/ppermute | solution.py:61
  49.4 1.4 %collective-permute-start.21 = (f32[1,2,128,128]{3,2,1,0:T(8,128)S(1)}, f32[1,2,128,128]{3,2,1,0:T(8,128)S(1)}, u32[]{:S(2)}, u32[]{:S(2)}) collective-permute-start(f32[1,2,128,128]{3,2,1,0:T(8,128)S(1)} %get-tuple-element.60), channel_id=1, source_target_pairs={{0,17},{1,16},{2,19},{3,18},{4,21},{5,20},{6,23},{7,22},{8,25},{9,... | collective-permute-start | bytes 393224 | tf_op jit(solution)/shard_map/ppermute | solution.py:61
  50.8 2.6 %collective-permute-start.13 = (f32[1,160,128]{2,1,0:T(8,128)S(1)}, f32[1,160,128]{2,1,0:T(8,128)S(1)}, u32[]{:S(2)}, u32[]{:S(2)}) collective-permute-start(f32[1,160,128]{2,1,0:T(8,128)S(1)} %shard_map.119.refs_0_), channel_id=1, source_target_pairs={{0,2},{1,3},{2,0},{3,1},{4,6},{5,7},{6,4},{7,5},{8,10},{9,11},{10,... | collective-permute-start | bytes 245768 | tf_op jit(solution)/shard_map/ppermute | solution.py:61
  53.4 1.0 %shard_map.121.base_ref = f32[2,128,128]{2,1,0:T(8,128)S(1)} custom-call(s32[3]{0:T(128)S(1)} %pad_add_fusion.index_ref, s32[8,12]{1,0:T(8,128)S(1)} %copy-done.1, s32[8]{0:T(128)S(1)} %copy-done.2, bf16[8,32,384]{2,1,0:T(8,128)(2,1)S(1)} %reshape.15.near_ref.block_ref, bf16[1,2,128,128]{3,2,1,0:T(8,128)(2,1)S(1)} %get-tuple-element.46.own_ref.refs_1_, ...), custom_call_target="tpu_custom_call" | custom-call | tf_op jit(solution)/shard_map/pallas_call | solution.py:590
  54.4 2.2 %collective-permute-done.14.refs_2_ = f32[1,160,128]{2,1,0:T(8,128)S(1)} collective-permute-done((f32[1,160,128]{2,1,0:T(8,128)S(1)}, f32[1,160,128]{2,1,0:T(8,128)S(1)}, u32[]{:S(2)}, u32[]{:S(2)}) %collective-permute-start.14) | collective-permute-done | bytes 81952 | tf_op jit(solution)/shard_map/ppermute | solution.py:61
  56.6 0.1 collective-permute-done.13.refs_1_
  56.8 1.0 %shard_map.125 = (f32[2,128,128]{2,1,0:T(8,128)S(1)}, f32[4,80,128]{2,1,0:T(8,128)S(1)}, f32[4,80,128]{2,1,0:T(8,128)S(1)}) custom-call(s32[3]{0:T(128)S(1)} %pad_add_fusion.index_ref, f32[1,160,128]{2,1,0:T(8,128)S(1)} %shard_map.120.half_hbm.right_ref, f32[128,128]{1,0:T(8,128)S(1)} %get-tuple-element.40.refs_0_.weight_ref, ...), custom_call_target="tpu_custom_call" | custom-call | tf_op jit(solution)/shard_map/pallas_call | solution.py:748
  57.9 0.1 collective-permute-start.22
  58.0 1.4 %collective-permute-done.22.refs_1_ = f32[4,80,128]{2,1,0:T(8,128)S(1)} collective-permute-done((f32[4,80,128]{2,1,0:T(8,128)S(1)}, f32[4,80,128]{2,1,0:T(8,128)S(1)}, u32[]{:S(2)}, u32[]{:S(2)}) %collective-permute-start.22) | collective-permute-done | bytes 163872 | tf_op jit(solution)/shard_map/ppermute | solution.py:61
  59.4 1.7 %collective-permute-start.23 = (f32[1,80,128]{2,1,0:T(8,128)S(1)}, f32[1,80,128]{2,1,0:T(8,128)S(1)}, u32[]{:S(2)}, u32[]{:S(2)}) collective-permute-start(f32[1,80,128]{2,1,0:T(8,128)S(1)} %get-tuple-element.65), channel_id=1, source_target_pairs={{0,1},{1,0},{2,3},{3,2},{4,5},{5,4},{6,7},{7,6},{8,9},{9,8},{10,11... | collective-permute-start | bytes 122888 | tf_op jit(solution)/shard_map/ppermute | solution.py:61
  61.1 1.0 %collective-permute-start.24 = (f32[1,80,128]{2,1,0:T(8,128)S(1)}, f32[1,80,128]{2,1,0:T(8,128)S(1)}, u32[]{:S(2)}, u32[]{:S(2)}) collective-permute-start(f32[1,80,128]{2,1,0:T(8,128)S(1)} %get-tuple-element.66), channel_id=1, source_target_pairs={{0,16},{1,17},{2,18},{3,19},{4,20},{5,21},{6,22},{7,23},{8,24},{9,... | collective-permute-start | bytes 122888 | tf_op jit(solution)/shard_map/ppermute | solution.py:61
  62.1 0.8 collective-permute-start.25
  62.9 0.5 collective-permute-done.23.refs_1_
  63.5 1.7 %collective-permute-done.24.refs_2_ = f32[1,80,128]{2,1,0:T(8,128)S(1)} collective-permute-done((f32[1,80,128]{2,1,0:T(8,128)S(1)}, f32[1,80,128]{2,1,0:T(8,128)S(1)}, u32[]{:S(2)}, u32[]{:S(2)}) %collective-permute-start.24) | collective-permute-done | bytes 40992 | tf_op jit(solution)/shard_map/ppermute | solution.py:61
  65.1 1.9 %collective-permute-done.25.refs_3_ = f32[1,80,128]{2,1,0:T(8,128)S(1)} collective-permute-done((f32[1,80,128]{2,1,0:T(8,128)S(1)}, f32[1,80,128]{2,1,0:T(8,128)S(1)}, u32[]{:S(2)}, u32[]{:S(2)}) %collective-permute-start.25) | collective-permute-done | bytes 40992 | tf_op jit(solution)/shard_map/ppermute | solution.py:61
  67.0 2.4 %collective-permute-start.28 = (f32[1,80,128]{2,1,0:T(8,128)S(1)}, f32[1,80,128]{2,1,0:T(8,128)S(1)}, u32[]{:S(2)}, u32[]{:S(2)}) collective-permute-start(f32[1,80,128]{2,1,0:T(8,128)S(1)} %shard_map.127.refs_0_), channel_id=1, source_target_pairs={{0,6},{1,7},{2,4},{3,5},{4,2},{5,3},{6,0},{7,1},{8,14},{9,15},{10,... | collective-permute-start | bytes 122888 | tf_op jit(solution)/shard_map/ppermute | solution.py:61
  69.5 0.6 collective-permute-start.27
  70.0 1.5 %collective-permute-start.26 = (f32[1,80,128]{2,1,0:T(8,128)S(1)}, f32[1,80,128]{2,1,0:T(8,128)S(1)}, u32[]{:S(2)}, u32[]{:S(2)}) collective-permute-start(f32[1,80,128]{2,1,0:T(8,128)S(1)} %shard_map.127.refs_0_), channel_id=1, source_target_pairs={{0,2},{1,3},{2,0},{3,1},{4,6},{5,7},{6,4},{7,5},{8,10},{9,11},{10,... | collective-permute-start | bytes 122888 | tf_op jit(solution)/shard_map/ppermute | solution.py:61
  71.5 1.7 %collective-permute-done.28.refs_3_ = f32[1,80,128]{2,1,0:T(8,128)S(1)} collective-permute-done((f32[1,80,128]{2,1,0:T(8,128)S(1)}, f32[1,80,128]{2,1,0:T(8,128)S(1)}, u32[]{:S(2)}, u32[]{:S(2)}) %collective-permute-start.28) | collective-permute-done | bytes 40992 | tf_op jit(solution)/shard_map/ppermute | solution.py:61
  73.2 1.3 %collective-permute-done.27.refs_2_ = f32[1,80,128]{2,1,0:T(8,128)S(1)} collective-permute-done((f32[1,80,128]{2,1,0:T(8,128)S(1)}, f32[1,80,128]{2,1,0:T(8,128)S(1)}, u32[]{:S(2)}, u32[]{:S(2)}) %collective-permute-start.27) | collective-permute-done | bytes 40992 | tf_op jit(solution)/shard_map/ppermute | solution.py:61
  74.5 1.5 %collective-permute-start.31 = (f32[1,240,128]{2,1,0:T(8,128)S(1)}, f32[1,240,128]{2,1,0:T(8,128)S(1)}, u32[]{:S(2)}, u32[]{:S(2)}) collective-permute-start(f32[1,240,128]{2,1,0:T(8,128)S(1)} %shard_map.129.refs_0_), channel_id=1, source_target_pairs={{0,17},{1,16},{2,19},{3,18},{4,21},{5,20},{6,23},{7,22},{8,25},{9,... | collective-permute-start | bytes 368648 | tf_op jit(solution)/shard_map/ppermute | solution.py:61
  76.0 0.7 collective-permute-start.30
  76.8 1.3 %collective-permute-start.29 = (f32[1,240,128]{2,1,0:T(8,128)S(1)}, f32[1,240,128]{2,1,0:T(8,128)S(1)}, u32[]{:S(2)}, u32[]{:S(2)}) collective-permute-start(f32[1,240,128]{2,1,0:T(8,128)S(1)} %shard_map.129.refs_0_), channel_id=1, source_target_pairs={{0,1},{1,0},{2,3},{3,2},{4,5},{5,4},{6,7},{7,6},{8,9},{9,8},{10,11... | collective-permute-start | bytes 368648 | tf_op jit(solution)/shard_map/ppermute | solution.py:61
  78.1 2.4 %collective-permute-done.31.refs_3_ = f32[1,240,128]{2,1,0:T(8,128)S(1)} collective-permute-done((f32[1,240,128]{2,1,0:T(8,128)S(1)}, f32[1,240,128]{2,1,0:T(8,128)S(1)}, u32[]{:S(2)}, u32[]{:S(2)}) %collective-permute-start.31) | collective-permute-done | bytes 122912 | tf_op jit(solution)/shard_map/ppermute | solution.py:61
  80.5 1.2 %collective-permute-done.30.refs_2_ = f32[1,240,128]{2,1,0:T(8,128)S(1)} collective-permute-done((f32[1,240,128]{2,1,0:T(8,128)S(1)}, f32[1,240,128]{2,1,0:T(8,128)S(1)}, u32[]{:S(2)}, u32[]{:S(2)}) %collective-permute-start.30) | collective-permute-done | bytes 122912 | tf_op jit(solution)/shard_map/ppermute | solution.py:61
  81.7 0.1 collective-permute-start.32
  81.8 1.9 %collective-permute-done.32.refs_1_ = f32[4,240,128]{2,1,0:T(8,128)S(1)} collective-permute-done((f32[4,240,128]{2,1,0:T(8,128)S(1)}, f32[4,240,128]{2,1,0:T(8,128)S(1)}, u32[]{:S(2)}, u32[]{:S(2)}) %collective-permute-start.32) | collective-permute-done | bytes 491552 | tf_op jit(solution)/shard_map/ppermute | solution.py:61
  83.7 6.7 %shard_map.131 = (f32[512,128]{1,0:T(8,128)}, f32[128,128]{1,0:T(8,128)}, f32[256,128]{1,0:T(8,128)}) custom-call(s32[3]{0:T(128)S(1)} %pad_add_fusion.index_ref, f32[4,2,128,128]{3,2,1,0:T(8,128)S(1)} %copy-done, f32[2,128,128]{2,1,0:T(8,128)S(1)} %get-tuple-element.61.image_ref, f32[4,240,128]{2,1,0:T(8,128)S(1)} %shard_map.130.refs_0_, ...), custom_call_target="tpu_custom_call" | custom-call | tf_op jit(solution)/shard_map/pallas_call | solution.py:590
  (31 shorter events, 0.3 us)
Async XLA Ops:
  1.8 8.3 %collective-permute-start.2 = (f32[1,56,128]{2,1,0:T(8,128)S(1)}, f32[1,56,128]{2,1,0:T(8,128)S(1)}, u32[]{:S(2)}, u32[]{:S(2)}) collective-permute-start(f32[1,56,128]{2,1,0:T(8,128)S(1)} %shard_map.112.pack_hbm.refs_1_), channel_id=1, source_target_pairs={{0,6},{1,7},{2,4},{3,5},{4,2},{5,3},{6,0},{7,1},{8,14},{9,15},{10,... | collective-permute-start | bytes 86024 | tf_op jit(solution)/shard_map/ppermute | solution.py:61
  6.9 4.8 %collective-permute-start.1 = (f32[1,56,128]{2,1,0:T(8,128)S(1)}, f32[1,56,128]{2,1,0:T(8,128)S(1)}, u32[]{:S(2)}, u32[]{:S(2)}) collective-permute-start(f32[1,56,128]{2,1,0:T(8,128)S(1)} %shard_map.112.pack_hbm.refs_1_), channel_id=1, source_target_pairs={{0,4},{1,5},{2,6},{3,7},{4,0},{5,1},{6,2},{7,3},{8,12},{9,13},{10,... | collective-permute-start | bytes 86024 | tf_op jit(solution)/shard_map/ppermute | solution.py:61
  6.9 4.8 %collective-permute-start = (f32[1,56,128]{2,1,0:T(8,128)S(1)}, f32[1,56,128]{2,1,0:T(8,128)S(1)}, u32[]{:S(2)}, u32[]{:S(2)}) collective-permute-start(f32[1,56,128]{2,1,0:T(8,128)S(1)} %shard_map.112.pack_hbm.refs_1_), channel_id=1, source_target_pairs={{0,2},{1,3},{2,0},{3,1},{4,6},{5,7},{6,4},{7,5},{8,10},{9,11},{10,... | collective-permute-start | bytes 86024 | tf_op jit(solution)/shard_map/ppermute | solution.py:61
  11.7 4.9 %collective-permute-start.3 = (f32[4,56,128]{2,1,0:T(8,128)S(1)}, f32[4,56,128]{2,1,0:T(8,128)S(1)}, u32[]{:S(2)}, u32[]{:S(2)}) collective-permute-start(f32[4,56,128]{2,1,0:T(8,128)S(1)} %shard_map.114.refs_0_), channel_id=1, source_target_pairs={{0,1},{1,0},{2,3},{3,2},{4,5},{5,4},{6,7},{7,6},{8,9},{9,8},{10,11... | collective-permute-start | bytes 344072 | tf_op jit(solution)/shard_map/ppermute | solution.py:61
  13.2 18.9 %collective-permute-start.9 = (f32[4,160,128]{2,1,0:T(8,128)S(1)}, f32[4,160,128]{2,1,0:T(8,128)S(1)}, u32[]{:S(2)}, u32[]{:S(2)}) collective-permute-start(f32[4,160,128]{2,1,0:T(8,128)S(1)} %get-tuple-element.48), channel_id=1, source_target_pairs={{0,8},{1,9},{2,10},{3,11},{4,12},{5,13},{6,14},{7,15},{8,0},{9,1},... | collective-permute-start | bytes 983048 | tf_op jit(solution)/shard_map/ppermute | solution.py:61
  17.4 1.3 %collective-permute-start.4 = (f32[2,64,128]{2,1,0:T(8,128)S(1)}, f32[2,64,128]{2,1,0:T(8,128)S(1)}, u32[]{:S(2)}, u32[]{:S(2)}) collective-permute-start(f32[2,64,128]{2,1,0:T(8,128)S(1)} %get-tuple-element.42), channel_id=1, source_target_pairs={{0,8},{1,9},{2,10},{3,11},{4,12},{5,13},{6,14},{7,15},{8,0},{9,1},... | collective-permute-start | bytes 196616 | tf_op jit(solution)/shard_map/ppermute | solution.py:61
  18.7 4.0 %collective-permute-start.5 = (f32[1,64,128]{2,1,0:T(8,128)S(1)}, f32[1,64,128]{2,1,0:T(8,128)S(1)}, u32[]{:S(2)}, u32[]{:S(2)}) collective-permute-start(f32[1,64,128]{2,1,0:T(8,128)S(1)} %get-tuple-element.45), channel_id=1, source_target_pairs={{0,16},{1,17},{2,18},{3,19},{4,20},{5,21},{6,22},{7,23},{8,24},{9,... | collective-permute-start | bytes 98312 | tf_op jit(solution)/shard_map/ppermute | solution.py:61
  23.5 6.5 %collective-permute-start.8 = (bf16[1,2,128,128]{3,2,1,0:T(8,128)(2,1)S(1)}, bf16[1,2,128,128]{3,2,1,0:T(8,128)(2,1)S(1)}, u32[]{:S(2)}, u32[]{:S(2)}) collective-permute-start(bf16[1,2,128,128]{3,2,1,0:T(8,128)(2,1)S(1)} %get-tuple-element.46.own_ref.refs_1_), channel_id=1, source_target_pairs={{0,6},{1,7},{2,4},{3,5},{4,2},{5,3},{6,0},{7,1},{8,14},{9,15},{10,... | collective-permute-start | bytes 196616 | tf_op jit(solution)/shard_map/ppermute | solution.py:61
  25.7 6.3 %collective-permute-start.7 = (bf16[1,2,128,128]{3,2,1,0:T(8,128)(2,1)S(1)}, bf16[1,2,128,128]{3,2,1,0:T(8,128)(2,1)S(1)}, u32[]{:S(2)}, u32[]{:S(2)}) collective-permute-start(bf16[1,2,128,128]{3,2,1,0:T(8,128)(2,1)S(1)} %get-tuple-element.46.own_ref.refs_1_), channel_id=1, source_target_pairs={{0,4},{1,5},{2,6},{3,7},{4,0},{5,1},{6,2},{7,3},{8,12},{9,13},{10,... | collective-permute-start | bytes 196616 | tf_op jit(solution)/shard_map/ppermute | solution.py:61
  25.7 6.3 %collective-permute-start.6 = (bf16[1,2,128,128]{3,2,1,0:T(8,128)(2,1)S(1)}, bf16[1,2,128,128]{3,2,1,0:T(8,128)(2,1)S(1)}, u32[]{:S(2)}, u32[]{:S(2)}) collective-permute-start(bf16[1,2,128,128]{3,2,1,0:T(8,128)(2,1)S(1)} %get-tuple-element.46.own_ref.refs_1_), channel_id=1, source_target_pairs={{0,2},{1,3},{2,0},{3,1},{4,6},{5,7},{6,4},{7,5},{8,10},{9,11},{10,... | collective-permute-start | bytes 196616 | tf_op jit(solution)/shard_map/ppermute | solution.py:61
  32.1 21.4 %copy-start.1 = (s32[8,12]{1,0:T(8,128)S(1)}, s32[8,12]{1,0:T(8,128)}, u32[]{:S(2)}) copy-start(s32[8,12]{1,0:T(8,128)} %panel_ref.1) | copy-start | bytes 1156
  32.1 21.3 %copy-start.2 = (s32[8]{0:T(128)S(1)}, s32[8]{0:T(128)}, u32[]{:S(2)}) copy-start(s32[8]{0:T(128)} %count_ref.1) | copy-start | bytes 100
  32.1 24.7 %copy-start = (f32[4,2,128,128]{3,2,1,0:T(8,128)S(1)}, f32[4,2,128,128]{3,2,1,0:T(8,128)}, u32[]{:S(2)}) copy-start(f32[4,2,128,128]{3,2,1,0:T(8,128)} %basis_ref.3) | copy-start | bytes 1572868
  32.1 10.8 %collective-permute-start.18 = (bf16[4,2,128,128]{3,2,1,0:T(8,128)(2,1)S(1)}, bf16[4,2,128,128]{3,2,1,0:T(8,128)(2,1)S(1)}, u32[]{:S(2)}, u32[]{:S(2)}) collective-permute-start(bf16[4,2,128,128]{3,2,1,0:T(8,128)(2,1)S(1)} %shard_map.123.refs_0_), channel_id=1, source_target_pairs={{0,8},{1,9},{2,10},{3,11},{4,12},{5,13},{6,14},{7,15},{8,0},{9,1},... | collective-permute-start | bytes 786440 | tf_op jit(solution)/shard_map/ppermute | solution.py:61
  32.2 5.0 %collective-permute-start.10 = (f32[1,160,128]{2,1,0:T(8,128)S(1)}, f32[1,160,128]{2,1,0:T(8,128)S(1)}, u32[]{:S(2)}, u32[]{:S(2)}) collective-permute-start(f32[1,160,128]{2,1,0:T(8,128)S(1)} %get-tuple-element.50), channel_id=1, source_target_pairs={{0,1},{1,0},{2,3},{3,2},{4,5},{5,4},{6,7},{7,6},{8,9},{9,8},{10,11... | collective-permute-start | bytes 245768 | tf_op jit(solution)/shard_map/ppermute | solution.py:61
  33.8 4.6 %collective-permute-start.11 = (f32[1,160,128]{2,1,0:T(8,128)S(1)}, f32[1,160,128]{2,1,0:T(8,128)S(1)}, u32[]{:S(2)}, u32[]{:S(2)}) collective-permute-start(f32[1,160,128]{2,1,0:T(8,128)S(1)} %get-tuple-element.51), channel_id=1, source_target_pairs={{0,16},{1,17},{2,18},{3,19},{4,20},{5,21},{6,22},{7,23},{8,24},{9,... | collective-permute-start | bytes 245768 | tf_op jit(solution)/shard_map/ppermute | solution.py:61
  35.1 5.5 %collective-permute-start.12 = (f32[1,160,128]{2,1,0:T(8,128)S(1)}, f32[1,160,128]{2,1,0:T(8,128)S(1)}, u32[]{:S(2)}, u32[]{:S(2)}) collective-permute-start(f32[1,160,128]{2,1,0:T(8,128)S(1)} %get-tuple-element.52), channel_id=1, source_target_pairs={{0,17},{1,16},{2,19},{3,18},{4,21},{5,20},{6,23},{7,22},{8,25},{9,... | collective-permute-start | bytes 245768 | tf_op jit(solution)/shard_map/ppermute | solution.py:61
  35.8 7.1 %collective-permute-start.16 = (bf16[2,64,128]{2,1,0:T(8,128)(2,1)S(1)}, bf16[2,64,128]{2,1,0:T(8,128)(2,1)S(1)}, u32[]{:S(2)}, u32[]{:S(2)}) collective-permute-start(bf16[2,64,128]{2,1,0:T(8,128)(2,1)S(1)} %get-tuple-element.53), channel_id=1, source_target_pairs={{0,1},{1,0},{2,3},{3,2},{4,5},{5,4},{6,7},{7,6},{8,9},{9,8},{10,11... | collective-permute-start | bytes 98312 | tf_op jit(solution)/shard_map/ppermute | solution.py:61
  37.3 5.7 %collective-permute-start.17 = (bf16[2,64,128]{2,1,0:T(8,128)(2,1)S(1)}, bf16[2,64,128]{2,1,0:T(8,128)(2,1)S(1)}, u32[]{:S(2)}, u32[]{:S(2)}) collective-permute-start(bf16[2,64,128]{2,1,0:T(8,128)(2,1)S(1)} %get-tuple-element.54), channel_id=1, source_target_pairs={{1,2},{3,4},{5,6},{7,8},{9,10},{11,12},{13,14},{15,16},{17,18},{19... | collective-permute-start | bytes 98312 | tf_op jit(solution)/shard_map/ppermute | solution.py:721
  40.7 10.1 %collective-permute-start.15 = (f32[1,160,128]{2,1,0:T(8,128)S(1)}, f32[1,160,128]{2,1,0:T(8,128)S(1)}, u32[]{:S(2)}, u32[]{:S(2)}) collective-permute-start(f32[1,160,128]{2,1,0:T(8,128)S(1)} %shard_map.119.refs_0_), channel_id=1, source_target_pairs={{0,6},{1,7},{2,4},{3,5},{4,2},{5,3},{6,0},{7,1},{8,14},{9,15},{10,... | collective-permute-start | bytes 245768 | tf_op jit(solution)/shard_map/ppermute | solution.py:61
  44.7 12.2 %collective-permute-start.19 = (f32[1,2,128,128]{3,2,1,0:T(8,128)S(1)}, f32[1,2,128,128]{3,2,1,0:T(8,128)S(1)}, u32[]{:S(2)}, u32[]{:S(2)}) collective-permute-start(f32[1,2,128,128]{3,2,1,0:T(8,128)S(1)} %get-tuple-element.58), channel_id=1, source_target_pairs={{0,1},{1,0},{2,3},{3,2},{4,5},{5,4},{6,7},{7,6},{8,9},{9,8},{10,11... | collective-permute-start | bytes 393224 | tf_op jit(solution)/shard_map/ppermute | solution.py:61
  47.4 9.4 %collective-permute-start.20 = (f32[1,2,128,128]{3,2,1,0:T(8,128)S(1)}, f32[1,2,128,128]{3,2,1,0:T(8,128)S(1)}, u32[]{:S(2)}, u32[]{:S(2)}) collective-permute-start(f32[1,2,128,128]{3,2,1,0:T(8,128)S(1)} %get-tuple-element.59), channel_id=1, source_target_pairs={{0,16},{1,17},{2,18},{3,19},{4,20},{5,21},{6,22},{7,23},{8,24},{9,... | collective-permute-start | bytes 393224 | tf_op jit(solution)/shard_map/ppermute | solution.py:61
  49.4 7.4 %collective-permute-start.21 = (f32[1,2,128,128]{3,2,1,0:T(8,128)S(1)}, f32[1,2,128,128]{3,2,1,0:T(8,128)S(1)}, u32[]{:S(2)}, u32[]{:S(2)}) collective-permute-start(f32[1,2,128,128]{3,2,1,0:T(8,128)S(1)} %get-tuple-element.60), channel_id=1, source_target_pairs={{0,17},{1,16},{2,19},{3,18},{4,21},{5,20},{6,23},{7,22},{8,25},{9,... | collective-permute-start | bytes 393224 | tf_op jit(solution)/shard_map/ppermute | solution.py:61
  50.8 5.9 %collective-permute-start.14 = (f32[1,160,128]{2,1,0:T(8,128)S(1)}, f32[1,160,128]{2,1,0:T(8,128)S(1)}, u32[]{:S(2)}, u32[]{:S(2)}) collective-permute-start(f32[1,160,128]{2,1,0:T(8,128)S(1)} %shard_map.119.refs_0_), channel_id=1, source_target_pairs={{0,4},{1,5},{2,6},{3,7},{4,0},{5,1},{6,2},{7,3},{8,12},{9,13},{10,... | collective-permute-start | bytes 245768 | tf_op jit(solution)/shard_map/ppermute | solution.py:61
  50.8 6.0 %collective-permute-start.13 = (f32[1,160,128]{2,1,0:T(8,128)S(1)}, f32[1,160,128]{2,1,0:T(8,128)S(1)}, u32[]{:S(2)}, u32[]{:S(2)}) collective-permute-start(f32[1,160,128]{2,1,0:T(8,128)S(1)} %shard_map.119.refs_0_), channel_id=1, source_target_pairs={{0,2},{1,3},{2,0},{3,1},{4,6},{5,7},{6,4},{7,5},{8,10},{9,11},{10,... | collective-permute-start | bytes 245768 | tf_op jit(solution)/shard_map/ppermute | solution.py:61
  57.9 1.5 %collective-permute-start.22 = (f32[4,80,128]{2,1,0:T(8,128)S(1)}, f32[4,80,128]{2,1,0:T(8,128)S(1)}, u32[]{:S(2)}, u32[]{:S(2)}) collective-permute-start(f32[4,80,128]{2,1,0:T(8,128)S(1)} %get-tuple-element.63), channel_id=1, source_target_pairs={{0,8},{1,9},{2,10},{3,11},{4,12},{5,13},{6,14},{7,15},{8,0},{9,1},... | collective-permute-start | bytes 491528 | tf_op jit(solution)/shard_map/ppermute | solution.py:61
  59.4 4.1 %collective-permute-start.23 = (f32[1,80,128]{2,1,0:T(8,128)S(1)}, f32[1,80,128]{2,1,0:T(8,128)S(1)}, u32[]{:S(2)}, u32[]{:S(2)}) collective-permute-start(f32[1,80,128]{2,1,0:T(8,128)S(1)} %get-tuple-element.65), channel_id=1, source_target_pairs={{0,1},{1,0},{2,3},{3,2},{4,5},{5,4},{6,7},{7,6},{8,9},{9,8},{10,11... | collective-permute-start | bytes 122888 | tf_op jit(solution)/shard_map/ppermute | solution.py:61
  61.1 4.0 %collective-permute-start.24 = (f32[1,80,128]{2,1,0:T(8,128)S(1)}, f32[1,80,128]{2,1,0:T(8,128)S(1)}, u32[]{:S(2)}, u32[]{:S(2)}) collective-permute-start(f32[1,80,128]{2,1,0:T(8,128)S(1)} %get-tuple-element.66), channel_id=1, source_target_pairs={{0,16},{1,17},{2,18},{3,19},{4,20},{5,21},{6,22},{7,23},{8,24},{9,... | collective-permute-start | bytes 122888 | tf_op jit(solution)/shard_map/ppermute | solution.py:61
  62.1 4.9 %collective-permute-start.25 = (f32[1,80,128]{2,1,0:T(8,128)S(1)}, f32[1,80,128]{2,1,0:T(8,128)S(1)}, u32[]{:S(2)}, u32[]{:S(2)}) collective-permute-start(f32[1,80,128]{2,1,0:T(8,128)S(1)} %get-tuple-element.67), channel_id=1, source_target_pairs={{0,17},{1,16},{2,19},{3,18},{4,21},{5,20},{6,23},{7,22},{8,25},{9,... | collective-permute-start | bytes 122888 | tf_op jit(solution)/shard_map/ppermute | solution.py:61
  67.0 6.1 %collective-permute-start.28 = (f32[1,80,128]{2,1,0:T(8,128)S(1)}, f32[1,80,128]{2,1,0:T(8,128)S(1)}, u32[]{:S(2)}, u32[]{:S(2)}) collective-permute-start(f32[1,80,128]{2,1,0:T(8,128)S(1)} %shard_map.127.refs_0_), channel_id=1, source_target_pairs={{0,6},{1,7},{2,4},{3,5},{4,2},{5,3},{6,0},{7,1},{8,14},{9,15},{10,... | collective-permute-start | bytes 122888 | tf_op jit(solution)/shard_map/ppermute | solution.py:61
  69.5 5.0 %collective-permute-start.27 = (f32[1,80,128]{2,1,0:T(8,128)S(1)}, f32[1,80,128]{2,1,0:T(8,128)S(1)}, u32[]{:S(2)}, u32[]{:S(2)}) collective-permute-start(f32[1,80,128]{2,1,0:T(8,128)S(1)} %shard_map.127.refs_0_), channel_id=1, source_target_pairs={{0,4},{1,5},{2,6},{3,7},{4,0},{5,1},{6,2},{7,3},{8,12},{9,13},{10,... | collective-permute-start | bytes 122888 | tf_op jit(solution)/shard_map/ppermute | solution.py:61
  70.0 4.4 %collective-permute-start.26 = (f32[1,80,128]{2,1,0:T(8,128)S(1)}, f32[1,80,128]{2,1,0:T(8,128)S(1)}, u32[]{:S(2)}, u32[]{:S(2)}) collective-permute-start(f32[1,80,128]{2,1,0:T(8,128)S(1)} %shard_map.127.refs_0_), channel_id=1, source_target_pairs={{0,2},{1,3},{2,0},{3,1},{4,6},{5,7},{6,4},{7,5},{8,10},{9,11},{10,... | collective-permute-start | bytes 122888 | tf_op jit(solution)/shard_map/ppermute | solution.py:61
  74.5 5.9 %collective-permute-start.31 = (f32[1,240,128]{2,1,0:T(8,128)S(1)}, f32[1,240,128]{2,1,0:T(8,128)S(1)}, u32[]{:S(2)}, u32[]{:S(2)}) collective-permute-start(f32[1,240,128]{2,1,0:T(8,128)S(1)} %shard_map.129.refs_0_), channel_id=1, source_target_pairs={{0,17},{1,16},{2,19},{3,18},{4,21},{5,20},{6,23},{7,22},{8,25},{9,... | collective-permute-start | bytes 368648 | tf_op jit(solution)/shard_map/ppermute | solution.py:61
  76.0 5.6 %collective-permute-start.30 = (f32[1,240,128]{2,1,0:T(8,128)S(1)}, f32[1,240,128]{2,1,0:T(8,128)S(1)}, u32[]{:S(2)}, u32[]{:S(2)}) collective-permute-start(f32[1,240,128]{2,1,0:T(8,128)S(1)} %shard_map.129.refs_0_), channel_id=1, source_target_pairs={{0,16},{1,17},{2,18},{3,19},{4,20},{5,21},{6,22},{7,23},{8,24},{9,... | collective-permute-start | bytes 368648 | tf_op jit(solution)/shard_map/ppermute | solution.py:61
  76.8 4.9 %collective-permute-start.29 = (f32[1,240,128]{2,1,0:T(8,128)S(1)}, f32[1,240,128]{2,1,0:T(8,128)S(1)}, u32[]{:S(2)}, u32[]{:S(2)}) collective-permute-start(f32[1,240,128]{2,1,0:T(8,128)S(1)} %shard_map.129.refs_0_), channel_id=1, source_target_pairs={{0,1},{1,0},{2,3},{3,2},{4,5},{5,4},{6,7},{7,6},{8,9},{9,8},{10,11... | collective-permute-start | bytes 368648 | tf_op jit(solution)/shard_map/ppermute | solution.py:61
  81.7 1.9 %collective-permute-start.32 = (f32[4,240,128]{2,1,0:T(8,128)S(1)}, f32[4,240,128]{2,1,0:T(8,128)S(1)}, u32[]{:S(2)}, u32[]{:S(2)}) collective-permute-start(f32[4,240,128]{2,1,0:T(8,128)S(1)} %shard_map.130.refs_0_), channel_id=1, source_target_pairs={{0,8},{1,9},{2,10},{3,11},{4,12},{5,13},{6,14},{7,15},{8,0},{9,1},... | collective-permute-start | bytes 1474568 | tf_op jit(solution)/shard_map/ppermute | solution.py:61

commit v9 on v8

--- a/solution.py
+++ b/solution.py
@@ -279,7 +279,7 @@
     return parts[k // size], k % size
 
 
-def coarse_kernel(order, ways, z_count, index_ref, inverse_ref, *refs):
+def coarse_kernel(order, ways, z_count, index_ref, near_ref, inverse_ref, *refs):
     narrow_count, coarse_count, _ = inverse_ref.shape
     packs = refs[: len(refs) - ways - 3]
     outs = refs[len(packs) : len(packs) + ways]
@@ -327,7 +327,7 @@
                 outs[j][k, first : first + EXTRA, :] = target_ref[t]
 
 
-def precond_kernel(index_ref, member_ref, smooth_ref, near_ref, *refs):
+def precond_kernel(index_ref, member_ref, smooth_ref, *refs):
     parts = refs[:-3]
     precond_ref, pair_ref, next_ref = refs[-3:]
     coarse_count = member_ref.shape[1]
@@ -372,7 +372,8 @@
         matrix_ref[0, 2, :, lanes] = (factor * (log_part + square_y * inverse)).astype(jnp.bfloat16)
 
 
-def far_kernel(ways, pair_hbm, next_hbm, matrix_ref, *refs):
+def far_kernel(ways, skip, *refs):
+    matrix_ref, *refs = refs[skip:]
     fields = refs[: len(refs) - ways - 1]
     outs = refs[len(fields) : len(fields) + ways]
     fields_ref = refs[-1]
@@ -553,8 +554,8 @@
             inverse_rows = jnp.where(row == m, solved_inverse[m], inverse_rows)
         upper_ref[start : start + ROWS, :] = jnp.where(lane >= row + start, upper_rows, 0.0)
         inverse_ref[start : start + ROWS, :] = inverse_rows
-        for later in range(block + 1, order // ROWS):
-            first = later * ROWS
+        if block + 1 < order // ROWS:
+            first = start + ROWS
             target = work_ref[first : first + ROWS, :]
             target_inverse = inverse_ref[first : first + ROWS, :]
             multiplier = []
@@ -566,6 +567,30 @@
             for m in range(ROWS):
                 target = target - multiplier[m] * solved[m]
                 target_inverse = target_inverse - multiplier[m] * solved_inverse[m]
+            work_ref[first : first + ROWS, :] = target
+            inverse_ref[first : first + ROWS, :] = target_inverse
+        if block + 2 < order // ROWS:
+            twice = [None] * ROWS
+            twice_inverse = [None] * ROWS
+            for m in reversed(range(ROWS)):
+                upper_row = solved[m]
+                inverse_row = solved_inverse[m]
+                for j in range(m + 1, ROWS):
+                    upper_row = upper_row - entry[j, m] * twice[j]
+                    inverse_row = inverse_row - entry[j, m] * twice_inverse[j]
+                twice[m] = upper_row * scale[m]
+                twice_inverse[m] = inverse_row * scale[m]
+        for later in range(block + 2, order // ROWS):
+            first = later * ROWS
+            target = work_ref[first : first + ROWS, :]
+            target_inverse = inverse_ref[first : first + ROWS, :]
+            values = [
+                jnp.broadcast_to(target[:, start + m : start + m + 1], tile) for m in range(ROWS)
+            ]
+            target = target - total_of([values[m] * twice[m] for m in range(ROWS)])
+            target_inverse = target_inverse - total_of(
+                [values[m] * twice_inverse[m] for m in range(ROWS)]
+            )
             work_ref[first : first + ROWS, :] = target
             inverse_ref[first : first + ROWS, :] = target_inverse
     image = jnp.concatenate([image_ref[0], image_ref[1]], axis=0)
@@ -667,7 +692,15 @@
         ],
         5,
     )
-    half_parts = flip_each(half_parts, [core])
+    half_parts = sum_parts(flip_each(half_parts, [core]), 2)
+    half_steps = []
+    for number, mask in enumerate([low] + across + high):
+        got = flip_each(half_parts, [mask])
+        half_steps.append(got[1])
+        half_parts = sum_parts(got, 2 if number < len(across) else 1)
+        if len(half_parts) == 1:
+            half_parts = half_parts * 2
+    half_total = half_parts[0]
     near_rows = jnp.transpose(near_block, (0, 2, 1, 3)).reshape(
         panels_dev, 2 * nodes, slot_total * 2 * nodes
     )
@@ -680,11 +713,11 @@
         ),
         out_shape=[f32(narrow_count // 2, coarse_count + source_rows, rhs_count)] * 2
         + [f32(high_count, EXTRA, point_count), f32(2, EXTRA, point_count)],
-        in_specs=[SMEM, VMEM] + [VMEM] * len(packs),
+        in_specs=[SMEM, ANY, VMEM] + [VMEM] * len(packs),
         out_specs=[VMEM] * 4,
         scratch_shapes=[pltpu.VMEM((wide_count * coarse_count, rhs_count), jnp.float32)],
         compiler_params=PARAMS,
-    )(index, inverse, *packs)
+    )(index, near_rows, inverse, *packs)
     own_sources = coarse_outs[2]
     kept, got = flip_each(coarse_outs[:2], [core])
     groups = in_pairs(across)
@@ -699,7 +732,7 @@
     precond, pair_edge, next_edge = call(
         precond_kernel,
         [b16(1, 2, point_count, rhs_count)] + [b16(2, width, rhs_count)] * 2,
-        (index, member, smooth, near_rows, *coarse_parts),
+        (index, member, smooth, *coarse_parts),
         1,
     )
     matrix_spec = pl.BlockSpec((1, 3, point_count, source_total), lambda k: (k, 0, 0, 0))
@@ -712,24 +745,23 @@
         compiler_params=PARAMS,
     )(own_sources, other_sources, *coarse_parts)
     fields = flip_each([precond] * (1 << len(source_groups[0])), source_groups[0])
-    half_parts = sum_parts(half_parts, 1 << len(plane_groups[0]), fields[1:])
-    (half_total,) = sum_parts(scatter_steps(half_parts, plane_groups), 1)
-    fields = gather_steps(join(fields, (matrix,)), source_groups[1:])
+    fields = gather_steps(join(fields, (matrix, half_steps[0])), source_groups[1:])
     device_count = narrow_count * wide_count
     pair_edge = flip(pair_edge, 1)
     pairs = [(i, i + 1) for i in range(1, device_count - 1, 2)]
     next_edge = lax.ppermute(next_edge, AXES, pairs + [(j, i) for i, j in pairs])
 
+    after = (pair_edge, next_edge, half_steps[1])
     ways = 1 << len(plane_groups[0])
     far_parts = pl.pallas_call(
-        functools.partial(far_kernel, ways),
+        functools.partial(far_kernel, ways, len(after)),
         out_shape=[f32(target_count // ways, 2, point_count, rhs_count)] * ways,
         grid=(target_count,),
-        in_specs=[ANY, ANY, matrix_spec] + [VMEM] * len(fields),
+        in_specs=[ANY] * len(after) + [matrix_spec] + [VMEM] * len(fields),
         out_specs=[VMEM] * ways,
         scratch_shapes=[pltpu.VMEM((source_total, 2 * rhs_count), jnp.bfloat16)],
         compiler_params=PARAMS,
-    )(pair_edge, next_edge, matrix, *fields)
+    )(*after, matrix, *fields)
     far_parts = scatter_steps(far_parts, plane_groups)
     base = call(
         near_kernel,
@@ -744,17 +776,16 @@
 
     hess_rows = block_total * rhs_count
     sum_rows = hess_rows + rhs_count
-    half_total = sum_butterfly(half_total, high_groups)
     image, *parts = pl.pallas_call(
         functools.partial(project_kernel, masks, 2),
         out_shape=[f32(2, point_count, rhs_count)]
         + [f32(narrow_count, sum_rows // (2 * narrow_count), rhs_count)] * 2,
-        in_specs=[SMEM, ANY] + [VMEM] * (3 + len(far_parts)),
+        in_specs=[SMEM] + [ANY] + [VMEM] * (3 + len(far_parts)),
         out_specs=[VMEM] * 3,
         scratch_shapes=[pltpu.VMEM((sum_rows, rhs_count), jnp.float32)],
         compiler_params=PARAMS,
-    )(index, half_total, weight, basis, base, *far_parts)
-    (total,) = sum_parts(scatter_steps(parts, halving), 1)
+    )(index, half_steps[2], weight, basis, base, *far_parts)
+    (total,) = sum_parts(scatter_steps(parts, halving), 1, half_steps[3:4])
     total = sum_butterfly(total, high_groups)
     parts = gather_steps(append(total, half_total), halving[::-1])
     hessenberg, upper_factor, new_block = call(

time: 90.6 us -> 93.3 us (1.030)
  waiting for transfers between devices: 27.6 us -> 33.2 us
  starting transfers between devices: 41.9 us -> 39.1 us
    ppermute x32 -> x30, waiting for transfers between devices: 27.5 us -> 33.2 us  [flip(): return lax.ppermute(block, AXES, [(i, i ^ mask) for i in range(count)])]
    ppermute x32 -> x30, starting transfers between devices: 41.3 us -> 38.4 us  [flip(): return lax.ppermute(block, AXES, [(i, i ^ mask) for i in range(count)])]
  transfers between devices with their start and end apart: 33 -> 31, of which waited for: 19 -> 17; matrix products, arithmetic and copies ran while one was open for 2% -> 2% of each run, Pallas kernels for 10% -> 5%
where the time goes in v9:
time: 93.3 us; the launch traced here: 93.1 us
  starting transfers between devices  39.1 us (42%)
  waiting for transfers between devices  33.2 us (36%)
  Pallas kernels  17.7 us (19%)
  local copies, waits for them, and re-layouts  2.2 us (2%)
    ppermute x30, starting transfers between devices, flip(): return lax.ppermute(block, AXES, [(i, i ^ mask) for i in range(count)])  38.4 us
    ppermute x30, waiting for transfers between devices, flip(): return lax.ppermute(block, AXES, [(i, i ^ mask) for i in range(count)])  33.2 us
    pallas_call x7, Pallas kernels, call(): pl.pallas_call(kernel, out_shape=out_shape, in_specs=[SMEM] * scalars + [...  12 us
    pallas_call x1, Pallas kernels, body(): pl.pallas_call(functools.partial(matrix_kernel, coarse_count), out_shape=...  1.88 us
  transfers between devices with their start and end apart: 31, of which 17 were waited for; matrix products, arithmetic and copies ran while one was open for 2% of the time, Pallas kernels for 5%

profile of v9, /device:TPU:0, one launch (start us, length us, event | category | flops | bytes accessed | tf_op | source)
XLA Modules:
  0.0 93.1 jit_solution(13010142255111112215)
XLA Ops:
  0.6 0.1 pad_add_fusion.index_ref
  0.7 1.2 %shard_map.112.pack_hbm.refs_1_ = f32[1,56,128]{2,1,0:T(8,128)S(1)} custom-call(s32[2,128]{1,0:T(2,128)} %agg_hbm.3, f32[4,2,128,128]{3,2,1,0:T(8,128)} %basis_ref.3, f32[2,128]{1,0:T(2,128)} %points_hbm.1, f32[1,128]{1,0:T(1,128)} %bitcast.8), custom_call_target="tpu_custom_call" | custom-call | tf_op jit(solution)/shard_map/pallas_call | solution.py:615
  1.9 2.4 %shard_map.113 = (f32[4,48,384]{2,1,0:T(8,128)S(1)}, f32[2,48,128]{2,1,0:T(8,128)S(1)}, f32[2,128,128]{2,1,0:T(8,128)S(1)}, f32[128,128]{1,0:T(8,128)S(1)}, f32[...) custom-call(s32[3]{0:T(128)S(1)} %pad_add_fusion.index_ref, f32[1,56,128]{2,1,0:T(8,128)S(1)} %shard_map.112.pack_hbm.refs_1_, ...), custom_call_target="tpu_custom_call" | custom-call | tf_op jit(solution)/shard_map/pallas_call | solution.py:615
  4.3 0.5 collective-permute-start
  4.8 2.7 %collective-permute-start.4 = (f32[1,56,128]{2,1,0:T(8,128)S(1)}, f32[1,56,128]{2,1,0:T(8,128)S(1)}, u32[]{:S(2)}, u32[]{:S(2)}) collective-permute-start(f32[1,56,128]{2,1,0:T(8,128)S(1)} %shard_map.112.pack_hbm.refs_1_), channel_id=1, source_target_pairs={{0,2},{1,3},{2,0},{3,1},{4,6},{5,7},{6,4},{7,5},{8,10},{9,11},{10,... | collective-permute-start | bytes 86024 | tf_op jit(solution)/shard_map/ppermute | solution.py:61
  7.5 2.6 %collective-permute-start.5 = (f32[1,56,128]{2,1,0:T(8,128)S(1)}, f32[1,56,128]{2,1,0:T(8,128)S(1)}, u32[]{:S(2)}, u32[]{:S(2)}) collective-permute-start(f32[1,56,128]{2,1,0:T(8,128)S(1)} %shard_map.112.pack_hbm.refs_1_), channel_id=1, source_target_pairs={{0,4},{1,5},{2,6},{3,7},{4,0},{5,1},{6,2},{7,3},{8,12},{9,13},{10,... | collective-permute-start | bytes 86024 | tf_op jit(solution)/shard_map/ppermute | solution.py:61
  10.1 2.5 %collective-permute-done.5.refs_3_ = f32[1,56,128]{2,1,0:T(8,128)S(1)} collective-permute-done((f32[1,56,128]{2,1,0:T(8,128)S(1)}, f32[1,56,128]{2,1,0:T(8,128)S(1)}, u32[]{:S(2)}, u32[]{:S(2)}) %collective-permute-start.5) | collective-permute-done | bytes 28704 | tf_op jit(solution)/shard_map/ppermute | solution.py:61
  12.6 3.2 %collective-permute-done.6.refs_4_ = f32[1,56,128]{2,1,0:T(8,128)S(1)} collective-permute-done((f32[1,56,128]{2,1,0:T(8,128)S(1)}, f32[1,56,128]{2,1,0:T(8,128)S(1)}, u32[]{:S(2)}, u32[]{:S(2)}) %collective-permute-start.6) | collective-permute-done | bytes 28704 | tf_op jit(solution)/shard_map/ppermute | solution.py:61
  15.7 1.6 %collective-permute-start.7 = (f32[4,56,128]{2,1,0:T(8,128)S(1)}, f32[4,56,128]{2,1,0:T(8,128)S(1)}, u32[]{:S(2)}, u32[]{:S(2)}) collective-permute-start(f32[4,56,128]{2,1,0:T(8,128)S(1)} %shard_map.117.refs_0_), channel_id=1, source_target_pairs={{0,1},{1,0},{2,3},{3,2},{4,5},{5,4},{6,7},{7,6},{8,9},{9,8},{10,11... | collective-permute-start | bytes 344072 | tf_op jit(solution)/shard_map/ppermute | solution.py:61
  17.3 1.5 %copy.13 = bf16[8,32,12,32]{3,2,1,0:T(8,128)(2,1)S(1)} copy(bf16[8,32,12,32]{3,1,2,0:T(8,128)(2,1)} %bitcast.7) | data formatting | bytes 393216 | tf_op jit(solution)/shard_map/transpose | solution.py:704
  18.8 0.7 reshape.15.near_ref.block_ref
  19.5 1.1 %collective-permute-done.7.refs_1_ = f32[4,56,128]{2,1,0:T(8,128)S(1)} collective-permute-done((f32[4,56,128]{2,1,0:T(8,128)S(1)}, f32[4,56,128]{2,1,0:T(8,128)S(1)}, u32[]{:S(2)}, u32[]{:S(2)}) %collective-permute-start.7) | collective-permute-done | bytes 114720 | tf_op jit(solution)/shard_map/ppermute | solution.py:61
  20.6 0.8 shard_map.118
  21.4 0.1 collective-permute-start.8
  21.5 0.0 collective-permute-done.refs_1_
  21.6 1.6 %collective-permute-start.1 = (f32[2,160,128]{2,1,0:T(8,128)S(1)}, f32[2,160,128]{2,1,0:T(8,128)S(1)}, u32[]{:S(2)}, u32[]{:S(2)}) collective-permute-start(f32[2,160,128]{2,1,0:T(8,128)S(1)} %get-tuple-element.40), channel_id=1, source_target_pairs={{0,1},{1,0},{2,3},{3,2},{4,5},{5,4},{6,7},{7,6},{8,9},{9,8},{10,11... | collective-permute-start | bytes 491528 | tf_op jit(solution)/shard_map/ppermute | solution.py:61
  23.1 0.0 collective-permute-done.8.got_ref
  23.1 1.6 %collective-permute-start.9 = (f32[1,64,128]{2,1,0:T(8,128)S(1)}, f32[1,64,128]{2,1,0:T(8,128)S(1)}, u32[]{:S(2)}, u32[]{:S(2)}) collective-permute-start(f32[1,64,128]{2,1,0:T(8,128)S(1)} %get-tuple-element.51), channel_id=1, source_target_pairs={{0,16},{1,17},{2,18},{3,19},{4,20},{5,21},{6,22},{7,23},{8,24},{9,... | collective-permute-start | bytes 98312 | tf_op jit(solution)/shard_map/ppermute | solution.py:61
  24.7 2.4 %collective-permute-done.9.refs_1_ = f32[1,64,128]{2,1,0:T(8,128)S(1)} collective-permute-done((f32[1,64,128]{2,1,0:T(8,128)S(1)}, f32[1,64,128]{2,1,0:T(8,128)S(1)}, u32[]{:S(2)}, u32[]{:S(2)}) %collective-permute-start.9) | collective-permute-done | bytes 32800 | tf_op jit(solution)/shard_map/ppermute | solution.py:61
  27.1 0.8 shard_map.120
  27.9 0.1 collective-permute-start.12
  28.0 0.9 collective-permute-start.13
  28.9 3.5 %collective-permute-start.14 = (bf16[1,2,128,128]{3,2,1,0:T(8,128)(2,1)S(1)}, bf16[1,2,128,128]{3,2,1,0:T(8,128)(2,1)S(1)}, u32[]{:S(2)}, u32[]{:S(2)}) collective-permute-start(bf16[1,2,128,128]{3,2,1,0:T(8,128)(2,1)S(1)} %get-tuple-element.52.own_ref.refs_2_), channel_id=1, source_target_pairs={{0,6},{1,7},{2,4},{3,5},{4,2},{5,3},{6,0},{7,1},{8,14},{9,15},{10,... | collective-permute-start | bytes 196616 | tf_op jit(solution)/shard_map/ppermute | solution.py:61
  32.4 1.9 %shard_map.122.refs_0_.refs_3_ = bf16[4,3,128,1024]{3,2,1,0:T(8,128)(2,1)S(1)} custom-call(f32[4,8,128]{2,1,0:T(8,128)S(1)} %get-tuple-element.55.own_ref, f32[4,8,128]{2,1,0:T(8,128)S(1)} %get-tuple-element.56.other_ref, f32[1,64,128]{2,1,0:T(8,128)S(1)} %get-tuple-element.50.refs_0_, f32[1,64,128]{2,1,0:T(8,128)S(1)} %collective-permute-done.9.refs_1_), custom_call_target="tpu_custom_call" | custom-call | tf_op jit(solution)/shard_map/pallas_call | solution.py:739
  34.3 1.5 %collective-permute-done.13.refs_4_ = bf16[1,2,128,128]{3,2,1,0:T(8,128)(2,1)S(1)} collective-permute-done((bf16[1,2,128,128]{3,2,1,0:T(8,128)(2,1)S(1)}, bf16[1,2,128,128]{3,2,1,0:T(8,128)(2,1)S(1)}, u32[]{:S(2)}, u32[]{:S(2)}) %collective-permute-start.13) | collective-permute-done | bytes 65568 | tf_op jit(solution)/shard_map/ppermute | solution.py:61
  35.8 0.0 copy-start.1
  35.9 0.0 copy-start.2
  35.9 0.0 copy-start
  35.9 0.1 collective-permute-start.15
  36.0 1.6 %collective-permute-start.2 = (f32[1,160,128]{2,1,0:T(8,128)S(1)}, f32[1,160,128]{2,1,0:T(8,128)S(1)}, u32[]{:S(2)}, u32[]{:S(2)}) collective-permute-start(f32[1,160,128]{2,1,0:T(8,128)S(1)} %get-tuple-element.42), channel_id=1, source_target_pairs={{0,16},{1,17},{2,18},{3,19},{4,20},{5,21},{6,22},{7,23},{8,24},{9,... | collective-permute-start | bytes 245768 | tf_op jit(solution)/shard_map/ppermute | solution.py:61
  37.6 1.1 %collective-permute-start.10 = (bf16[2,64,128]{2,1,0:T(8,128)(2,1)S(1)}, bf16[2,64,128]{2,1,0:T(8,128)(2,1)S(1)}, u32[]{:S(2)}, u32[]{:S(2)}) collective-permute-start(bf16[2,64,128]{2,1,0:T(8,128)(2,1)S(1)} %get-tuple-element.53), channel_id=1, source_target_pairs={{0,1},{1,0},{2,3},{3,2},{4,5},{5,4},{6,7},{7,6},{8,9},{9,8},{10,11... | collective-permute-start | bytes 98312 | tf_op jit(solution)/shard_map/ppermute | solution.py:61
  38.7 0.7 collective-permute-start.11
  39.3 2.2 %collective-permute-done.10.pair_ref.refs_0_ = bf16[2,64,128]{2,1,0:T(8,128)(2,1)S(1)} collective-permute-done((bf16[2,64,128]{2,1,0:T(8,128)(2,1)S(1)}, bf16[2,64,128]{2,1,0:T(8,128)(2,1)S(1)}, u32[]{:S(2)}, u32[]{:S(2)}) %collective-permute-start.10) | collective-permute-done | bytes 32800 | tf_op jit(solution)/shard_map/ppermute | solution.py:61
  41.5 1.7 %shard_map.124 = (f32[1,2,128,128]{3,2,1,0:T(8,128)S(1)}, f32[1,2,128,128]{3,2,1,0:T(8,128)S(1)}, f32[1,2,128,128]{3,2,1,0:T(8,128)S(1)}, f32[1,2,128,128]{3,2,1,0:T(8,128)S(1)}) custom-call(bf16[2,64,128]{2,1,0:T(8,128)(2,1)S(1)} %collective-permute-done.10.pair_ref.refs_0_, bf16[2,64,128]{2,1,0:T(8,128)(2,1)S(1)} %collective-permute-done.11.next_ref.refs_1_, ...), custom_call_target="tpu_custom_call" | custom-call | tf_op jit(solution)/shard_map/pallas_call | solution.py:756
  43.2 4.8 %collective-permute-start.16 = (f32[1,2,128,128]{3,2,1,0:T(8,128)S(1)}, f32[1,2,128,128]{3,2,1,0:T(8,128)S(1)}, u32[]{:S(2)}, u32[]{:S(2)}) collective-permute-start(f32[1,2,128,128]{3,2,1,0:T(8,128)S(1)} %get-tuple-element.58), channel_id=1, source_target_pairs={{0,1},{1,0},{2,3},{3,2},{4,5},{5,4},{6,7},{7,6},{8,9},{9,8},{10,11... | collective-permute-start | bytes 393224 | tf_op jit(solution)/shard_map/ppermute | solution.py:61
  48.1 1.9 %collective-permute-start.17 = (f32[1,2,128,128]{3,2,1,0:T(8,128)S(1)}, f32[1,2,128,128]{3,2,1,0:T(8,128)S(1)}, u32[]{:S(2)}, u32[]{:S(2)}) collective-permute-start(f32[1,2,128,128]{3,2,1,0:T(8,128)S(1)} %get-tuple-element.59), channel_id=1, source_target_pairs={{0,16},{1,17},{2,18},{3,19},{4,20},{5,21},{6,22},{7,23},{8,24},{9,... | collective-permute-start | bytes 393224 | tf_op jit(solution)/shard_map/ppermute | solution.py:61
  50.0 1.4 %collective-permute-start.18 = (f32[1,2,128,128]{3,2,1,0:T(8,128)S(1)}, f32[1,2,128,128]{3,2,1,0:T(8,128)S(1)}, u32[]{:S(2)}, u32[]{:S(2)}) collective-permute-start(f32[1,2,128,128]{3,2,1,0:T(8,128)S(1)} %get-tuple-element.60), channel_id=1, source_target_pairs={{0,17},{1,16},{2,19},{3,18},{4,21},{5,20},{6,23},{7,22},{8,25},{9,... | collective-permute-start | bytes 393224 | tf_op jit(solution)/shard_map/ppermute | solution.py:61
  51.4 0.5 collective-permute-start.3
  52.0 1.0 %shard_map.121.base_ref = f32[2,128,128]{2,1,0:T(8,128)S(1)} custom-call(s32[3]{0:T(128)S(1)} %pad_add_fusion.index_ref, s32[8,12]{1,0:T(8,128)S(1)} %copy-done.1, s32[8]{0:T(128)S(1)} %copy-done.2, bf16[8,32,384]{2,1,0:T(8,128)(2,1)S(1)} %reshape.15.near_ref.block_ref, bf16[1,2,128,128]{3,2,1,0:T(8,128)(2,1)S(1)} %get-tuple-element.52.own_ref.refs_2_, ...), custom_call_target="tpu_custom_call" | custom-call | tf_op jit(solution)/shard_map/pallas_call | solution.py:615
  53.0 2.9 %collective-permute-done.3.half_hbm.refs_1_ = f32[1,160,128]{2,1,0:T(8,128)S(1)} collective-permute-done((f32[1,160,128]{2,1,0:T(8,128)S(1)}, f32[1,160,128]{2,1,0:T(8,128)S(1)}, u32[]{:S(2)}, u32[]{:S(2)}) %collective-permute-start.3) | collective-permute-done | bytes 81952 | tf_op jit(solution)/shard_map/ppermute | solution.py:61
  55.9 0.8 collective-permute-done.17.refs_2_
  56.8 1.0 %shard_map.125 = (f32[2,128,128]{2,1,0:T(8,128)S(1)}, f32[4,80,128]{2,1,0:T(8,128)S(1)}, f32[4,80,128]{2,1,0:T(8,128)S(1)}) custom-call(s32[3]{0:T(128)S(1)} %pad_add_fusion.index_ref, f32[1,160,128]{2,1,0:T(8,128)S(1)} %collective-permute-done.3.half_hbm.refs_1_, f32[128,128]{1,0:T(8,128)S(1)} %get-tuple-element.43.refs_0_.weight_ref, ...), custom_call_target="tpu_custom_call" | custom-call | tf_op jit(solution)/shard_map/pallas_call | solution.py:779
  57.8 0.1 collective-permute-start.20
  57.9 0.3 collective-permute-start.19
  58.2 1.0 %collective-permute-done.20.refs_1_ = f32[4,80,128]{2,1,0:T(8,128)S(1)} collective-permute-done((f32[4,80,128]{2,1,0:T(8,128)S(1)}, f32[4,80,128]{2,1,0:T(8,128)S(1)}, u32[]{:S(2)}, u32[]{:S(2)}) %collective-permute-start.20) | collective-permute-done | bytes 163872 | tf_op jit(solution)/shard_map/ppermute | solution.py:61
  59.3 1.7 %collective-permute-start.21 = (f32[1,80,128]{2,1,0:T(8,128)S(1)}, f32[1,80,128]{2,1,0:T(8,128)S(1)}, u32[]{:S(2)}, u32[]{:S(2)}) collective-permute-start(f32[1,80,128]{2,1,0:T(8,128)S(1)} %get-tuple-element.65), channel_id=1, source_target_pairs={{0,1},{1,0},{2,3},{3,2},{4,5},{5,4},{6,7},{7,6},{8,9},{9,8},{10,11... | collective-permute-start | bytes 122888 | tf_op jit(solution)/shard_map/ppermute | solution.py:61
  61.0 1.3 %collective-permute-start.22 = (f32[1,80,128]{2,1,0:T(8,128)S(1)}, f32[1,80,128]{2,1,0:T(8,128)S(1)}, u32[]{:S(2)}, u32[]{:S(2)}) collective-permute-start(f32[1,80,128]{2,1,0:T(8,128)S(1)} %get-tuple-element.66), channel_id=1, source_target_pairs={{0,16},{1,17},{2,18},{3,19},{4,20},{5,21},{6,22},{7,23},{8,24},{9,... | collective-permute-start | bytes 122888 | tf_op jit(solution)/shard_map/ppermute | solution.py:61
  62.3 0.5 collective-permute-start.23
  62.8 2.6 %collective-permute-done.19.refs_0_.refs_1_ = f32[1,160,128]{2,1,0:T(8,128)S(1)} collective-permute-done((f32[1,160,128]{2,1,0:T(8,128)S(1)}, f32[1,160,128]{2,1,0:T(8,128)S(1)}, u32[]{:S(2)}, u32[]{:S(2)}) %collective-permute-start.19) | collective-permute-done | bytes 81952 | tf_op jit(solution)/shard_map/ppermute | solution.py:61
  65.5 1.8 %collective-permute-done.23.refs_4_ = f32[1,80,128]{2,1,0:T(8,128)S(1)} collective-permute-done((f32[1,80,128]{2,1,0:T(8,128)S(1)}, f32[1,80,128]{2,1,0:T(8,128)S(1)}, u32[]{:S(2)}, u32[]{:S(2)}) %collective-permute-start.23) | collective-permute-done | bytes 40992 | tf_op jit(solution)/shard_map/ppermute | solution.py:61
  67.3 2.0 %collective-permute-start.24 = (f32[1,80,128]{2,1,0:T(8,128)S(1)}, f32[1,80,128]{2,1,0:T(8,128)S(1)}, u32[]{:S(2)}, u32[]{:S(2)}) collective-permute-start(f32[1,80,128]{2,1,0:T(8,128)S(1)} %shard_map.128.refs_0_), channel_id=1, source_target_pairs={{0,2},{1,3},{2,0},{3,1},{4,6},{5,7},{6,4},{7,5},{8,10},{9,11},{10,... | collective-permute-start | bytes 122888 | tf_op jit(solution)/shard_map/ppermute | solution.py:61
  69.3 1.3 %collective-permute-start.25 = (f32[1,80,128]{2,1,0:T(8,128)S(1)}, f32[1,80,128]{2,1,0:T(8,128)S(1)}, u32[]{:S(2)}, u32[]{:S(2)}) collective-permute-start(f32[1,80,128]{2,1,0:T(8,128)S(1)} %shard_map.128.refs_0_), channel_id=1, source_target_pairs={{0,4},{1,5},{2,6},{3,7},{4,0},{5,1},{6,2},{7,3},{8,12},{9,13},{10,... | collective-permute-start | bytes 122888 | tf_op jit(solution)/shard_map/ppermute | solution.py:61
  70.6 1.1 %collective-permute-start.26 = (f32[1,80,128]{2,1,0:T(8,128)S(1)}, f32[1,80,128]{2,1,0:T(8,128)S(1)}, u32[]{:S(2)}, u32[]{:S(2)}) collective-permute-start(f32[1,80,128]{2,1,0:T(8,128)S(1)} %shard_map.128.refs_0_), channel_id=1, source_target_pairs={{0,6},{1,7},{2,4},{3,5},{4,2},{5,3},{6,0},{7,1},{8,14},{9,15},{10,... | collective-permute-start | bytes 122888 | tf_op jit(solution)/shard_map/ppermute | solution.py:61
  71.7 2.4 %collective-permute-done.25.refs_2_ = f32[1,80,128]{2,1,0:T(8,128)S(1)} collective-permute-done((f32[1,80,128]{2,1,0:T(8,128)S(1)}, f32[1,80,128]{2,1,0:T(8,128)S(1)}, u32[]{:S(2)}, u32[]{:S(2)}) %collective-permute-start.25) | collective-permute-done | bytes 40992 | tf_op jit(solution)/shard_map/ppermute | solution.py:61
  74.2 2.2 %collective-permute-done.26.refs_3_ = f32[1,80,128]{2,1,0:T(8,128)S(1)} collective-permute-done((f32[1,80,128]{2,1,0:T(8,128)S(1)}, f32[1,80,128]{2,1,0:T(8,128)S(1)}, u32[]{:S(2)}, u32[]{:S(2)}) %collective-permute-start.26) | collective-permute-done | bytes 40992 | tf_op jit(solution)/shard_map/ppermute | solution.py:61
  76.4 0.6 collective-permute-start.27
  77.0 1.7 %collective-permute-start.28 = (f32[1,240,128]{2,1,0:T(8,128)S(1)}, f32[1,240,128]{2,1,0:T(8,128)S(1)}, u32[]{:S(2)}, u32[]{:S(2)}) collective-permute-start(f32[1,240,128]{2,1,0:T(8,128)S(1)} %shard_map.131.refs_0_), channel_id=1, source_target_pairs={{0,16},{1,17},{2,18},{3,19},{4,20},{5,21},{6,22},{7,23},{8,24},{9,... | collective-permute-start | bytes 368648 | tf_op jit(solution)/shard_map/ppermute | solution.py:61
  78.8 1.2 %collective-permute-start.29 = (f32[1,240,128]{2,1,0:T(8,128)S(1)}, f32[1,240,128]{2,1,0:T(8,128)S(1)}, u32[]{:S(2)}, u32[]{:S(2)}) collective-permute-start(f32[1,240,128]{2,1,0:T(8,128)S(1)} %shard_map.131.refs_0_), channel_id=1, source_target_pairs={{0,17},{1,16},{2,19},{3,18},{4,21},{5,20},{6,23},{7,22},{8,25},{9,... | collective-permute-start | bytes 368648 | tf_op jit(solution)/shard_map/ppermute | solution.py:61
  80.0 1.4 %collective-permute-done.27.refs_1_ = f32[1,240,128]{2,1,0:T(8,128)S(1)} collective-permute-done((f32[1,240,128]{2,1,0:T(8,128)S(1)}, f32[1,240,128]{2,1,0:T(8,128)S(1)}, u32[]{:S(2)}, u32[]{:S(2)}) %collective-permute-start.27) | collective-permute-done | bytes 122912 | tf_op jit(solution)/shard_map/ppermute | solution.py:61
  81.4 0.6 collective-permute-done.28.refs_2_
  81.9 2.6 %collective-permute-done.29.refs_3_ = f32[1,240,128]{2,1,0:T(8,128)S(1)} collective-permute-done((f32[1,240,128]{2,1,0:T(8,128)S(1)}, f32[1,240,128]{2,1,0:T(8,128)S(1)}, u32[]{:S(2)}, u32[]{:S(2)}) %collective-permute-start.29) | collective-permute-done | bytes 122912 | tf_op jit(solution)/shard_map/ppermute | solution.py:61
  84.6 0.1 collective-permute-start.30
  84.7 1.9 %collective-permute-done.30.refs_1_ = f32[4,240,128]{2,1,0:T(8,128)S(1)} collective-permute-done((f32[4,240,128]{2,1,0:T(8,128)S(1)}, f32[4,240,128]{2,1,0:T(8,128)S(1)}, u32[]{:S(2)}, u32[]{:S(2)}) %collective-permute-start.30) | collective-permute-done | bytes 491552 | tf_op jit(solution)/shard_map/ppermute | solution.py:61
  86.5 6.6 %shard_map.133 = (f32[512,128]{1,0:T(8,128)}, f32[128,128]{1,0:T(8,128)}, f32[256,128]{1,0:T(8,128)}) custom-call(s32[3]{0:T(128)S(1)} %pad_add_fusion.index_ref, f32[4,2,128,128]{3,2,1,0:T(8,128)S(1)} %copy-done, f32[2,128,128]{2,1,0:T(8,128)S(1)} %get-tuple-element.61.image_ref, f32[4,240,128]{2,1,0:T(8,128)S(1)} %shard_map.132.refs_0_, ...), custom_call_target="tpu_custom_call" | custom-call | tf_op jit(solution)/shard_map/pallas_call | solution.py:615
  (29 shorter events, 0.3 us)
Async XLA Ops:
  4.3 17.2 %collective-permute-start = (f32[4,160,128]{2,1,0:T(8,128)S(1)}, f32[4,160,128]{2,1,0:T(8,128)S(1)}, u32[]{:S(2)}, u32[]{:S(2)}) collective-permute-start(f32[4,160,128]{2,1,0:T(8,128)S(1)} %get-tuple-element.38), channel_id=1, source_target_pairs={{0,8},{1,9},{2,10},{3,11},{4,12},{5,13},{6,14},{7,15},{8,0},{9,1},... | collective-permute-start | bytes 983048 | tf_op jit(solution)/shard_map/ppermute | solution.py:61
  4.8 5.2 %collective-permute-start.4 = (f32[1,56,128]{2,1,0:T(8,128)S(1)}, f32[1,56,128]{2,1,0:T(8,128)S(1)}, u32[]{:S(2)}, u32[]{:S(2)}) collective-permute-start(f32[1,56,128]{2,1,0:T(8,128)S(1)} %shard_map.112.pack_hbm.refs_1_), channel_id=1, source_target_pairs={{0,2},{1,3},{2,0},{3,1},{4,6},{5,7},{6,4},{7,5},{8,10},{9,11},{10,... | collective-permute-start | bytes 86024 | tf_op jit(solution)/shard_map/ppermute | solution.py:61
  7.5 5.1 %collective-permute-start.5 = (f32[1,56,128]{2,1,0:T(8,128)S(1)}, f32[1,56,128]{2,1,0:T(8,128)S(1)}, u32[]{:S(2)}, u32[]{:S(2)}) collective-permute-start(f32[1,56,128]{2,1,0:T(8,128)S(1)} %shard_map.112.pack_hbm.refs_1_), channel_id=1, source_target_pairs={{0,4},{1,5},{2,6},{3,7},{4,0},{5,1},{6,2},{7,3},{8,12},{9,13},{10,... | collective-permute-start | bytes 86024 | tf_op jit(solution)/shard_map/ppermute | solution.py:61
  10.1 5.7 %collective-permute-start.6 = (f32[1,56,128]{2,1,0:T(8,128)S(1)}, f32[1,56,128]{2,1,0:T(8,128)S(1)}, u32[]{:S(2)}, u32[]{:S(2)}) collective-permute-start(f32[1,56,128]{2,1,0:T(8,128)S(1)} %shard_map.112.pack_hbm.refs_1_), channel_id=1, source_target_pairs={{0,6},{1,7},{2,4},{3,5},{4,2},{5,3},{6,0},{7,1},{8,14},{9,15},{10,... | collective-permute-start | bytes 86024 | tf_op jit(solution)/shard_map/ppermute | solution.py:61
  15.7 4.9 %collective-permute-start.7 = (f32[4,56,128]{2,1,0:T(8,128)S(1)}, f32[4,56,128]{2,1,0:T(8,128)S(1)}, u32[]{:S(2)}, u32[]{:S(2)}) collective-permute-start(f32[4,56,128]{2,1,0:T(8,128)S(1)} %shard_map.117.refs_0_), channel_id=1, source_target_pairs={{0,1},{1,0},{2,3},{3,2},{4,5},{5,4},{6,7},{7,6},{8,9},{9,8},{10,11... | collective-permute-start | bytes 344072 | tf_op jit(solution)/shard_map/ppermute | solution.py:61
  21.4 1.7 %collective-permute-start.8 = (f32[2,64,128]{2,1,0:T(8,128)S(1)}, f32[2,64,128]{2,1,0:T(8,128)S(1)}, u32[]{:S(2)}, u32[]{:S(2)}) collective-permute-start(f32[2,64,128]{2,1,0:T(8,128)S(1)} %get-tuple-element.48), channel_id=1, source_target_pairs={{0,8},{1,9},{2,10},{3,11},{4,12},{5,13},{6,14},{7,15},{8,0},{9,1},... | collective-permute-start | bytes 196616 | tf_op jit(solution)/shard_map/ppermute | solution.py:61
  21.6 14.3 %collective-permute-start.1 = (f32[2,160,128]{2,1,0:T(8,128)S(1)}, f32[2,160,128]{2,1,0:T(8,128)S(1)}, u32[]{:S(2)}, u32[]{:S(2)}) collective-permute-start(f32[2,160,128]{2,1,0:T(8,128)S(1)} %get-tuple-element.40), channel_id=1, source_target_pairs={{0,1},{1,0},{2,3},{3,2},{4,5},{5,4},{6,7},{7,6},{8,9},{9,8},{10,11... | collective-permute-start | bytes 491528 | tf_op jit(solution)/shard_map/ppermute | solution.py:61
  23.1 4.0 %collective-permute-start.9 = (f32[1,64,128]{2,1,0:T(8,128)S(1)}, f32[1,64,128]{2,1,0:T(8,128)S(1)}, u32[]{:S(2)}, u32[]{:S(2)}) collective-permute-start(f32[1,64,128]{2,1,0:T(8,128)S(1)} %get-tuple-element.51), channel_id=1, source_target_pairs={{0,16},{1,17},{2,18},{3,19},{4,20},{5,21},{6,22},{7,23},{8,24},{9,... | collective-permute-start | bytes 98312 | tf_op jit(solution)/shard_map/ppermute | solution.py:61
  27.9 6.3 %collective-permute-start.12 = (bf16[1,2,128,128]{3,2,1,0:T(8,128)(2,1)S(1)}, bf16[1,2,128,128]{3,2,1,0:T(8,128)(2,1)S(1)}, u32[]{:S(2)}, u32[]{:S(2)}) collective-permute-start(bf16[1,2,128,128]{3,2,1,0:T(8,128)(2,1)S(1)} %get-tuple-element.52.own_ref.refs_2_), channel_id=1, source_target_pairs={{0,2},{1,3},{2,0},{3,1},{4,6},{5,7},{6,4},{7,5},{8,10},{9,11},{10,... | collective-permute-start | bytes 196616 | tf_op jit(solution)/shard_map/ppermute | solution.py:61
  28.0 7.8 %collective-permute-start.13 = (bf16[1,2,128,128]{3,2,1,0:T(8,128)(2,1)S(1)}, bf16[1,2,128,128]{3,2,1,0:T(8,128)(2,1)S(1)}, u32[]{:S(2)}, u32[]{:S(2)}) collective-permute-start(bf16[1,2,128,128]{3,2,1,0:T(8,128)(2,1)S(1)} %get-tuple-element.52.own_ref.refs_2_), channel_id=1, source_target_pairs={{0,4},{1,5},{2,6},{3,7},{4,0},{5,1},{6,2},{7,3},{8,12},{9,13},{10,... | collective-permute-start | bytes 196616 | tf_op jit(solution)/shard_map/ppermute | solution.py:61
  28.9 6.9 %collective-permute-start.14 = (bf16[1,2,128,128]{3,2,1,0:T(8,128)(2,1)S(1)}, bf16[1,2,128,128]{3,2,1,0:T(8,128)(2,1)S(1)}, u32[]{:S(2)}, u32[]{:S(2)}) collective-permute-start(bf16[1,2,128,128]{3,2,1,0:T(8,128)(2,1)S(1)} %get-tuple-element.52.own_ref.refs_2_), channel_id=1, source_target_pairs={{0,6},{1,7},{2,4},{3,5},{4,2},{5,3},{6,0},{7,1},{8,14},{9,15},{10,... | collective-permute-start | bytes 196616 | tf_op jit(solution)/shard_map/ppermute | solution.py:61
  35.8 16.1 %copy-start.1 = (s32[8,12]{1,0:T(8,128)S(1)}, s32[8,12]{1,0:T(8,128)}, u32[]{:S(2)}) copy-start(s32[8,12]{1,0:T(8,128)} %panel_ref.1) | copy-start | bytes 1156
  35.9 16.1 %copy-start.2 = (s32[8]{0:T(128)S(1)}, s32[8]{0:T(128)}, u32[]{:S(2)}) copy-start(s32[8]{0:T(128)} %count_ref.1) | copy-start | bytes 100
  35.9 20.9 %copy-start = (f32[4,2,128,128]{3,2,1,0:T(8,128)S(1)}, f32[4,2,128,128]{3,2,1,0:T(8,128)}, u32[]{:S(2)}) copy-start(f32[4,2,128,128]{3,2,1,0:T(8,128)} %basis_ref.3) | copy-start | bytes 1572868
  35.9 5.6 %collective-permute-start.15 = (bf16[4,2,128,128]{3,2,1,0:T(8,128)(2,1)S(1)}, bf16[4,2,128,128]{3,2,1,0:T(8,128)(2,1)S(1)}, u32[]{:S(2)}, u32[]{:S(2)}) collective-permute-start(bf16[4,2,128,128]{3,2,1,0:T(8,128)(2,1)S(1)} %shard_map.123.refs_4_), channel_id=1, source_target_pairs={{0,8},{1,9},{2,10},{3,11},{4,12},{5,13},{6,14},{7,15},{8,0},{9,1},... | collective-permute-start | bytes 786440 | tf_op jit(solution)/shard_map/ppermute | solution.py:61
  36.0 5.5 %collective-permute-start.2 = (f32[1,160,128]{2,1,0:T(8,128)S(1)}, f32[1,160,128]{2,1,0:T(8,128)S(1)}, u32[]{:S(2)}, u32[]{:S(2)}) collective-permute-start(f32[1,160,128]{2,1,0:T(8,128)S(1)} %get-tuple-element.42), channel_id=1, source_target_pairs={{0,16},{1,17},{2,18},{3,19},{4,20},{5,21},{6,22},{7,23},{8,24},{9,... | collective-permute-start | bytes 245768 | tf_op jit(solution)/shard_map/ppermute | solution.py:61
  37.6 3.9 %collective-permute-start.10 = (bf16[2,64,128]{2,1,0:T(8,128)(2,1)S(1)}, bf16[2,64,128]{2,1,0:T(8,128)(2,1)S(1)}, u32[]{:S(2)}, u32[]{:S(2)}) collective-permute-start(bf16[2,64,128]{2,1,0:T(8,128)(2,1)S(1)} %get-tuple-element.53), channel_id=1, source_target_pairs={{0,1},{1,0},{2,3},{3,2},{4,5},{5,4},{6,7},{7,6},{8,9},{9,8},{10,11... | collective-permute-start | bytes 98312 | tf_op jit(solution)/shard_map/ppermute | solution.py:61
  38.7 2.8 %collective-permute-start.11 = (bf16[2,64,128]{2,1,0:T(8,128)(2,1)S(1)}, bf16[2,64,128]{2,1,0:T(8,128)(2,1)S(1)}, u32[]{:S(2)}, u32[]{:S(2)}) collective-permute-start(bf16[2,64,128]{2,1,0:T(8,128)(2,1)S(1)} %get-tuple-element.54), channel_id=1, source_target_pairs={{1,2},{3,4},{5,6},{7,8},{9,10},{11,12},{13,14},{15,16},{17,18},{19... | collective-permute-start | bytes 98312 | tf_op jit(solution)/shard_map/ppermute | solution.py:752
  43.2 12.7 %collective-permute-start.16 = (f32[1,2,128,128]{3,2,1,0:T(8,128)S(1)}, f32[1,2,128,128]{3,2,1,0:T(8,128)S(1)}, u32[]{:S(2)}, u32[]{:S(2)}) collective-permute-start(f32[1,2,128,128]{3,2,1,0:T(8,128)S(1)} %get-tuple-element.58), channel_id=1, source_target_pairs={{0,1},{1,0},{2,3},{3,2},{4,5},{5,4},{6,7},{7,6},{8,9},{9,8},{10,11... | collective-permute-start | bytes 393224 | tf_op jit(solution)/shard_map/ppermute | solution.py:61
  48.1 8.7 %collective-permute-start.17 = (f32[1,2,128,128]{3,2,1,0:T(8,128)S(1)}, f32[1,2,128,128]{3,2,1,0:T(8,128)S(1)}, u32[]{:S(2)}, u32[]{:S(2)}) collective-permute-start(f32[1,2,128,128]{3,2,1,0:T(8,128)S(1)} %get-tuple-element.59), channel_id=1, source_target_pairs={{0,16},{1,17},{2,18},{3,19},{4,20},{5,21},{6,22},{7,23},{8,24},{9,... | collective-permute-start | bytes 393224 | tf_op jit(solution)/shard_map/ppermute | solution.py:61
  50.0 6.7 %collective-permute-start.18 = (f32[1,2,128,128]{3,2,1,0:T(8,128)S(1)}, f32[1,2,128,128]{3,2,1,0:T(8,128)S(1)}, u32[]{:S(2)}, u32[]{:S(2)}) collective-permute-start(f32[1,2,128,128]{3,2,1,0:T(8,128)S(1)} %get-tuple-element.60), channel_id=1, source_target_pairs={{0,17},{1,16},{2,19},{3,18},{4,21},{5,20},{6,23},{7,22},{8,25},{9,... | collective-permute-start | bytes 393224 | tf_op jit(solution)/shard_map/ppermute | solution.py:61
  51.4 4.5 %collective-permute-start.3 = (f32[1,160,128]{2,1,0:T(8,128)S(1)}, f32[1,160,128]{2,1,0:T(8,128)S(1)}, u32[]{:S(2)}, u32[]{:S(2)}) collective-permute-start(f32[1,160,128]{2,1,0:T(8,128)S(1)} %shard_map.116.refs_0_), channel_id=1, source_target_pairs={{0,2},{1,3},{2,0},{3,1},{4,6},{5,7},{6,4},{7,5},{8,10},{9,11},{10,... | collective-permute-start | bytes 245768 | tf_op jit(solution)/shard_map/ppermute | solution.py:61
  57.8 1.5 %collective-permute-start.20 = (f32[4,80,128]{2,1,0:T(8,128)S(1)}, f32[4,80,128]{2,1,0:T(8,128)S(1)}, u32[]{:S(2)}, u32[]{:S(2)}) collective-permute-start(f32[4,80,128]{2,1,0:T(8,128)S(1)} %get-tuple-element.63), channel_id=1, source_target_pairs={{0,8},{1,9},{2,10},{3,11},{4,12},{5,13},{6,14},{7,15},{8,0},{9,1},... | collective-permute-start | bytes 491528 | tf_op jit(solution)/shard_map/ppermute | solution.py:61
  57.9 7.6 %collective-permute-start.19 = (f32[1,160,128]{2,1,0:T(8,128)S(1)}, f32[1,160,128]{2,1,0:T(8,128)S(1)}, u32[]{:S(2)}, u32[]{:S(2)}) collective-permute-start(f32[1,160,128]{2,1,0:T(8,128)S(1)} %shard_map.126.refs_0_), channel_id=1, source_target_pairs={{0,4},{1,5},{2,6},{3,7},{4,0},{5,1},{6,2},{7,3},{8,12},{9,13},{10,... | collective-permute-start | bytes 245768 | tf_op jit(solution)/shard_map/ppermute | solution.py:61
  59.3 6.2 %collective-permute-start.21 = (f32[1,80,128]{2,1,0:T(8,128)S(1)}, f32[1,80,128]{2,1,0:T(8,128)S(1)}, u32[]{:S(2)}, u32[]{:S(2)}) collective-permute-start(f32[1,80,128]{2,1,0:T(8,128)S(1)} %get-tuple-element.65), channel_id=1, source_target_pairs={{0,1},{1,0},{2,3},{3,2},{4,5},{5,4},{6,7},{7,6},{8,9},{9,8},{10,11... | collective-permute-start | bytes 122888 | tf_op jit(solution)/shard_map/ppermute | solution.py:61
  61.0 4.4 %collective-permute-start.22 = (f32[1,80,128]{2,1,0:T(8,128)S(1)}, f32[1,80,128]{2,1,0:T(8,128)S(1)}, u32[]{:S(2)}, u32[]{:S(2)}) collective-permute-start(f32[1,80,128]{2,1,0:T(8,128)S(1)} %get-tuple-element.66), channel_id=1, source_target_pairs={{0,16},{1,17},{2,18},{3,19},{4,20},{5,21},{6,22},{7,23},{8,24},{9,... | collective-permute-start | bytes 122888 | tf_op jit(solution)/shard_map/ppermute | solution.py:61
  62.3 4.9 %collective-permute-start.23 = (f32[1,80,128]{2,1,0:T(8,128)S(1)}, f32[1,80,128]{2,1,0:T(8,128)S(1)}, u32[]{:S(2)}, u32[]{:S(2)}) collective-permute-start(f32[1,80,128]{2,1,0:T(8,128)S(1)} %get-tuple-element.67), channel_id=1, source_target_pairs={{0,17},{1,16},{2,19},{3,18},{4,21},{5,20},{6,23},{7,22},{8,25},{9,... | collective-permute-start | bytes 122888 | tf_op jit(solution)/shard_map/ppermute | solution.py:61
  67.3 4.5 %collective-permute-start.24 = (f32[1,80,128]{2,1,0:T(8,128)S(1)}, f32[1,80,128]{2,1,0:T(8,128)S(1)}, u32[]{:S(2)}, u32[]{:S(2)}) collective-permute-start(f32[1,80,128]{2,1,0:T(8,128)S(1)} %shard_map.128.refs_0_), channel_id=1, source_target_pairs={{0,2},{1,3},{2,0},{3,1},{4,6},{5,7},{6,4},{7,5},{8,10},{9,11},{10,... | collective-permute-start | bytes 122888 | tf_op jit(solution)/shard_map/ppermute | solution.py:61
  69.3 4.9 %collective-permute-start.25 = (f32[1,80,128]{2,1,0:T(8,128)S(1)}, f32[1,80,128]{2,1,0:T(8,128)S(1)}, u32[]{:S(2)}, u32[]{:S(2)}) collective-permute-start(f32[1,80,128]{2,1,0:T(8,128)S(1)} %shard_map.128.refs_0_), channel_id=1, source_target_pairs={{0,4},{1,5},{2,6},{3,7},{4,0},{5,1},{6,2},{7,3},{8,12},{9,13},{10,... | collective-permute-start | bytes 122888 | tf_op jit(solution)/shard_map/ppermute | solution.py:61
  70.6 5.8 %collective-permute-start.26 = (f32[1,80,128]{2,1,0:T(8,128)S(1)}, f32[1,80,128]{2,1,0:T(8,128)S(1)}, u32[]{:S(2)}, u32[]{:S(2)}) collective-permute-start(f32[1,80,128]{2,1,0:T(8,128)S(1)} %shard_map.128.refs_0_), channel_id=1, source_target_pairs={{0,6},{1,7},{2,4},{3,5},{4,2},{5,3},{6,0},{7,1},{8,14},{9,15},{10,... | collective-permute-start | bytes 122888 | tf_op jit(solution)/shard_map/ppermute | solution.py:61
  76.4 4.9 %collective-permute-start.27 = (f32[1,240,128]{2,1,0:T(8,128)S(1)}, f32[1,240,128]{2,1,0:T(8,128)S(1)}, u32[]{:S(2)}, u32[]{:S(2)}) collective-permute-start(f32[1,240,128]{2,1,0:T(8,128)S(1)} %shard_map.131.refs_0_), channel_id=1, source_target_pairs={{0,1},{1,0},{2,3},{3,2},{4,5},{5,4},{6,7},{7,6},{8,9},{9,8},{10,11... | collective-permute-start | bytes 368648 | tf_op jit(solution)/shard_map/ppermute | solution.py:61
  77.0 4.9 %collective-permute-start.28 = (f32[1,240,128]{2,1,0:T(8,128)S(1)}, f32[1,240,128]{2,1,0:T(8,128)S(1)}, u32[]{:S(2)}, u32[]{:S(2)}) collective-permute-start(f32[1,240,128]{2,1,0:T(8,128)S(1)} %shard_map.131.refs_0_), channel_id=1, source_target_pairs={{0,16},{1,17},{2,18},{3,19},{4,20},{5,21},{6,22},{7,23},{8,24},{9,... | collective-permute-start | bytes 368648 | tf_op jit(solution)/shard_map/ppermute | solution.py:61
  78.8 5.8 %collective-permute-start.29 = (f32[1,240,128]{2,1,0:T(8,128)S(1)}, f32[1,240,128]{2,1,0:T(8,128)S(1)}, u32[]{:S(2)}, u32[]{:S(2)}) collective-permute-start(f32[1,240,128]{2,1,0:T(8,128)S(1)} %shard_map.131.refs_0_), channel_id=1, source_target_pairs={{0,17},{1,16},{2,19},{3,18},{4,21},{5,20},{6,23},{7,22},{8,25},{9,... | collective-permute-start | bytes 368648 | tf_op jit(solution)/shard_map/ppermute | solution.py:61
  84.6 1.9 %collective-permute-start.30 = (f32[4,240,128]{2,1,0:T(8,128)S(1)}, f32[4,240,128]{2,1,0:T(8,128)S(1)}, u32[]{:S(2)}, u32[]{:S(2)}) collective-permute-start(f32[4,240,128]{2,1,0:T(8,128)S(1)} %shard_map.132.refs_0_), channel_id=1, source_target_pairs={{0,8},{1,9},{2,10},{3,11},{4,12},{5,13},{6,14},{7,15},{8,0},{9,1},... | collective-permute-start | bytes 1474568 | tf_op jit(solution)/shard_map/ppermute | solution.py:61

commit v10 on v8

--- a/solution.py
+++ b/solution.py
@@ -279,7 +279,7 @@
     return parts[k // size], k % size
 
 
-def coarse_kernel(order, ways, z_count, index_ref, inverse_ref, *refs):
+def coarse_kernel(order, ways, z_count, index_ref, near_ref, inverse_ref, *refs):
     narrow_count, coarse_count, _ = inverse_ref.shape
     packs = refs[: len(refs) - ways - 3]
     outs = refs[len(packs) : len(packs) + ways]
@@ -327,7 +327,7 @@
                 outs[j][k, first : first + EXTRA, :] = target_ref[t]
 
 
-def precond_kernel(index_ref, member_ref, smooth_ref, near_ref, *refs):
+def precond_kernel(index_ref, member_ref, smooth_ref, *refs):
     parts = refs[:-3]
     precond_ref, pair_ref, next_ref = refs[-3:]
     coarse_count = member_ref.shape[1]
@@ -372,7 +372,8 @@
         matrix_ref[0, 2, :, lanes] = (factor * (log_part + square_y * inverse)).astype(jnp.bfloat16)
 
 
-def far_kernel(ways, pair_hbm, next_hbm, matrix_ref, *refs):
+def far_kernel(ways, skip, *refs):
+    matrix_ref, *refs = refs[skip:]
     fields = refs[: len(refs) - ways - 1]
     outs = refs[len(fields) : len(fields) + ways]
     fields_ref = refs[-1]
@@ -667,11 +668,13 @@
         ],
         5,
     )
-    half_parts = flip_each(half_parts, [core])
     near_rows = jnp.transpose(near_block, (0, 2, 1, 3)).reshape(
         panels_dev, 2 * nodes, slot_total * 2 * nodes
     )
-    packs = gather_steps(pack, wide_groups, (weight,))
+    packs = flip_each([pack] * (1 << len(wide_groups[0])), wide_groups[0])
+    pack = join(packs, (weight,))
+    half_send = join(half_parts[1:], (pack,))
+    packs = gather_steps(pack, wide_groups[1:])
     source_rows = high_count * EXTRA // (narrow_count // 2)
     target_rows = 2 * EXTRA
     coarse_outs = pl.pallas_call(
@@ -680,11 +683,11 @@
         ),
         out_shape=[f32(narrow_count // 2, coarse_count + source_rows, rhs_count)] * 2
         + [f32(high_count, EXTRA, point_count), f32(2, EXTRA, point_count)],
-        in_specs=[SMEM, VMEM] + [VMEM] * len(packs),
+        in_specs=[SMEM, ANY, VMEM] + [VMEM] * len(packs),
         out_specs=[VMEM] * 4,
         scratch_shapes=[pltpu.VMEM((wide_count * coarse_count, rhs_count), jnp.float32)],
         compiler_params=PARAMS,
-    )(index, inverse, *packs)
+    )(index, near_rows, inverse, *packs)
     own_sources = coarse_outs[2]
     kept, got = flip_each(coarse_outs[:2], [core])
     groups = in_pairs(across)
@@ -695,11 +698,21 @@
         + [f32(high_count, EXTRA, point_count)],
         (kept, got, coarse_outs[3]),
     )
+    half_parts = flip_each([half_parts[0], half_send], [core])
+    half_parts = sum_parts(half_parts, 2, coarse_parts[:1])
+    half_steps = []
+    for number, mask in enumerate([low] + across + high):
+        got = flip_each(half_parts, [mask])
+        half_steps.append(got[1])
+        half_parts = sum_parts(got, 2 if number < len(across) else 1)
+        if len(half_parts) == 1:
+            half_parts = half_parts * 2
+    half_total = half_parts[0]
     coarse_parts = scatter_steps(coarse_parts, groups)
     precond, pair_edge, next_edge = call(
         precond_kernel,
         [b16(1, 2, point_count, rhs_count)] + [b16(2, width, rhs_count)] * 2,
-        (index, member, smooth, near_rows, *coarse_parts),
+        (index, member, smooth, *coarse_parts),
         1,
     )
     matrix_spec = pl.BlockSpec((1, 3, point_count, source_total), lambda k: (k, 0, 0, 0))
@@ -711,25 +724,25 @@
         out_specs=matrix_spec,
         compiler_params=PARAMS,
     )(own_sources, other_sources, *coarse_parts)
-    fields = flip_each([precond] * (1 << len(source_groups[0])), source_groups[0])
-    half_parts = sum_parts(half_parts, 1 << len(plane_groups[0]), fields[1:])
-    (half_total,) = sum_parts(scatter_steps(half_parts, plane_groups), 1)
-    fields = gather_steps(join(fields, (matrix,)), source_groups[1:])
     device_count = narrow_count * wide_count
     pair_edge = flip(pair_edge, 1)
     pairs = [(i, i + 1) for i in range(1, device_count - 1, 2)]
     next_edge = lax.ppermute(next_edge, AXES, pairs + [(j, i) for i, j in pairs])
-
+    fields = flip_each([precond] * (1 << len(source_groups[0])), source_groups[0])
+    after = (matrix, half_steps[0], pair_edge, next_edge)
+    fields = gather_steps(join(fields, after), source_groups[1:])
+
+    after = (half_steps[1],)
     ways = 1 << len(plane_groups[0])
     far_parts = pl.pallas_call(
-        functools.partial(far_kernel, ways),
+        functools.partial(far_kernel, ways, len(after)),
         out_shape=[f32(target_count // ways, 2, point_count, rhs_count)] * ways,
         grid=(target_count,),
-        in_specs=[ANY, ANY, matrix_spec] + [VMEM] * len(fields),
+        in_specs=[ANY] * len(after) + [matrix_spec] + [VMEM] * len(fields),
         out_specs=[VMEM] * ways,
         scratch_shapes=[pltpu.VMEM((source_total, 2 * rhs_count), jnp.bfloat16)],
         compiler_params=PARAMS,
-    )(pair_edge, next_edge, matrix, *fields)
+    )(*after, matrix, *fields)
     far_parts = scatter_steps(far_parts, plane_groups)
     base = call(
         near_kernel,
@@ -744,17 +757,16 @@
 
     hess_rows = block_total * rhs_count
     sum_rows = hess_rows + rhs_count
-    half_total = sum_butterfly(half_total, high_groups)
     image, *parts = pl.pallas_call(
         functools.partial(project_kernel, masks, 2),
         out_shape=[f32(2, point_count, rhs_count)]
         + [f32(narrow_count, sum_rows // (2 * narrow_count), rhs_count)] * 2,
-        in_specs=[SMEM, ANY] + [VMEM] * (3 + len(far_parts)),
+        in_specs=[SMEM] + [ANY] + [VMEM] * (3 + len(far_parts)),
         out_specs=[VMEM] * 3,
         scratch_shapes=[pltpu.VMEM((sum_rows, rhs_count), jnp.float32)],
         compiler_params=PARAMS,
-    )(index, half_total, weight, basis, base, *far_parts)
-    (total,) = sum_parts(scatter_steps(parts, halving), 1)
+    )(index, half_steps[2], weight, basis, base, *far_parts)
+    (total,) = sum_parts(scatter_steps(parts, halving), 1, half_steps[3:4])
     total = sum_butterfly(total, high_groups)
     parts = gather_steps(append(total, half_total), halving[::-1])
     hessenberg, upper_factor, new_block = call(

time: 90.6 us -> 90.8 us (level)
  waiting for transfers between devices: 27.6 us -> 30.9 us
  starting transfers between devices: 41.9 us -> 38.7 us
    ppermute x32 -> x30, waiting for transfers between devices: 27.5 us -> 30.9 us  [flip(): return lax.ppermute(block, AXES, [(i, i ^ mask) for i in range(count)])]
    ppermute x32 -> x30, starting transfers between devices: 41.3 us -> 38 us  [flip(): return lax.ppermute(block, AXES, [(i, i ^ mask) for i in range(count)])]
  transfers between devices with their start and end apart: 33 -> 31, of which waited for: 19 -> 19; matrix products, arithmetic and copies ran while one was open for 2% -> 2% of each run, Pallas kernels for 10% -> 8%
where the time goes in v10:
time: 90.8 us; the launch traced here: 90.6 us
  starting transfers between devices  38.7 us (43%)
  waiting for transfers between devices  30.9 us (34%)
  Pallas kernels  17.8 us (20%)
  local copies, waits for them, and re-layouts  2.2 us (2%)
  between operations  0.95 us (1%)
    ppermute x30, starting transfers between devices, flip(): return lax.ppermute(block, AXES, [(i, i ^ mask) for i in range(count)])  38 us
    ppermute x30, waiting for transfers between devices, flip(): return lax.ppermute(block, AXES, [(i, i ^ mask) for i in range(count)])  30.9 us
    pallas_call x7, Pallas kernels, call(): pl.pallas_call(kernel, out_shape=out_shape, in_specs=[SMEM] * scalars + [...  12.1 us
    pallas_call x1, Pallas kernels, body(): pl.pallas_call(functools.partial(matrix_kernel, coarse_count), out_shape=...  1.9 us
  transfers between devices with their start and end apart: 31, of which 19 were waited for; matrix products, arithmetic and copies ran while one was open for 2% of the time, Pallas kernels for 8%

profile of v10, /device:TPU:0, one launch (start us, length us, event | category | flops | bytes accessed | tf_op | source)
XLA Modules:
  0.0 90.6 jit_solution(7897578377252321821)
XLA Ops:
  0.6 1.2 %shard_map.112.pack_hbm.refs_1_ = f32[1,56,128]{2,1,0:T(8,128)S(1)} custom-call(s32[2,128]{1,0:T(2,128)} %agg_hbm.3, f32[4,2,128,128]{3,2,1,0:T(8,128)} %basis_ref.3, f32[2,128]{1,0:T(2,128)} %points_hbm.1, f32[1,128]{1,0:T(1,128)} %bitcast.8), custom_call_target="tpu_custom_call" | custom-call | tf_op jit(solution)/shard_map/pallas_call | solution.py:591
  1.8 3.1 %collective-permute-start = (f32[1,56,128]{2,1,0:T(8,128)S(1)}, f32[1,56,128]{2,1,0:T(8,128)S(1)}, u32[]{:S(2)}, u32[]{:S(2)}) collective-permute-start(f32[1,56,128]{2,1,0:T(8,128)S(1)} %shard_map.112.pack_hbm.refs_1_), channel_id=1, source_target_pairs={{0,2},{1,3},{2,0},{3,1},{4,6},{5,7},{6,4},{7,5},{8,10},{9,11},{10,... | collective-permute-start | bytes 86024 | tf_op jit(solution)/shard_map/ppermute | solution.py:61
  4.9 2.6 %collective-permute-start.1 = (f32[1,56,128]{2,1,0:T(8,128)S(1)}, f32[1,56,128]{2,1,0:T(8,128)S(1)}, u32[]{:S(2)}, u32[]{:S(2)}) collective-permute-start(f32[1,56,128]{2,1,0:T(8,128)S(1)} %shard_map.112.pack_hbm.refs_1_), channel_id=1, source_target_pairs={{0,4},{1,5},{2,6},{3,7},{4,0},{5,1},{6,2},{7,3},{8,12},{9,13},{10,... | collective-permute-start | bytes 86024 | tf_op jit(solution)/shard_map/ppermute | solution.py:61
  7.5 0.0 collective-permute-start.2
  7.5 0.1 pad_add_fusion.index_ref
  7.5 2.4 %shard_map.113 = (f32[4,48,384]{2,1,0:T(8,128)S(1)}, f32[2,48,128]{2,1,0:T(8,128)S(1)}, f32[2,128,128]{2,1,0:T(8,128)S(1)}, f32[128,128]{1,0:T(8,128)S(1)}, f32[...) custom-call(s32[3]{0:T(128)S(1)} %pad_add_fusion.index_ref, f32[1,56,128]{2,1,0:T(8,128)S(1)} %shard_map.112.pack_hbm.refs_1_, ...), custom_call_target="tpu_custom_call" | custom-call | tf_op jit(solution)/shard_map/pallas_call | solution.py:591
  10.0 0.1 collective-permute-done.1.refs_3_
  10.1 3.0 %collective-permute-done.2.refs_4_ = f32[1,56,128]{2,1,0:T(8,128)S(1)} collective-permute-done((f32[1,56,128]{2,1,0:T(8,128)S(1)}, f32[1,56,128]{2,1,0:T(8,128)S(1)}, u32[]{:S(2)}, u32[]{:S(2)}) %collective-permute-start.2) | collective-permute-done | bytes 28704 | tf_op jit(solution)/shard_map/ppermute | solution.py:61
  13.2 0.1 collective-permute-start.5
  13.3 1.6 %collective-permute-start.3 = (f32[4,56,128]{2,1,0:T(8,128)S(1)}, f32[4,56,128]{2,1,0:T(8,128)S(1)}, u32[]{:S(2)}, u32[]{:S(2)}) collective-permute-start(f32[4,56,128]{2,1,0:T(8,128)S(1)} %shard_map.114.refs_0_), channel_id=1, source_target_pairs={{0,1},{1,0},{2,3},{3,2},{4,5},{5,4},{6,7},{7,6},{8,9},{9,8},{10,11... | collective-permute-start | bytes 344072 | tf_op jit(solution)/shard_map/ppermute | solution.py:61
  14.8 1.5 %copy.13 = bf16[8,32,12,32]{3,2,1,0:T(8,128)(2,1)S(1)} copy(bf16[8,32,12,32]{3,1,2,0:T(8,128)(2,1)} %bitcast.7) | data formatting | bytes 393216 | tf_op jit(solution)/shard_map/transpose | solution.py:671
  16.3 0.7 reshape.15.near_ref.block_ref
  17.0 1.8 %collective-permute-done.3.refs_1_ = f32[4,56,128]{2,1,0:T(8,128)S(1)} collective-permute-done((f32[4,56,128]{2,1,0:T(8,128)S(1)}, f32[4,56,128]{2,1,0:T(8,128)S(1)}, u32[]{:S(2)}, u32[]{:S(2)}) %collective-permute-start.3) | collective-permute-done | bytes 114720 | tf_op jit(solution)/shard_map/ppermute | solution.py:61
  18.8 0.8 shard_map.115
  19.7 0.1 collective-permute-start.4
  19.7 1.2 %collective-permute-done.4.got_ref = f32[2,64,128]{2,1,0:T(8,128)S(1)} collective-permute-done((f32[2,64,128]{2,1,0:T(8,128)S(1)}, f32[2,64,128]{2,1,0:T(8,128)S(1)}, u32[]{:S(2)}, u32[]{:S(2)}) %collective-permute-start.4) | collective-permute-done | bytes 65568 | tf_op jit(solution)/shard_map/ppermute | solution.py:61
  21.1 1.6 %collective-permute-start.6 = (f32[2,160,128]{2,1,0:T(8,128)S(1)}, f32[2,160,128]{2,1,0:T(8,128)S(1)}, u32[]{:S(2)}, u32[]{:S(2)}) collective-permute-start(f32[2,160,128]{2,1,0:T(8,128)S(1)} %get-tuple-element.46), channel_id=1, source_target_pairs={{0,1},{1,0},{2,3},{3,2},{4,5},{5,4},{6,7},{7,6},{8,9},{9,8},{10,11... | collective-permute-start | bytes 491528 | tf_op jit(solution)/shard_map/ppermute | solution.py:61
  22.6 1.5 %collective-permute-start.9 = (f32[1,64,128]{2,1,0:T(8,128)S(1)}, f32[1,64,128]{2,1,0:T(8,128)S(1)}, u32[]{:S(2)}, u32[]{:S(2)}) collective-permute-start(f32[1,64,128]{2,1,0:T(8,128)S(1)} %get-tuple-element.51), channel_id=1, source_target_pairs={{0,16},{1,17},{2,18},{3,19},{4,20},{5,21},{6,22},{7,23},{8,24},{9,... | collective-permute-start | bytes 98312 | tf_op jit(solution)/shard_map/ppermute | solution.py:61
  24.1 2.4 %collective-permute-done.9.refs_1_ = f32[1,64,128]{2,1,0:T(8,128)S(1)} collective-permute-done((f32[1,64,128]{2,1,0:T(8,128)S(1)}, f32[1,64,128]{2,1,0:T(8,128)S(1)}, u32[]{:S(2)}, u32[]{:S(2)}) %collective-permute-start.9) | collective-permute-done | bytes 32800 | tf_op jit(solution)/shard_map/ppermute | solution.py:61
  26.5 0.8 shard_map.121
  27.3 0.6 collective-permute-start.10
  27.9 1.3 %collective-permute-start.13 = (bf16[1,2,128,128]{3,2,1,0:T(8,128)(2,1)S(1)}, bf16[1,2,128,128]{3,2,1,0:T(8,128)(2,1)S(1)}, u32[]{:S(2)}, u32[]{:S(2)}) collective-permute-start(bf16[1,2,128,128]{3,2,1,0:T(8,128)(2,1)S(1)} %get-tuple-element.52.own_ref.refs_4_), channel_id=1, source_target_pairs={{0,4},{1,5},{2,6},{3,7},{4,0},{5,1},{6,2},{7,3},{8,12},{9,13},{10,... | collective-permute-start | bytes 196616 | tf_op jit(solution)/shard_map/ppermute | solution.py:61
  29.2 3.1 %collective-permute-start.14 = (bf16[1,2,128,128]{3,2,1,0:T(8,128)(2,1)S(1)}, bf16[1,2,128,128]{3,2,1,0:T(8,128)(2,1)S(1)}, u32[]{:S(2)}, u32[]{:S(2)}) collective-permute-start(bf16[1,2,128,128]{3,2,1,0:T(8,128)(2,1)S(1)} %get-tuple-element.52.own_ref.refs_4_), channel_id=1, source_target_pairs={{0,6},{1,7},{2,4},{3,5},{4,2},{5,3},{6,0},{7,1},{8,14},{9,15},{10,... | collective-permute-start | bytes 196616 | tf_op jit(solution)/shard_map/ppermute | solution.py:61
  32.3 0.7 collective-permute-start.11
  33.0 1.9 %shard_map.123.refs_0_.refs_1_ = bf16[4,3,128,1024]{3,2,1,0:T(8,128)(2,1)S(1)} custom-call(f32[4,8,128]{2,1,0:T(8,128)S(1)} %get-tuple-element.55.own_ref, f32[4,8,128]{2,1,0:T(8,128)S(1)} %get-tuple-element.56.other_ref, f32[1,64,128]{2,1,0:T(8,128)S(1)} %get-tuple-element.42.refs_0_, f32[1,64,128]{2,1,0:T(8,128)S(1)} %collective-permute-done.9.refs_1_), custom_call_target="tpu_custom_call" | custom-call | tf_op jit(solution)/shard_map/pallas_call | solution.py:719
  34.9 0.0 copy-start.1
  34.9 0.0 copy-start.2
  34.9 0.7 collective-permute-done.14.refs_7_
  35.6 0.0 copy-start
  35.6 2.4 %collective-permute-start.15 = (bf16[4,2,128,128]{3,2,1,0:T(8,128)(2,1)S(1)}, bf16[4,2,128,128]{3,2,1,0:T(8,128)(2,1)S(1)}, u32[]{:S(2)}, u32[]{:S(2)}) collective-permute-start(bf16[4,2,128,128]{3,2,1,0:T(8,128)(2,1)S(1)} %shard_map.124.refs_2_), channel_id=1, source_target_pairs={{0,8},{1,9},{2,10},{3,11},{4,12},{5,13},{6,14},{7,15},{8,0},{9,1},... | collective-permute-start | bytes 786440 | tf_op jit(solution)/shard_map/ppermute | solution.py:61
  38.1 4.8 %collective-permute-start.7 = (f32[1,160,128]{2,1,0:T(8,128)S(1)}, f32[1,160,128]{2,1,0:T(8,128)S(1)}, u32[]{:S(2)}, u32[]{:S(2)}) collective-permute-start(f32[1,160,128]{2,1,0:T(8,128)S(1)} %get-tuple-element.48), channel_id=1, source_target_pairs={{0,16},{1,17},{2,18},{3,19},{4,20},{5,21},{6,22},{7,23},{8,24},{9,... | collective-permute-start | bytes 245768 | tf_op jit(solution)/shard_map/ppermute | solution.py:61
  42.9 3.1 %collective-permute-done.7.refs_1_.refs_0_ = f32[1,160,128]{2,1,0:T(8,128)S(1)} collective-permute-done((f32[1,160,128]{2,1,0:T(8,128)S(1)}, f32[1,160,128]{2,1,0:T(8,128)S(1)}, u32[]{:S(2)}, u32[]{:S(2)}) %collective-permute-start.7) | collective-permute-done | bytes 81952 | tf_op jit(solution)/shard_map/ppermute | solution.py:61
  46.0 1.7 %shard_map.125 = (f32[1,2,128,128]{3,2,1,0:T(8,128)S(1)}, f32[1,2,128,128]{3,2,1,0:T(8,128)S(1)}, f32[1,2,128,128]{3,2,1,0:T(8,128)S(1)}, f32[1,2,128,128]{3,2,1,0:T(8,128)S(1)}) custom-call(f32[1,160,128]{2,1,0:T(8,128)S(1)} %collective-permute-done.7.refs_1_.refs_0_, bf16[4,3,128,1024]{3,2,1,0:T(8,128)(2,1)S(1)} %shard_map.123.refs_0_.refs_1_, ...), custom_call_target="tpu_custom_call" | custom-call | tf_op jit(solution)/shard_map/pallas_call | solution.py:737
  47.7 0.1 collective-permute-start.16
  47.8 1.8 %collective-permute-start.17 = (f32[1,2,128,128]{3,2,1,0:T(8,128)S(1)}, f32[1,2,128,128]{3,2,1,0:T(8,128)S(1)}, u32[]{:S(2)}, u32[]{:S(2)}) collective-permute-start(f32[1,2,128,128]{3,2,1,0:T(8,128)S(1)} %get-tuple-element.59), channel_id=1, source_target_pairs={{0,16},{1,17},{2,18},{3,19},{4,20},{5,21},{6,22},{7,23},{8,24},{9,... | collective-permute-start | bytes 393224 | tf_op jit(solution)/shard_map/ppermute | solution.py:61
  49.6 1.7 %collective-permute-start.18 = (f32[1,2,128,128]{3,2,1,0:T(8,128)S(1)}, f32[1,2,128,128]{3,2,1,0:T(8,128)S(1)}, u32[]{:S(2)}, u32[]{:S(2)}) collective-permute-start(f32[1,2,128,128]{3,2,1,0:T(8,128)S(1)} %get-tuple-element.60), channel_id=1, source_target_pairs={{0,17},{1,16},{2,19},{3,18},{4,21},{5,20},{6,23},{7,22},{8,25},{9,... | collective-permute-start | bytes 393224 | tf_op jit(solution)/shard_map/ppermute | solution.py:61
  51.2 0.1 collective-permute-start.8
  51.3 1.0 %shard_map.122.base_ref = f32[2,128,128]{2,1,0:T(8,128)S(1)} custom-call(s32[3]{0:T(128)S(1)} %pad_add_fusion.index_ref, s32[8,12]{1,0:T(8,128)S(1)} %copy-done.1, s32[8]{0:T(128)S(1)} %copy-done.2, bf16[8,32,384]{2,1,0:T(8,128)(2,1)S(1)} %reshape.15.near_ref.block_ref, bf16[1,2,128,128]{3,2,1,0:T(8,128)(2,1)S(1)} %get-tuple-element.52.own_ref.refs_4_, ...), custom_call_target="tpu_custom_call" | custom-call | tf_op jit(solution)/shard_map/pallas_call | solution.py:591
  52.4 3.4 %collective-permute-done.8.half_hbm.refs_1_ = f32[1,160,128]{2,1,0:T(8,128)S(1)} collective-permute-done((f32[1,160,128]{2,1,0:T(8,128)S(1)}, f32[1,160,128]{2,1,0:T(8,128)S(1)}, u32[]{:S(2)}, u32[]{:S(2)}) %collective-permute-start.8) | collective-permute-done | bytes 81952 | tf_op jit(solution)/shard_map/ppermute | solution.py:61
  55.8 1.1 %collective-permute-done.18.refs_3_ = f32[1,2,128,128]{3,2,1,0:T(8,128)S(1)} collective-permute-done((f32[1,2,128,128]{3,2,1,0:T(8,128)S(1)}, f32[1,2,128,128]{3,2,1,0:T(8,128)S(1)}, u32[]{:S(2)}, u32[]{:S(2)}) %collective-permute-start.18) | collective-permute-done | bytes 131104 | tf_op jit(solution)/shard_map/ppermute | solution.py:61
  56.8 1.0 %shard_map.126 = (f32[2,128,128]{2,1,0:T(8,128)S(1)}, f32[4,80,128]{2,1,0:T(8,128)S(1)}, f32[4,80,128]{2,1,0:T(8,128)S(1)}) custom-call(s32[3]{0:T(128)S(1)} %pad_add_fusion.index_ref, f32[1,160,128]{2,1,0:T(8,128)S(1)} %collective-permute-done.8.half_hbm.refs_1_, f32[128,128]{1,0:T(8,128)S(1)} %get-tuple-element.38.refs_0_.weight_ref, ...), custom_call_target="tpu_custom_call" | custom-call | tf_op jit(solution)/shard_map/pallas_call | solution.py:760
  57.9 0.1 collective-permute-start.20
  58.0 0.1 collective-permute-start.19
  58.1 1.3 %collective-permute-done.20.refs_1_ = f32[4,80,128]{2,1,0:T(8,128)S(1)} collective-permute-done((f32[4,80,128]{2,1,0:T(8,128)S(1)}, f32[4,80,128]{2,1,0:T(8,128)S(1)}, u32[]{:S(2)}, u32[]{:S(2)}) %collective-permute-start.20) | collective-permute-done | bytes 163872 | tf_op jit(solution)/shard_map/ppermute | solution.py:61
  59.4 0.8 collective-permute-start.21
  60.2 1.5 %collective-permute-start.22 = (f32[1,80,128]{2,1,0:T(8,128)S(1)}, f32[1,80,128]{2,1,0:T(8,128)S(1)}, u32[]{:S(2)}, u32[]{:S(2)}) collective-permute-start(f32[1,80,128]{2,1,0:T(8,128)S(1)} %get-tuple-element.66), channel_id=1, source_target_pairs={{0,16},{1,17},{2,18},{3,19},{4,20},{5,21},{6,22},{7,23},{8,24},{9,... | collective-permute-start | bytes 122888 | tf_op jit(solution)/shard_map/ppermute | solution.py:61
  61.8 1.2 %collective-permute-start.23 = (f32[1,80,128]{2,1,0:T(8,128)S(1)}, f32[1,80,128]{2,1,0:T(8,128)S(1)}, u32[]{:S(2)}, u32[]{:S(2)}) collective-permute-start(f32[1,80,128]{2,1,0:T(8,128)S(1)} %get-tuple-element.67), channel_id=1, source_target_pairs={{0,17},{1,16},{2,19},{3,18},{4,21},{5,20},{6,23},{7,22},{8,25},{9,... | collective-permute-start | bytes 122888 | tf_op jit(solution)/shard_map/ppermute | solution.py:61
  62.9 1.0 %collective-permute-done.19.refs_0_.refs_1_ = f32[1,160,128]{2,1,0:T(8,128)S(1)} collective-permute-done((f32[1,160,128]{2,1,0:T(8,128)S(1)}, f32[1,160,128]{2,1,0:T(8,128)S(1)}, u32[]{:S(2)}, u32[]{:S(2)}) %collective-permute-start.19) | collective-permute-done | bytes 81952 | tf_op jit(solution)/shard_map/ppermute | solution.py:61
  63.9 0.3 collective-permute-done.22.refs_3_
  64.2 2.4 %collective-permute-done.23.refs_4_ = f32[1,80,128]{2,1,0:T(8,128)S(1)} collective-permute-done((f32[1,80,128]{2,1,0:T(8,128)S(1)}, f32[1,80,128]{2,1,0:T(8,128)S(1)}, u32[]{:S(2)}, u32[]{:S(2)}) %collective-permute-start.23) | collective-permute-done | bytes 40992 | tf_op jit(solution)/shard_map/ppermute | solution.py:61
  66.7 0.1 collective-permute-start.24
  66.8 1.7 %collective-permute-start.25 = (f32[1,80,128]{2,1,0:T(8,128)S(1)}, f32[1,80,128]{2,1,0:T(8,128)S(1)}, u32[]{:S(2)}, u32[]{:S(2)}) collective-permute-start(f32[1,80,128]{2,1,0:T(8,128)S(1)} %shard_map.129.refs_0_), channel_id=1, source_target_pairs={{0,4},{1,5},{2,6},{3,7},{4,0},{5,1},{6,2},{7,3},{8,12},{9,13},{10,... | collective-permute-start | bytes 122888 | tf_op jit(solution)/shard_map/ppermute | solution.py:61
  68.5 2.7 %collective-permute-start.26 = (f32[1,80,128]{2,1,0:T(8,128)S(1)}, f32[1,80,128]{2,1,0:T(8,128)S(1)}, u32[]{:S(2)}, u32[]{:S(2)}) collective-permute-start(f32[1,80,128]{2,1,0:T(8,128)S(1)} %shard_map.129.refs_0_), channel_id=1, source_target_pairs={{0,6},{1,7},{2,4},{3,5},{4,2},{5,3},{6,0},{7,1},{8,14},{9,15},{10,... | collective-permute-start | bytes 122888 | tf_op jit(solution)/shard_map/ppermute | solution.py:61
  71.2 0.8 collective-permute-done.25.refs_2_
  71.9 2.3 %collective-permute-done.26.refs_3_ = f32[1,80,128]{2,1,0:T(8,128)S(1)} collective-permute-done((f32[1,80,128]{2,1,0:T(8,128)S(1)}, f32[1,80,128]{2,1,0:T(8,128)S(1)}, u32[]{:S(2)}, u32[]{:S(2)}) %collective-permute-start.26) | collective-permute-done | bytes 40992 | tf_op jit(solution)/shard_map/ppermute | solution.py:61
  74.3 0.5 collective-permute-start.27
  74.8 1.3 %collective-permute-start.28 = (f32[1,240,128]{2,1,0:T(8,128)S(1)}, f32[1,240,128]{2,1,0:T(8,128)S(1)}, u32[]{:S(2)}, u32[]{:S(2)}) collective-permute-start(f32[1,240,128]{2,1,0:T(8,128)S(1)} %shard_map.132.refs_0_), channel_id=1, source_target_pairs={{0,16},{1,17},{2,18},{3,19},{4,20},{5,21},{6,22},{7,23},{8,24},{9,... | collective-permute-start | bytes 368648 | tf_op jit(solution)/shard_map/ppermute | solution.py:61
  76.1 1.8 %collective-permute-start.29 = (f32[1,240,128]{2,1,0:T(8,128)S(1)}, f32[1,240,128]{2,1,0:T(8,128)S(1)}, u32[]{:S(2)}, u32[]{:S(2)}) collective-permute-start(f32[1,240,128]{2,1,0:T(8,128)S(1)} %shard_map.132.refs_0_), channel_id=1, source_target_pairs={{0,17},{1,16},{2,19},{3,18},{4,21},{5,20},{6,23},{7,22},{8,25},{9,... | collective-permute-start | bytes 368648 | tf_op jit(solution)/shard_map/ppermute | solution.py:61
  77.9 1.4 %collective-permute-done.27.refs_1_ = f32[1,240,128]{2,1,0:T(8,128)S(1)} collective-permute-done((f32[1,240,128]{2,1,0:T(8,128)S(1)}, f32[1,240,128]{2,1,0:T(8,128)S(1)}, u32[]{:S(2)}, u32[]{:S(2)}) %collective-permute-start.27) | collective-permute-done | bytes 122912 | tf_op jit(solution)/shard_map/ppermute | solution.py:61
  79.3 0.4 collective-permute-done.28.refs_2_
  79.7 2.2 %collective-permute-done.29.refs_3_ = f32[1,240,128]{2,1,0:T(8,128)S(1)} collective-permute-done((f32[1,240,128]{2,1,0:T(8,128)S(1)}, f32[1,240,128]{2,1,0:T(8,128)S(1)}, u32[]{:S(2)}, u32[]{:S(2)}) %collective-permute-start.29) | collective-permute-done | bytes 122912 | tf_op jit(solution)/shard_map/ppermute | solution.py:61
  81.9 0.1 collective-permute-start.30
  82.0 1.9 %collective-permute-done.30.refs_1_ = f32[4,240,128]{2,1,0:T(8,128)S(1)} collective-permute-done((f32[4,240,128]{2,1,0:T(8,128)S(1)}, f32[4,240,128]{2,1,0:T(8,128)S(1)}, u32[]{:S(2)}, u32[]{:S(2)}) %collective-permute-start.30) | collective-permute-done | bytes 491552 | tf_op jit(solution)/shard_map/ppermute | solution.py:61
  83.9 6.7 %shard_map.134 = (f32[512,128]{1,0:T(8,128)}, f32[128,128]{1,0:T(8,128)}, f32[256,128]{1,0:T(8,128)}) custom-call(s32[3]{0:T(128)S(1)} %pad_add_fusion.index_ref, f32[4,2,128,128]{3,2,1,0:T(8,128)S(1)} %copy-done, f32[2,128,128]{2,1,0:T(8,128)S(1)} %get-tuple-element.61.image_ref, f32[4,240,128]{2,1,0:T(8,128)S(1)} %shard_map.133.refs_0_, ...), custom_call_target="tpu_custom_call" | custom-call | tf_op jit(solution)/shard_map/pallas_call | solution.py:591
  (30 shorter events, 0.3 us)
Async XLA Ops:
  1.8 8.2 %collective-permute-start = (f32[1,56,128]{2,1,0:T(8,128)S(1)}, f32[1,56,128]{2,1,0:T(8,128)S(1)}, u32[]{:S(2)}, u32[]{:S(2)}) collective-permute-start(f32[1,56,128]{2,1,0:T(8,128)S(1)} %shard_map.112.pack_hbm.refs_1_), channel_id=1, source_target_pairs={{0,2},{1,3},{2,0},{3,1},{4,6},{5,7},{6,4},{7,5},{8,10},{9,11},{10,... | collective-permute-start | bytes 86024 | tf_op jit(solution)/shard_map/ppermute | solution.py:61
  4.9 5.2 %collective-permute-start.1 = (f32[1,56,128]{2,1,0:T(8,128)S(1)}, f32[1,56,128]{2,1,0:T(8,128)S(1)}, u32[]{:S(2)}, u32[]{:S(2)}) collective-permute-start(f32[1,56,128]{2,1,0:T(8,128)S(1)} %shard_map.112.pack_hbm.refs_1_), channel_id=1, source_target_pairs={{0,4},{1,5},{2,6},{3,7},{4,0},{5,1},{6,2},{7,3},{8,12},{9,13},{10,... | collective-permute-start | bytes 86024 | tf_op jit(solution)/shard_map/ppermute | solution.py:61
  7.5 5.7 %collective-permute-start.2 = (f32[1,56,128]{2,1,0:T(8,128)S(1)}, f32[1,56,128]{2,1,0:T(8,128)S(1)}, u32[]{:S(2)}, u32[]{:S(2)}) collective-permute-start(f32[1,56,128]{2,1,0:T(8,128)S(1)} %shard_map.112.pack_hbm.refs_1_), channel_id=1, source_target_pairs={{0,6},{1,7},{2,4},{3,5},{4,2},{5,3},{6,0},{7,1},{8,14},{9,15},{10,... | collective-permute-start | bytes 86024 | tf_op jit(solution)/shard_map/ppermute | solution.py:61
  13.2 7.8 %collective-permute-start.5 = (f32[4,160,128]{2,1,0:T(8,128)S(1)}, f32[4,160,128]{2,1,0:T(8,128)S(1)}, u32[]{:S(2)}, u32[]{:S(2)}) collective-permute-start(f32[4,160,128]{2,1,0:T(8,128)S(1)} %shard_map.117), channel_id=1, source_target_pairs={{0,8},{1,9},{2,10},{3,11},{4,12},{5,13},{6,14},{7,15},{8,0},{9,1},... | collective-permute-start | bytes 983048 | tf_op jit(solution)/shard_map/ppermute | solution.py:61
  13.3 5.6 %collective-permute-start.3 = (f32[4,56,128]{2,1,0:T(8,128)S(1)}, f32[4,56,128]{2,1,0:T(8,128)S(1)}, u32[]{:S(2)}, u32[]{:S(2)}) collective-permute-start(f32[4,56,128]{2,1,0:T(8,128)S(1)} %shard_map.114.refs_0_), channel_id=1, source_target_pairs={{0,1},{1,0},{2,3},{3,2},{4,5},{5,4},{6,7},{7,6},{8,9},{9,8},{10,11... | collective-permute-start | bytes 344072 | tf_op jit(solution)/shard_map/ppermute | solution.py:61
  19.7 1.3 %collective-permute-start.4 = (f32[2,64,128]{2,1,0:T(8,128)S(1)}, f32[2,64,128]{2,1,0:T(8,128)S(1)}, u32[]{:S(2)}, u32[]{:S(2)}) collective-permute-start(f32[2,64,128]{2,1,0:T(8,128)S(1)} %get-tuple-element.40), channel_id=1, source_target_pairs={{0,8},{1,9},{2,10},{3,11},{4,12},{5,13},{6,14},{7,15},{8,0},{9,1},... | collective-permute-start | bytes 196616 | tf_op jit(solution)/shard_map/ppermute | solution.py:61
  21.1 14.5 %collective-permute-start.6 = (f32[2,160,128]{2,1,0:T(8,128)S(1)}, f32[2,160,128]{2,1,0:T(8,128)S(1)}, u32[]{:S(2)}, u32[]{:S(2)}) collective-permute-start(f32[2,160,128]{2,1,0:T(8,128)S(1)} %get-tuple-element.46), channel_id=1, source_target_pairs={{0,1},{1,0},{2,3},{3,2},{4,5},{5,4},{6,7},{7,6},{8,9},{9,8},{10,11... | collective-permute-start | bytes 491528 | tf_op jit(solution)/shard_map/ppermute | solution.py:61
  22.6 3.9 %collective-permute-start.9 = (f32[1,64,128]{2,1,0:T(8,128)S(1)}, f32[1,64,128]{2,1,0:T(8,128)S(1)}, u32[]{:S(2)}, u32[]{:S(2)}) collective-permute-start(f32[1,64,128]{2,1,0:T(8,128)S(1)} %get-tuple-element.51), channel_id=1, source_target_pairs={{0,16},{1,17},{2,18},{3,19},{4,20},{5,21},{6,22},{7,23},{8,24},{9,... | collective-permute-start | bytes 98312 | tf_op jit(solution)/shard_map/ppermute | solution.py:61
  27.3 5.0 %collective-permute-start.10 = (bf16[2,64,128]{2,1,0:T(8,128)(2,1)S(1)}, bf16[2,64,128]{2,1,0:T(8,128)(2,1)S(1)}, u32[]{:S(2)}, u32[]{:S(2)}) collective-permute-start(bf16[2,64,128]{2,1,0:T(8,128)(2,1)S(1)} %get-tuple-element.53), channel_id=1, source_target_pairs={{0,1},{1,0},{2,3},{3,2},{4,5},{5,4},{6,7},{7,6},{8,9},{9,8},{10,11... | collective-permute-start | bytes 98312 | tf_op jit(solution)/shard_map/ppermute | solution.py:61
  27.9 7.0 %collective-permute-start.12 = (bf16[1,2,128,128]{3,2,1,0:T(8,128)(2,1)S(1)}, bf16[1,2,128,128]{3,2,1,0:T(8,128)(2,1)S(1)}, u32[]{:S(2)}, u32[]{:S(2)}) collective-permute-start(bf16[1,2,128,128]{3,2,1,0:T(8,128)(2,1)S(1)} %get-tuple-element.52.own_ref.refs_4_), channel_id=1, source_target_pairs={{0,2},{1,3},{2,0},{3,1},{4,6},{5,7},{6,4},{7,5},{8,10},{9,11},{10,... | collective-permute-start | bytes 196616 | tf_op jit(solution)/shard_map/ppermute | solution.py:61
  27.9 7.0 %collective-permute-start.13 = (bf16[1,2,128,128]{3,2,1,0:T(8,128)(2,1)S(1)}, bf16[1,2,128,128]{3,2,1,0:T(8,128)(2,1)S(1)}, u32[]{:S(2)}, u32[]{:S(2)}) collective-permute-start(bf16[1,2,128,128]{3,2,1,0:T(8,128)(2,1)S(1)} %get-tuple-element.52.own_ref.refs_4_), channel_id=1, source_target_pairs={{0,4},{1,5},{2,6},{3,7},{4,0},{5,1},{6,2},{7,3},{8,12},{9,13},{10,... | collective-permute-start | bytes 196616 | tf_op jit(solution)/shard_map/ppermute | solution.py:61
  29.2 6.4 %collective-permute-start.14 = (bf16[1,2,128,128]{3,2,1,0:T(8,128)(2,1)S(1)}, bf16[1,2,128,128]{3,2,1,0:T(8,128)(2,1)S(1)}, u32[]{:S(2)}, u32[]{:S(2)}) collective-permute-start(bf16[1,2,128,128]{3,2,1,0:T(8,128)(2,1)S(1)} %get-tuple-element.52.own_ref.refs_4_), channel_id=1, source_target_pairs={{0,6},{1,7},{2,4},{3,5},{4,2},{5,3},{6,0},{7,1},{8,14},{9,15},{10,... | collective-permute-start | bytes 196616 | tf_op jit(solution)/shard_map/ppermute | solution.py:61
  32.3 2.6 %collective-permute-start.11 = (bf16[2,64,128]{2,1,0:T(8,128)(2,1)S(1)}, bf16[2,64,128]{2,1,0:T(8,128)(2,1)S(1)}, u32[]{:S(2)}, u32[]{:S(2)}) collective-permute-start(bf16[2,64,128]{2,1,0:T(8,128)(2,1)S(1)} %get-tuple-element.54), channel_id=1, source_target_pairs={{1,2},{3,4},{5,6},{7,8},{9,10},{11,12},{13,14},{15,16},{17,18},{19... | collective-permute-start | bytes 98312 | tf_op jit(solution)/shard_map/ppermute | solution.py:730
  34.9 16.5 %copy-start.1 = (s32[8,12]{1,0:T(8,128)S(1)}, s32[8,12]{1,0:T(8,128)}, u32[]{:S(2)}) copy-start(s32[8,12]{1,0:T(8,128)} %panel_ref.1) | copy-start | bytes 1156
  34.9 16.5 %copy-start.2 = (s32[8]{0:T(128)S(1)}, s32[8]{0:T(128)}, u32[]{:S(2)}) copy-start(s32[8]{0:T(128)} %count_ref.1) | copy-start | bytes 100
  35.6 21.2 %copy-start = (f32[4,2,128,128]{3,2,1,0:T(8,128)S(1)}, f32[4,2,128,128]{3,2,1,0:T(8,128)}, u32[]{:S(2)}) copy-start(f32[4,2,128,128]{3,2,1,0:T(8,128)} %basis_ref.3) | copy-start | bytes 1572868
  35.6 10.3 %collective-permute-start.15 = (bf16[4,2,128,128]{3,2,1,0:T(8,128)(2,1)S(1)}, bf16[4,2,128,128]{3,2,1,0:T(8,128)(2,1)S(1)}, u32[]{:S(2)}, u32[]{:S(2)}) collective-permute-start(bf16[4,2,128,128]{3,2,1,0:T(8,128)(2,1)S(1)} %shard_map.124.refs_2_), channel_id=1, source_target_pairs={{0,8},{1,9},{2,10},{3,11},{4,12},{5,13},{6,14},{7,15},{8,0},{9,1},... | collective-permute-start | bytes 786440 | tf_op jit(solution)/shard_map/ppermute | solution.py:61
  38.1 7.9 %collective-permute-start.7 = (f32[1,160,128]{2,1,0:T(8,128)S(1)}, f32[1,160,128]{2,1,0:T(8,128)S(1)}, u32[]{:S(2)}, u32[]{:S(2)}) collective-permute-start(f32[1,160,128]{2,1,0:T(8,128)S(1)} %get-tuple-element.48), channel_id=1, source_target_pairs={{0,16},{1,17},{2,18},{3,19},{4,20},{5,21},{6,22},{7,23},{8,24},{9,... | collective-permute-start | bytes 245768 | tf_op jit(solution)/shard_map/ppermute | solution.py:61
  47.7 8.1 %collective-permute-start.16 = (f32[1,2,128,128]{3,2,1,0:T(8,128)S(1)}, f32[1,2,128,128]{3,2,1,0:T(8,128)S(1)}, u32[]{:S(2)}, u32[]{:S(2)}) collective-permute-start(f32[1,2,128,128]{3,2,1,0:T(8,128)S(1)} %get-tuple-element.58), channel_id=1, source_target_pairs={{0,1},{1,0},{2,3},{3,2},{4,5},{5,4},{6,7},{7,6},{8,9},{9,8},{10,11... | collective-permute-start | bytes 393224 | tf_op jit(solution)/shard_map/ppermute | solution.py:61
  47.8 8.0 %collective-permute-start.17 = (f32[1,2,128,128]{3,2,1,0:T(8,128)S(1)}, f32[1,2,128,128]{3,2,1,0:T(8,128)S(1)}, u32[]{:S(2)}, u32[]{:S(2)}) collective-permute-start(f32[1,2,128,128]{3,2,1,0:T(8,128)S(1)} %get-tuple-element.59), channel_id=1, source_target_pairs={{0,16},{1,17},{2,18},{3,19},{4,20},{5,21},{6,22},{7,23},{8,24},{9,... | collective-permute-start | bytes 393224 | tf_op jit(solution)/shard_map/ppermute | solution.py:61
  49.6 7.3 %collective-permute-start.18 = (f32[1,2,128,128]{3,2,1,0:T(8,128)S(1)}, f32[1,2,128,128]{3,2,1,0:T(8,128)S(1)}, u32[]{:S(2)}, u32[]{:S(2)}) collective-permute-start(f32[1,2,128,128]{3,2,1,0:T(8,128)S(1)} %get-tuple-element.60), channel_id=1, source_target_pairs={{0,17},{1,16},{2,19},{3,18},{4,21},{5,20},{6,23},{7,22},{8,25},{9,... | collective-permute-start | bytes 393224 | tf_op jit(solution)/shard_map/ppermute | solution.py:61
  51.2 4.5 %collective-permute-start.8 = (f32[1,160,128]{2,1,0:T(8,128)S(1)}, f32[1,160,128]{2,1,0:T(8,128)S(1)}, u32[]{:S(2)}, u32[]{:S(2)}) collective-permute-start(f32[1,160,128]{2,1,0:T(8,128)S(1)} %shard_map.120.refs_0_), channel_id=1, source_target_pairs={{0,2},{1,3},{2,0},{3,1},{4,6},{5,7},{6,4},{7,5},{8,10},{9,11},{10,... | collective-permute-start | bytes 245768 | tf_op jit(solution)/shard_map/ppermute | solution.py:61
  57.9 1.5 %collective-permute-start.20 = (f32[4,80,128]{2,1,0:T(8,128)S(1)}, f32[4,80,128]{2,1,0:T(8,128)S(1)}, u32[]{:S(2)}, u32[]{:S(2)}) collective-permute-start(f32[4,80,128]{2,1,0:T(8,128)S(1)} %get-tuple-element.63), channel_id=1, source_target_pairs={{0,8},{1,9},{2,10},{3,11},{4,12},{5,13},{6,14},{7,15},{8,0},{9,1},... | collective-permute-start | bytes 491528 | tf_op jit(solution)/shard_map/ppermute | solution.py:61
  58.0 5.9 %collective-permute-start.19 = (f32[1,160,128]{2,1,0:T(8,128)S(1)}, f32[1,160,128]{2,1,0:T(8,128)S(1)}, u32[]{:S(2)}, u32[]{:S(2)}) collective-permute-start(f32[1,160,128]{2,1,0:T(8,128)S(1)} %shard_map.127.refs_0_), channel_id=1, source_target_pairs={{0,4},{1,5},{2,6},{3,7},{4,0},{5,1},{6,2},{7,3},{8,12},{9,13},{10,... | collective-permute-start | bytes 245768 | tf_op jit(solution)/shard_map/ppermute | solution.py:61
  59.4 4.6 %collective-permute-start.21 = (f32[1,80,128]{2,1,0:T(8,128)S(1)}, f32[1,80,128]{2,1,0:T(8,128)S(1)}, u32[]{:S(2)}, u32[]{:S(2)}) collective-permute-start(f32[1,80,128]{2,1,0:T(8,128)S(1)} %get-tuple-element.65), channel_id=1, source_target_pairs={{0,1},{1,0},{2,3},{3,2},{4,5},{5,4},{6,7},{7,6},{8,9},{9,8},{10,11... | collective-permute-start | bytes 122888 | tf_op jit(solution)/shard_map/ppermute | solution.py:61
  60.2 4.0 %collective-permute-start.22 = (f32[1,80,128]{2,1,0:T(8,128)S(1)}, f32[1,80,128]{2,1,0:T(8,128)S(1)}, u32[]{:S(2)}, u32[]{:S(2)}) collective-permute-start(f32[1,80,128]{2,1,0:T(8,128)S(1)} %get-tuple-element.66), channel_id=1, source_target_pairs={{0,16},{1,17},{2,18},{3,19},{4,20},{5,21},{6,22},{7,23},{8,24},{9,... | collective-permute-start | bytes 122888 | tf_op jit(solution)/shard_map/ppermute | solution.py:61
  61.8 4.9 %collective-permute-start.23 = (f32[1,80,128]{2,1,0:T(8,128)S(1)}, f32[1,80,128]{2,1,0:T(8,128)S(1)}, u32[]{:S(2)}, u32[]{:S(2)}) collective-permute-start(f32[1,80,128]{2,1,0:T(8,128)S(1)} %get-tuple-element.67), channel_id=1, source_target_pairs={{0,17},{1,16},{2,19},{3,18},{4,21},{5,20},{6,23},{7,22},{8,25},{9,... | collective-permute-start | bytes 122888 | tf_op jit(solution)/shard_map/ppermute | solution.py:61
  66.7 4.5 %collective-permute-start.24 = (f32[1,80,128]{2,1,0:T(8,128)S(1)}, f32[1,80,128]{2,1,0:T(8,128)S(1)}, u32[]{:S(2)}, u32[]{:S(2)}) collective-permute-start(f32[1,80,128]{2,1,0:T(8,128)S(1)} %shard_map.129.refs_0_), channel_id=1, source_target_pairs={{0,2},{1,3},{2,0},{3,1},{4,6},{5,7},{6,4},{7,5},{8,10},{9,11},{10,... | collective-permute-start | bytes 122888 | tf_op jit(solution)/shard_map/ppermute | solution.py:61
  66.8 5.2 %collective-permute-start.25 = (f32[1,80,128]{2,1,0:T(8,128)S(1)}, f32[1,80,128]{2,1,0:T(8,128)S(1)}, u32[]{:S(2)}, u32[]{:S(2)}) collective-permute-start(f32[1,80,128]{2,1,0:T(8,128)S(1)} %shard_map.129.refs_0_), channel_id=1, source_target_pairs={{0,4},{1,5},{2,6},{3,7},{4,0},{5,1},{6,2},{7,3},{8,12},{9,13},{10,... | collective-permute-start | bytes 122888 | tf_op jit(solution)/shard_map/ppermute | solution.py:61
  68.5 5.8 %collective-permute-start.26 = (f32[1,80,128]{2,1,0:T(8,128)S(1)}, f32[1,80,128]{2,1,0:T(8,128)S(1)}, u32[]{:S(2)}, u32[]{:S(2)}) collective-permute-start(f32[1,80,128]{2,1,0:T(8,128)S(1)} %shard_map.129.refs_0_), channel_id=1, source_target_pairs={{0,6},{1,7},{2,4},{3,5},{4,2},{5,3},{6,0},{7,1},{8,14},{9,15},{10,... | collective-permute-start | bytes 122888 | tf_op jit(solution)/shard_map/ppermute | solution.py:61
  74.3 4.9 %collective-permute-start.27 = (f32[1,240,128]{2,1,0:T(8,128)S(1)}, f32[1,240,128]{2,1,0:T(8,128)S(1)}, u32[]{:S(2)}, u32[]{:S(2)}) collective-permute-start(f32[1,240,128]{2,1,0:T(8,128)S(1)} %shard_map.132.refs_0_), channel_id=1, source_target_pairs={{0,1},{1,0},{2,3},{3,2},{4,5},{5,4},{6,7},{7,6},{8,9},{9,8},{10,11... | collective-permute-start | bytes 368648 | tf_op jit(solution)/shard_map/ppermute | solution.py:61
  74.8 4.9 %collective-permute-start.28 = (f32[1,240,128]{2,1,0:T(8,128)S(1)}, f32[1,240,128]{2,1,0:T(8,128)S(1)}, u32[]{:S(2)}, u32[]{:S(2)}) collective-permute-start(f32[1,240,128]{2,1,0:T(8,128)S(1)} %shard_map.132.refs_0_), channel_id=1, source_target_pairs={{0,16},{1,17},{2,18},{3,19},{4,20},{5,21},{6,22},{7,23},{8,24},{9,... | collective-permute-start | bytes 368648 | tf_op jit(solution)/shard_map/ppermute | solution.py:61
  76.1 5.8 %collective-permute-start.29 = (f32[1,240,128]{2,1,0:T(8,128)S(1)}, f32[1,240,128]{2,1,0:T(8,128)S(1)}, u32[]{:S(2)}, u32[]{:S(2)}) collective-permute-start(f32[1,240,128]{2,1,0:T(8,128)S(1)} %shard_map.132.refs_0_), channel_id=1, source_target_pairs={{0,17},{1,16},{2,19},{3,18},{4,21},{5,20},{6,23},{7,22},{8,25},{9,... | collective-permute-start | bytes 368648 | tf_op jit(solution)/shard_map/ppermute | solution.py:61
  81.9 1.9 %collective-permute-start.30 = (f32[4,240,128]{2,1,0:T(8,128)S(1)}, f32[4,240,128]{2,1,0:T(8,128)S(1)}, u32[]{:S(2)}, u32[]{:S(2)}) collective-permute-start(f32[4,240,128]{2,1,0:T(8,128)S(1)} %shard_map.133.refs_0_), channel_id=1, source_target_pairs={{0,8},{1,9},{2,10},{3,11},{4,12},{5,13},{6,14},{7,15},{8,0},{9,1},... | collective-permute-start | bytes 1474568 | tf_op jit(solution)/shard_map/ppermute | solution.py:61

commit v11 on v10

--- a/solution.py
+++ b/solution.py
@@ -327,7 +327,7 @@
                 outs[j][k, first : first + EXTRA, :] = target_ref[t]
 
 
-def precond_kernel(index_ref, member_ref, smooth_ref, *refs):
+def precond_kernel(index_ref, half_hbm, member_ref, smooth_ref, *refs):
     parts = refs[:-3]
     precond_ref, pair_ref, next_ref = refs[-3:]
     coarse_count = member_ref.shape[1]
@@ -699,7 +699,7 @@
         (kept, got, coarse_outs[3]),
     )
     half_parts = flip_each([half_parts[0], half_send], [core])
-    half_parts = sum_parts(half_parts, 2, coarse_parts[:1])
+    half_parts = sum_parts(half_parts, 2)
     half_steps = []
     for number, mask in enumerate([low] + across + high):
         got = flip_each(half_parts, [mask])
@@ -709,12 +709,13 @@
             half_parts = half_parts * 2
     half_total = half_parts[0]
     coarse_parts = scatter_steps(coarse_parts, groups)
-    precond, pair_edge, next_edge = call(
+    precond, pair_edge, next_edge = pl.pallas_call(
         precond_kernel,
-        [b16(1, 2, point_count, rhs_count)] + [b16(2, width, rhs_count)] * 2,
-        (index, member, smooth, *coarse_parts),
-        1,
-    )
+        out_shape=[b16(1, 2, point_count, rhs_count)] + [b16(2, width, rhs_count)] * 2,
+        in_specs=[SMEM, ANY] + [VMEM] * (2 + len(coarse_parts)),
+        out_specs=[VMEM] * 3,
+        compiler_params=PARAMS,
+    )(index, half_steps[0], member, smooth, *coarse_parts)
     matrix_spec = pl.BlockSpec((1, 3, point_count, source_total), lambda k: (k, 0, 0, 0))
     matrix = pl.pallas_call(
         functools.partial(matrix_kernel, coarse_count),
@@ -729,10 +730,10 @@
     pairs = [(i, i + 1) for i in range(1, device_count - 1, 2)]
     next_edge = lax.ppermute(next_edge, AXES, pairs + [(j, i) for i, j in pairs])
     fields = flip_each([precond] * (1 << len(source_groups[0])), source_groups[0])
-    after = (matrix, half_steps[0], pair_edge, next_edge)
+    after = (matrix, half_steps[1], pair_edge, next_edge)
     fields = gather_steps(join(fields, after), source_groups[1:])
 
-    after = (half_steps[1],)
+    after = ()
     ways = 1 << len(plane_groups[0])
     far_parts = pl.pallas_call(
         functools.partial(far_kernel, ways, len(after)),

time: 90.8 us -> 87.9 us (0.968)
  waiting for transfers between devices: 30.9 us -> 28.7 us
  local copies, waits for them, and re-layouts: 2.2 us -> 1.07 us
    ppermute x30, waiting for transfers between devices: 30.9 us -> 28.7 us  [flip(): return lax.ppermute(block, AXES, [(i, i ^ mask) for i in range(count)])]
    transpose x1, local copies, waits for them, and re-layouts: 1.47 us -> 0.34 us  [body(): jnp.transpose(near_block, (0, 2, 1, 3))]
    pallas_call x7 -> x6, Pallas kernels: 12.1 us -> 11.4 us  [call(): pl.pallas_call(kernel, out_shape=out_shape, in_specs=[SMEM] * scalars + [...]
  transfers between devices with their start and end apart: 31 -> 31, of which waited for: 19 -> 20; matrix products, arithmetic and copies ran while one was open for 2% -> 1% of each run, Pallas kernels for 8% -> 8%
where the time goes in v11:
time: 87.9 us; the launch traced here: 87.8 us
  starting transfers between devices  39.1 us (44%)
  waiting for transfers between devices  28.7 us (33%)
  Pallas kernels  17.8 us (20%)
  local copies, waits for them, and re-layouts  1.07 us (1%)
  between operations  0.93 us (1%)
    ppermute x30, starting transfers between devices, flip(): return lax.ppermute(block, AXES, [(i, i ^ mask) for i in range(count)])  38.5 us
    ppermute x30, waiting for transfers between devices, flip(): return lax.ppermute(block, AXES, [(i, i ^ mask) for i in range(count)])  28.7 us
    pallas_call x6, Pallas kernels, call(): pl.pallas_call(kernel, out_shape=out_shape, in_specs=[SMEM] * scalars + [...  11.4 us
    pallas_call x1, Pallas kernels, body(): pl.pallas_call(functools.partial(matrix_kernel, coarse_count), out_shape=...  1.9 us
  transfers between devices with their start and end apart: 31, of which 20 were waited for; matrix products, arithmetic and copies ran while one was open for 1% of the time, Pallas kernels for 8%

profile of v11, /device:TPU:0, one launch (start us, length us, event | category | flops | bytes accessed | tf_op | source)
XLA Modules:
  0.0 87.8 jit_solution(13686174466444459063)
XLA Ops:
  0.6 1.2 %shard_map.112.pack_hbm.refs_1_ = f32[1,56,128]{2,1,0:T(8,128)S(1)} custom-call(s32[2,128]{1,0:T(2,128)} %agg_hbm.3, f32[4,2,128,128]{3,2,1,0:T(8,128)} %basis_ref.3, f32[2,128]{1,0:T(2,128)} %points_hbm.1, f32[1,128]{1,0:T(1,128)} %bitcast.8), custom_call_target="tpu_custom_call" | custom-call | tf_op jit(solution)/shard_map/pallas_call | solution.py:591
  1.9 3.1 %collective-permute-start = (f32[1,56,128]{2,1,0:T(8,128)S(1)}, f32[1,56,128]{2,1,0:T(8,128)S(1)}, u32[]{:S(2)}, u32[]{:S(2)}) collective-permute-start(f32[1,56,128]{2,1,0:T(8,128)S(1)} %shard_map.112.pack_hbm.refs_1_), channel_id=1, source_target_pairs={{0,2},{1,3},{2,0},{3,1},{4,6},{5,7},{6,4},{7,5},{8,10},{9,11},{10,... | collective-permute-start | bytes 86024 | tf_op jit(solution)/shard_map/ppermute | solution.py:61
  5.0 2.6 %collective-permute-start.1 = (f32[1,56,128]{2,1,0:T(8,128)S(1)}, f32[1,56,128]{2,1,0:T(8,128)S(1)}, u32[]{:S(2)}, u32[]{:S(2)}) collective-permute-start(f32[1,56,128]{2,1,0:T(8,128)S(1)} %shard_map.112.pack_hbm.refs_1_), channel_id=1, source_target_pairs={{0,4},{1,5},{2,6},{3,7},{4,0},{5,1},{6,2},{7,3},{8,12},{9,13},{10,... | collective-permute-start | bytes 86024 | tf_op jit(solution)/shard_map/ppermute | solution.py:61
  7.6 0.1 pad_add_fusion.index_ref
  7.6 2.4 %shard_map.113 = (f32[4,48,384]{2,1,0:T(8,128)S(1)}, f32[2,48,128]{2,1,0:T(8,128)S(1)}, f32[2,128,128]{2,1,0:T(8,128)S(1)}, f32[128,128]{1,0:T(8,128)S(1)}, f32[...) custom-call(s32[3]{0:T(128)S(1)} %pad_add_fusion.index_ref, f32[1,56,128]{2,1,0:T(8,128)S(1)} %shard_map.112.pack_hbm.refs_1_, ...), custom_call_target="tpu_custom_call" | custom-call | tf_op jit(solution)/shard_map/pallas_call | solution.py:591
  10.1 0.1 collective-permute-done.1.refs_3_
  10.2 3.0 %collective-permute-done.2.refs_4_ = f32[1,56,128]{2,1,0:T(8,128)S(1)} collective-permute-done((f32[1,56,128]{2,1,0:T(8,128)S(1)}, f32[1,56,128]{2,1,0:T(8,128)S(1)}, u32[]{:S(2)}, u32[]{:S(2)}) %collective-permute-start.2) | collective-permute-done | bytes 28704 | tf_op jit(solution)/shard_map/ppermute | solution.py:61
  13.3 0.1 collective-permute-start.3
  13.3 1.6 %collective-permute-start.7 = (f32[4,56,128]{2,1,0:T(8,128)S(1)}, f32[4,56,128]{2,1,0:T(8,128)S(1)}, u32[]{:S(2)}, u32[]{:S(2)}) collective-permute-start(f32[4,56,128]{2,1,0:T(8,128)S(1)} %shard_map.114.refs_0_), channel_id=1, source_target_pairs={{0,1},{1,0},{2,3},{3,2},{4,5},{5,4},{6,7},{7,6},{8,9},{9,8},{10,11... | collective-permute-start | bytes 344072 | tf_op jit(solution)/shard_map/ppermute | solution.py:61
  14.9 0.1 collective-permute-done.3.refs_1_
  15.0 1.6 %collective-permute-start.4 = (f32[2,160,128]{2,1,0:T(8,128)S(1)}, f32[2,160,128]{2,1,0:T(8,128)S(1)}, u32[]{:S(2)}, u32[]{:S(2)}) collective-permute-start(f32[2,160,128]{2,1,0:T(8,128)S(1)} %get-tuple-element.41), channel_id=1, source_target_pairs={{0,1},{1,0},{2,3},{3,2},{4,5},{5,4},{6,7},{7,6},{8,9},{9,8},{10,11... | collective-permute-start | bytes 491528 | tf_op jit(solution)/shard_map/ppermute | solution.py:61
  16.6 0.3 copy.13
  16.9 0.7 reshape.15.near_ref.block_ref
  17.6 1.7 %collective-permute-done.7.refs_1_ = f32[4,56,128]{2,1,0:T(8,128)S(1)} collective-permute-done((f32[4,56,128]{2,1,0:T(8,128)S(1)}, f32[4,56,128]{2,1,0:T(8,128)S(1)}, u32[]{:S(2)}, u32[]{:S(2)}) %collective-permute-start.7) | collective-permute-done | bytes 114720 | tf_op jit(solution)/shard_map/ppermute | solution.py:61
  19.4 0.8 shard_map.119
  20.2 0.1 collective-permute-start.8
  20.3 1.2 %collective-permute-done.8.got_ref = f32[2,64,128]{2,1,0:T(8,128)S(1)} collective-permute-done((f32[2,64,128]{2,1,0:T(8,128)S(1)}, f32[2,64,128]{2,1,0:T(8,128)S(1)}, u32[]{:S(2)}, u32[]{:S(2)}) %collective-permute-start.8) | collective-permute-done | bytes 65568 | tf_op jit(solution)/shard_map/ppermute | solution.py:61
  21.5 1.6 %collective-permute-start.9 = (f32[1,64,128]{2,1,0:T(8,128)S(1)}, f32[1,64,128]{2,1,0:T(8,128)S(1)}, u32[]{:S(2)}, u32[]{:S(2)}) collective-permute-start(f32[1,64,128]{2,1,0:T(8,128)S(1)} %get-tuple-element.51), channel_id=1, source_target_pairs={{0,16},{1,17},{2,18},{3,19},{4,20},{5,21},{6,22},{7,23},{8,24},{9,... | collective-permute-start | bytes 98312 | tf_op jit(solution)/shard_map/ppermute | solution.py:61
  23.1 0.9 %collective-permute-start.5 = (f32[1,160,128]{2,1,0:T(8,128)S(1)}, f32[1,160,128]{2,1,0:T(8,128)S(1)}, u32[]{:S(2)}, u32[]{:S(2)}) collective-permute-start(f32[1,160,128]{2,1,0:T(8,128)S(1)} %get-tuple-element.43), channel_id=1, source_target_pairs={{0,16},{1,17},{2,18},{3,19},{4,20},{5,21},{6,22},{7,23},{8,24},{9,... | collective-permute-start | bytes 245768 | tf_op jit(solution)/shard_map/ppermute | solution.py:61
  24.0 1.5 %collective-permute-done.9.refs_1_ = f32[1,64,128]{2,1,0:T(8,128)S(1)} collective-permute-done((f32[1,64,128]{2,1,0:T(8,128)S(1)}, f32[1,64,128]{2,1,0:T(8,128)S(1)}, u32[]{:S(2)}, u32[]{:S(2)}) %collective-permute-start.9) | collective-permute-done | bytes 32800 | tf_op jit(solution)/shard_map/ppermute | solution.py:61
  25.5 0.8 shard_map.121
  26.3 1.6 %collective-permute-start.10 = (bf16[2,64,128]{2,1,0:T(8,128)(2,1)S(1)}, bf16[2,64,128]{2,1,0:T(8,128)(2,1)S(1)}, u32[]{:S(2)}, u32[]{:S(2)}) collective-permute-start(bf16[2,64,128]{2,1,0:T(8,128)(2,1)S(1)} %get-tuple-element.53), channel_id=1, source_target_pairs={{0,1},{1,0},{2,3},{3,2},{4,5},{5,4},{6,7},{7,6},{8,9},{9,8},{10,11... | collective-permute-start | bytes 98312 | tf_op jit(solution)/shard_map/ppermute | solution.py:61
  27.9 1.3 %collective-permute-start.13 = (bf16[1,2,128,128]{3,2,1,0:T(8,128)(2,1)S(1)}, bf16[1,2,128,128]{3,2,1,0:T(8,128)(2,1)S(1)}, u32[]{:S(2)}, u32[]{:S(2)}) collective-permute-start(bf16[1,2,128,128]{3,2,1,0:T(8,128)(2,1)S(1)} %get-tuple-element.52.own_ref.refs_4_), channel_id=1, source_target_pairs={{0,4},{1,5},{2,6},{3,7},{4,0},{5,1},{6,2},{7,3},{8,12},{9,13},{10,... | collective-permute-start | bytes 196616 | tf_op jit(solution)/shard_map/ppermute | solution.py:61
  29.1 3.1 %collective-permute-start.14 = (bf16[1,2,128,128]{3,2,1,0:T(8,128)(2,1)S(1)}, bf16[1,2,128,128]{3,2,1,0:T(8,128)(2,1)S(1)}, u32[]{:S(2)}, u32[]{:S(2)}) collective-permute-start(bf16[1,2,128,128]{3,2,1,0:T(8,128)(2,1)S(1)} %get-tuple-element.52.own_ref.refs_4_), channel_id=1, source_target_pairs={{0,6},{1,7},{2,4},{3,5},{4,2},{5,3},{6,0},{7,1},{8,14},{9,15},{10,... | collective-permute-start | bytes 196616 | tf_op jit(solution)/shard_map/ppermute | solution.py:61
  32.2 0.7 collective-permute-start.11
  32.9 1.9 %shard_map.123.refs_0_ = bf16[4,3,128,1024]{3,2,1,0:T(8,128)(2,1)S(1)} custom-call(f32[4,8,128]{2,1,0:T(8,128)S(1)} %get-tuple-element.55.own_ref, f32[4,8,128]{2,1,0:T(8,128)S(1)} %get-tuple-element.56.other_ref, f32[1,64,128]{2,1,0:T(8,128)S(1)} %get-tuple-element.50.refs_0_, f32[1,64,128]{2,1,0:T(8,128)S(1)} %collective-permute-done.9.refs_1_), custom_call_target="tpu_custom_call" | custom-call | tf_op jit(solution)/shard_map/pallas_call | solution.py:720
  34.8 0.0 copy-start.1
  34.8 0.0 copy-start.2
  34.9 0.7 collective-permute-done.14.refs_7_
  35.6 0.0 copy-start
  35.6 2.6 %collective-permute-start.15 = (bf16[4,2,128,128]{3,2,1,0:T(8,128)(2,1)S(1)}, bf16[4,2,128,128]{3,2,1,0:T(8,128)(2,1)S(1)}, u32[]{:S(2)}, u32[]{:S(2)}) collective-permute-start(bf16[4,2,128,128]{3,2,1,0:T(8,128)(2,1)S(1)} %shard_map.124.refs_1_), channel_id=1, source_target_pairs={{0,8},{1,9},{2,10},{3,11},{4,12},{5,13},{6,14},{7,15},{8,0},{9,1},... | collective-permute-start | bytes 786440 | tf_op jit(solution)/shard_map/ppermute | solution.py:61
  38.2 1.2 %collective-permute-done.15.refs_2_ = bf16[4,2,128,128]{3,2,1,0:T(8,128)(2,1)S(1)} collective-permute-done((bf16[4,2,128,128]{3,2,1,0:T(8,128)(2,1)S(1)}, bf16[4,2,128,128]{3,2,1,0:T(8,128)(2,1)S(1)}, u32[]{:S(2)}, u32[]{:S(2)}) %collective-permute-start.15) | collective-permute-done | bytes 262176 | tf_op jit(solution)/shard_map/ppermute | solution.py:61
  39.3 1.7 %shard_map.125 = (f32[1,2,128,128]{3,2,1,0:T(8,128)S(1)}, f32[1,2,128,128]{3,2,1,0:T(8,128)S(1)}, f32[1,2,128,128]{3,2,1,0:T(8,128)S(1)}, f32[1,2,128,128]{3,2,1,0:T(8,128)S(1)}) custom-call(bf16[4,3,128,1024]{3,2,1,0:T(8,128)(2,1)S(1)} %shard_map.123.refs_0_, bf16[4,2,128,128]{3,2,1,0:T(8,128)(2,1)S(1)} %shard_map.124.refs_1_, ...), custom_call_target="tpu_custom_call" | custom-call | tf_op jit(solution)/shard_map/pallas_call | solution.py:738
  41.0 1.9 %collective-permute-start.16 = (f32[1,2,128,128]{3,2,1,0:T(8,128)S(1)}, f32[1,2,128,128]{3,2,1,0:T(8,128)S(1)}, u32[]{:S(2)}, u32[]{:S(2)}) collective-permute-start(f32[1,2,128,128]{3,2,1,0:T(8,128)S(1)} %get-tuple-element.58), channel_id=1, source_target_pairs={{0,1},{1,0},{2,3},{3,2},{4,5},{5,4},{6,7},{7,6},{8,9},{9,8},{10,11... | collective-permute-start | bytes 393224 | tf_op jit(solution)/shard_map/ppermute | solution.py:61
  42.9 3.4 %collective-permute-start.17 = (f32[1,2,128,128]{3,2,1,0:T(8,128)S(1)}, f32[1,2,128,128]{3,2,1,0:T(8,128)S(1)}, u32[]{:S(2)}, u32[]{:S(2)}) collective-permute-start(f32[1,2,128,128]{3,2,1,0:T(8,128)S(1)} %get-tuple-element.59), channel_id=1, source_target_pairs={{0,16},{1,17},{2,18},{3,19},{4,20},{5,21},{6,22},{7,23},{8,24},{9,... | collective-permute-start | bytes 393224 | tf_op jit(solution)/shard_map/ppermute | solution.py:61
  46.3 1.4 %collective-permute-start.18 = (f32[1,2,128,128]{3,2,1,0:T(8,128)S(1)}, f32[1,2,128,128]{3,2,1,0:T(8,128)S(1)}, u32[]{:S(2)}, u32[]{:S(2)}) collective-permute-start(f32[1,2,128,128]{3,2,1,0:T(8,128)S(1)} %get-tuple-element.60), channel_id=1, source_target_pairs={{0,17},{1,16},{2,19},{3,18},{4,21},{5,20},{6,23},{7,22},{8,25},{9,... | collective-permute-start | bytes 393224 | tf_op jit(solution)/shard_map/ppermute | solution.py:61
  47.7 0.1 collective-permute-start.6
  47.8 1.0 %shard_map.122.base_ref = f32[2,128,128]{2,1,0:T(8,128)S(1)} custom-call(s32[3]{0:T(128)S(1)} %pad_add_fusion.index_ref, s32[8,12]{1,0:T(8,128)S(1)} %copy-done.1, s32[8]{0:T(128)S(1)} %copy-done.2, bf16[8,32,384]{2,1,0:T(8,128)(2,1)S(1)} %reshape.15.near_ref.block_ref, bf16[1,2,128,128]{3,2,1,0:T(8,128)(2,1)S(1)} %get-tuple-element.52.own_ref.refs_4_, ...), custom_call_target="tpu_custom_call" | custom-call | tf_op jit(solution)/shard_map/pallas_call | solution.py:591
  48.9 3.4 %collective-permute-done.6.half_hbm.refs_1_ = f32[1,160,128]{2,1,0:T(8,128)S(1)} collective-permute-done((f32[1,160,128]{2,1,0:T(8,128)S(1)}, f32[1,160,128]{2,1,0:T(8,128)S(1)}, u32[]{:S(2)}, u32[]{:S(2)}) %collective-permute-start.6) | collective-permute-done | bytes 81952 | tf_op jit(solution)/shard_map/ppermute | solution.py:61
  52.2 1.8 %collective-permute-done.18.refs_3_ = f32[1,2,128,128]{3,2,1,0:T(8,128)S(1)} collective-permute-done((f32[1,2,128,128]{3,2,1,0:T(8,128)S(1)}, f32[1,2,128,128]{3,2,1,0:T(8,128)S(1)}, u32[]{:S(2)}, u32[]{:S(2)}) %collective-permute-start.18) | collective-permute-done | bytes 131104 | tf_op jit(solution)/shard_map/ppermute | solution.py:61
  54.0 1.0 %shard_map.126 = (f32[2,128,128]{2,1,0:T(8,128)S(1)}, f32[4,80,128]{2,1,0:T(8,128)S(1)}, f32[4,80,128]{2,1,0:T(8,128)S(1)}) custom-call(s32[3]{0:T(128)S(1)} %pad_add_fusion.index_ref, f32[1,160,128]{2,1,0:T(8,128)S(1)} %collective-permute-done.6.half_hbm.refs_1_, f32[128,128]{1,0:T(8,128)S(1)} %get-tuple-element.38.refs_0_.weight_ref, ...), custom_call_target="tpu_custom_call" | custom-call | tf_op jit(solution)/shard_map/pallas_call | solution.py:761
  55.1 0.1 collective-permute-start.20
  55.2 0.1 collective-permute-start.19
  55.3 1.3 %collective-permute-done.20.refs_1_ = f32[4,80,128]{2,1,0:T(8,128)S(1)} collective-permute-done((f32[4,80,128]{2,1,0:T(8,128)S(1)}, f32[4,80,128]{2,1,0:T(8,128)S(1)}, u32[]{:S(2)}, u32[]{:S(2)}) %collective-permute-start.20) | collective-permute-done | bytes 163872 | tf_op jit(solution)/shard_map/ppermute | solution.py:61
  56.6 0.6 collective-permute-start.21
  57.2 1.7 %collective-permute-start.22 = (f32[1,80,128]{2,1,0:T(8,128)S(1)}, f32[1,80,128]{2,1,0:T(8,128)S(1)}, u32[]{:S(2)}, u32[]{:S(2)}) collective-permute-start(f32[1,80,128]{2,1,0:T(8,128)S(1)} %get-tuple-element.66), channel_id=1, source_target_pairs={{0,16},{1,17},{2,18},{3,19},{4,20},{5,21},{6,22},{7,23},{8,24},{9,... | collective-permute-start | bytes 122888 | tf_op jit(solution)/shard_map/ppermute | solution.py:61
  59.0 1.2 %collective-permute-start.23 = (f32[1,80,128]{2,1,0:T(8,128)S(1)}, f32[1,80,128]{2,1,0:T(8,128)S(1)}, u32[]{:S(2)}, u32[]{:S(2)}) collective-permute-start(f32[1,80,128]{2,1,0:T(8,128)S(1)} %get-tuple-element.67), channel_id=1, source_target_pairs={{0,17},{1,16},{2,19},{3,18},{4,21},{5,20},{6,23},{7,22},{8,25},{9,... | collective-permute-start | bytes 122888 | tf_op jit(solution)/shard_map/ppermute | solution.py:61
  60.1 0.9 collective-permute-done.19.refs_0_.refs_1_
  61.0 0.2 collective-permute-done.22.refs_3_
  61.2 2.6 %collective-permute-done.23.refs_4_ = f32[1,80,128]{2,1,0:T(8,128)S(1)} collective-permute-done((f32[1,80,128]{2,1,0:T(8,128)S(1)}, f32[1,80,128]{2,1,0:T(8,128)S(1)}, u32[]{:S(2)}, u32[]{:S(2)}) %collective-permute-start.23) | collective-permute-done | bytes 40992 | tf_op jit(solution)/shard_map/ppermute | solution.py:61
  63.9 0.1 collective-permute-start.24
  64.0 1.7 %collective-permute-start.25 = (f32[1,80,128]{2,1,0:T(8,128)S(1)}, f32[1,80,128]{2,1,0:T(8,128)S(1)}, u32[]{:S(2)}, u32[]{:S(2)}) collective-permute-start(f32[1,80,128]{2,1,0:T(8,128)S(1)} %shard_map.129.refs_0_), channel_id=1, source_target_pairs={{0,4},{1,5},{2,6},{3,7},{4,0},{5,1},{6,2},{7,3},{8,12},{9,13},{10,... | collective-permute-start | bytes 122888 | tf_op jit(solution)/shard_map/ppermute | solution.py:61
  65.6 2.7 %collective-permute-start.26 = (f32[1,80,128]{2,1,0:T(8,128)S(1)}, f32[1,80,128]{2,1,0:T(8,128)S(1)}, u32[]{:S(2)}, u32[]{:S(2)}) collective-permute-start(f32[1,80,128]{2,1,0:T(8,128)S(1)} %shard_map.129.refs_0_), channel_id=1, source_target_pairs={{0,6},{1,7},{2,4},{3,5},{4,2},{5,3},{6,0},{7,1},{8,14},{9,15},{10,... | collective-permute-start | bytes 122888 | tf_op jit(solution)/shard_map/ppermute | solution.py:61
  68.3 0.8 collective-permute-done.25.refs_2_
  69.1 2.3 %collective-permute-done.26.refs_3_ = f32[1,80,128]{2,1,0:T(8,128)S(1)} collective-permute-done((f32[1,80,128]{2,1,0:T(8,128)S(1)}, f32[1,80,128]{2,1,0:T(8,128)S(1)}, u32[]{:S(2)}, u32[]{:S(2)}) %collective-permute-start.26) | collective-permute-done | bytes 40992 | tf_op jit(solution)/shard_map/ppermute | solution.py:61
  71.5 0.4 collective-permute-start.27
  71.9 1.4 %collective-permute-start.28 = (f32[1,240,128]{2,1,0:T(8,128)S(1)}, f32[1,240,128]{2,1,0:T(8,128)S(1)}, u32[]{:S(2)}, u32[]{:S(2)}) collective-permute-start(f32[1,240,128]{2,1,0:T(8,128)S(1)} %shard_map.132.refs_0_), channel_id=1, source_target_pairs={{0,16},{1,17},{2,18},{3,19},{4,20},{5,21},{6,22},{7,23},{8,24},{9,... | collective-permute-start | bytes 368648 | tf_op jit(solution)/shard_map/ppermute | solution.py:61
  73.3 1.8 %collective-permute-start.29 = (f32[1,240,128]{2,1,0:T(8,128)S(1)}, f32[1,240,128]{2,1,0:T(8,128)S(1)}, u32[]{:S(2)}, u32[]{:S(2)}) collective-permute-start(f32[1,240,128]{2,1,0:T(8,128)S(1)} %shard_map.132.refs_0_), channel_id=1, source_target_pairs={{0,17},{1,16},{2,19},{3,18},{4,21},{5,20},{6,23},{7,22},{8,25},{9,... | collective-permute-start | bytes 368648 | tf_op jit(solution)/shard_map/ppermute | solution.py:61
  75.1 1.4 %collective-permute-done.27.refs_1_ = f32[1,240,128]{2,1,0:T(8,128)S(1)} collective-permute-done((f32[1,240,128]{2,1,0:T(8,128)S(1)}, f32[1,240,128]{2,1,0:T(8,128)S(1)}, u32[]{:S(2)}, u32[]{:S(2)}) %collective-permute-start.27) | collective-permute-done | bytes 122912 | tf_op jit(solution)/shard_map/ppermute | solution.py:61
  76.5 0.4 collective-permute-done.28.refs_2_
  76.8 2.3 %collective-permute-done.29.refs_3_ = f32[1,240,128]{2,1,0:T(8,128)S(1)} collective-permute-done((f32[1,240,128]{2,1,0:T(8,128)S(1)}, f32[1,240,128]{2,1,0:T(8,128)S(1)}, u32[]{:S(2)}, u32[]{:S(2)}) %collective-permute-start.29) | collective-permute-done | bytes 122912 | tf_op jit(solution)/shard_map/ppermute | solution.py:61
  79.1 0.1 collective-permute-start.30
  79.2 1.9 %collective-permute-done.30.refs_1_ = f32[4,240,128]{2,1,0:T(8,128)S(1)} collective-permute-done((f32[4,240,128]{2,1,0:T(8,128)S(1)}, f32[4,240,128]{2,1,0:T(8,128)S(1)}, u32[]{:S(2)}, u32[]{:S(2)}) %collective-permute-start.30) | collective-permute-done | bytes 491552 | tf_op jit(solution)/shard_map/ppermute | solution.py:61
  81.1 6.7 %shard_map.134 = (f32[512,128]{1,0:T(8,128)}, f32[128,128]{1,0:T(8,128)}, f32[256,128]{1,0:T(8,128)}) custom-call(s32[3]{0:T(128)S(1)} %pad_add_fusion.index_ref, f32[4,2,128,128]{3,2,1,0:T(8,128)S(1)} %copy-done, f32[2,128,128]{2,1,0:T(8,128)S(1)} %get-tuple-element.61.image_ref, f32[4,240,128]{2,1,0:T(8,128)S(1)} %shard_map.133.refs_0_, ...), custom_call_target="tpu_custom_call" | custom-call | tf_op jit(solution)/shard_map/pallas_call | solution.py:591
  (32 shorter events, 0.3 us)
Async XLA Ops:
  0.6 15.9 %copy-start.3 = (bf16[8,12,32,32]{3,2,1,0:T(8,128)(2,1)S(1)}, bf16[8,12,32,32]{3,2,1,0:T(8,128)(2,1)}, u32[]{:S(2)}) copy-start(bf16[8,12,32,32]{3,2,1,0:T(8,128)(2,1)} %param.15) | copy-start | bytes 589828
  1.9 8.2 %collective-permute-start = (f32[1,56,128]{2,1,0:T(8,128)S(1)}, f32[1,56,128]{2,1,0:T(8,128)S(1)}, u32[]{:S(2)}, u32[]{:S(2)}) collective-permute-start(f32[1,56,128]{2,1,0:T(8,128)S(1)} %shard_map.112.pack_hbm.refs_1_), channel_id=1, source_target_pairs={{0,2},{1,3},{2,0},{3,1},{4,6},{5,7},{6,4},{7,5},{8,10},{9,11},{10,... | collective-permute-start | bytes 86024 | tf_op jit(solution)/shard_map/ppermute | solution.py:61
  5.0 5.2 %collective-permute-start.1 = (f32[1,56,128]{2,1,0:T(8,128)S(1)}, f32[1,56,128]{2,1,0:T(8,128)S(1)}, u32[]{:S(2)}, u32[]{:S(2)}) collective-permute-start(f32[1,56,128]{2,1,0:T(8,128)S(1)} %shard_map.112.pack_hbm.refs_1_), channel_id=1, source_target_pairs={{0,4},{1,5},{2,6},{3,7},{4,0},{5,1},{6,2},{7,3},{8,12},{9,13},{10,... | collective-permute-start | bytes 86024 | tf_op jit(solution)/shard_map/ppermute | solution.py:61
  7.6 5.7 %collective-permute-start.2 = (f32[1,56,128]{2,1,0:T(8,128)S(1)}, f32[1,56,128]{2,1,0:T(8,128)S(1)}, u32[]{:S(2)}, u32[]{:S(2)}) collective-permute-start(f32[1,56,128]{2,1,0:T(8,128)S(1)} %shard_map.112.pack_hbm.refs_1_), channel_id=1, source_target_pairs={{0,6},{1,7},{2,4},{3,5},{4,2},{5,3},{6,0},{7,1},{8,14},{9,15},{10,... | collective-permute-start | bytes 86024 | tf_op jit(solution)/shard_map/ppermute | solution.py:61
  13.3 1.7 %collective-permute-start.3 = (f32[4,160,128]{2,1,0:T(8,128)S(1)}, f32[4,160,128]{2,1,0:T(8,128)S(1)}, u32[]{:S(2)}, u32[]{:S(2)}) collective-permute-start(f32[4,160,128]{2,1,0:T(8,128)S(1)} %shard_map.115), channel_id=1, source_target_pairs={{0,8},{1,9},{2,10},{3,11},{4,12},{5,13},{6,14},{7,15},{8,0},{9,1},... | collective-permute-start | bytes 983048 | tf_op jit(solution)/shard_map/ppermute | solution.py:61
  13.3 6.0 %collective-permute-start.7 = (f32[4,56,128]{2,1,0:T(8,128)S(1)}, f32[4,56,128]{2,1,0:T(8,128)S(1)}, u32[]{:S(2)}, u32[]{:S(2)}) collective-permute-start(f32[4,56,128]{2,1,0:T(8,128)S(1)} %shard_map.114.refs_0_), channel_id=1, source_target_pairs={{0,1},{1,0},{2,3},{3,2},{4,5},{5,4},{6,7},{7,6},{8,9},{9,8},{10,11... | collective-permute-start | bytes 344072 | tf_op jit(solution)/shard_map/ppermute | solution.py:61
  15.0 8.1 %collective-permute-start.4 = (f32[2,160,128]{2,1,0:T(8,128)S(1)}, f32[2,160,128]{2,1,0:T(8,128)S(1)}, u32[]{:S(2)}, u32[]{:S(2)}) collective-permute-start(f32[2,160,128]{2,1,0:T(8,128)S(1)} %get-tuple-element.41), channel_id=1, source_target_pairs={{0,1},{1,0},{2,3},{3,2},{4,5},{5,4},{6,7},{7,6},{8,9},{9,8},{10,11... | collective-permute-start | bytes 491528 | tf_op jit(solution)/shard_map/ppermute | solution.py:61
  20.2 1.3 %collective-permute-start.8 = (f32[2,64,128]{2,1,0:T(8,128)S(1)}, f32[2,64,128]{2,1,0:T(8,128)S(1)}, u32[]{:S(2)}, u32[]{:S(2)}) collective-permute-start(f32[2,64,128]{2,1,0:T(8,128)S(1)} %get-tuple-element.48), channel_id=1, source_target_pairs={{0,8},{1,9},{2,10},{3,11},{4,12},{5,13},{6,14},{7,15},{8,0},{9,1},... | collective-permute-start | bytes 196616 | tf_op jit(solution)/shard_map/ppermute | solution.py:61
  21.5 4.0 %collective-permute-start.9 = (f32[1,64,128]{2,1,0:T(8,128)S(1)}, f32[1,64,128]{2,1,0:T(8,128)S(1)}, u32[]{:S(2)}, u32[]{:S(2)}) collective-permute-start(f32[1,64,128]{2,1,0:T(8,128)S(1)} %get-tuple-element.51), channel_id=1, source_target_pairs={{0,16},{1,17},{2,18},{3,19},{4,20},{5,21},{6,22},{7,23},{8,24},{9,... | collective-permute-start | bytes 98312 | tf_op jit(solution)/shard_map/ppermute | solution.py:61
  23.1 12.4 %collective-permute-start.5 = (f32[1,160,128]{2,1,0:T(8,128)S(1)}, f32[1,160,128]{2,1,0:T(8,128)S(1)}, u32[]{:S(2)}, u32[]{:S(2)}) collective-permute-start(f32[1,160,128]{2,1,0:T(8,128)S(1)} %get-tuple-element.43), channel_id=1, source_target_pairs={{0,16},{1,17},{2,18},{3,19},{4,20},{5,21},{6,22},{7,23},{8,24},{9,... | collective-permute-start | bytes 245768 | tf_op jit(solution)/shard_map/ppermute | solution.py:61
  26.3 5.9 %collective-permute-start.10 = (bf16[2,64,128]{2,1,0:T(8,128)(2,1)S(1)}, bf16[2,64,128]{2,1,0:T(8,128)(2,1)S(1)}, u32[]{:S(2)}, u32[]{:S(2)}) collective-permute-start(bf16[2,64,128]{2,1,0:T(8,128)(2,1)S(1)} %get-tuple-element.53), channel_id=1, source_target_pairs={{0,1},{1,0},{2,3},{3,2},{4,5},{5,4},{6,7},{7,6},{8,9},{9,8},{10,11... | collective-permute-start | bytes 98312 | tf_op jit(solution)/shard_map/ppermute | solution.py:61
  27.9 7.0 %collective-permute-start.12 = (bf16[1,2,128,128]{3,2,1,0:T(8,128)(2,1)S(1)}, bf16[1,2,128,128]{3,2,1,0:T(8,128)(2,1)S(1)}, u32[]{:S(2)}, u32[]{:S(2)}) collective-permute-start(bf16[1,2,128,128]{3,2,1,0:T(8,128)(2,1)S(1)} %get-tuple-element.52.own_ref.refs_4_), channel_id=1, source_target_pairs={{0,2},{1,3},{2,0},{3,1},{4,6},{5,7},{6,4},{7,5},{8,10},{9,11},{10,... | collective-permute-start | bytes 196616 | tf_op jit(solution)/shard_map/ppermute | solution.py:61
  27.9 7.0 %collective-permute-start.13 = (bf16[1,2,128,128]{3,2,1,0:T(8,128)(2,1)S(1)}, bf16[1,2,128,128]{3,2,1,0:T(8,128)(2,1)S(1)}, u32[]{:S(2)}, u32[]{:S(2)}) collective-permute-start(bf16[1,2,128,128]{3,2,1,0:T(8,128)(2,1)S(1)} %get-tuple-element.52.own_ref.refs_4_), channel_id=1, source_target_pairs={{0,4},{1,5},{2,6},{3,7},{4,0},{5,1},{6,2},{7,3},{8,12},{9,13},{10,... | collective-permute-start | bytes 196616 | tf_op jit(solution)/shard_map/ppermute | solution.py:61
  29.1 6.4 %collective-permute-start.14 = (bf16[1,2,128,128]{3,2,1,0:T(8,128)(2,1)S(1)}, bf16[1,2,128,128]{3,2,1,0:T(8,128)(2,1)S(1)}, u32[]{:S(2)}, u32[]{:S(2)}) collective-permute-start(bf16[1,2,128,128]{3,2,1,0:T(8,128)(2,1)S(1)} %get-tuple-element.52.own_ref.refs_4_), channel_id=1, source_target_pairs={{0,6},{1,7},{2,4},{3,5},{4,2},{5,3},{6,0},{7,1},{8,14},{9,15},{10,... | collective-permute-start | bytes 196616 | tf_op jit(solution)/shard_map/ppermute | solution.py:61
  32.2 2.6 %collective-permute-start.11 = (bf16[2,64,128]{2,1,0:T(8,128)(2,1)S(1)}, bf16[2,64,128]{2,1,0:T(8,128)(2,1)S(1)}, u32[]{:S(2)}, u32[]{:S(2)}) collective-permute-start(bf16[2,64,128]{2,1,0:T(8,128)(2,1)S(1)} %get-tuple-element.54), channel_id=1, source_target_pairs={{1,2},{3,4},{5,6},{7,8},{9,10},{11,12},{13,14},{15,16},{17,18},{19... | collective-permute-start | bytes 98312 | tf_op jit(solution)/shard_map/ppermute | solution.py:731
  34.8 13.0 %copy-start.1 = (s32[8,12]{1,0:T(8,128)S(1)}, s32[8,12]{1,0:T(8,128)}, u32[]{:S(2)}) copy-start(s32[8,12]{1,0:T(8,128)} %panel_ref.1) | copy-start | bytes 1156
  34.8 13.0 %copy-start.2 = (s32[8]{0:T(128)S(1)}, s32[8]{0:T(128)}, u32[]{:S(2)}) copy-start(s32[8]{0:T(128)} %count_ref.1) | copy-start | bytes 100
  35.6 18.5 %copy-start = (f32[4,2,128,128]{3,2,1,0:T(8,128)S(1)}, f32[4,2,128,128]{3,2,1,0:T(8,128)}, u32[]{:S(2)}) copy-start(f32[4,2,128,128]{3,2,1,0:T(8,128)} %basis_ref.3) | copy-start | bytes 1572868
  35.6 3.8 %collective-permute-start.15 = (bf16[4,2,128,128]{3,2,1,0:T(8,128)(2,1)S(1)}, bf16[4,2,128,128]{3,2,1,0:T(8,128)(2,1)S(1)}, u32[]{:S(2)}, u32[]{:S(2)}) collective-permute-start(bf16[4,2,128,128]{3,2,1,0:T(8,128)(2,1)S(1)} %shard_map.124.refs_1_), channel_id=1, source_target_pairs={{0,8},{1,9},{2,10},{3,11},{4,12},{5,13},{6,14},{7,15},{8,0},{9,1},... | collective-permute-start | bytes 786440 | tf_op jit(solution)/shard_map/ppermute | solution.py:61
  41.0 11.2 %collective-permute-start.16 = (f32[1,2,128,128]{3,2,1,0:T(8,128)S(1)}, f32[1,2,128,128]{3,2,1,0:T(8,128)S(1)}, u32[]{:S(2)}, u32[]{:S(2)}) collective-permute-start(f32[1,2,128,128]{3,2,1,0:T(8,128)S(1)} %get-tuple-element.58), channel_id=1, source_target_pairs={{0,1},{1,0},{2,3},{3,2},{4,5},{5,4},{6,7},{7,6},{8,9},{9,8},{10,11... | collective-permute-start | bytes 393224 | tf_op jit(solution)/shard_map/ppermute | solution.py:61
  42.9 9.4 %collective-permute-start.17 = (f32[1,2,128,128]{3,2,1,0:T(8,128)S(1)}, f32[1,2,128,128]{3,2,1,0:T(8,128)S(1)}, u32[]{:S(2)}, u32[]{:S(2)}) collective-permute-start(f32[1,2,128,128]{3,2,1,0:T(8,128)S(1)} %get-tuple-element.59), channel_id=1, source_target_pairs={{0,16},{1,17},{2,18},{3,19},{4,20},{5,21},{6,22},{7,23},{8,24},{9,... | collective-permute-start | bytes 393224 | tf_op jit(solution)/shard_map/ppermute | solution.py:61
  46.3 7.7 %collective-permute-start.18 = (f32[1,2,128,128]{3,2,1,0:T(8,128)S(1)}, f32[1,2,128,128]{3,2,1,0:T(8,128)S(1)}, u32[]{:S(2)}, u32[]{:S(2)}) collective-permute-start(f32[1,2,128,128]{3,2,1,0:T(8,128)S(1)} %get-tuple-element.60), channel_id=1, source_target_pairs={{0,17},{1,16},{2,19},{3,18},{4,21},{5,20},{6,23},{7,22},{8,25},{9,... | collective-permute-start | bytes 393224 | tf_op jit(solution)/shard_map/ppermute | solution.py:61
  47.7 4.5 %collective-permute-start.6 = (f32[1,160,128]{2,1,0:T(8,128)S(1)}, f32[1,160,128]{2,1,0:T(8,128)S(1)}, u32[]{:S(2)}, u32[]{:S(2)}) collective-permute-start(f32[1,160,128]{2,1,0:T(8,128)S(1)} %shard_map.118.refs_0_), channel_id=1, source_target_pairs={{0,2},{1,3},{2,0},{3,1},{4,6},{5,7},{6,4},{7,5},{8,10},{9,11},{10,... | collective-permute-start | bytes 245768 | tf_op jit(solution)/shard_map/ppermute | solution.py:61
  55.1 1.5 %collective-permute-start.20 = (f32[4,80,128]{2,1,0:T(8,128)S(1)}, f32[4,80,128]{2,1,0:T(8,128)S(1)}, u32[]{:S(2)}, u32[]{:S(2)}) collective-permute-start(f32[4,80,128]{2,1,0:T(8,128)S(1)} %get-tuple-element.63), channel_id=1, source_target_pairs={{0,8},{1,9},{2,10},{3,11},{4,12},{5,13},{6,14},{7,15},{8,0},{9,1},... | collective-permute-start | bytes 491528 | tf_op jit(solution)/shard_map/ppermute | solution.py:61
  55.2 5.8 %collective-permute-start.19 = (f32[1,160,128]{2,1,0:T(8,128)S(1)}, f32[1,160,128]{2,1,0:T(8,128)S(1)}, u32[]{:S(2)}, u32[]{:S(2)}) collective-permute-start(f32[1,160,128]{2,1,0:T(8,128)S(1)} %shard_map.127.refs_0_), channel_id=1, source_target_pairs={{0,4},{1,5},{2,6},{3,7},{4,0},{5,1},{6,2},{7,3},{8,12},{9,13},{10,... | collective-permute-start | bytes 245768 | tf_op jit(solution)/shard_map/ppermute | solution.py:61
  56.6 4.4 %collective-permute-start.21 = (f32[1,80,128]{2,1,0:T(8,128)S(1)}, f32[1,80,128]{2,1,0:T(8,128)S(1)}, u32[]{:S(2)}, u32[]{:S(2)}) collective-permute-start(f32[1,80,128]{2,1,0:T(8,128)S(1)} %get-tuple-element.65), channel_id=1, source_target_pairs={{0,1},{1,0},{2,3},{3,2},{4,5},{5,4},{6,7},{7,6},{8,9},{9,8},{10,11... | collective-permute-start | bytes 122888 | tf_op jit(solution)/shard_map/ppermute | solution.py:61
  57.2 4.0 %collective-permute-start.22 = (f32[1,80,128]{2,1,0:T(8,128)S(1)}, f32[1,80,128]{2,1,0:T(8,128)S(1)}, u32[]{:S(2)}, u32[]{:S(2)}) collective-permute-start(f32[1,80,128]{2,1,0:T(8,128)S(1)} %get-tuple-element.66), channel_id=1, source_target_pairs={{0,16},{1,17},{2,18},{3,19},{4,20},{5,21},{6,22},{7,23},{8,24},{9,... | collective-permute-start | bytes 122888 | tf_op jit(solution)/shard_map/ppermute | solution.py:61
  59.0 4.9 %collective-permute-start.23 = (f32[1,80,128]{2,1,0:T(8,128)S(1)}, f32[1,80,128]{2,1,0:T(8,128)S(1)}, u32[]{:S(2)}, u32[]{:S(2)}) collective-permute-start(f32[1,80,128]{2,1,0:T(8,128)S(1)} %get-tuple-element.67), channel_id=1, source_target_pairs={{0,17},{1,16},{2,19},{3,18},{4,21},{5,20},{6,23},{7,22},{8,25},{9,... | collective-permute-start | bytes 122888 | tf_op jit(solution)/shard_map/ppermute | solution.py:61
  63.9 4.5 %collective-permute-start.24 = (f32[1,80,128]{2,1,0:T(8,128)S(1)}, f32[1,80,128]{2,1,0:T(8,128)S(1)}, u32[]{:S(2)}, u32[]{:S(2)}) collective-permute-start(f32[1,80,128]{2,1,0:T(8,128)S(1)} %shard_map.129.refs_0_), channel_id=1, source_target_pairs={{0,2},{1,3},{2,0},{3,1},{4,6},{5,7},{6,4},{7,5},{8,10},{9,11},{10,... | collective-permute-start | bytes 122888 | tf_op jit(solution)/shard_map/ppermute | solution.py:61
  64.0 5.2 %collective-permute-start.25 = (f32[1,80,128]{2,1,0:T(8,128)S(1)}, f32[1,80,128]{2,1,0:T(8,128)S(1)}, u32[]{:S(2)}, u32[]{:S(2)}) collective-permute-start(f32[1,80,128]{2,1,0:T(8,128)S(1)} %shard_map.129.refs_0_), channel_id=1, source_target_pairs={{0,4},{1,5},{2,6},{3,7},{4,0},{5,1},{6,2},{7,3},{8,12},{9,13},{10,... | collective-permute-start | bytes 122888 | tf_op jit(solution)/shard_map/ppermute | solution.py:61
  65.6 5.8 %collective-permute-start.26 = (f32[1,80,128]{2,1,0:T(8,128)S(1)}, f32[1,80,128]{2,1,0:T(8,128)S(1)}, u32[]{:S(2)}, u32[]{:S(2)}) collective-permute-start(f32[1,80,128]{2,1,0:T(8,128)S(1)} %shard_map.129.refs_0_), channel_id=1, source_target_pairs={{0,6},{1,7},{2,4},{3,5},{4,2},{5,3},{6,0},{7,1},{8,14},{9,15},{10,... | collective-permute-start | bytes 122888 | tf_op jit(solution)/shard_map/ppermute | solution.py:61
  71.5 4.9 %collective-permute-start.27 = (f32[1,240,128]{2,1,0:T(8,128)S(1)}, f32[1,240,128]{2,1,0:T(8,128)S(1)}, u32[]{:S(2)}, u32[]{:S(2)}) collective-permute-start(f32[1,240,128]{2,1,0:T(8,128)S(1)} %shard_map.132.refs_0_), channel_id=1, source_target_pairs={{0,1},{1,0},{2,3},{3,2},{4,5},{5,4},{6,7},{7,6},{8,9},{9,8},{10,11... | collective-permute-start | bytes 368648 | tf_op jit(solution)/shard_map/ppermute | solution.py:61
  71.9 4.9 %collective-permute-start.28 = (f32[1,240,128]{2,1,0:T(8,128)S(1)}, f32[1,240,128]{2,1,0:T(8,128)S(1)}, u32[]{:S(2)}, u32[]{:S(2)}) collective-permute-start(f32[1,240,128]{2,1,0:T(8,128)S(1)} %shard_map.132.refs_0_), channel_id=1, source_target_pairs={{0,16},{1,17},{2,18},{3,19},{4,20},{5,21},{6,22},{7,23},{8,24},{9,... | collective-permute-start | bytes 368648 | tf_op jit(solution)/shard_map/ppermute | solution.py:61
  73.3 5.8 %collective-permute-start.29 = (f32[1,240,128]{2,1,0:T(8,128)S(1)}, f32[1,240,128]{2,1,0:T(8,128)S(1)}, u32[]{:S(2)}, u32[]{:S(2)}) collective-permute-start(f32[1,240,128]{2,1,0:T(8,128)S(1)} %shard_map.132.refs_0_), channel_id=1, source_target_pairs={{0,17},{1,16},{2,19},{3,18},{4,21},{5,20},{6,23},{7,22},{8,25},{9,... | collective-permute-start | bytes 368648 | tf_op jit(solution)/shard_map/ppermute | solution.py:61
  79.1 1.9 %collective-permute-start.30 = (f32[4,240,128]{2,1,0:T(8,128)S(1)}, f32[4,240,128]{2,1,0:T(8,128)S(1)}, u32[]{:S(2)}, u32[]{:S(2)}) collective-permute-start(f32[4,240,128]{2,1,0:T(8,128)S(1)} %shard_map.133.refs_0_), channel_id=1, source_target_pairs={{0,8},{1,9},{2,10},{3,11},{4,12},{5,13},{6,14},{7,15},{8,0},{9,1},... | collective-permute-start | bytes 1474568 | tf_op jit(solution)/shard_map/ppermute | solution.py:61

commit v12 on v11

--- a/solution.py
+++ b/solution.py
@@ -372,21 +372,17 @@
         matrix_ref[0, 2, :, lanes] = (factor * (log_part + square_y * inverse)).astype(jnp.bfloat16)
 
 
-def far_kernel(ways, skip, *refs):
-    matrix_ref, *refs = refs[skip:]
-    fields = refs[: len(refs) - ways - 1]
-    outs = refs[len(fields) : len(fields) + ways]
-    fields_ref = refs[-1]
-    point_count, rhs_count = fields[0].shape[2:]
+def far_kernel(ways, matrix_ref, field_ref, *refs):
+    earlier, outs, fields_ref = refs[: -1 - ways], refs[-1 - ways : -1], refs[-1]
+    point_count, rhs_count = field_ref.shape[2:]
     step = pl.program_id(0)
 
     @pl.when(step == 0)
     def _():
-        for s in range(fields_ref.shape[0] // point_count):
-            ref, row = part_at(fields, s)
+        for s in range(field_ref.shape[0]):
             for b in range(2):
                 rows = slice(s * point_count, (s + 1) * point_count)
-                fields_ref[rows, b * rhs_count : (b + 1) * rhs_count] = ref[row, b]
+                fields_ref[rows, b * rhs_count : (b + 1) * rhs_count] = field_ref[s, b]
 
     mixed = dot16(matrix_ref[0, 1], fields_ref[...])
     out_x = dot16(matrix_ref[0, 0], fields_ref[:, :rhs_count]) + mixed[:, rhs_count:]
@@ -394,9 +390,14 @@
     for j, out_ref in enumerate(outs):
 
         @pl.when(lax.rem(step, ways) == j)
-        def _(out_ref=out_ref):
-            out_ref[step // ways, 0] = out_x
-            out_ref[step // ways, 1] = out_y
+        def _(j=j, out_ref=out_ref):
+            row = step // ways
+            if earlier:
+                out_ref[row, 0] = out_x + earlier[j][row, 0]
+                out_ref[row, 1] = out_y + earlier[j][row, 1]
+            else:
+                out_ref[row, 0] = out_x
+                out_ref[row, 1] = out_y
 
 
 def near_kernel(
@@ -730,20 +731,27 @@
     pairs = [(i, i + 1) for i in range(1, device_count - 1, 2)]
     next_edge = lax.ppermute(next_edge, AXES, pairs + [(j, i) for i, j in pairs])
     fields = flip_each([precond] * (1 << len(source_groups[0])), source_groups[0])
-    after = (matrix, half_steps[1], pair_edge, next_edge)
+    after = (matrix, half_steps[1], next_edge)
     fields = gather_steps(join(fields, after), source_groups[1:])
 
-    after = ()
     ways = 1 << len(plane_groups[0])
-    far_parts = pl.pallas_call(
-        functools.partial(far_kernel, ways, len(after)),
-        out_shape=[f32(target_count // ways, 2, point_count, rhs_count)] * ways,
-        grid=(target_count,),
-        in_specs=[ANY] * len(after) + [matrix_spec] + [VMEM] * len(fields),
-        out_specs=[VMEM] * ways,
-        scratch_shapes=[pltpu.VMEM((source_total, 2 * rhs_count), jnp.bfloat16)],
-        compiler_params=PARAMS,
-    )(*after, matrix, *fields)
+    far_parts = []
+    for number, field in enumerate(fields):
+        far_parts = pl.pallas_call(
+            functools.partial(far_kernel, ways),
+            out_shape=[f32(target_count // ways, 2, point_count, rhs_count)] * ways,
+            grid=(target_count,),
+            in_specs=[
+                pl.BlockSpec(
+                    (1, 3, point_count, source_total // 2),
+                    lambda k, number=number: (k, 0, 0, number),
+                )
+            ]
+            + [VMEM] * (1 + len(far_parts)),
+            out_specs=[VMEM] * ways,
+            scratch_shapes=[pltpu.VMEM((source_total // 2, 2 * rhs_count), jnp.bfloat16)],
+            compiler_params=PARAMS,
+        )(matrix, field, *far_parts)
     far_parts = scatter_steps(far_parts, plane_groups)
     base = call(
         near_kernel,

time: 87.9 us -> 87.3 us (level)
  Pallas kernels: 17.8 us -> 18.9 us
  starting transfers between devices: 39.1 us -> 38.1 us
    ppermute x30, starting transfers between devices: 38.5 us -> 37.4 us  [flip(): return lax.ppermute(block, AXES, [(i, i ^ mask) for i in range(count)])]
    pallas_call x1 -> x2, Pallas kernels: 1.67 us -> 2.73 us  [body(): pl.pallas_call(functools.partial(far_kernel, ways), out_shape=[f32(target...]
  transfers between devices with their start and end apart: 31 -> 31, of which waited for: 20 -> 18; matrix products, arithmetic and copies ran while one was open for 1% -> 1% of each run, Pallas kernels for 8% -> 10%
where the time goes in v12:
time: 87.3 us; the launch traced here: 87.1 us
  starting transfers between devices  38.1 us (44%)
  waiting for transfers between devices  28 us (32%)
  Pallas kernels  18.9 us (22%)
  local copies, waits for them, and re-layouts  1.07 us (1%)
  between operations  0.95 us (1%)
    ppermute x30, starting transfers between devices, flip(): return lax.ppermute(block, AXES, [(i, i ^ mask) for i in range(count)])  37.4 us
    ppermute x30, waiting for transfers between devices, flip(): return lax.ppermute(block, AXES, [(i, i ^ mask) for i in range(count)])  28 us
    pallas_call x6, Pallas kernels, call(): pl.pallas_call(kernel, out_shape=out_shape, in_specs=[SMEM] * scalars + [...  11.4 us
    pallas_call x2, Pallas kernels, body(): pl.pallas_call(functools.partial(far_kernel, ways), out_shape=[f32(target...  2.73 us
    pallas_call x1, Pallas kernels, body(): pl.pallas_call(functools.partial(matrix_kernel, coarse_count), out_shape=...  1.91 us
  transfers between devices with their start and end apart: 31, of which 18 were waited for; matrix products, arithmetic and copies ran while one was open for 1% of the time, Pallas kernels for 10%

profile of v12, /device:TPU:0, one launch (start us, length us, event | category | flops | bytes accessed | tf_op | source)
XLA Modules:
  0.0 87.1 jit_solution(396774997371217714)
XLA Ops:
  0.6 1.2 %shard_map.112.pack_hbm.refs_1_ = f32[1,56,128]{2,1,0:T(8,128)S(1)} custom-call(s32[2,128]{1,0:T(2,128)} %agg_hbm.3, f32[4,2,128,128]{3,2,1,0:T(8,128)} %basis_ref.3, f32[2,128]{1,0:T(2,128)} %points_hbm.1, f32[1,128]{1,0:T(1,128)} %bitcast.8), custom_call_target="tpu_custom_call" | custom-call | tf_op jit(solution)/shard_map/pallas_call | solution.py:592
  1.9 3.1 %collective-permute-start = (f32[1,56,128]{2,1,0:T(8,128)S(1)}, f32[1,56,128]{2,1,0:T(8,128)S(1)}, u32[]{:S(2)}, u32[]{:S(2)}) collective-permute-start(f32[1,56,128]{2,1,0:T(8,128)S(1)} %shard_map.112.pack_hbm.refs_1_), channel_id=1, source_target_pairs={{0,2},{1,3},{2,0},{3,1},{4,6},{5,7},{6,4},{7,5},{8,10},{9,11},{10,... | collective-permute-start | bytes 86024 | tf_op jit(solution)/shard_map/ppermute | solution.py:61
  5.0 2.6 %collective-permute-start.1 = (f32[1,56,128]{2,1,0:T(8,128)S(1)}, f32[1,56,128]{2,1,0:T(8,128)S(1)}, u32[]{:S(2)}, u32[]{:S(2)}) collective-permute-start(f32[1,56,128]{2,1,0:T(8,128)S(1)} %shard_map.112.pack_hbm.refs_1_), channel_id=1, source_target_pairs={{0,4},{1,5},{2,6},{3,7},{4,0},{5,1},{6,2},{7,3},{8,12},{9,13},{10,... | collective-permute-start | bytes 86024 | tf_op jit(solution)/shard_map/ppermute | solution.py:61
  7.6 0.0 collective-permute-start.2
  7.6 0.1 pad_add_fusion.index_ref
  7.6 2.4 %shard_map.113 = (f32[4,48,384]{2,1,0:T(8,128)S(1)}, f32[2,48,128]{2,1,0:T(8,128)S(1)}, f32[2,128,128]{2,1,0:T(8,128)S(1)}, f32[128,128]{1,0:T(8,128)S(1)}, f32[...) custom-call(s32[3]{0:T(128)S(1)} %pad_add_fusion.index_ref, f32[1,56,128]{2,1,0:T(8,128)S(1)} %shard_map.112.pack_hbm.refs_1_, ...), custom_call_target="tpu_custom_call" | custom-call | tf_op jit(solution)/shard_map/pallas_call | solution.py:592
  10.1 0.1 collective-permute-done.1.refs_3_
  10.2 3.0 %collective-permute-done.2.refs_4_ = f32[1,56,128]{2,1,0:T(8,128)S(1)} collective-permute-done((f32[1,56,128]{2,1,0:T(8,128)S(1)}, f32[1,56,128]{2,1,0:T(8,128)S(1)}, u32[]{:S(2)}, u32[]{:S(2)}) %collective-permute-start.2) | collective-permute-done | bytes 28704 | tf_op jit(solution)/shard_map/ppermute | solution.py:61
  13.3 0.1 collective-permute-start.3
  13.3 1.6 %collective-permute-start.7 = (f32[4,56,128]{2,1,0:T(8,128)S(1)}, f32[4,56,128]{2,1,0:T(8,128)S(1)}, u32[]{:S(2)}, u32[]{:S(2)}) collective-permute-start(f32[4,56,128]{2,1,0:T(8,128)S(1)} %shard_map.114.refs_0_), channel_id=1, source_target_pairs={{0,1},{1,0},{2,3},{3,2},{4,5},{5,4},{6,7},{7,6},{8,9},{9,8},{10,11... | collective-permute-start | bytes 344072 | tf_op jit(solution)/shard_map/ppermute | solution.py:61
  14.9 0.1 collective-permute-done.3.refs_1_
  15.0 1.6 %collective-permute-start.4 = (f32[2,160,128]{2,1,0:T(8,128)S(1)}, f32[2,160,128]{2,1,0:T(8,128)S(1)}, u32[]{:S(2)}, u32[]{:S(2)}) collective-permute-start(f32[2,160,128]{2,1,0:T(8,128)S(1)} %get-tuple-element.45), channel_id=1, source_target_pairs={{0,1},{1,0},{2,3},{3,2},{4,5},{5,4},{6,7},{7,6},{8,9},{9,8},{10,11... | collective-permute-start | bytes 491528 | tf_op jit(solution)/shard_map/ppermute | solution.py:61
  16.6 0.3 copy.13
  16.9 0.7 reshape.15.near_ref.block_ref
  17.6 1.7 %collective-permute-done.7.refs_1_ = f32[4,56,128]{2,1,0:T(8,128)S(1)} collective-permute-done((f32[4,56,128]{2,1,0:T(8,128)S(1)}, f32[4,56,128]{2,1,0:T(8,128)S(1)}, u32[]{:S(2)}, u32[]{:S(2)}) %collective-permute-start.7) | collective-permute-done | bytes 114720 | tf_op jit(solution)/shard_map/ppermute | solution.py:61
  19.4 0.8 shard_map.119
  20.2 0.1 collective-permute-start.8
  20.3 1.2 %collective-permute-done.8.got_ref = f32[2,64,128]{2,1,0:T(8,128)S(1)} collective-permute-done((f32[2,64,128]{2,1,0:T(8,128)S(1)}, f32[2,64,128]{2,1,0:T(8,128)S(1)}, u32[]{:S(2)}, u32[]{:S(2)}) %collective-permute-start.8) | collective-permute-done | bytes 65568 | tf_op jit(solution)/shard_map/ppermute | solution.py:61
  21.5 1.6 %collective-permute-start.9 = (f32[1,64,128]{2,1,0:T(8,128)S(1)}, f32[1,64,128]{2,1,0:T(8,128)S(1)}, u32[]{:S(2)}, u32[]{:S(2)}) collective-permute-start(f32[1,64,128]{2,1,0:T(8,128)S(1)} %get-tuple-element.55), channel_id=1, source_target_pairs={{0,16},{1,17},{2,18},{3,19},{4,20},{5,21},{6,22},{7,23},{8,24},{9,... | collective-permute-start | bytes 98312 | tf_op jit(solution)/shard_map/ppermute | solution.py:61
  23.1 0.9 %collective-permute-start.5 = (f32[1,160,128]{2,1,0:T(8,128)S(1)}, f32[1,160,128]{2,1,0:T(8,128)S(1)}, u32[]{:S(2)}, u32[]{:S(2)}) collective-permute-start(f32[1,160,128]{2,1,0:T(8,128)S(1)} %get-tuple-element.47), channel_id=1, source_target_pairs={{0,16},{1,17},{2,18},{3,19},{4,20},{5,21},{6,22},{7,23},{8,24},{9,... | collective-permute-start | bytes 245768 | tf_op jit(solution)/shard_map/ppermute | solution.py:61
  24.0 1.5 %collective-permute-done.9.refs_1_ = f32[1,64,128]{2,1,0:T(8,128)S(1)} collective-permute-done((f32[1,64,128]{2,1,0:T(8,128)S(1)}, f32[1,64,128]{2,1,0:T(8,128)S(1)}, u32[]{:S(2)}, u32[]{:S(2)}) %collective-permute-start.9) | collective-permute-done | bytes 32800 | tf_op jit(solution)/shard_map/ppermute | solution.py:61
  25.5 0.8 shard_map.121
  26.3 0.1 collective-permute-start.12
  26.4 1.2 %collective-permute-start.13 = (bf16[1,2,128,128]{3,2,1,0:T(8,128)(2,1)S(1)}, bf16[1,2,128,128]{3,2,1,0:T(8,128)(2,1)S(1)}, u32[]{:S(2)}, u32[]{:S(2)}) collective-permute-start(bf16[1,2,128,128]{3,2,1,0:T(8,128)(2,1)S(1)} %get-tuple-element.56.own_ref.refs_3_), channel_id=1, source_target_pairs={{0,4},{1,5},{2,6},{3,7},{4,0},{5,1},{6,2},{7,3},{8,12},{9,13},{10,... | collective-permute-start | bytes 196616 | tf_op jit(solution)/shard_map/ppermute | solution.py:61
  27.6 3.1 %collective-permute-start.14 = (bf16[1,2,128,128]{3,2,1,0:T(8,128)(2,1)S(1)}, bf16[1,2,128,128]{3,2,1,0:T(8,128)(2,1)S(1)}, u32[]{:S(2)}, u32[]{:S(2)}) collective-permute-start(bf16[1,2,128,128]{3,2,1,0:T(8,128)(2,1)S(1)} %get-tuple-element.56.own_ref.refs_3_), channel_id=1, source_target_pairs={{0,6},{1,7},{2,4},{3,5},{4,2},{5,3},{6,0},{7,1},{8,14},{9,15},{10,... | collective-permute-start | bytes 196616 | tf_op jit(solution)/shard_map/ppermute | solution.py:61
  30.7 0.7 collective-permute-start.11
  31.4 1.9 %shard_map.123.refs_0_.matrix_ref = bf16[4,3,128,1024]{3,2,1,0:T(8,128)(2,1)S(1)} custom-call(f32[4,8,128]{2,1,0:T(8,128)S(1)} %get-tuple-element.59.own_ref, f32[4,8,128]{2,1,0:T(8,128)S(1)} %get-tuple-element.60.other_ref, f32[1,64,128]{2,1,0:T(8,128)S(1)} %get-tuple-element.54.refs_0_, f32[1,64,128]{2,1,0:T(8,128)S(1)} %collective-permute-done.9.refs_1_), custom_call_target="tpu_custom_call" | custom-call | tf_op jit(solution)/shard_map/pallas_call | solution.py:721
  33.3 0.1 collective-permute-done.13.refs_5_
  33.4 0.6 collective-permute-done.14.refs_6_
  34.1 0.0 copy-start.1
  34.1 0.0 copy-start.2
  34.1 2.9 %collective-permute-start.15 = (bf16[4,2,128,128]{3,2,1,0:T(8,128)(2,1)S(1)}, bf16[4,2,128,128]{3,2,1,0:T(8,128)(2,1)S(1)}, u32[]{:S(2)}, u32[]{:S(2)}) collective-permute-start(bf16[4,2,128,128]{3,2,1,0:T(8,128)(2,1)S(1)} %shard_map.124.field_ref), channel_id=1, source_target_pairs={{0,8},{1,9},{2,10},{3,11},{4,12},{5,13},{6,14},{7,15},{8,0},{9,1},... | collective-permute-start | bytes 786440 | tf_op jit(solution)/shard_map/ppermute | solution.py:61
  37.0 1.4 %shard_map.125 = (f32[1,2,128,128]{3,2,1,0:T(8,128)S(1)}, f32[1,2,128,128]{3,2,1,0:T(8,128)S(1)}, f32[1,2,128,128]{3,2,1,0:T(8,128)S(1)}, f32[1,2,128,128]{3,2,1,0:T(8,128)S(1)}) custom-call(bf16[4,3,128,1024]{3,2,1,0:T(8,128)(2,1)S(1)} %shard_map.123.refs_0_.matrix_ref, bf16[4,2,128,128]{3,2,1,0:T(8,128)(2,1)S(1)} %shard_map.124.field_ref), custom_call_target="tpu_custom_call" | custom-call | tf_op jit(solution)/shard_map/pallas_call | solution.py:740
  38.3 0.0 copy-start
  38.4 1.4 %shard_map.126 = (f32[1,2,128,128]{3,2,1,0:T(8,128)S(1)}, f32[1,2,128,128]{3,2,1,0:T(8,128)S(1)}, f32[1,2,128,128]{3,2,1,0:T(8,128)S(1)}, f32[1,2,128,128]{3,2,1,0:T(8,128)S(1)}) custom-call(bf16[4,3,128,1024]{3,2,1,0:T(8,128)(2,1)S(1)} %shard_map.123.refs_0_.matrix_ref, bf16[4,2,128,128]{3,2,1,0:T(8,128)(2,1)S(1)} %collective-permute-done.15.field_ref, ...), custom_call_target="tpu_custom_call" | custom-call | tf_op jit(solution)/shard_map/pallas_call | solution.py:740
  39.7 2.3 %collective-permute-start.16 = (f32[1,2,128,128]{3,2,1,0:T(8,128)S(1)}, f32[1,2,128,128]{3,2,1,0:T(8,128)S(1)}, u32[]{:S(2)}, u32[]{:S(2)}) collective-permute-start(f32[1,2,128,128]{3,2,1,0:T(8,128)S(1)} %get-tuple-element.66), channel_id=1, source_target_pairs={{0,1},{1,0},{2,3},{3,2},{4,5},{5,4},{6,7},{7,6},{8,9},{9,8},{10,11... | collective-permute-start | bytes 393224 | tf_op jit(solution)/shard_map/ppermute | solution.py:61
  42.1 2.5 %collective-permute-start.17 = (f32[1,2,128,128]{3,2,1,0:T(8,128)S(1)}, f32[1,2,128,128]{3,2,1,0:T(8,128)S(1)}, u32[]{:S(2)}, u32[]{:S(2)}) collective-permute-start(f32[1,2,128,128]{3,2,1,0:T(8,128)S(1)} %get-tuple-element.67), channel_id=1, source_target_pairs={{0,16},{1,17},{2,18},{3,19},{4,20},{5,21},{6,22},{7,23},{8,24},{9,... | collective-permute-start | bytes 393224 | tf_op jit(solution)/shard_map/ppermute | solution.py:61
  44.6 1.4 %collective-permute-start.18 = (f32[1,2,128,128]{3,2,1,0:T(8,128)S(1)}, f32[1,2,128,128]{3,2,1,0:T(8,128)S(1)}, u32[]{:S(2)}, u32[]{:S(2)}) collective-permute-start(f32[1,2,128,128]{3,2,1,0:T(8,128)S(1)} %get-tuple-element.68), channel_id=1, source_target_pairs={{0,17},{1,16},{2,19},{3,18},{4,21},{5,20},{6,23},{7,22},{8,25},{9,... | collective-permute-start | bytes 393224 | tf_op jit(solution)/shard_map/ppermute | solution.py:61
  46.0 0.1 collective-permute-start.6
  46.0 0.6 collective-permute-start.10
  46.7 4.0 %collective-permute-done.10.pair_ref = bf16[2,64,128]{2,1,0:T(8,128)(2,1)S(1)} collective-permute-done((bf16[2,64,128]{2,1,0:T(8,128)(2,1)S(1)}, bf16[2,64,128]{2,1,0:T(8,128)(2,1)S(1)}, u32[]{:S(2)}, u32[]{:S(2)}) %collective-permute-start.10) | collective-permute-done | bytes 32800 | tf_op jit(solution)/shard_map/ppermute | solution.py:61
  50.7 1.0 %shard_map.122.base_ref = f32[2,128,128]{2,1,0:T(8,128)S(1)} custom-call(s32[3]{0:T(128)S(1)} %pad_add_fusion.index_ref, s32[8,12]{1,0:T(8,128)S(1)} %copy-done.1, s32[8]{0:T(128)S(1)} %copy-done.2, bf16[8,32,384]{2,1,0:T(8,128)(2,1)S(1)} %reshape.15.near_ref.block_ref, bf16[1,2,128,128]{3,2,1,0:T(8,128)(2,1)S(1)} %get-tuple-element.56.own_ref.refs_3_, ...), custom_call_target="tpu_custom_call" | custom-call | tf_op jit(solution)/shard_map/pallas_call | solution.py:592
  51.8 1.1 %collective-permute-done.18.refs_3_ = f32[1,2,128,128]{3,2,1,0:T(8,128)S(1)} collective-permute-done((f32[1,2,128,128]{3,2,1,0:T(8,128)S(1)}, f32[1,2,128,128]{3,2,1,0:T(8,128)S(1)}, u32[]{:S(2)}, u32[]{:S(2)}) %collective-permute-start.18) | collective-permute-done | bytes 131104 | tf_op jit(solution)/shard_map/ppermute | solution.py:61
  52.8 1.0 %shard_map.127 = (f32[2,128,128]{2,1,0:T(8,128)S(1)}, f32[4,80,128]{2,1,0:T(8,128)S(1)}, f32[4,80,128]{2,1,0:T(8,128)S(1)}) custom-call(s32[3]{0:T(128)S(1)} %pad_add_fusion.index_ref, f32[1,160,128]{2,1,0:T(8,128)S(1)} %collective-permute-done.6.half_hbm.refs_1_, f32[128,128]{1,0:T(8,128)S(1)} %get-tuple-element.42.refs_0_.weight_ref, ...), custom_call_target="tpu_custom_call" | custom-call | tf_op jit(solution)/shard_map/pallas_call | solution.py:769
  53.9 0.1 collective-permute-start.20
  54.0 0.1 collective-permute-start.19
  54.1 1.3 %collective-permute-done.20.refs_1_ = f32[4,80,128]{2,1,0:T(8,128)S(1)} collective-permute-done((f32[4,80,128]{2,1,0:T(8,128)S(1)}, f32[4,80,128]{2,1,0:T(8,128)S(1)}, u32[]{:S(2)}, u32[]{:S(2)}) %collective-permute-start.20) | collective-permute-done | bytes 163872 | tf_op jit(solution)/shard_map/ppermute | solution.py:61
  55.4 0.5 collective-permute-start.21
  55.9 1.9 %collective-permute-start.22 = (f32[1,80,128]{2,1,0:T(8,128)S(1)}, f32[1,80,128]{2,1,0:T(8,128)S(1)}, u32[]{:S(2)}, u32[]{:S(2)}) collective-permute-start(f32[1,80,128]{2,1,0:T(8,128)S(1)} %get-tuple-element.74), channel_id=1, source_target_pairs={{0,16},{1,17},{2,18},{3,19},{4,20},{5,21},{6,22},{7,23},{8,24},{9,... | collective-permute-start | bytes 122888 | tf_op jit(solution)/shard_map/ppermute | solution.py:61
  57.8 1.2 %collective-permute-start.23 = (f32[1,80,128]{2,1,0:T(8,128)S(1)}, f32[1,80,128]{2,1,0:T(8,128)S(1)}, u32[]{:S(2)}, u32[]{:S(2)}) collective-permute-start(f32[1,80,128]{2,1,0:T(8,128)S(1)} %get-tuple-element.75), channel_id=1, source_target_pairs={{0,17},{1,16},{2,19},{3,18},{4,21},{5,20},{6,23},{7,22},{8,25},{9,... | collective-permute-start | bytes 122888 | tf_op jit(solution)/shard_map/ppermute | solution.py:61
  58.9 2.3 %collective-permute-done.19.refs_0_.refs_1_ = f32[1,160,128]{2,1,0:T(8,128)S(1)} collective-permute-done((f32[1,160,128]{2,1,0:T(8,128)S(1)}, f32[1,160,128]{2,1,0:T(8,128)S(1)}, u32[]{:S(2)}, u32[]{:S(2)}) %collective-permute-start.19) | collective-permute-done | bytes 81952 | tf_op jit(solution)/shard_map/ppermute | solution.py:61
  61.2 1.5 %collective-permute-done.23.refs_4_ = f32[1,80,128]{2,1,0:T(8,128)S(1)} collective-permute-done((f32[1,80,128]{2,1,0:T(8,128)S(1)}, f32[1,80,128]{2,1,0:T(8,128)S(1)}, u32[]{:S(2)}, u32[]{:S(2)}) %collective-permute-start.23) | collective-permute-done | bytes 40992 | tf_op jit(solution)/shard_map/ppermute | solution.py:61
  62.7 0.3 collective-permute-start.24
  63.0 1.5 %collective-permute-start.25 = (f32[1,80,128]{2,1,0:T(8,128)S(1)}, f32[1,80,128]{2,1,0:T(8,128)S(1)}, u32[]{:S(2)}, u32[]{:S(2)}) collective-permute-start(f32[1,80,128]{2,1,0:T(8,128)S(1)} %shard_map.130.refs_0_), channel_id=1, source_target_pairs={{0,4},{1,5},{2,6},{3,7},{4,0},{5,1},{6,2},{7,3},{8,12},{9,13},{10,... | collective-permute-start | bytes 122888 | tf_op jit(solution)/shard_map/ppermute | solution.py:61
  64.5 2.7 %collective-permute-start.26 = (f32[1,80,128]{2,1,0:T(8,128)S(1)}, f32[1,80,128]{2,1,0:T(8,128)S(1)}, u32[]{:S(2)}, u32[]{:S(2)}) collective-permute-start(f32[1,80,128]{2,1,0:T(8,128)S(1)} %shard_map.130.refs_0_), channel_id=1, source_target_pairs={{0,6},{1,7},{2,4},{3,5},{4,2},{5,3},{6,0},{7,1},{8,14},{9,15},{10,... | collective-permute-start | bytes 122888 | tf_op jit(solution)/shard_map/ppermute | solution.py:61
  67.2 0.9 collective-permute-done.25.refs_2_
  68.0 2.3 %collective-permute-done.26.refs_3_ = f32[1,80,128]{2,1,0:T(8,128)S(1)} collective-permute-done((f32[1,80,128]{2,1,0:T(8,128)S(1)}, f32[1,80,128]{2,1,0:T(8,128)S(1)}, u32[]{:S(2)}, u32[]{:S(2)}) %collective-permute-start.26) | collective-permute-done | bytes 40992 | tf_op jit(solution)/shard_map/ppermute | solution.py:61
  70.3 1.9 %collective-permute-start.27 = (f32[1,240,128]{2,1,0:T(8,128)S(1)}, f32[1,240,128]{2,1,0:T(8,128)S(1)}, u32[]{:S(2)}, u32[]{:S(2)}) collective-permute-start(f32[1,240,128]{2,1,0:T(8,128)S(1)} %shard_map.133.refs_0_), channel_id=1, source_target_pairs={{0,1},{1,0},{2,3},{3,2},{4,5},{5,4},{6,7},{7,6},{8,9},{9,8},{10,11... | collective-permute-start | bytes 368648 | tf_op jit(solution)/shard_map/ppermute | solution.py:61
  72.2 1.7 %collective-permute-start.29 = (f32[1,240,128]{2,1,0:T(8,128)S(1)}, f32[1,240,128]{2,1,0:T(8,128)S(1)}, u32[]{:S(2)}, u32[]{:S(2)}) collective-permute-start(f32[1,240,128]{2,1,0:T(8,128)S(1)} %shard_map.133.refs_0_), channel_id=1, source_target_pairs={{0,17},{1,16},{2,19},{3,18},{4,21},{5,20},{6,23},{7,22},{8,25},{9,... | collective-permute-start | bytes 368648 | tf_op jit(solution)/shard_map/ppermute | solution.py:61
  73.9 1.5 %collective-permute-done.27.refs_1_ = f32[1,240,128]{2,1,0:T(8,128)S(1)} collective-permute-done((f32[1,240,128]{2,1,0:T(8,128)S(1)}, f32[1,240,128]{2,1,0:T(8,128)S(1)}, u32[]{:S(2)}, u32[]{:S(2)}) %collective-permute-start.27) | collective-permute-done | bytes 122912 | tf_op jit(solution)/shard_map/ppermute | solution.py:61
  75.4 3.0 %collective-permute-done.28.refs_2_ = f32[1,240,128]{2,1,0:T(8,128)S(1)} collective-permute-done((f32[1,240,128]{2,1,0:T(8,128)S(1)}, f32[1,240,128]{2,1,0:T(8,128)S(1)}, u32[]{:S(2)}, u32[]{:S(2)}) %collective-permute-start.28) | collective-permute-done | bytes 122912 | tf_op jit(solution)/shard_map/ppermute | solution.py:61
  78.4 0.1 collective-permute-start.30
  78.5 1.9 %collective-permute-done.30.refs_1_ = f32[4,240,128]{2,1,0:T(8,128)S(1)} collective-permute-done((f32[4,240,128]{2,1,0:T(8,128)S(1)}, f32[4,240,128]{2,1,0:T(8,128)S(1)}, u32[]{:S(2)}, u32[]{:S(2)}) %collective-permute-start.30) | collective-permute-done | bytes 491552 | tf_op jit(solution)/shard_map/ppermute | solution.py:61
  80.4 6.7 %shard_map.135 = (f32[512,128]{1,0:T(8,128)}, f32[128,128]{1,0:T(8,128)}, f32[256,128]{1,0:T(8,128)}) custom-call(s32[3]{0:T(128)S(1)} %pad_add_fusion.index_ref, f32[4,2,128,128]{3,2,1,0:T(8,128)S(1)} %copy-done, f32[2,128,128]{2,1,0:T(8,128)S(1)} %get-tuple-element.69.image_ref, f32[4,240,128]{2,1,0:T(8,128)S(1)} %shard_map.134.refs_0_, ...), custom_call_target="tpu_custom_call" | custom-call | tf_op jit(solution)/shard_map/pallas_call | solution.py:592
  (33 shorter events, 0.3 us)
Async XLA Ops:
  0.6 15.9 %copy-start.3 = (bf16[8,12,32,32]{3,2,1,0:T(8,128)(2,1)S(1)}, bf16[8,12,32,32]{3,2,1,0:T(8,128)(2,1)}, u32[]{:S(2)}) copy-start(bf16[8,12,32,32]{3,2,1,0:T(8,128)(2,1)} %param.15) | copy-start | bytes 589828
  1.9 8.2 %collective-permute-start = (f32[1,56,128]{2,1,0:T(8,128)S(1)}, f32[1,56,128]{2,1,0:T(8,128)S(1)}, u32[]{:S(2)}, u32[]{:S(2)}) collective-permute-start(f32[1,56,128]{2,1,0:T(8,128)S(1)} %shard_map.112.pack_hbm.refs_1_), channel_id=1, source_target_pairs={{0,2},{1,3},{2,0},{3,1},{4,6},{5,7},{6,4},{7,5},{8,10},{9,11},{10,... | collective-permute-start | bytes 86024 | tf_op jit(solution)/shard_map/ppermute | solution.py:61
  5.0 5.2 %collective-permute-start.1 = (f32[1,56,128]{2,1,0:T(8,128)S(1)}, f32[1,56,128]{2,1,0:T(8,128)S(1)}, u32[]{:S(2)}, u32[]{:S(2)}) collective-permute-start(f32[1,56,128]{2,1,0:T(8,128)S(1)} %shard_map.112.pack_hbm.refs_1_), channel_id=1, source_target_pairs={{0,4},{1,5},{2,6},{3,7},{4,0},{5,1},{6,2},{7,3},{8,12},{9,13},{10,... | collective-permute-start | bytes 86024 | tf_op jit(solution)/shard_map/ppermute | solution.py:61
  7.6 5.7 %collective-permute-start.2 = (f32[1,56,128]{2,1,0:T(8,128)S(1)}, f32[1,56,128]{2,1,0:T(8,128)S(1)}, u32[]{:S(2)}, u32[]{:S(2)}) collective-permute-start(f32[1,56,128]{2,1,0:T(8,128)S(1)} %shard_map.112.pack_hbm.refs_1_), channel_id=1, source_target_pairs={{0,6},{1,7},{2,4},{3,5},{4,2},{5,3},{6,0},{7,1},{8,14},{9,15},{10,... | collective-permute-start | bytes 86024 | tf_op jit(solution)/shard_map/ppermute | solution.py:61
  13.3 1.7 %collective-permute-start.3 = (f32[4,160,128]{2,1,0:T(8,128)S(1)}, f32[4,160,128]{2,1,0:T(8,128)S(1)}, u32[]{:S(2)}, u32[]{:S(2)}) collective-permute-start(f32[4,160,128]{2,1,0:T(8,128)S(1)} %shard_map.115), channel_id=1, source_target_pairs={{0,8},{1,9},{2,10},{3,11},{4,12},{5,13},{6,14},{7,15},{8,0},{9,1},... | collective-permute-start | bytes 983048 | tf_op jit(solution)/shard_map/ppermute | solution.py:61
  13.3 6.0 %collective-permute-start.7 = (f32[4,56,128]{2,1,0:T(8,128)S(1)}, f32[4,56,128]{2,1,0:T(8,128)S(1)}, u32[]{:S(2)}, u32[]{:S(2)}) collective-permute-start(f32[4,56,128]{2,1,0:T(8,128)S(1)} %shard_map.114.refs_0_), channel_id=1, source_target_pairs={{0,1},{1,0},{2,3},{3,2},{4,5},{5,4},{6,7},{7,6},{8,9},{9,8},{10,11... | collective-permute-start | bytes 344072 | tf_op jit(solution)/shard_map/ppermute | solution.py:61
  15.0 8.1 %collective-permute-start.4 = (f32[2,160,128]{2,1,0:T(8,128)S(1)}, f32[2,160,128]{2,1,0:T(8,128)S(1)}, u32[]{:S(2)}, u32[]{:S(2)}) collective-permute-start(f32[2,160,128]{2,1,0:T(8,128)S(1)} %get-tuple-element.45), channel_id=1, source_target_pairs={{0,1},{1,0},{2,3},{3,2},{4,5},{5,4},{6,7},{7,6},{8,9},{9,8},{10,11... | collective-permute-start | bytes 491528 | tf_op jit(solution)/shard_map/ppermute | solution.py:61
  20.2 1.3 %collective-permute-start.8 = (f32[2,64,128]{2,1,0:T(8,128)S(1)}, f32[2,64,128]{2,1,0:T(8,128)S(1)}, u32[]{:S(2)}, u32[]{:S(2)}) collective-permute-start(f32[2,64,128]{2,1,0:T(8,128)S(1)} %get-tuple-element.52), channel_id=1, source_target_pairs={{0,8},{1,9},{2,10},{3,11},{4,12},{5,13},{6,14},{7,15},{8,0},{9,1},... | collective-permute-start | bytes 196616 | tf_op jit(solution)/shard_map/ppermute | solution.py:61
  21.5 4.0 %collective-permute-start.9 = (f32[1,64,128]{2,1,0:T(8,128)S(1)}, f32[1,64,128]{2,1,0:T(8,128)S(1)}, u32[]{:S(2)}, u32[]{:S(2)}) collective-permute-start(f32[1,64,128]{2,1,0:T(8,128)S(1)} %get-tuple-element.55), channel_id=1, source_target_pairs={{0,16},{1,17},{2,18},{3,19},{4,20},{5,21},{6,22},{7,23},{8,24},{9,... | collective-permute-start | bytes 98312 | tf_op jit(solution)/shard_map/ppermute | solution.py:61
  23.1 10.9 %collective-permute-start.5 = (f32[1,160,128]{2,1,0:T(8,128)S(1)}, f32[1,160,128]{2,1,0:T(8,128)S(1)}, u32[]{:S(2)}, u32[]{:S(2)}) collective-permute-start(f32[1,160,128]{2,1,0:T(8,128)S(1)} %get-tuple-element.47), channel_id=1, source_target_pairs={{0,16},{1,17},{2,18},{3,19},{4,20},{5,21},{6,22},{7,23},{8,24},{9,... | collective-permute-start | bytes 245768 | tf_op jit(solution)/shard_map/ppermute | solution.py:61
  26.3 7.0 %collective-permute-start.12 = (bf16[1,2,128,128]{3,2,1,0:T(8,128)(2,1)S(1)}, bf16[1,2,128,128]{3,2,1,0:T(8,128)(2,1)S(1)}, u32[]{:S(2)}, u32[]{:S(2)}) collective-permute-start(bf16[1,2,128,128]{3,2,1,0:T(8,128)(2,1)S(1)} %get-tuple-element.56.own_ref.refs_3_), channel_id=1, source_target_pairs={{0,2},{1,3},{2,0},{3,1},{4,6},{5,7},{6,4},{7,5},{8,10},{9,11},{10,... | collective-permute-start | bytes 196616 | tf_op jit(solution)/shard_map/ppermute | solution.py:61
  26.4 7.1 %collective-permute-start.13 = (bf16[1,2,128,128]{3,2,1,0:T(8,128)(2,1)S(1)}, bf16[1,2,128,128]{3,2,1,0:T(8,128)(2,1)S(1)}, u32[]{:S(2)}, u32[]{:S(2)}) collective-permute-start(bf16[1,2,128,128]{3,2,1,0:T(8,128)(2,1)S(1)} %get-tuple-element.56.own_ref.refs_3_), channel_id=1, source_target_pairs={{0,4},{1,5},{2,6},{3,7},{4,0},{5,1},{6,2},{7,3},{8,12},{9,13},{10,... | collective-permute-start | bytes 196616 | tf_op jit(solution)/shard_map/ppermute | solution.py:61
  27.6 6.4 %collective-permute-start.14 = (bf16[1,2,128,128]{3,2,1,0:T(8,128)(2,1)S(1)}, bf16[1,2,128,128]{3,2,1,0:T(8,128)(2,1)S(1)}, u32[]{:S(2)}, u32[]{:S(2)}) collective-permute-start(bf16[1,2,128,128]{3,2,1,0:T(8,128)(2,1)S(1)} %get-tuple-element.56.own_ref.refs_3_), channel_id=1, source_target_pairs={{0,6},{1,7},{2,4},{3,5},{4,2},{5,3},{6,0},{7,1},{8,14},{9,15},{10,... | collective-permute-start | bytes 196616 | tf_op jit(solution)/shard_map/ppermute | solution.py:61
  30.7 2.6 %collective-permute-start.11 = (bf16[2,64,128]{2,1,0:T(8,128)(2,1)S(1)}, bf16[2,64,128]{2,1,0:T(8,128)(2,1)S(1)}, u32[]{:S(2)}, u32[]{:S(2)}) collective-permute-start(bf16[2,64,128]{2,1,0:T(8,128)(2,1)S(1)} %get-tuple-element.58), channel_id=1, source_target_pairs={{1,2},{3,4},{5,6},{7,8},{9,10},{11,12},{13,14},{15,16},{17,18},{19... | collective-permute-start | bytes 98312 | tf_op jit(solution)/shard_map/ppermute | solution.py:732
  34.1 16.6 %copy-start.1 = (s32[8,12]{1,0:T(8,128)S(1)}, s32[8,12]{1,0:T(8,128)}, u32[]{:S(2)}) copy-start(s32[8,12]{1,0:T(8,128)} %panel_ref.1) | copy-start | bytes 1156
  34.1 16.6 %copy-start.2 = (s32[8]{0:T(128)S(1)}, s32[8]{0:T(128)}, u32[]{:S(2)}) copy-start(s32[8]{0:T(128)} %count_ref.1) | copy-start | bytes 100
  34.1 4.3 %collective-permute-start.15 = (bf16[4,2,128,128]{3,2,1,0:T(8,128)(2,1)S(1)}, bf16[4,2,128,128]{3,2,1,0:T(8,128)(2,1)S(1)}, u32[]{:S(2)}, u32[]{:S(2)}) collective-permute-start(bf16[4,2,128,128]{3,2,1,0:T(8,128)(2,1)S(1)} %shard_map.124.field_ref), channel_id=1, source_target_pairs={{0,8},{1,9},{2,10},{3,11},{4,12},{5,13},{6,14},{7,15},{8,0},{9,1},... | collective-permute-start | bytes 786440 | tf_op jit(solution)/shard_map/ppermute | solution.py:61
  38.3 14.5 %copy-start = (f32[4,2,128,128]{3,2,1,0:T(8,128)S(1)}, f32[4,2,128,128]{3,2,1,0:T(8,128)}, u32[]{:S(2)}) copy-start(f32[4,2,128,128]{3,2,1,0:T(8,128)} %basis_ref.3) | copy-start | bytes 1572868
  39.7 12.0 %collective-permute-start.16 = (f32[1,2,128,128]{3,2,1,0:T(8,128)S(1)}, f32[1,2,128,128]{3,2,1,0:T(8,128)S(1)}, u32[]{:S(2)}, u32[]{:S(2)}) collective-permute-start(f32[1,2,128,128]{3,2,1,0:T(8,128)S(1)} %get-tuple-element.66), channel_id=1, source_target_pairs={{0,1},{1,0},{2,3},{3,2},{4,5},{5,4},{6,7},{7,6},{8,9},{9,8},{10,11... | collective-permute-start | bytes 393224 | tf_op jit(solution)/shard_map/ppermute | solution.py:61
  42.1 9.7 %collective-permute-start.17 = (f32[1,2,128,128]{3,2,1,0:T(8,128)S(1)}, f32[1,2,128,128]{3,2,1,0:T(8,128)S(1)}, u32[]{:S(2)}, u32[]{:S(2)}) collective-permute-start(f32[1,2,128,128]{3,2,1,0:T(8,128)S(1)} %get-tuple-element.67), channel_id=1, source_target_pairs={{0,16},{1,17},{2,18},{3,19},{4,20},{5,21},{6,22},{7,23},{8,24},{9,... | collective-permute-start | bytes 393224 | tf_op jit(solution)/shard_map/ppermute | solution.py:61
  44.6 8.3 %collective-permute-start.18 = (f32[1,2,128,128]{3,2,1,0:T(8,128)S(1)}, f32[1,2,128,128]{3,2,1,0:T(8,128)S(1)}, u32[]{:S(2)}, u32[]{:S(2)}) collective-permute-start(f32[1,2,128,128]{3,2,1,0:T(8,128)S(1)} %get-tuple-element.68), channel_id=1, source_target_pairs={{0,17},{1,16},{2,19},{3,18},{4,21},{5,20},{6,23},{7,22},{8,25},{9,... | collective-permute-start | bytes 393224 | tf_op jit(solution)/shard_map/ppermute | solution.py:61
  46.0 5.8 %collective-permute-start.6 = (f32[1,160,128]{2,1,0:T(8,128)S(1)}, f32[1,160,128]{2,1,0:T(8,128)S(1)}, u32[]{:S(2)}, u32[]{:S(2)}) collective-permute-start(f32[1,160,128]{2,1,0:T(8,128)S(1)} %shard_map.118.refs_0_), channel_id=1, source_target_pairs={{0,2},{1,3},{2,0},{3,1},{4,6},{5,7},{6,4},{7,5},{8,10},{9,11},{10,... | collective-permute-start | bytes 245768 | tf_op jit(solution)/shard_map/ppermute | solution.py:61
  46.0 4.7 %collective-permute-start.10 = (bf16[2,64,128]{2,1,0:T(8,128)(2,1)S(1)}, bf16[2,64,128]{2,1,0:T(8,128)(2,1)S(1)}, u32[]{:S(2)}, u32[]{:S(2)}) collective-permute-start(bf16[2,64,128]{2,1,0:T(8,128)(2,1)S(1)} %get-tuple-element.57), channel_id=1, source_target_pairs={{0,1},{1,0},{2,3},{3,2},{4,5},{5,4},{6,7},{7,6},{8,9},{9,8},{10,11... | collective-permute-start | bytes 98312 | tf_op jit(solution)/shard_map/ppermute | solution.py:61
  53.9 1.5 %collective-permute-start.20 = (f32[4,80,128]{2,1,0:T(8,128)S(1)}, f32[4,80,128]{2,1,0:T(8,128)S(1)}, u32[]{:S(2)}, u32[]{:S(2)}) collective-permute-start(f32[4,80,128]{2,1,0:T(8,128)S(1)} %get-tuple-element.71), channel_id=1, source_target_pairs={{0,8},{1,9},{2,10},{3,11},{4,12},{5,13},{6,14},{7,15},{8,0},{9,1},... | collective-permute-start | bytes 491528 | tf_op jit(solution)/shard_map/ppermute | solution.py:61
  54.0 7.2 %collective-permute-start.19 = (f32[1,160,128]{2,1,0:T(8,128)S(1)}, f32[1,160,128]{2,1,0:T(8,128)S(1)}, u32[]{:S(2)}, u32[]{:S(2)}) collective-permute-start(f32[1,160,128]{2,1,0:T(8,128)S(1)} %shard_map.128.refs_0_), channel_id=1, source_target_pairs={{0,4},{1,5},{2,6},{3,7},{4,0},{5,1},{6,2},{7,3},{8,12},{9,13},{10,... | collective-permute-start | bytes 245768 | tf_op jit(solution)/shard_map/ppermute | solution.py:61
  55.4 5.8 %collective-permute-start.21 = (f32[1,80,128]{2,1,0:T(8,128)S(1)}, f32[1,80,128]{2,1,0:T(8,128)S(1)}, u32[]{:S(2)}, u32[]{:S(2)}) collective-permute-start(f32[1,80,128]{2,1,0:T(8,128)S(1)} %get-tuple-element.73), channel_id=1, source_target_pairs={{0,1},{1,0},{2,3},{3,2},{4,5},{5,4},{6,7},{7,6},{8,9},{9,8},{10,11... | collective-permute-start | bytes 122888 | tf_op jit(solution)/shard_map/ppermute | solution.py:61
  55.9 5.3 %collective-permute-start.22 = (f32[1,80,128]{2,1,0:T(8,128)S(1)}, f32[1,80,128]{2,1,0:T(8,128)S(1)}, u32[]{:S(2)}, u32[]{:S(2)}) collective-permute-start(f32[1,80,128]{2,1,0:T(8,128)S(1)} %get-tuple-element.74), channel_id=1, source_target_pairs={{0,16},{1,17},{2,18},{3,19},{4,20},{5,21},{6,22},{7,23},{8,24},{9,... | collective-permute-start | bytes 122888 | tf_op jit(solution)/shard_map/ppermute | solution.py:61
  57.8 4.9 %collective-permute-start.23 = (f32[1,80,128]{2,1,0:T(8,128)S(1)}, f32[1,80,128]{2,1,0:T(8,128)S(1)}, u32[]{:S(2)}, u32[]{:S(2)}) collective-permute-start(f32[1,80,128]{2,1,0:T(8,128)S(1)} %get-tuple-element.75), channel_id=1, source_target_pairs={{0,17},{1,16},{2,19},{3,18},{4,21},{5,20},{6,23},{7,22},{8,25},{9,... | collective-permute-start | bytes 122888 | tf_op jit(solution)/shard_map/ppermute | solution.py:61
  62.7 4.5 %collective-permute-start.24 = (f32[1,80,128]{2,1,0:T(8,128)S(1)}, f32[1,80,128]{2,1,0:T(8,128)S(1)}, u32[]{:S(2)}, u32[]{:S(2)}) collective-permute-start(f32[1,80,128]{2,1,0:T(8,128)S(1)} %shard_map.130.refs_0_), channel_id=1, source_target_pairs={{0,2},{1,3},{2,0},{3,1},{4,6},{5,7},{6,4},{7,5},{8,10},{9,11},{10,... | collective-permute-start | bytes 122888 | tf_op jit(solution)/shard_map/ppermute | solution.py:61
  63.0 5.0 %collective-permute-start.25 = (f32[1,80,128]{2,1,0:T(8,128)S(1)}, f32[1,80,128]{2,1,0:T(8,128)S(1)}, u32[]{:S(2)}, u32[]{:S(2)}) collective-permute-start(f32[1,80,128]{2,1,0:T(8,128)S(1)} %shard_map.130.refs_0_), channel_id=1, source_target_pairs={{0,4},{1,5},{2,6},{3,7},{4,0},{5,1},{6,2},{7,3},{8,12},{9,13},{10,... | collective-permute-start | bytes 122888 | tf_op jit(solution)/shard_map/ppermute | solution.py:61
  64.5 5.8 %collective-permute-start.26 = (f32[1,80,128]{2,1,0:T(8,128)S(1)}, f32[1,80,128]{2,1,0:T(8,128)S(1)}, u32[]{:S(2)}, u32[]{:S(2)}) collective-permute-start(f32[1,80,128]{2,1,0:T(8,128)S(1)} %shard_map.130.refs_0_), channel_id=1, source_target_pairs={{0,6},{1,7},{2,4},{3,5},{4,2},{5,3},{6,0},{7,1},{8,14},{9,15},{10,... | collective-permute-start | bytes 122888 | tf_op jit(solution)/shard_map/ppermute | solution.py:61
  70.3 5.1 %collective-permute-start.27 = (f32[1,240,128]{2,1,0:T(8,128)S(1)}, f32[1,240,128]{2,1,0:T(8,128)S(1)}, u32[]{:S(2)}, u32[]{:S(2)}) collective-permute-start(f32[1,240,128]{2,1,0:T(8,128)S(1)} %shard_map.133.refs_0_), channel_id=1, source_target_pairs={{0,1},{1,0},{2,3},{3,2},{4,5},{5,4},{6,7},{7,6},{8,9},{9,8},{10,11... | collective-permute-start | bytes 368648 | tf_op jit(solution)/shard_map/ppermute | solution.py:61
  72.2 6.2 %collective-permute-start.28 = (f32[1,240,128]{2,1,0:T(8,128)S(1)}, f32[1,240,128]{2,1,0:T(8,128)S(1)}, u32[]{:S(2)}, u32[]{:S(2)}) collective-permute-start(f32[1,240,128]{2,1,0:T(8,128)S(1)} %shard_map.133.refs_0_), channel_id=1, source_target_pairs={{0,16},{1,17},{2,18},{3,19},{4,20},{5,21},{6,22},{7,23},{8,24},{9,... | collective-permute-start | bytes 368648 | tf_op jit(solution)/shard_map/ppermute | solution.py:61
  72.2 6.2 %collective-permute-start.29 = (f32[1,240,128]{2,1,0:T(8,128)S(1)}, f32[1,240,128]{2,1,0:T(8,128)S(1)}, u32[]{:S(2)}, u32[]{:S(2)}) collective-permute-start(f32[1,240,128]{2,1,0:T(8,128)S(1)} %shard_map.133.refs_0_), channel_id=1, source_target_pairs={{0,17},{1,16},{2,19},{3,18},{4,21},{5,20},{6,23},{7,22},{8,25},{9,... | collective-permute-start | bytes 368648 | tf_op jit(solution)/shard_map/ppermute | solution.py:61
  78.4 1.9 %collective-permute-start.30 = (f32[4,240,128]{2,1,0:T(8,128)S(1)}, f32[4,240,128]{2,1,0:T(8,128)S(1)}, u32[]{:S(2)}, u32[]{:S(2)}) collective-permute-start(f32[4,240,128]{2,1,0:T(8,128)S(1)} %shard_map.134.refs_0_), channel_id=1, source_target_pairs={{0,8},{1,9},{2,10},{3,11},{4,12},{5,13},{6,14},{7,15},{8,0},{9,1},... | collective-permute-start | bytes 1474568 | tf_op jit(solution)/shard_map/ppermute | solution.py:61

commit v13 on v12

--- a/solution.py
+++ b/solution.py
@@ -81,8 +81,12 @@
     return [parts[0]] + [flip(parts[j], combined(group, j)) for j in range(1, 1 << len(group))]
 
 
+def farthest_first(parts):
+    return [parts[0], *parts[:0:-1]]
+
+
 def join_kernel(count, *refs):
-    parts, out_ref = refs[-1 - count : -1], refs[-1]
+    parts, out_ref = farthest_first(refs[-1 - count : -1]), refs[-1]
     size = parts[0].shape[0]
     for j, ref in enumerate(parts):
         out_ref[j * size : (j + 1) * size] = ref[...]
@@ -96,7 +100,7 @@
         in_specs=[ANY] * len(after) + [VMEM] * len(parts),
         out_specs=VMEM,
         compiler_params=PARAMS,
-    )(*after, *parts)
+    )(*after, *farthest_first(parts))
 
 
 def gather_steps(held, groups, after=()):
@@ -137,7 +141,7 @@
         in_specs=[ANY] * len(after) + [VMEM] * len(parts),
         out_specs=[VMEM] * ways,
         compiler_params=PARAMS,
-    )(*after, *parts)
+    )(*after, *farthest_first(parts))
 
 
 def scatter_steps(parts, groups):
@@ -774,7 +778,7 @@
         out_specs=[VMEM] * 3,
         scratch_shapes=[pltpu.VMEM((sum_rows, rhs_count), jnp.float32)],
         compiler_params=PARAMS,
-    )(index, half_steps[2], weight, basis, base, *far_parts)
+    )(index, half_steps[2], weight, basis, base, *farthest_first(far_parts))
     (total,) = sum_parts(scatter_steps(parts, halving), 1, half_steps[3:4])
     total = sum_butterfly(total, high_groups)
     parts = gather_steps(append(total, half_total), halving[::-1])

time: 87.3 us -> 84.8 us (0.971)
  waiting for transfers between devices: 28 us -> 26.5 us
  starting transfers between devices: 38.1 us -> 37.1 us
    ppermute x30, waiting for transfers between devices: 28 us -> 26.5 us  [flip(): return lax.ppermute(block, AXES, [(i, i ^ mask) for i in range(count)])]
    ppermute x30, starting transfers between devices: 37.4 us -> 36.5 us  [flip(): return lax.ppermute(block, AXES, [(i, i ^ mask) for i in range(count)])]
where the time goes in v13:
time: 84.8 us; the launch traced here: 84.7 us
  starting transfers between devices  37.1 us (44%)
  waiting for transfers between devices  26.5 us (31%)
  Pallas kernels  18.9 us (22%)
  local copies, waits for them, and re-layouts  1.07 us (1%)
  between operations  0.95 us (1%)
    ppermute x30, starting transfers between devices, flip(): return lax.ppermute(block, AXES, [(i, i ^ mask) for i in range(count)])  36.5 us
    ppermute x30, waiting for transfers between devices, flip(): return lax.ppermute(block, AXES, [(i, i ^ mask) for i in range(count)])  26.5 us
    pallas_call x6, Pallas kernels, call(): pl.pallas_call(kernel, out_shape=out_shape, in_specs=[SMEM] * scalars + [...  11.4 us
    pallas_call x2, Pallas kernels, body(): pl.pallas_call(functools.partial(far_kernel, ways), out_shape=[f32(target...  2.73 us
    pallas_call x1, Pallas kernels, body(): pl.pallas_call(functools.partial(matrix_kernel, coarse_count), out_shape=...  1.91 us
  transfers between devices with their start and end apart: 31, of which 18 were waited for; matrix products, arithmetic and copies ran while one was open for 1% of the time, Pallas kernels for 10%

profile of v13, /device:TPU:0, one launch (start us, length us, event | category | flops | bytes accessed | tf_op | source)
XLA Modules:
  0.0 84.7 jit_solution(1135445047908951436)
XLA Ops:
  0.6 1.2 %shard_map.112.pack_hbm.refs_1_ = f32[1,56,128]{2,1,0:T(8,128)S(1)} custom-call(s32[2,128]{1,0:T(2,128)} %agg_hbm.3, f32[4,2,128,128]{3,2,1,0:T(8,128)} %basis_ref.3, f32[2,128]{1,0:T(2,128)} %points_hbm.1, f32[1,128]{1,0:T(1,128)} %bitcast.8), custom_call_target="tpu_custom_call" | custom-call | tf_op jit(solution)/shard_map/pallas_call | solution.py:596
  1.9 5.1 %collective-permute-start = (f32[1,56,128]{2,1,0:T(8,128)S(1)}, f32[1,56,128]{2,1,0:T(8,128)S(1)}, u32[]{:S(2)}, u32[]{:S(2)}) collective-permute-start(f32[1,56,128]{2,1,0:T(8,128)S(1)} %shard_map.112.pack_hbm.refs_1_), channel_id=1, source_target_pairs={{0,6},{1,7},{2,4},{3,5},{4,2},{5,3},{6,0},{7,1},{8,14},{9,15},{10,... | collective-permute-start | bytes 86024 | tf_op jit(solution)/shard_map/ppermute | solution.py:61
  7.0 0.6 collective-permute-start.2
  7.6 0.1 pad_add_fusion.index_ref
  7.7 2.4 %shard_map.113 = (f32[4,48,384]{2,1,0:T(8,128)S(1)}, f32[2,48,128]{2,1,0:T(8,128)S(1)}, f32[2,128,128]{2,1,0:T(8,128)S(1)}, f32[128,128]{1,0:T(8,128)S(1)}, f32[...) custom-call(s32[3]{0:T(128)S(1)} %pad_add_fusion.index_ref, f32[1,56,128]{2,1,0:T(8,128)S(1)} %shard_map.112.pack_hbm.refs_1_, ...), custom_call_target="tpu_custom_call" | custom-call | tf_op jit(solution)/shard_map/pallas_call | solution.py:596
  10.1 0.0 collective-permute-done.refs_2_
  10.1 1.6 %collective-permute-done.1.refs_3_ = f32[1,56,128]{2,1,0:T(8,128)S(1)} collective-permute-done((f32[1,56,128]{2,1,0:T(8,128)S(1)}, f32[1,56,128]{2,1,0:T(8,128)S(1)}, u32[]{:S(2)}, u32[]{:S(2)}) %collective-permute-start.1) | collective-permute-done | bytes 28704 | tf_op jit(solution)/shard_map/ppermute | solution.py:61
  11.8 0.1 collective-permute-start.3
  11.9 1.6 %collective-permute-start.7 = (f32[4,56,128]{2,1,0:T(8,128)S(1)}, f32[4,56,128]{2,1,0:T(8,128)S(1)}, u32[]{:S(2)}, u32[]{:S(2)}) collective-permute-start(f32[4,56,128]{2,1,0:T(8,128)S(1)} %shard_map.114.refs_0_), channel_id=1, source_target_pairs={{0,1},{1,0},{2,3},{3,2},{4,5},{5,4},{6,7},{7,6},{8,9},{9,8},{10,11... | collective-permute-start | bytes 344072 | tf_op jit(solution)/shard_map/ppermute | solution.py:61
  13.4 0.1 collective-permute-done.3.refs_1_
  13.5 1.6 %collective-permute-start.4 = (f32[2,160,128]{2,1,0:T(8,128)S(1)}, f32[2,160,128]{2,1,0:T(8,128)S(1)}, u32[]{:S(2)}, u32[]{:S(2)}) collective-permute-start(f32[2,160,128]{2,1,0:T(8,128)S(1)} %get-tuple-element.45), channel_id=1, source_target_pairs={{0,1},{1,0},{2,3},{3,2},{4,5},{5,4},{6,7},{7,6},{8,9},{9,8},{10,11... | collective-permute-start | bytes 491528 | tf_op jit(solution)/shard_map/ppermute | solution.py:61
  15.1 0.3 copy.13
  15.4 0.7 reshape.15.near_ref.block_ref
  16.2 1.7 %collective-permute-done.7.refs_1_ = f32[4,56,128]{2,1,0:T(8,128)S(1)} collective-permute-done((f32[4,56,128]{2,1,0:T(8,128)S(1)}, f32[4,56,128]{2,1,0:T(8,128)S(1)}, u32[]{:S(2)}, u32[]{:S(2)}) %collective-permute-start.7) | collective-permute-done | bytes 114720 | tf_op jit(solution)/shard_map/ppermute | solution.py:61
  17.9 0.8 shard_map.119
  18.7 0.1 collective-permute-start.8
  18.8 1.2 %collective-permute-done.8.got_ref = f32[2,64,128]{2,1,0:T(8,128)S(1)} collective-permute-done((f32[2,64,128]{2,1,0:T(8,128)S(1)}, f32[2,64,128]{2,1,0:T(8,128)S(1)}, u32[]{:S(2)}, u32[]{:S(2)}) %collective-permute-start.8) | collective-permute-done | bytes 65568 | tf_op jit(solution)/shard_map/ppermute | solution.py:61
  20.1 1.6 %collective-permute-start.9 = (f32[1,64,128]{2,1,0:T(8,128)S(1)}, f32[1,64,128]{2,1,0:T(8,128)S(1)}, u32[]{:S(2)}, u32[]{:S(2)}) collective-permute-start(f32[1,64,128]{2,1,0:T(8,128)S(1)} %get-tuple-element.55), channel_id=1, source_target_pairs={{0,16},{1,17},{2,18},{3,19},{4,20},{5,21},{6,22},{7,23},{8,24},{9,... | collective-permute-start | bytes 98312 | tf_op jit(solution)/shard_map/ppermute | solution.py:61
  21.7 0.9 %collective-permute-start.5 = (f32[1,160,128]{2,1,0:T(8,128)S(1)}, f32[1,160,128]{2,1,0:T(8,128)S(1)}, u32[]{:S(2)}, u32[]{:S(2)}) collective-permute-start(f32[1,160,128]{2,1,0:T(8,128)S(1)} %get-tuple-element.47), channel_id=1, source_target_pairs={{0,16},{1,17},{2,18},{3,19},{4,20},{5,21},{6,22},{7,23},{8,24},{9,... | collective-permute-start | bytes 245768 | tf_op jit(solution)/shard_map/ppermute | solution.py:61
  22.6 1.5 %collective-permute-done.9.refs_1_ = f32[1,64,128]{2,1,0:T(8,128)S(1)} collective-permute-done((f32[1,64,128]{2,1,0:T(8,128)S(1)}, f32[1,64,128]{2,1,0:T(8,128)S(1)}, u32[]{:S(2)}, u32[]{:S(2)}) %collective-permute-start.9) | collective-permute-done | bytes 32800 | tf_op jit(solution)/shard_map/ppermute | solution.py:61
  24.1 0.8 shard_map.121
  24.8 2.2 %collective-permute-start.12 = (bf16[1,2,128,128]{3,2,1,0:T(8,128)(2,1)S(1)}, bf16[1,2,128,128]{3,2,1,0:T(8,128)(2,1)S(1)}, u32[]{:S(2)}, u32[]{:S(2)}) collective-permute-start(bf16[1,2,128,128]{3,2,1,0:T(8,128)(2,1)S(1)} %get-tuple-element.56.own_ref.refs_3_), channel_id=1, source_target_pairs={{0,6},{1,7},{2,4},{3,5},{4,2},{5,3},{6,0},{7,1},{8,14},{9,15},{10,... | collective-permute-start | bytes 196616 | tf_op jit(solution)/shard_map/ppermute | solution.py:61
  27.1 2.2 %collective-permute-start.14 = (bf16[1,2,128,128]{3,2,1,0:T(8,128)(2,1)S(1)}, bf16[1,2,128,128]{3,2,1,0:T(8,128)(2,1)S(1)}, u32[]{:S(2)}, u32[]{:S(2)}) collective-permute-start(bf16[1,2,128,128]{3,2,1,0:T(8,128)(2,1)S(1)} %get-tuple-element.56.own_ref.refs_3_), channel_id=1, source_target_pairs={{0,2},{1,3},{2,0},{3,1},{4,6},{5,7},{6,4},{7,5},{8,10},{9,11},{10,... | collective-permute-start | bytes 196616 | tf_op jit(solution)/shard_map/ppermute | solution.py:61
  29.3 0.7 collective-permute-start.11
  30.0 1.9 %shard_map.123.refs_0_.matrix_ref = bf16[4,3,128,1024]{3,2,1,0:T(8,128)(2,1)S(1)} custom-call(f32[4,8,128]{2,1,0:T(8,128)S(1)} %get-tuple-element.59.own_ref, f32[4,8,128]{2,1,0:T(8,128)S(1)} %get-tuple-element.60.other_ref, f32[1,64,128]{2,1,0:T(8,128)S(1)} %get-tuple-element.54.refs_0_, f32[1,64,128]{2,1,0:T(8,128)S(1)} %collective-permute-done.9.refs_1_), custom_call_target="tpu_custom_call" | custom-call | tf_op jit(solution)/shard_map/pallas_call | solution.py:725
  31.9 1.8 %collective-permute-done.13.refs_5_ = bf16[1,2,128,128]{3,2,1,0:T(8,128)(2,1)S(1)} collective-permute-done((bf16[1,2,128,128]{3,2,1,0:T(8,128)(2,1)S(1)}, bf16[1,2,128,128]{3,2,1,0:T(8,128)(2,1)S(1)}, u32[]{:S(2)}, u32[]{:S(2)}) %collective-permute-start.13) | collective-permute-done | bytes 65568 | tf_op jit(solution)/shard_map/ppermute | solution.py:61
  33.7 0.0 copy-start.1
  33.7 0.0 copy-start.2
  33.7 2.8 %collective-permute-start.15 = (bf16[4,2,128,128]{3,2,1,0:T(8,128)(2,1)S(1)}, bf16[4,2,128,128]{3,2,1,0:T(8,128)(2,1)S(1)}, u32[]{:S(2)}, u32[]{:S(2)}) collective-permute-start(bf16[4,2,128,128]{3,2,1,0:T(8,128)(2,1)S(1)} %shard_map.124.field_ref), channel_id=1, source_target_pairs={{0,8},{1,9},{2,10},{3,11},{4,12},{5,13},{6,14},{7,15},{8,0},{9,1},... | collective-permute-start | bytes 786440 | tf_op jit(solution)/shard_map/ppermute | solution.py:61
  36.5 1.4 %shard_map.125 = (f32[1,2,128,128]{3,2,1,0:T(8,128)S(1)}, f32[1,2,128,128]{3,2,1,0:T(8,128)S(1)}, f32[1,2,128,128]{3,2,1,0:T(8,128)S(1)}, f32[1,2,128,128]{3,2,1,0:T(8,128)S(1)}) custom-call(bf16[4,3,128,1024]{3,2,1,0:T(8,128)(2,1)S(1)} %shard_map.123.refs_0_.matrix_ref, bf16[4,2,128,128]{3,2,1,0:T(8,128)(2,1)S(1)} %shard_map.124.field_ref), custom_call_target="tpu_custom_call" | custom-call | tf_op jit(solution)/shard_map/pallas_call | solution.py:744
  37.8 0.0 copy-start
  37.9 1.4 %shard_map.126 = (f32[1,2,128,128]{3,2,1,0:T(8,128)S(1)}, f32[1,2,128,128]{3,2,1,0:T(8,128)S(1)}, f32[1,2,128,128]{3,2,1,0:T(8,128)S(1)}, f32[1,2,128,128]{3,2,1,0:T(8,128)S(1)}) custom-call(bf16[4,3,128,1024]{3,2,1,0:T(8,128)(2,1)S(1)} %shard_map.123.refs_0_.matrix_ref, bf16[4,2,128,128]{3,2,1,0:T(8,128)(2,1)S(1)} %collective-permute-done.15.field_ref, ...), custom_call_target="tpu_custom_call" | custom-call | tf_op jit(solution)/shard_map/pallas_call | solution.py:744
  39.2 2.6 %collective-permute-start.16 = (f32[1,2,128,128]{3,2,1,0:T(8,128)S(1)}, f32[1,2,128,128]{3,2,1,0:T(8,128)S(1)}, u32[]{:S(2)}, u32[]{:S(2)}) collective-permute-start(f32[1,2,128,128]{3,2,1,0:T(8,128)S(1)} %get-tuple-element.66), channel_id=1, source_target_pairs={{0,17},{1,16},{2,19},{3,18},{4,21},{5,20},{6,23},{7,22},{8,25},{9,... | collective-permute-start | bytes 393224 | tf_op jit(solution)/shard_map/ppermute | solution.py:61
  41.8 1.3 %collective-permute-start.17 = (f32[1,2,128,128]{3,2,1,0:T(8,128)S(1)}, f32[1,2,128,128]{3,2,1,0:T(8,128)S(1)}, u32[]{:S(2)}, u32[]{:S(2)}) collective-permute-start(f32[1,2,128,128]{3,2,1,0:T(8,128)S(1)} %get-tuple-element.67), channel_id=1, source_target_pairs={{0,16},{1,17},{2,18},{3,19},{4,20},{5,21},{6,22},{7,23},{8,24},{9,... | collective-permute-start | bytes 393224 | tf_op jit(solution)/shard_map/ppermute | solution.py:61
  43.1 1.4 %collective-permute-start.18 = (f32[1,2,128,128]{3,2,1,0:T(8,128)S(1)}, f32[1,2,128,128]{3,2,1,0:T(8,128)S(1)}, u32[]{:S(2)}, u32[]{:S(2)}) collective-permute-start(f32[1,2,128,128]{3,2,1,0:T(8,128)S(1)} %get-tuple-element.68), channel_id=1, source_target_pairs={{0,1},{1,0},{2,3},{3,2},{4,5},{5,4},{6,7},{7,6},{8,9},{9,8},{10,11... | collective-permute-start | bytes 393224 | tf_op jit(solution)/shard_map/ppermute | solution.py:61
  44.5 0.1 collective-permute-start.6
  44.6 0.7 collective-permute-start.10
  45.3 6.5 %collective-permute-done.10.pair_ref = bf16[2,64,128]{2,1,0:T(8,128)(2,1)S(1)} collective-permute-done((bf16[2,64,128]{2,1,0:T(8,128)(2,1)S(1)}, bf16[2,64,128]{2,1,0:T(8,128)(2,1)S(1)}, u32[]{:S(2)}, u32[]{:S(2)}) %collective-permute-start.10) | collective-permute-done | bytes 32800 | tf_op jit(solution)/shard_map/ppermute | solution.py:61
  51.8 1.0 %shard_map.122.base_ref = f32[2,128,128]{2,1,0:T(8,128)S(1)} custom-call(s32[3]{0:T(128)S(1)} %pad_add_fusion.index_ref, s32[8,12]{1,0:T(8,128)S(1)} %copy-done.1, s32[8]{0:T(128)S(1)} %copy-done.2, bf16[8,32,384]{2,1,0:T(8,128)(2,1)S(1)} %reshape.15.near_ref.block_ref, bf16[1,2,128,128]{3,2,1,0:T(8,128)(2,1)S(1)} %get-tuple-element.56.own_ref.refs_3_, ...), custom_call_target="tpu_custom_call" | custom-call | tf_op jit(solution)/shard_map/pallas_call | solution.py:596
  52.9 1.0 %shard_map.127 = (f32[2,128,128]{2,1,0:T(8,128)S(1)}, f32[4,80,128]{2,1,0:T(8,128)S(1)}, f32[4,80,128]{2,1,0:T(8,128)S(1)}) custom-call(s32[3]{0:T(128)S(1)} %pad_add_fusion.index_ref, f32[1,160,128]{2,1,0:T(8,128)S(1)} %collective-permute-done.6.half_hbm.refs_1_, f32[128,128]{1,0:T(8,128)S(1)} %get-tuple-element.42.refs_0_.weight_ref, ...), custom_call_target="tpu_custom_call" | custom-call | tf_op jit(solution)/shard_map/pallas_call | solution.py:773
  53.9 0.1 collective-permute-start.20
  54.0 0.1 collective-permute-start.19
  54.1 1.3 %collective-permute-done.20.refs_1_ = f32[4,80,128]{2,1,0:T(8,128)S(1)} collective-permute-done((f32[4,80,128]{2,1,0:T(8,128)S(1)}, f32[4,80,128]{2,1,0:T(8,128)S(1)}, u32[]{:S(2)}, u32[]{:S(2)}) %collective-permute-start.20) | collective-permute-done | bytes 163872 | tf_op jit(solution)/shard_map/ppermute | solution.py:61
  55.4 0.3 collective-permute-start.21
  55.7 0.8 collective-permute-start.22
  56.5 2.5 %collective-permute-start.23 = (f32[1,80,128]{2,1,0:T(8,128)S(1)}, f32[1,80,128]{2,1,0:T(8,128)S(1)}, u32[]{:S(2)}, u32[]{:S(2)}) collective-permute-start(f32[1,80,128]{2,1,0:T(8,128)S(1)} %get-tuple-element.75), channel_id=1, source_target_pairs={{0,1},{1,0},{2,3},{3,2},{4,5},{5,4},{6,7},{7,6},{8,9},{9,8},{10,11... | collective-permute-start | bytes 122888 | tf_op jit(solution)/shard_map/ppermute | solution.py:61
  59.0 0.9 %collective-permute-done.19.refs_0_.refs_1_ = f32[1,160,128]{2,1,0:T(8,128)S(1)} collective-permute-done((f32[1,160,128]{2,1,0:T(8,128)S(1)}, f32[1,160,128]{2,1,0:T(8,128)S(1)}, u32[]{:S(2)}, u32[]{:S(2)}) %collective-permute-start.19) | collective-permute-done | bytes 81952 | tf_op jit(solution)/shard_map/ppermute | solution.py:61
  59.8 0.6 collective-permute-done.21.refs_2_
  60.4 0.5 collective-permute-done.23.refs_4_
  60.9 2.8 %collective-permute-start.24 = (f32[1,80,128]{2,1,0:T(8,128)S(1)}, f32[1,80,128]{2,1,0:T(8,128)S(1)}, u32[]{:S(2)}, u32[]{:S(2)}) collective-permute-start(f32[1,80,128]{2,1,0:T(8,128)S(1)} %shard_map.130.refs_0_), channel_id=1, source_target_pairs={{0,6},{1,7},{2,4},{3,5},{4,2},{5,3},{6,0},{7,1},{8,14},{9,15},{10,... | collective-permute-start | bytes 122888 | tf_op jit(solution)/shard_map/ppermute | solution.py:61
  63.8 0.7 collective-permute-start.25
  64.5 0.9 %collective-permute-start.26 = (f32[1,80,128]{2,1,0:T(8,128)S(1)}, f32[1,80,128]{2,1,0:T(8,128)S(1)}, u32[]{:S(2)}, u32[]{:S(2)}) collective-permute-start(f32[1,80,128]{2,1,0:T(8,128)S(1)} %shard_map.130.refs_0_), channel_id=1, source_target_pairs={{0,2},{1,3},{2,0},{3,1},{4,6},{5,7},{6,4},{7,5},{8,10},{9,11},{10,... | collective-permute-start | bytes 122888 | tf_op jit(solution)/shard_map/ppermute | solution.py:61
  65.4 1.6 %collective-permute-done.24.refs_1_ = f32[1,80,128]{2,1,0:T(8,128)S(1)} collective-permute-done((f32[1,80,128]{2,1,0:T(8,128)S(1)}, f32[1,80,128]{2,1,0:T(8,128)S(1)}, u32[]{:S(2)}, u32[]{:S(2)}) %collective-permute-start.24) | collective-permute-done | bytes 40992 | tf_op jit(solution)/shard_map/ppermute | solution.py:61
  67.0 1.7 %collective-permute-done.25.refs_2_ = f32[1,80,128]{2,1,0:T(8,128)S(1)} collective-permute-done((f32[1,80,128]{2,1,0:T(8,128)S(1)}, f32[1,80,128]{2,1,0:T(8,128)S(1)}, u32[]{:S(2)}, u32[]{:S(2)}) %collective-permute-start.25) | collective-permute-done | bytes 40992 | tf_op jit(solution)/shard_map/ppermute | solution.py:61
  68.8 0.2 collective-permute-done.26.refs_3_
  69.0 0.7 collective-permute-start.27
  69.6 1.5 %collective-permute-start.28 = (f32[1,240,128]{2,1,0:T(8,128)S(1)}, f32[1,240,128]{2,1,0:T(8,128)S(1)}, u32[]{:S(2)}, u32[]{:S(2)}) collective-permute-start(f32[1,240,128]{2,1,0:T(8,128)S(1)} %shard_map.133.refs_0_), channel_id=1, source_target_pairs={{0,16},{1,17},{2,18},{3,19},{4,20},{5,21},{6,22},{7,23},{8,24},{9,... | collective-permute-start | bytes 368648 | tf_op jit(solution)/shard_map/ppermute | solution.py:61
  71.1 1.4 %collective-permute-start.29 = (f32[1,240,128]{2,1,0:T(8,128)S(1)}, f32[1,240,128]{2,1,0:T(8,128)S(1)}, u32[]{:S(2)}, u32[]{:S(2)}) collective-permute-start(f32[1,240,128]{2,1,0:T(8,128)S(1)} %shard_map.133.refs_0_), channel_id=1, source_target_pairs={{0,1},{1,0},{2,3},{3,2},{4,5},{5,4},{6,7},{7,6},{8,9},{9,8},{10,11... | collective-permute-start | bytes 368648 | tf_op jit(solution)/shard_map/ppermute | solution.py:61
  72.5 2.4 %collective-permute-done.27.refs_1_ = f32[1,240,128]{2,1,0:T(8,128)S(1)} collective-permute-done((f32[1,240,128]{2,1,0:T(8,128)S(1)}, f32[1,240,128]{2,1,0:T(8,128)S(1)}, u32[]{:S(2)}, u32[]{:S(2)}) %collective-permute-start.27) | collective-permute-done | bytes 122912 | tf_op jit(solution)/shard_map/ppermute | solution.py:61
  74.9 0.9 %collective-permute-done.28.refs_2_ = f32[1,240,128]{2,1,0:T(8,128)S(1)} collective-permute-done((f32[1,240,128]{2,1,0:T(8,128)S(1)}, f32[1,240,128]{2,1,0:T(8,128)S(1)}, u32[]{:S(2)}, u32[]{:S(2)}) %collective-permute-start.28) | collective-permute-done | bytes 122912 | tf_op jit(solution)/shard_map/ppermute | solution.py:61
  75.8 0.1 collective-permute-done.29.refs_3_
  76.0 0.1 collective-permute-start.30
  76.1 1.9 %collective-permute-done.30.refs_1_ = f32[4,240,128]{2,1,0:T(8,128)S(1)} collective-permute-done((f32[4,240,128]{2,1,0:T(8,128)S(1)}, f32[4,240,128]{2,1,0:T(8,128)S(1)}, u32[]{:S(2)}, u32[]{:S(2)}) %collective-permute-start.30) | collective-permute-done | bytes 491552 | tf_op jit(solution)/shard_map/ppermute | solution.py:61
  78.0 6.7 %shard_map.135 = (f32[512,128]{1,0:T(8,128)}, f32[128,128]{1,0:T(8,128)}, f32[256,128]{1,0:T(8,128)}) custom-call(s32[3]{0:T(128)S(1)} %pad_add_fusion.index_ref, f32[4,2,128,128]{3,2,1,0:T(8,128)S(1)} %copy-done, f32[2,128,128]{2,1,0:T(8,128)S(1)} %get-tuple-element.69.image_ref, f32[4,240,128]{2,1,0:T(8,128)S(1)} %shard_map.134.refs_0_, ...), custom_call_target="tpu_custom_call" | custom-call | tf_op jit(solution)/shard_map/pallas_call | solution.py:596
  (33 shorter events, 0.3 us)
Async XLA Ops:
  0.6 14.5 %copy-start.3 = (bf16[8,12,32,32]{3,2,1,0:T(8,128)(2,1)S(1)}, bf16[8,12,32,32]{3,2,1,0:T(8,128)(2,1)}, u32[]{:S(2)}) copy-start(bf16[8,12,32,32]{3,2,1,0:T(8,128)(2,1)} %param.15) | copy-start | bytes 589828
  1.9 8.3 %collective-permute-start = (f32[1,56,128]{2,1,0:T(8,128)S(1)}, f32[1,56,128]{2,1,0:T(8,128)S(1)}, u32[]{:S(2)}, u32[]{:S(2)}) collective-permute-start(f32[1,56,128]{2,1,0:T(8,128)S(1)} %shard_map.112.pack_hbm.refs_1_), channel_id=1, source_target_pairs={{0,6},{1,7},{2,4},{3,5},{4,2},{5,3},{6,0},{7,1},{8,14},{9,15},{10,... | collective-permute-start | bytes 86024 | tf_op jit(solution)/shard_map/ppermute | solution.py:61
  7.0 4.8 %collective-permute-start.1 = (f32[1,56,128]{2,1,0:T(8,128)S(1)}, f32[1,56,128]{2,1,0:T(8,128)S(1)}, u32[]{:S(2)}, u32[]{:S(2)}) collective-permute-start(f32[1,56,128]{2,1,0:T(8,128)S(1)} %shard_map.112.pack_hbm.refs_1_), channel_id=1, source_target_pairs={{0,4},{1,5},{2,6},{3,7},{4,0},{5,1},{6,2},{7,3},{8,12},{9,13},{10,... | collective-permute-start | bytes 86024 | tf_op jit(solution)/shard_map/ppermute | solution.py:61
  7.0 4.8 %collective-permute-start.2 = (f32[1,56,128]{2,1,0:T(8,128)S(1)}, f32[1,56,128]{2,1,0:T(8,128)S(1)}, u32[]{:S(2)}, u32[]{:S(2)}) collective-permute-start(f32[1,56,128]{2,1,0:T(8,128)S(1)} %shard_map.112.pack_hbm.refs_1_), channel_id=1, source_target_pairs={{0,2},{1,3},{2,0},{3,1},{4,6},{5,7},{6,4},{7,5},{8,10},{9,11},{10,... | collective-permute-start | bytes 86024 | tf_op jit(solution)/shard_map/ppermute | solution.py:61
  11.8 1.7 %collective-permute-start.3 = (f32[4,160,128]{2,1,0:T(8,128)S(1)}, f32[4,160,128]{2,1,0:T(8,128)S(1)}, u32[]{:S(2)}, u32[]{:S(2)}) collective-permute-start(f32[4,160,128]{2,1,0:T(8,128)S(1)} %shard_map.115), channel_id=1, source_target_pairs={{0,8},{1,9},{2,10},{3,11},{4,12},{5,13},{6,14},{7,15},{8,0},{9,1},... | collective-permute-start | bytes 983048 | tf_op jit(solution)/shard_map/ppermute | solution.py:61
  11.9 6.0 %collective-permute-start.7 = (f32[4,56,128]{2,1,0:T(8,128)S(1)}, f32[4,56,128]{2,1,0:T(8,128)S(1)}, u32[]{:S(2)}, u32[]{:S(2)}) collective-permute-start(f32[4,56,128]{2,1,0:T(8,128)S(1)} %shard_map.114.refs_0_), channel_id=1, source_target_pairs={{0,1},{1,0},{2,3},{3,2},{4,5},{5,4},{6,7},{7,6},{8,9},{9,8},{10,11... | collective-permute-start | bytes 344072 | tf_op jit(solution)/shard_map/ppermute | solution.py:61
  13.5 8.1 %collective-permute-start.4 = (f32[2,160,128]{2,1,0:T(8,128)S(1)}, f32[2,160,128]{2,1,0:T(8,128)S(1)}, u32[]{:S(2)}, u32[]{:S(2)}) collective-permute-start(f32[2,160,128]{2,1,0:T(8,128)S(1)} %get-tuple-element.45), channel_id=1, source_target_pairs={{0,1},{1,0},{2,3},{3,2},{4,5},{5,4},{6,7},{7,6},{8,9},{9,8},{10,11... | collective-permute-start | bytes 491528 | tf_op jit(solution)/shard_map/ppermute | solution.py:61
  18.7 1.3 %collective-permute-start.8 = (f32[2,64,128]{2,1,0:T(8,128)S(1)}, f32[2,64,128]{2,1,0:T(8,128)S(1)}, u32[]{:S(2)}, u32[]{:S(2)}) collective-permute-start(f32[2,64,128]{2,1,0:T(8,128)S(1)} %get-tuple-element.52), channel_id=1, source_target_pairs={{0,8},{1,9},{2,10},{3,11},{4,12},{5,13},{6,14},{7,15},{8,0},{9,1},... | collective-permute-start | bytes 196616 | tf_op jit(solution)/shard_map/ppermute | solution.py:61
  20.1 4.0 %collective-permute-start.9 = (f32[1,64,128]{2,1,0:T(8,128)S(1)}, f32[1,64,128]{2,1,0:T(8,128)S(1)}, u32[]{:S(2)}, u32[]{:S(2)}) collective-permute-start(f32[1,64,128]{2,1,0:T(8,128)S(1)} %get-tuple-element.55), channel_id=1, source_target_pairs={{0,16},{1,17},{2,18},{3,19},{4,20},{5,21},{6,22},{7,23},{8,24},{9,... | collective-permute-start | bytes 98312 | tf_op jit(solution)/shard_map/ppermute | solution.py:61
  21.7 12.0 %collective-permute-start.5 = (f32[1,160,128]{2,1,0:T(8,128)S(1)}, f32[1,160,128]{2,1,0:T(8,128)S(1)}, u32[]{:S(2)}, u32[]{:S(2)}) collective-permute-start(f32[1,160,128]{2,1,0:T(8,128)S(1)} %get-tuple-element.47), channel_id=1, source_target_pairs={{0,16},{1,17},{2,18},{3,19},{4,20},{5,21},{6,22},{7,23},{8,24},{9,... | collective-permute-start | bytes 245768 | tf_op jit(solution)/shard_map/ppermute | solution.py:61
  24.8 7.0 %collective-permute-start.12 = (bf16[1,2,128,128]{3,2,1,0:T(8,128)(2,1)S(1)}, bf16[1,2,128,128]{3,2,1,0:T(8,128)(2,1)S(1)}, u32[]{:S(2)}, u32[]{:S(2)}) collective-permute-start(bf16[1,2,128,128]{3,2,1,0:T(8,128)(2,1)S(1)} %get-tuple-element.56.own_ref.refs_3_), channel_id=1, source_target_pairs={{0,6},{1,7},{2,4},{3,5},{4,2},{5,3},{6,0},{7,1},{8,14},{9,15},{10,... | collective-permute-start | bytes 196616 | tf_op jit(solution)/shard_map/ppermute | solution.py:61
  27.1 6.6 %collective-permute-start.13 = (bf16[1,2,128,128]{3,2,1,0:T(8,128)(2,1)S(1)}, bf16[1,2,128,128]{3,2,1,0:T(8,128)(2,1)S(1)}, u32[]{:S(2)}, u32[]{:S(2)}) collective-permute-start(bf16[1,2,128,128]{3,2,1,0:T(8,128)(2,1)S(1)} %get-tuple-element.56.own_ref.refs_3_), channel_id=1, source_target_pairs={{0,4},{1,5},{2,6},{3,7},{4,0},{5,1},{6,2},{7,3},{8,12},{9,13},{10,... | collective-permute-start | bytes 196616 | tf_op jit(solution)/shard_map/ppermute | solution.py:61
  27.1 6.6 %collective-permute-start.14 = (bf16[1,2,128,128]{3,2,1,0:T(8,128)(2,1)S(1)}, bf16[1,2,128,128]{3,2,1,0:T(8,128)(2,1)S(1)}, u32[]{:S(2)}, u32[]{:S(2)}) collective-permute-start(bf16[1,2,128,128]{3,2,1,0:T(8,128)(2,1)S(1)} %get-tuple-element.56.own_ref.refs_3_), channel_id=1, source_target_pairs={{0,2},{1,3},{2,0},{3,1},{4,6},{5,7},{6,4},{7,5},{8,10},{9,11},{10,... | collective-permute-start | bytes 196616 | tf_op jit(solution)/shard_map/ppermute | solution.py:61
  29.3 2.6 %collective-permute-start.11 = (bf16[2,64,128]{2,1,0:T(8,128)(2,1)S(1)}, bf16[2,64,128]{2,1,0:T(8,128)(2,1)S(1)}, u32[]{:S(2)}, u32[]{:S(2)}) collective-permute-start(bf16[2,64,128]{2,1,0:T(8,128)(2,1)S(1)} %get-tuple-element.58), channel_id=1, source_target_pairs={{1,2},{3,4},{5,6},{7,8},{9,10},{11,12},{13,14},{15,16},{17,18},{19... | collective-permute-start | bytes 98312 | tf_op jit(solution)/shard_map/ppermute | solution.py:736
  33.7 18.1 %copy-start.1 = (s32[8,12]{1,0:T(8,128)S(1)}, s32[8,12]{1,0:T(8,128)}, u32[]{:S(2)}) copy-start(s32[8,12]{1,0:T(8,128)} %panel_ref.1) | copy-start | bytes 1156
  33.7 18.1 %copy-start.2 = (s32[8]{0:T(128)S(1)}, s32[8]{0:T(128)}, u32[]{:S(2)}) copy-start(s32[8]{0:T(128)} %count_ref.1) | copy-start | bytes 100
  33.7 4.1 %collective-permute-start.15 = (bf16[4,2,128,128]{3,2,1,0:T(8,128)(2,1)S(1)}, bf16[4,2,128,128]{3,2,1,0:T(8,128)(2,1)S(1)}, u32[]{:S(2)}, u32[]{:S(2)}) collective-permute-start(bf16[4,2,128,128]{3,2,1,0:T(8,128)(2,1)S(1)} %shard_map.124.field_ref), channel_id=1, source_target_pairs={{0,8},{1,9},{2,10},{3,11},{4,12},{5,13},{6,14},{7,15},{8,0},{9,1},... | collective-permute-start | bytes 786440 | tf_op jit(solution)/shard_map/ppermute | solution.py:61
  37.8 15.0 %copy-start = (f32[4,2,128,128]{3,2,1,0:T(8,128)S(1)}, f32[4,2,128,128]{3,2,1,0:T(8,128)}, u32[]{:S(2)}) copy-start(f32[4,2,128,128]{3,2,1,0:T(8,128)} %basis_ref.3) | copy-start | bytes 1572868
  39.2 13.6 %collective-permute-start.16 = (f32[1,2,128,128]{3,2,1,0:T(8,128)S(1)}, f32[1,2,128,128]{3,2,1,0:T(8,128)S(1)}, u32[]{:S(2)}, u32[]{:S(2)}) collective-permute-start(f32[1,2,128,128]{3,2,1,0:T(8,128)S(1)} %get-tuple-element.66), channel_id=1, source_target_pairs={{0,17},{1,16},{2,19},{3,18},{4,21},{5,20},{6,23},{7,22},{8,25},{9,... | collective-permute-start | bytes 393224 | tf_op jit(solution)/shard_map/ppermute | solution.py:61
  41.8 11.0 %collective-permute-start.17 = (f32[1,2,128,128]{3,2,1,0:T(8,128)S(1)}, f32[1,2,128,128]{3,2,1,0:T(8,128)S(1)}, u32[]{:S(2)}, u32[]{:S(2)}) collective-permute-start(f32[1,2,128,128]{3,2,1,0:T(8,128)S(1)} %get-tuple-element.67), channel_id=1, source_target_pairs={{0,16},{1,17},{2,18},{3,19},{4,20},{5,21},{6,22},{7,23},{8,24},{9,... | collective-permute-start | bytes 393224 | tf_op jit(solution)/shard_map/ppermute | solution.py:61
  43.1 9.7 %collective-permute-start.18 = (f32[1,2,128,128]{3,2,1,0:T(8,128)S(1)}, f32[1,2,128,128]{3,2,1,0:T(8,128)S(1)}, u32[]{:S(2)}, u32[]{:S(2)}) collective-permute-start(f32[1,2,128,128]{3,2,1,0:T(8,128)S(1)} %get-tuple-element.68), channel_id=1, source_target_pairs={{0,1},{1,0},{2,3},{3,2},{4,5},{5,4},{6,7},{7,6},{8,9},{9,8},{10,11... | collective-permute-start | bytes 393224 | tf_op jit(solution)/shard_map/ppermute | solution.py:61
  44.5 8.3 %collective-permute-start.6 = (f32[1,160,128]{2,1,0:T(8,128)S(1)}, f32[1,160,128]{2,1,0:T(8,128)S(1)}, u32[]{:S(2)}, u32[]{:S(2)}) collective-permute-start(f32[1,160,128]{2,1,0:T(8,128)S(1)} %shard_map.118.refs_0_), channel_id=1, source_target_pairs={{0,2},{1,3},{2,0},{3,1},{4,6},{5,7},{6,4},{7,5},{8,10},{9,11},{10,... | collective-permute-start | bytes 245768 | tf_op jit(solution)/shard_map/ppermute | solution.py:61
  44.6 7.2 %collective-permute-start.10 = (bf16[2,64,128]{2,1,0:T(8,128)(2,1)S(1)}, bf16[2,64,128]{2,1,0:T(8,128)(2,1)S(1)}, u32[]{:S(2)}, u32[]{:S(2)}) collective-permute-start(bf16[2,64,128]{2,1,0:T(8,128)(2,1)S(1)} %get-tuple-element.57), channel_id=1, source_target_pairs={{0,1},{1,0},{2,3},{3,2},{4,5},{5,4},{6,7},{7,6},{8,9},{9,8},{10,11... | collective-permute-start | bytes 98312 | tf_op jit(solution)/shard_map/ppermute | solution.py:61
  53.9 1.5 %collective-permute-start.20 = (f32[4,80,128]{2,1,0:T(8,128)S(1)}, f32[4,80,128]{2,1,0:T(8,128)S(1)}, u32[]{:S(2)}, u32[]{:S(2)}) collective-permute-start(f32[4,80,128]{2,1,0:T(8,128)S(1)} %get-tuple-element.71), channel_id=1, source_target_pairs={{0,8},{1,9},{2,10},{3,11},{4,12},{5,13},{6,14},{7,15},{8,0},{9,1},... | collective-permute-start | bytes 491528 | tf_op jit(solution)/shard_map/ppermute | solution.py:61
  54.0 5.8 %collective-permute-start.19 = (f32[1,160,128]{2,1,0:T(8,128)S(1)}, f32[1,160,128]{2,1,0:T(8,128)S(1)}, u32[]{:S(2)}, u32[]{:S(2)}) collective-permute-start(f32[1,160,128]{2,1,0:T(8,128)S(1)} %shard_map.128.refs_0_), channel_id=1, source_target_pairs={{0,4},{1,5},{2,6},{3,7},{4,0},{5,1},{6,2},{7,3},{8,12},{9,13},{10,... | collective-permute-start | bytes 245768 | tf_op jit(solution)/shard_map/ppermute | solution.py:61
  55.4 5.0 %collective-permute-start.21 = (f32[1,80,128]{2,1,0:T(8,128)S(1)}, f32[1,80,128]{2,1,0:T(8,128)S(1)}, u32[]{:S(2)}, u32[]{:S(2)}) collective-permute-start(f32[1,80,128]{2,1,0:T(8,128)S(1)} %get-tuple-element.73), channel_id=1, source_target_pairs={{0,17},{1,16},{2,19},{3,18},{4,21},{5,20},{6,23},{7,22},{8,25},{9,... | collective-permute-start | bytes 122888 | tf_op jit(solution)/shard_map/ppermute | solution.py:61
  55.7 4.7 %collective-permute-start.22 = (f32[1,80,128]{2,1,0:T(8,128)S(1)}, f32[1,80,128]{2,1,0:T(8,128)S(1)}, u32[]{:S(2)}, u32[]{:S(2)}) collective-permute-start(f32[1,80,128]{2,1,0:T(8,128)S(1)} %get-tuple-element.74), channel_id=1, source_target_pairs={{0,16},{1,17},{2,18},{3,19},{4,20},{5,21},{6,22},{7,23},{8,24},{9,... | collective-permute-start | bytes 122888 | tf_op jit(solution)/shard_map/ppermute | solution.py:61
  56.5 4.5 %collective-permute-start.23 = (f32[1,80,128]{2,1,0:T(8,128)S(1)}, f32[1,80,128]{2,1,0:T(8,128)S(1)}, u32[]{:S(2)}, u32[]{:S(2)}) collective-permute-start(f32[1,80,128]{2,1,0:T(8,128)S(1)} %get-tuple-element.75), channel_id=1, source_target_pairs={{0,1},{1,0},{2,3},{3,2},{4,5},{5,4},{6,7},{7,6},{8,9},{9,8},{10,11... | collective-permute-start | bytes 122888 | tf_op jit(solution)/shard_map/ppermute | solution.py:61
  60.9 6.1 %collective-permute-start.24 = (f32[1,80,128]{2,1,0:T(8,128)S(1)}, f32[1,80,128]{2,1,0:T(8,128)S(1)}, u32[]{:S(2)}, u32[]{:S(2)}) collective-permute-start(f32[1,80,128]{2,1,0:T(8,128)S(1)} %shard_map.130.refs_0_), channel_id=1, source_target_pairs={{0,6},{1,7},{2,4},{3,5},{4,2},{5,3},{6,0},{7,1},{8,14},{9,15},{10,... | collective-permute-start | bytes 122888 | tf_op jit(solution)/shard_map/ppermute | solution.py:61
  63.8 5.0 %collective-permute-start.25 = (f32[1,80,128]{2,1,0:T(8,128)S(1)}, f32[1,80,128]{2,1,0:T(8,128)S(1)}, u32[]{:S(2)}, u32[]{:S(2)}) collective-permute-start(f32[1,80,128]{2,1,0:T(8,128)S(1)} %shard_map.130.refs_0_), channel_id=1, source_target_pairs={{0,4},{1,5},{2,6},{3,7},{4,0},{5,1},{6,2},{7,3},{8,12},{9,13},{10,... | collective-permute-start | bytes 122888 | tf_op jit(solution)/shard_map/ppermute | solution.py:61
  64.5 4.4 %collective-permute-start.26 = (f32[1,80,128]{2,1,0:T(8,128)S(1)}, f32[1,80,128]{2,1,0:T(8,128)S(1)}, u32[]{:S(2)}, u32[]{:S(2)}) collective-permute-start(f32[1,80,128]{2,1,0:T(8,128)S(1)} %shard_map.130.refs_0_), channel_id=1, source_target_pairs={{0,2},{1,3},{2,0},{3,1},{4,6},{5,7},{6,4},{7,5},{8,10},{9,11},{10,... | collective-permute-start | bytes 122888 | tf_op jit(solution)/shard_map/ppermute | solution.py:61
  69.0 6.0 %collective-permute-start.27 = (f32[1,240,128]{2,1,0:T(8,128)S(1)}, f32[1,240,128]{2,1,0:T(8,128)S(1)}, u32[]{:S(2)}, u32[]{:S(2)}) collective-permute-start(f32[1,240,128]{2,1,0:T(8,128)S(1)} %shard_map.133.refs_0_), channel_id=1, source_target_pairs={{0,17},{1,16},{2,19},{3,18},{4,21},{5,20},{6,23},{7,22},{8,25},{9,... | collective-permute-start | bytes 368648 | tf_op jit(solution)/shard_map/ppermute | solution.py:61
  69.6 6.2 %collective-permute-start.28 = (f32[1,240,128]{2,1,0:T(8,128)S(1)}, f32[1,240,128]{2,1,0:T(8,128)S(1)}, u32[]{:S(2)}, u32[]{:S(2)}) collective-permute-start(f32[1,240,128]{2,1,0:T(8,128)S(1)} %shard_map.133.refs_0_), channel_id=1, source_target_pairs={{0,16},{1,17},{2,18},{3,19},{4,20},{5,21},{6,22},{7,23},{8,24},{9,... | collective-permute-start | bytes 368648 | tf_op jit(solution)/shard_map/ppermute | solution.py:61
  71.1 4.9 %collective-permute-start.29 = (f32[1,240,128]{2,1,0:T(8,128)S(1)}, f32[1,240,128]{2,1,0:T(8,128)S(1)}, u32[]{:S(2)}, u32[]{:S(2)}) collective-permute-start(f32[1,240,128]{2,1,0:T(8,128)S(1)} %shard_map.133.refs_0_), channel_id=1, source_target_pairs={{0,1},{1,0},{2,3},{3,2},{4,5},{5,4},{6,7},{7,6},{8,9},{9,8},{10,11... | collective-permute-start | bytes 368648 | tf_op jit(solution)/shard_map/ppermute | solution.py:61
  76.0 1.9 %collective-permute-start.30 = (f32[4,240,128]{2,1,0:T(8,128)S(1)}, f32[4,240,128]{2,1,0:T(8,128)S(1)}, u32[]{:S(2)}, u32[]{:S(2)}) collective-permute-start(f32[4,240,128]{2,1,0:T(8,128)S(1)} %shard_map.134.refs_0_), channel_id=1, source_target_pairs={{0,8},{1,9},{2,10},{3,11},{4,12},{5,13},{6,14},{7,15},{8,0},{9,1},... | collective-permute-start | bytes 1474568 | tf_op jit(solution)/shard_map/ppermute | solution.py:61

commit v14 on v13

--- a/solution.py
+++ b/solution.py
@@ -15,6 +15,7 @@
 ELASTIC = 40.0
 AXES = ("narrow", "wide")
 EXTRA = 8
+WHOLE_BYTES = 8 * 1024 * 1024
 ROWS = 8
 SMEM = pl.BlockSpec(memory_space=pltpu.SMEM)
 VMEM = pl.BlockSpec(memory_space=pltpu.VMEM)
@@ -402,6 +403,26 @@
             else:
                 out_ref[row, 0] = out_x
                 out_ref[row, 1] = out_y
+
+
+def far_whole_kernel(ways, number, matrix_ref, field_ref, *refs):
+    earlier, outs, fields_ref = refs[: -1 - ways], refs[-1 - ways : -1], refs[-1]
+    point_count, rhs_count = field_ref.shape[2:]
+    for s in range(field_ref.shape[0]):
+        for b in range(2):
+            rows = slice(s * point_count, (s + 1) * point_count)
+            fields_ref[rows, b * rhs_count : (b + 1) * rhs_count] = field_ref[s, b]
+    size = fields_ref.shape[0]
+    lanes = slice(number * size, (number + 1) * size)
+    for k in range(matrix_ref.shape[0]):
+        mixed = dot16(matrix_ref[k, 1, :, lanes], fields_ref[...])
+        out_x = dot16(matrix_ref[k, 0, :, lanes], fields_ref[:, :rhs_count])
+        out_y = dot16(matrix_ref[k, 2, :, lanes], fields_ref[:, rhs_count:])
+        sums = [out_x + mixed[:, rhs_count:], out_y + mixed[:, :rhs_count]]
+        for a in range(2):
+            if earlier:
+                sums[a] = sums[a] + earlier[k % ways][k // ways, a]
+            outs[k % ways][k // ways, a] = sums[a]
 
 
 def near_kernel(
@@ -740,10 +761,16 @@
 
     ways = 1 << len(plane_groups[0])
     far_parts = []
+    far_out = [f32(target_count // ways, 2, point_count, rhs_count)] * ways
+    far_scratch = [pltpu.VMEM((source_total // 2, 2 * rhs_count), jnp.bfloat16)]
     for number, field in enumerate(fields):
+        if matrix.size * 2 <= WHOLE_BYTES:
+            kernel = functools.partial(far_whole_kernel, ways, number)
+            far_parts = call(kernel, far_out, (matrix, field, *far_parts), 0, far_scratch)
+            continue
         far_parts = pl.pallas_call(
             functools.partial(far_kernel, ways),
-            out_shape=[f32(target_count // ways, 2, point_count, rhs_count)] * ways,
+            out_shape=far_out,
             grid=(target_count,),
             in_specs=[
                 pl.BlockSpec(
@@ -753,7 +780,7 @@
             ]
             + [VMEM] * (1 + len(far_parts)),
             out_specs=[VMEM] * ways,
-            scratch_shapes=[pltpu.VMEM((source_total // 2, 2 * rhs_count), jnp.bfloat16)],
+            scratch_shapes=far_scratch,
             compiler_params=PARAMS,
         )(matrix, field, *far_parts)
     far_parts = scatter_steps(far_parts, plane_groups)

time: 84.8 us -> 83.8 us (0.988)
  Pallas kernels: 18.9 us -> 17.3 us
    pallas_call x2 -> x0, Pallas kernels: 2.73 us -> none  [body(): pl.pallas_call(functools.partial(far_kernel, ways), out_shape=[f32(target...]
    pallas_call x6 -> x8, Pallas kernels: 11.4 us -> 12.6 us  [call(): pl.pallas_call(kernel, out_shape=out_shape, in_specs=[SMEM] * scalars + [...]
  transfers between devices with their start and end apart: 31 -> 31, of which waited for: 18 -> 19; matrix products, arithmetic and copies ran while one was open for 1% -> 1% of each run, Pallas kernels for 10% -> 9%
where the time goes in v14:
time: 83.8 us; the launch traced here: 83.7 us
  starting transfers between devices  37.4 us (45%)
  waiting for transfers between devices  26.9 us (32%)
  Pallas kernels  17.3 us (21%)
  local copies, waits for them, and re-layouts  1.07 us (1%)
  between operations  0.95 us (1%)
    ppermute x30, starting transfers between devices, flip(): return lax.ppermute(block, AXES, [(i, i ^ mask) for i in range(count)])  36.7 us
    ppermute x30, waiting for transfers between devices, flip(): return lax.ppermute(block, AXES, [(i, i ^ mask) for i in range(count)])  26.9 us
    pallas_call x8, Pallas kernels, call(): pl.pallas_call(kernel, out_shape=out_shape, in_specs=[SMEM] * scalars + [...  12.6 us
    pallas_call x1, Pallas kernels, body(): pl.pallas_call(functools.partial(matrix_kernel, coarse_count), out_shape=...  1.91 us
  transfers between devices with their start and end apart: 31, of which 19 were waited for; matrix products, arithmetic and copies ran while one was open for 1% of the time, Pallas kernels for 9%

profile of v14, /device:TPU:0, one launch (start us, length us, event | category | flops | bytes accessed | tf_op | source)
XLA Modules:
  0.0 83.7 jit_solution(10506996572216759726)
XLA Ops:
  0.6 1.2 %shard_map.112.pack_hbm.refs_1_ = f32[1,56,128]{2,1,0:T(8,128)S(1)} custom-call(s32[2,128]{1,0:T(2,128)} %agg_hbm.3, f32[4,2,128,128]{3,2,1,0:T(8,128)} %basis_ref.3, f32[2,128]{1,0:T(2,128)} %points_hbm.1, f32[1,128]{1,0:T(1,128)} %bitcast.8), custom_call_target="tpu_custom_call" | custom-call | tf_op jit(solution)/shard_map/pallas_call | solution.py:617
  1.9 5.1 %collective-permute-start = (f32[1,56,128]{2,1,0:T(8,128)S(1)}, f32[1,56,128]{2,1,0:T(8,128)S(1)}, u32[]{:S(2)}, u32[]{:S(2)}) collective-permute-start(f32[1,56,128]{2,1,0:T(8,128)S(1)} %shard_map.112.pack_hbm.refs_1_), channel_id=1, source_target_pairs={{0,6},{1,7},{2,4},{3,5},{4,2},{5,3},{6,0},{7,1},{8,14},{9,15},{10,... | collective-permute-start | bytes 86024 | tf_op jit(solution)/shard_map/ppermute | solution.py:62
  7.0 0.6 collective-permute-start.2
  7.6 0.1 pad_add_fusion.index_ref
  7.7 2.4 %shard_map.113 = (f32[4,48,384]{2,1,0:T(8,128)S(1)}, f32[2,48,128]{2,1,0:T(8,128)S(1)}, f32[2,128,128]{2,1,0:T(8,128)S(1)}, f32[128,128]{1,0:T(8,128)S(1)}, f32[...) custom-call(s32[3]{0:T(128)S(1)} %pad_add_fusion.index_ref, f32[1,56,128]{2,1,0:T(8,128)S(1)} %shard_map.112.pack_hbm.refs_1_, ...), custom_call_target="tpu_custom_call" | custom-call | tf_op jit(solution)/shard_map/pallas_call | solution.py:617
  10.1 1.6 %collective-permute-done.1.refs_3_ = f32[1,56,128]{2,1,0:T(8,128)S(1)} collective-permute-done((f32[1,56,128]{2,1,0:T(8,128)S(1)}, f32[1,56,128]{2,1,0:T(8,128)S(1)}, u32[]{:S(2)}, u32[]{:S(2)}) %collective-permute-start.1) | collective-permute-done | bytes 28704 | tf_op jit(solution)/shard_map/ppermute | solution.py:62
  11.8 0.1 collective-permute-start.3
  11.9 1.6 %collective-permute-start.7 = (f32[4,56,128]{2,1,0:T(8,128)S(1)}, f32[4,56,128]{2,1,0:T(8,128)S(1)}, u32[]{:S(2)}, u32[]{:S(2)}) collective-permute-start(f32[4,56,128]{2,1,0:T(8,128)S(1)} %shard_map.114.refs_0_), channel_id=1, source_target_pairs={{0,1},{1,0},{2,3},{3,2},{4,5},{5,4},{6,7},{7,6},{8,9},{9,8},{10,11... | collective-permute-start | bytes 344072 | tf_op jit(solution)/shard_map/ppermute | solution.py:62
  13.4 0.1 collective-permute-done.3.refs_1_
  13.5 1.6 %collective-permute-start.4 = (f32[2,160,128]{2,1,0:T(8,128)S(1)}, f32[2,160,128]{2,1,0:T(8,128)S(1)}, u32[]{:S(2)}, u32[]{:S(2)}) collective-permute-start(f32[2,160,128]{2,1,0:T(8,128)S(1)} %get-tuple-element.45), channel_id=1, source_target_pairs={{0,1},{1,0},{2,3},{3,2},{4,5},{5,4},{6,7},{7,6},{8,9},{9,8},{10,11... | collective-permute-start | bytes 491528 | tf_op jit(solution)/shard_map/ppermute | solution.py:62
  15.1 0.3 copy.13
  15.4 0.7 reshape.15.near_ref.block_ref
  16.2 1.7 %collective-permute-done.7.refs_1_ = f32[4,56,128]{2,1,0:T(8,128)S(1)} collective-permute-done((f32[4,56,128]{2,1,0:T(8,128)S(1)}, f32[4,56,128]{2,1,0:T(8,128)S(1)}, u32[]{:S(2)}, u32[]{:S(2)}) %collective-permute-start.7) | collective-permute-done | bytes 114720 | tf_op jit(solution)/shard_map/ppermute | solution.py:62
  17.9 0.8 %shard_map.119 = (f32[2,64,128]{2,1,0:T(8,128)S(1)}, f32[2,64,128]{2,1,0:T(8,128)S(1)}, f32[4,8,128]{2,1,0:T(8,128)S(1)}, f32[2,8,128]{2,1,0:T(8,128)S(1)}) custom-call(s32[3]{0:T(128)S(1)} %pad_add_fusion.index_ref, bf16[8,32,384]{2,1,0:T(8,128)(2,1)S(1)} %reshape.15.near_ref.block_ref, f32[4,48,384]{2,1,0:T(8,128)S(1)} %get-tuple-element.50.inverse_ref, ...), custom_call_target="tpu_custom_call" | custom-call | tf_op jit(solution)/shard_map/pallas_call | solution.py:706
  18.7 0.1 collective-permute-start.8
  18.8 1.2 %collective-permute-done.8.got_ref = f32[2,64,128]{2,1,0:T(8,128)S(1)} collective-permute-done((f32[2,64,128]{2,1,0:T(8,128)S(1)}, f32[2,64,128]{2,1,0:T(8,128)S(1)}, u32[]{:S(2)}, u32[]{:S(2)}) %collective-permute-start.8) | collective-permute-done | bytes 65568 | tf_op jit(solution)/shard_map/ppermute | solution.py:62
  20.1 1.6 %collective-permute-start.9 = (f32[1,64,128]{2,1,0:T(8,128)S(1)}, f32[1,64,128]{2,1,0:T(8,128)S(1)}, u32[]{:S(2)}, u32[]{:S(2)}) collective-permute-start(f32[1,64,128]{2,1,0:T(8,128)S(1)} %get-tuple-element.55), channel_id=1, source_target_pairs={{0,16},{1,17},{2,18},{3,19},{4,20},{5,21},{6,22},{7,23},{8,24},{9,... | collective-permute-start | bytes 98312 | tf_op jit(solution)/shard_map/ppermute | solution.py:62
  21.7 0.9 %collective-permute-start.5 = (f32[1,160,128]{2,1,0:T(8,128)S(1)}, f32[1,160,128]{2,1,0:T(8,128)S(1)}, u32[]{:S(2)}, u32[]{:S(2)}) collective-permute-start(f32[1,160,128]{2,1,0:T(8,128)S(1)} %get-tuple-element.47), channel_id=1, source_target_pairs={{0,16},{1,17},{2,18},{3,19},{4,20},{5,21},{6,22},{7,23},{8,24},{9,... | collective-permute-start | bytes 245768 | tf_op jit(solution)/shard_map/ppermute | solution.py:62
  22.6 1.5 %collective-permute-done.9.refs_1_ = f32[1,64,128]{2,1,0:T(8,128)S(1)} collective-permute-done((f32[1,64,128]{2,1,0:T(8,128)S(1)}, f32[1,64,128]{2,1,0:T(8,128)S(1)}, u32[]{:S(2)}, u32[]{:S(2)}) %collective-permute-start.9) | collective-permute-done | bytes 32800 | tf_op jit(solution)/shard_map/ppermute | solution.py:62
  24.1 0.8 shard_map.121
  24.8 2.2 %collective-permute-start.12 = (bf16[1,2,128,128]{3,2,1,0:T(8,128)(2,1)S(1)}, bf16[1,2,128,128]{3,2,1,0:T(8,128)(2,1)S(1)}, u32[]{:S(2)}, u32[]{:S(2)}) collective-permute-start(bf16[1,2,128,128]{3,2,1,0:T(8,128)(2,1)S(1)} %get-tuple-element.56.own_ref.refs_3_), channel_id=1, source_target_pairs={{0,6},{1,7},{2,4},{3,5},{4,2},{5,3},{6,0},{7,1},{8,14},{9,15},{10,... | collective-permute-start | bytes 196616 | tf_op jit(solution)/shard_map/ppermute | solution.py:62
  27.1 2.2 %collective-permute-start.14 = (bf16[1,2,128,128]{3,2,1,0:T(8,128)(2,1)S(1)}, bf16[1,2,128,128]{3,2,1,0:T(8,128)(2,1)S(1)}, u32[]{:S(2)}, u32[]{:S(2)}) collective-permute-start(bf16[1,2,128,128]{3,2,1,0:T(8,128)(2,1)S(1)} %get-tuple-element.56.own_ref.refs_3_), channel_id=1, source_target_pairs={{0,2},{1,3},{2,0},{3,1},{4,6},{5,7},{6,4},{7,5},{8,10},{9,11},{10,... | collective-permute-start | bytes 196616 | tf_op jit(solution)/shard_map/ppermute | solution.py:62
  29.3 0.7 collective-permute-start.11
  30.0 1.9 %shard_map.123.refs_0_.matrix_ref = bf16[4,3,128,1024]{3,2,1,0:T(8,128)(2,1)S(1)} custom-call(f32[4,8,128]{2,1,0:T(8,128)S(1)} %get-tuple-element.59.own_ref, f32[4,8,128]{2,1,0:T(8,128)S(1)} %get-tuple-element.60.other_ref, f32[1,64,128]{2,1,0:T(8,128)S(1)} %get-tuple-element.54.refs_0_, f32[1,64,128]{2,1,0:T(8,128)S(1)} %collective-permute-done.9.refs_1_), custom_call_target="tpu_custom_call" | custom-call | tf_op jit(solution)/shard_map/pallas_call | solution.py:746
  31.9 1.8 %collective-permute-done.13.refs_5_ = bf16[1,2,128,128]{3,2,1,0:T(8,128)(2,1)S(1)} collective-permute-done((bf16[1,2,128,128]{3,2,1,0:T(8,128)(2,1)S(1)}, bf16[1,2,128,128]{3,2,1,0:T(8,128)(2,1)S(1)}, u32[]{:S(2)}, u32[]{:S(2)}) %collective-permute-start.13) | collective-permute-done | bytes 65568 | tf_op jit(solution)/shard_map/ppermute | solution.py:62
  33.7 0.0 copy-start.1
  33.7 0.0 copy-start.2
  33.7 2.8 %collective-permute-start.15 = (bf16[4,2,128,128]{3,2,1,0:T(8,128)(2,1)S(1)}, bf16[4,2,128,128]{3,2,1,0:T(8,128)(2,1)S(1)}, u32[]{:S(2)}, u32[]{:S(2)}) collective-permute-start(bf16[4,2,128,128]{3,2,1,0:T(8,128)(2,1)S(1)} %shard_map.124.field_ref), channel_id=1, source_target_pairs={{0,8},{1,9},{2,10},{3,11},{4,12},{5,13},{6,14},{7,15},{8,0},{9,1},... | collective-permute-start | bytes 786440 | tf_op jit(solution)/shard_map/ppermute | solution.py:62
  36.5 0.6 shard_map.125
  37.1 0.0 copy-start
  37.1 0.6 collective-permute-done.15.field_ref
  37.6 0.6 shard_map.126
  38.2 2.8 %collective-permute-start.16 = (f32[1,2,128,128]{3,2,1,0:T(8,128)S(1)}, f32[1,2,128,128]{3,2,1,0:T(8,128)S(1)}, u32[]{:S(2)}, u32[]{:S(2)}) collective-permute-start(f32[1,2,128,128]{3,2,1,0:T(8,128)S(1)} %get-tuple-element.66), channel_id=1, source_target_pairs={{0,17},{1,16},{2,19},{3,18},{4,21},{5,20},{6,23},{7,22},{8,25},{9,... | collective-permute-start | bytes 393224 | tf_op jit(solution)/shard_map/ppermute | solution.py:62
  41.0 1.3 %collective-permute-start.17 = (f32[1,2,128,128]{3,2,1,0:T(8,128)S(1)}, f32[1,2,128,128]{3,2,1,0:T(8,128)S(1)}, u32[]{:S(2)}, u32[]{:S(2)}) collective-permute-start(f32[1,2,128,128]{3,2,1,0:T(8,128)S(1)} %get-tuple-element.67), channel_id=1, source_target_pairs={{0,16},{1,17},{2,18},{3,19},{4,20},{5,21},{6,22},{7,23},{8,24},{9,... | collective-permute-start | bytes 393224 | tf_op jit(solution)/shard_map/ppermute | solution.py:62
  42.3 1.4 %collective-permute-start.18 = (f32[1,2,128,128]{3,2,1,0:T(8,128)S(1)}, f32[1,2,128,128]{3,2,1,0:T(8,128)S(1)}, u32[]{:S(2)}, u32[]{:S(2)}) collective-permute-start(f32[1,2,128,128]{3,2,1,0:T(8,128)S(1)} %get-tuple-element.68), channel_id=1, source_target_pairs={{0,1},{1,0},{2,3},{3,2},{4,5},{5,4},{6,7},{7,6},{8,9},{9,8},{10,11... | collective-permute-start | bytes 393224 | tf_op jit(solution)/shard_map/ppermute | solution.py:62
  43.7 0.1 collective-permute-start.6
  43.8 0.7 collective-permute-start.10
  44.5 6.3 %collective-permute-done.10.pair_ref = bf16[2,64,128]{2,1,0:T(8,128)(2,1)S(1)} collective-permute-done((bf16[2,64,128]{2,1,0:T(8,128)(2,1)S(1)}, bf16[2,64,128]{2,1,0:T(8,128)(2,1)S(1)}, u32[]{:S(2)}, u32[]{:S(2)}) %collective-permute-start.10) | collective-permute-done | bytes 32800 | tf_op jit(solution)/shard_map/ppermute | solution.py:62
  50.8 1.0 %shard_map.122.base_ref = f32[2,128,128]{2,1,0:T(8,128)S(1)} custom-call(s32[3]{0:T(128)S(1)} %pad_add_fusion.index_ref, s32[8,12]{1,0:T(8,128)S(1)} %copy-done.1, s32[8]{0:T(128)S(1)} %copy-done.2, bf16[8,32,384]{2,1,0:T(8,128)(2,1)S(1)} %reshape.15.near_ref.block_ref, bf16[1,2,128,128]{3,2,1,0:T(8,128)(2,1)S(1)} %get-tuple-element.56.own_ref.refs_3_, ...), custom_call_target="tpu_custom_call" | custom-call | tf_op jit(solution)/shard_map/pallas_call | solution.py:617
  51.8 1.0 %shard_map.127 = (f32[2,128,128]{2,1,0:T(8,128)S(1)}, f32[4,80,128]{2,1,0:T(8,128)S(1)}, f32[4,80,128]{2,1,0:T(8,128)S(1)}) custom-call(s32[3]{0:T(128)S(1)} %pad_add_fusion.index_ref, f32[1,160,128]{2,1,0:T(8,128)S(1)} %collective-permute-done.6.half_hbm.refs_1_, f32[128,128]{1,0:T(8,128)S(1)} %get-tuple-element.42.refs_0_.weight_ref, ...), custom_call_target="tpu_custom_call" | custom-call | tf_op jit(solution)/shard_map/pallas_call | solution.py:800
  52.9 0.1 collective-permute-start.20
  53.0 0.1 collective-permute-start.19
  53.1 1.3 %collective-permute-done.20.refs_1_ = f32[4,80,128]{2,1,0:T(8,128)S(1)} collective-permute-done((f32[4,80,128]{2,1,0:T(8,128)S(1)}, f32[4,80,128]{2,1,0:T(8,128)S(1)}, u32[]{:S(2)}, u32[]{:S(2)}) %collective-permute-start.20) | collective-permute-done | bytes 163872 | tf_op jit(solution)/shard_map/ppermute | solution.py:62
  54.4 0.5 collective-permute-start.21
  54.9 0.6 collective-permute-start.22
  55.5 2.5 %collective-permute-start.23 = (f32[1,80,128]{2,1,0:T(8,128)S(1)}, f32[1,80,128]{2,1,0:T(8,128)S(1)}, u32[]{:S(2)}, u32[]{:S(2)}) collective-permute-start(f32[1,80,128]{2,1,0:T(8,128)S(1)} %get-tuple-element.75), channel_id=1, source_target_pairs={{0,1},{1,0},{2,3},{3,2},{4,5},{5,4},{6,7},{7,6},{8,9},{9,8},{10,11... | collective-permute-start | bytes 122888 | tf_op jit(solution)/shard_map/ppermute | solution.py:62
  57.9 1.0 %collective-permute-done.19.refs_0_.refs_1_ = f32[1,160,128]{2,1,0:T(8,128)S(1)} collective-permute-done((f32[1,160,128]{2,1,0:T(8,128)S(1)}, f32[1,160,128]{2,1,0:T(8,128)S(1)}, u32[]{:S(2)}, u32[]{:S(2)}) %collective-permute-start.19) | collective-permute-done | bytes 81952 | tf_op jit(solution)/shard_map/ppermute | solution.py:62
  59.0 0.5 collective-permute-done.21.refs_2_
  59.4 0.5 collective-permute-done.23.refs_4_
  59.9 2.8 %collective-permute-start.24 = (f32[1,80,128]{2,1,0:T(8,128)S(1)}, f32[1,80,128]{2,1,0:T(8,128)S(1)}, u32[]{:S(2)}, u32[]{:S(2)}) collective-permute-start(f32[1,80,128]{2,1,0:T(8,128)S(1)} %shard_map.130.refs_0_), channel_id=1, source_target_pairs={{0,6},{1,7},{2,4},{3,5},{4,2},{5,3},{6,0},{7,1},{8,14},{9,15},{10,... | collective-permute-start | bytes 122888 | tf_op jit(solution)/shard_map/ppermute | solution.py:62
  62.7 0.7 collective-permute-start.25
  63.5 0.9 %collective-permute-start.26 = (f32[1,80,128]{2,1,0:T(8,128)S(1)}, f32[1,80,128]{2,1,0:T(8,128)S(1)}, u32[]{:S(2)}, u32[]{:S(2)}) collective-permute-start(f32[1,80,128]{2,1,0:T(8,128)S(1)} %shard_map.130.refs_0_), channel_id=1, source_target_pairs={{0,2},{1,3},{2,0},{3,1},{4,6},{5,7},{6,4},{7,5},{8,10},{9,11},{10,... | collective-permute-start | bytes 122888 | tf_op jit(solution)/shard_map/ppermute | solution.py:62
  64.4 1.6 %collective-permute-done.24.refs_1_ = f32[1,80,128]{2,1,0:T(8,128)S(1)} collective-permute-done((f32[1,80,128]{2,1,0:T(8,128)S(1)}, f32[1,80,128]{2,1,0:T(8,128)S(1)}, u32[]{:S(2)}, u32[]{:S(2)}) %collective-permute-start.24) | collective-permute-done | bytes 40992 | tf_op jit(solution)/shard_map/ppermute | solution.py:62
  66.0 1.7 %collective-permute-done.25.refs_2_ = f32[1,80,128]{2,1,0:T(8,128)S(1)} collective-permute-done((f32[1,80,128]{2,1,0:T(8,128)S(1)}, f32[1,80,128]{2,1,0:T(8,128)S(1)}, u32[]{:S(2)}, u32[]{:S(2)}) %collective-permute-start.25) | collective-permute-done | bytes 40992 | tf_op jit(solution)/shard_map/ppermute | solution.py:62
  67.8 0.2 collective-permute-done.26.refs_3_
  68.0 0.8 collective-permute-start.27
  68.7 1.4 %collective-permute-start.28 = (f32[1,240,128]{2,1,0:T(8,128)S(1)}, f32[1,240,128]{2,1,0:T(8,128)S(1)}, u32[]{:S(2)}, u32[]{:S(2)}) collective-permute-start(f32[1,240,128]{2,1,0:T(8,128)S(1)} %shard_map.133.refs_0_), channel_id=1, source_target_pairs={{0,16},{1,17},{2,18},{3,19},{4,20},{5,21},{6,22},{7,23},{8,24},{9,... | collective-permute-start | bytes 368648 | tf_op jit(solution)/shard_map/ppermute | solution.py:62
  70.1 1.4 %collective-permute-start.29 = (f32[1,240,128]{2,1,0:T(8,128)S(1)}, f32[1,240,128]{2,1,0:T(8,128)S(1)}, u32[]{:S(2)}, u32[]{:S(2)}) collective-permute-start(f32[1,240,128]{2,1,0:T(8,128)S(1)} %shard_map.133.refs_0_), channel_id=1, source_target_pairs={{0,1},{1,0},{2,3},{3,2},{4,5},{5,4},{6,7},{7,6},{8,9},{9,8},{10,11... | collective-permute-start | bytes 368648 | tf_op jit(solution)/shard_map/ppermute | solution.py:62
  71.5 2.4 %collective-permute-done.27.refs_1_ = f32[1,240,128]{2,1,0:T(8,128)S(1)} collective-permute-done((f32[1,240,128]{2,1,0:T(8,128)S(1)}, f32[1,240,128]{2,1,0:T(8,128)S(1)}, u32[]{:S(2)}, u32[]{:S(2)}) %collective-permute-start.27) | collective-permute-done | bytes 122912 | tf_op jit(solution)/shard_map/ppermute | solution.py:62
  73.9 1.0 %collective-permute-done.28.refs_2_ = f32[1,240,128]{2,1,0:T(8,128)S(1)} collective-permute-done((f32[1,240,128]{2,1,0:T(8,128)S(1)}, f32[1,240,128]{2,1,0:T(8,128)S(1)}, u32[]{:S(2)}, u32[]{:S(2)}) %collective-permute-start.28) | collective-permute-done | bytes 122912 | tf_op jit(solution)/shard_map/ppermute | solution.py:62
  74.9 0.1 collective-permute-done.29.refs_3_
  75.0 0.1 collective-permute-start.30
  75.1 1.9 %collective-permute-done.30.refs_1_ = f32[4,240,128]{2,1,0:T(8,128)S(1)} collective-permute-done((f32[4,240,128]{2,1,0:T(8,128)S(1)}, f32[4,240,128]{2,1,0:T(8,128)S(1)}, u32[]{:S(2)}, u32[]{:S(2)}) %collective-permute-start.30) | collective-permute-done | bytes 491552 | tf_op jit(solution)/shard_map/ppermute | solution.py:62
  76.9 6.7 %shard_map.135 = (f32[512,128]{1,0:T(8,128)}, f32[128,128]{1,0:T(8,128)}, f32[256,128]{1,0:T(8,128)}) custom-call(s32[3]{0:T(128)S(1)} %pad_add_fusion.index_ref, f32[4,2,128,128]{3,2,1,0:T(8,128)S(1)} %copy-done, f32[2,128,128]{2,1,0:T(8,128)S(1)} %get-tuple-element.69.image_ref, f32[4,240,128]{2,1,0:T(8,128)S(1)} %shard_map.134.refs_0_, ...), custom_call_target="tpu_custom_call" | custom-call | tf_op jit(solution)/shard_map/pallas_call | solution.py:617
  (33 shorter events, 0.3 us)
Async XLA Ops:
  0.6 14.5 %copy-start.3 = (bf16[8,12,32,32]{3,2,1,0:T(8,128)(2,1)S(1)}, bf16[8,12,32,32]{3,2,1,0:T(8,128)(2,1)}, u32[]{:S(2)}) copy-start(bf16[8,12,32,32]{3,2,1,0:T(8,128)(2,1)} %param.15) | copy-start | bytes 589828
  1.9 8.3 %collective-permute-start = (f32[1,56,128]{2,1,0:T(8,128)S(1)}, f32[1,56,128]{2,1,0:T(8,128)S(1)}, u32[]{:S(2)}, u32[]{:S(2)}) collective-permute-start(f32[1,56,128]{2,1,0:T(8,128)S(1)} %shard_map.112.pack_hbm.refs_1_), channel_id=1, source_target_pairs={{0,6},{1,7},{2,4},{3,5},{4,2},{5,3},{6,0},{7,1},{8,14},{9,15},{10,... | collective-permute-start | bytes 86024 | tf_op jit(solution)/shard_map/ppermute | solution.py:62
  7.0 4.8 %collective-permute-start.1 = (f32[1,56,128]{2,1,0:T(8,128)S(1)}, f32[1,56,128]{2,1,0:T(8,128)S(1)}, u32[]{:S(2)}, u32[]{:S(2)}) collective-permute-start(f32[1,56,128]{2,1,0:T(8,128)S(1)} %shard_map.112.pack_hbm.refs_1_), channel_id=1, source_target_pairs={{0,4},{1,5},{2,6},{3,7},{4,0},{5,1},{6,2},{7,3},{8,12},{9,13},{10,... | collective-permute-start | bytes 86024 | tf_op jit(solution)/shard_map/ppermute | solution.py:62
  7.0 4.8 %collective-permute-start.2 = (f32[1,56,128]{2,1,0:T(8,128)S(1)}, f32[1,56,128]{2,1,0:T(8,128)S(1)}, u32[]{:S(2)}, u32[]{:S(2)}) collective-permute-start(f32[1,56,128]{2,1,0:T(8,128)S(1)} %shard_map.112.pack_hbm.refs_1_), channel_id=1, source_target_pairs={{0,2},{1,3},{2,0},{3,1},{4,6},{5,7},{6,4},{7,5},{8,10},{9,11},{10,... | collective-permute-start | bytes 86024 | tf_op jit(solution)/shard_map/ppermute | solution.py:62
  11.8 1.7 %collective-permute-start.3 = (f32[4,160,128]{2,1,0:T(8,128)S(1)}, f32[4,160,128]{2,1,0:T(8,128)S(1)}, u32[]{:S(2)}, u32[]{:S(2)}) collective-permute-start(f32[4,160,128]{2,1,0:T(8,128)S(1)} %shard_map.115), channel_id=1, source_target_pairs={{0,8},{1,9},{2,10},{3,11},{4,12},{5,13},{6,14},{7,15},{8,0},{9,1},... | collective-permute-start | bytes 983048 | tf_op jit(solution)/shard_map/ppermute | solution.py:62
  11.9 6.0 %collective-permute-start.7 = (f32[4,56,128]{2,1,0:T(8,128)S(1)}, f32[4,56,128]{2,1,0:T(8,128)S(1)}, u32[]{:S(2)}, u32[]{:S(2)}) collective-permute-start(f32[4,56,128]{2,1,0:T(8,128)S(1)} %shard_map.114.refs_0_), channel_id=1, source_target_pairs={{0,1},{1,0},{2,3},{3,2},{4,5},{5,4},{6,7},{7,6},{8,9},{9,8},{10,11... | collective-permute-start | bytes 344072 | tf_op jit(solution)/shard_map/ppermute | solution.py:62
  13.5 8.1 %collective-permute-start.4 = (f32[2,160,128]{2,1,0:T(8,128)S(1)}, f32[2,160,128]{2,1,0:T(8,128)S(1)}, u32[]{:S(2)}, u32[]{:S(2)}) collective-permute-start(f32[2,160,128]{2,1,0:T(8,128)S(1)} %get-tuple-element.45), channel_id=1, source_target_pairs={{0,1},{1,0},{2,3},{3,2},{4,5},{5,4},{6,7},{7,6},{8,9},{9,8},{10,11... | collective-permute-start | bytes 491528 | tf_op jit(solution)/shard_map/ppermute | solution.py:62
  18.7 1.3 %collective-permute-start.8 = (f32[2,64,128]{2,1,0:T(8,128)S(1)}, f32[2,64,128]{2,1,0:T(8,128)S(1)}, u32[]{:S(2)}, u32[]{:S(2)}) collective-permute-start(f32[2,64,128]{2,1,0:T(8,128)S(1)} %get-tuple-element.52), channel_id=1, source_target_pairs={{0,8},{1,9},{2,10},{3,11},{4,12},{5,13},{6,14},{7,15},{8,0},{9,1},... | collective-permute-start | bytes 196616 | tf_op jit(solution)/shard_map/ppermute | solution.py:62
  20.1 4.0 %collective-permute-start.9 = (f32[1,64,128]{2,1,0:T(8,128)S(1)}, f32[1,64,128]{2,1,0:T(8,128)S(1)}, u32[]{:S(2)}, u32[]{:S(2)}) collective-permute-start(f32[1,64,128]{2,1,0:T(8,128)S(1)} %get-tuple-element.55), channel_id=1, source_target_pairs={{0,16},{1,17},{2,18},{3,19},{4,20},{5,21},{6,22},{7,23},{8,24},{9,... | collective-permute-start | bytes 98312 | tf_op jit(solution)/shard_map/ppermute | solution.py:62
  21.7 12.0 %collective-permute-start.5 = (f32[1,160,128]{2,1,0:T(8,128)S(1)}, f32[1,160,128]{2,1,0:T(8,128)S(1)}, u32[]{:S(2)}, u32[]{:S(2)}) collective-permute-start(f32[1,160,128]{2,1,0:T(8,128)S(1)} %get-tuple-element.47), channel_id=1, source_target_pairs={{0,16},{1,17},{2,18},{3,19},{4,20},{5,21},{6,22},{7,23},{8,24},{9,... | collective-permute-start | bytes 245768 | tf_op jit(solution)/shard_map/ppermute | solution.py:62
  24.8 7.0 %collective-permute-start.12 = (bf16[1,2,128,128]{3,2,1,0:T(8,128)(2,1)S(1)}, bf16[1,2,128,128]{3,2,1,0:T(8,128)(2,1)S(1)}, u32[]{:S(2)}, u32[]{:S(2)}) collective-permute-start(bf16[1,2,128,128]{3,2,1,0:T(8,128)(2,1)S(1)} %get-tuple-element.56.own_ref.refs_3_), channel_id=1, source_target_pairs={{0,6},{1,7},{2,4},{3,5},{4,2},{5,3},{6,0},{7,1},{8,14},{9,15},{10,... | collective-permute-start | bytes 196616 | tf_op jit(solution)/shard_map/ppermute | solution.py:62
  27.1 6.6 %collective-permute-start.13 = (bf16[1,2,128,128]{3,2,1,0:T(8,128)(2,1)S(1)}, bf16[1,2,128,128]{3,2,1,0:T(8,128)(2,1)S(1)}, u32[]{:S(2)}, u32[]{:S(2)}) collective-permute-start(bf16[1,2,128,128]{3,2,1,0:T(8,128)(2,1)S(1)} %get-tuple-element.56.own_ref.refs_3_), channel_id=1, source_target_pairs={{0,4},{1,5},{2,6},{3,7},{4,0},{5,1},{6,2},{7,3},{8,12},{9,13},{10,... | collective-permute-start | bytes 196616 | tf_op jit(solution)/shard_map/ppermute | solution.py:62
  27.1 6.6 %collective-permute-start.14 = (bf16[1,2,128,128]{3,2,1,0:T(8,128)(2,1)S(1)}, bf16[1,2,128,128]{3,2,1,0:T(8,128)(2,1)S(1)}, u32[]{:S(2)}, u32[]{:S(2)}) collective-permute-start(bf16[1,2,128,128]{3,2,1,0:T(8,128)(2,1)S(1)} %get-tuple-element.56.own_ref.refs_3_), channel_id=1, source_target_pairs={{0,2},{1,3},{2,0},{3,1},{4,6},{5,7},{6,4},{7,5},{8,10},{9,11},{10,... | collective-permute-start | bytes 196616 | tf_op jit(solution)/shard_map/ppermute | solution.py:62
  29.3 2.6 %collective-permute-start.11 = (bf16[2,64,128]{2,1,0:T(8,128)(2,1)S(1)}, bf16[2,64,128]{2,1,0:T(8,128)(2,1)S(1)}, u32[]{:S(2)}, u32[]{:S(2)}) collective-permute-start(bf16[2,64,128]{2,1,0:T(8,128)(2,1)S(1)} %get-tuple-element.58), channel_id=1, source_target_pairs={{1,2},{3,4},{5,6},{7,8},{9,10},{11,12},{13,14},{15,16},{17,18},{19... | collective-permute-start | bytes 98312 | tf_op jit(solution)/shard_map/ppermute | solution.py:757
  33.7 17.1 %copy-start.1 = (s32[8,12]{1,0:T(8,128)S(1)}, s32[8,12]{1,0:T(8,128)}, u32[]{:S(2)}) copy-start(s32[8,12]{1,0:T(8,128)} %panel_ref.1) | copy-start | bytes 1156
  33.7 17.1 %copy-start.2 = (s32[8]{0:T(128)S(1)}, s32[8]{0:T(128)}, u32[]{:S(2)}) copy-start(s32[8]{0:T(128)} %count_ref.1) | copy-start | bytes 100
  33.7 3.9 %collective-permute-start.15 = (bf16[4,2,128,128]{3,2,1,0:T(8,128)(2,1)S(1)}, bf16[4,2,128,128]{3,2,1,0:T(8,128)(2,1)S(1)}, u32[]{:S(2)}, u32[]{:S(2)}) collective-permute-start(bf16[4,2,128,128]{3,2,1,0:T(8,128)(2,1)S(1)} %shard_map.124.field_ref), channel_id=1, source_target_pairs={{0,8},{1,9},{2,10},{3,11},{4,12},{5,13},{6,14},{7,15},{8,0},{9,1},... | collective-permute-start | bytes 786440 | tf_op jit(solution)/shard_map/ppermute | solution.py:62
  37.1 14.8 %copy-start = (f32[4,2,128,128]{3,2,1,0:T(8,128)S(1)}, f32[4,2,128,128]{3,2,1,0:T(8,128)}, u32[]{:S(2)}) copy-start(f32[4,2,128,128]{3,2,1,0:T(8,128)} %basis_ref.3) | copy-start | bytes 1572868
  38.2 13.6 %collective-permute-start.16 = (f32[1,2,128,128]{3,2,1,0:T(8,128)S(1)}, f32[1,2,128,128]{3,2,1,0:T(8,128)S(1)}, u32[]{:S(2)}, u32[]{:S(2)}) collective-permute-start(f32[1,2,128,128]{3,2,1,0:T(8,128)S(1)} %get-tuple-element.66), channel_id=1, source_target_pairs={{0,17},{1,16},{2,19},{3,18},{4,21},{5,20},{6,23},{7,22},{8,25},{9,... | collective-permute-start | bytes 393224 | tf_op jit(solution)/shard_map/ppermute | solution.py:62
  41.0 10.8 %collective-permute-start.17 = (f32[1,2,128,128]{3,2,1,0:T(8,128)S(1)}, f32[1,2,128,128]{3,2,1,0:T(8,128)S(1)}, u32[]{:S(2)}, u32[]{:S(2)}) collective-permute-start(f32[1,2,128,128]{3,2,1,0:T(8,128)S(1)} %get-tuple-element.67), channel_id=1, source_target_pairs={{0,16},{1,17},{2,18},{3,19},{4,20},{5,21},{6,22},{7,23},{8,24},{9,... | collective-permute-start | bytes 393224 | tf_op jit(solution)/shard_map/ppermute | solution.py:62
  42.3 9.5 %collective-permute-start.18 = (f32[1,2,128,128]{3,2,1,0:T(8,128)S(1)}, f32[1,2,128,128]{3,2,1,0:T(8,128)S(1)}, u32[]{:S(2)}, u32[]{:S(2)}) collective-permute-start(f32[1,2,128,128]{3,2,1,0:T(8,128)S(1)} %get-tuple-element.68), channel_id=1, source_target_pairs={{0,1},{1,0},{2,3},{3,2},{4,5},{5,4},{6,7},{7,6},{8,9},{9,8},{10,11... | collective-permute-start | bytes 393224 | tf_op jit(solution)/shard_map/ppermute | solution.py:62
  43.7 8.1 %collective-permute-start.6 = (f32[1,160,128]{2,1,0:T(8,128)S(1)}, f32[1,160,128]{2,1,0:T(8,128)S(1)}, u32[]{:S(2)}, u32[]{:S(2)}) collective-permute-start(f32[1,160,128]{2,1,0:T(8,128)S(1)} %shard_map.118.refs_0_), channel_id=1, source_target_pairs={{0,2},{1,3},{2,0},{3,1},{4,6},{5,7},{6,4},{7,5},{8,10},{9,11},{10,... | collective-permute-start | bytes 245768 | tf_op jit(solution)/shard_map/ppermute | solution.py:62
  43.8 7.0 %collective-permute-start.10 = (bf16[2,64,128]{2,1,0:T(8,128)(2,1)S(1)}, bf16[2,64,128]{2,1,0:T(8,128)(2,1)S(1)}, u32[]{:S(2)}, u32[]{:S(2)}) collective-permute-start(bf16[2,64,128]{2,1,0:T(8,128)(2,1)S(1)} %get-tuple-element.57), channel_id=1, source_target_pairs={{0,1},{1,0},{2,3},{3,2},{4,5},{5,4},{6,7},{7,6},{8,9},{9,8},{10,11... | collective-permute-start | bytes 98312 | tf_op jit(solution)/shard_map/ppermute | solution.py:62
  52.9 1.5 %collective-permute-start.20 = (f32[4,80,128]{2,1,0:T(8,128)S(1)}, f32[4,80,128]{2,1,0:T(8,128)S(1)}, u32[]{:S(2)}, u32[]{:S(2)}) collective-permute-start(f32[4,80,128]{2,1,0:T(8,128)S(1)} %get-tuple-element.71), channel_id=1, source_target_pairs={{0,8},{1,9},{2,10},{3,11},{4,12},{5,13},{6,14},{7,15},{8,0},{9,1},... | collective-permute-start | bytes 491528 | tf_op jit(solution)/shard_map/ppermute | solution.py:62
  53.0 6.0 %collective-permute-start.19 = (f32[1,160,128]{2,1,0:T(8,128)S(1)}, f32[1,160,128]{2,1,0:T(8,128)S(1)}, u32[]{:S(2)}, u32[]{:S(2)}) collective-permute-start(f32[1,160,128]{2,1,0:T(8,128)S(1)} %shard_map.128.refs_0_), channel_id=1, source_target_pairs={{0,4},{1,5},{2,6},{3,7},{4,0},{5,1},{6,2},{7,3},{8,12},{9,13},{10,... | collective-permute-start | bytes 245768 | tf_op jit(solution)/shard_map/ppermute | solution.py:62
  54.4 5.1 %collective-permute-start.21 = (f32[1,80,128]{2,1,0:T(8,128)S(1)}, f32[1,80,128]{2,1,0:T(8,128)S(1)}, u32[]{:S(2)}, u32[]{:S(2)}) collective-permute-start(f32[1,80,128]{2,1,0:T(8,128)S(1)} %get-tuple-element.73), channel_id=1, source_target_pairs={{0,17},{1,16},{2,19},{3,18},{4,21},{5,20},{6,23},{7,22},{8,25},{9,... | collective-permute-start | bytes 122888 | tf_op jit(solution)/shard_map/ppermute | solution.py:62
  54.9 4.6 %collective-permute-start.22 = (f32[1,80,128]{2,1,0:T(8,128)S(1)}, f32[1,80,128]{2,1,0:T(8,128)S(1)}, u32[]{:S(2)}, u32[]{:S(2)}) collective-permute-start(f32[1,80,128]{2,1,0:T(8,128)S(1)} %get-tuple-element.74), channel_id=1, source_target_pairs={{0,16},{1,17},{2,18},{3,19},{4,20},{5,21},{6,22},{7,23},{8,24},{9,... | collective-permute-start | bytes 122888 | tf_op jit(solution)/shard_map/ppermute | solution.py:62
  55.5 4.5 %collective-permute-start.23 = (f32[1,80,128]{2,1,0:T(8,128)S(1)}, f32[1,80,128]{2,1,0:T(8,128)S(1)}, u32[]{:S(2)}, u32[]{:S(2)}) collective-permute-start(f32[1,80,128]{2,1,0:T(8,128)S(1)} %get-tuple-element.75), channel_id=1, source_target_pairs={{0,1},{1,0},{2,3},{3,2},{4,5},{5,4},{6,7},{7,6},{8,9},{9,8},{10,11... | collective-permute-start | bytes 122888 | tf_op jit(solution)/shard_map/ppermute | solution.py:62
  59.9 6.1 %collective-permute-start.24 = (f32[1,80,128]{2,1,0:T(8,128)S(1)}, f32[1,80,128]{2,1,0:T(8,128)S(1)}, u32[]{:S(2)}, u32[]{:S(2)}) collective-permute-start(f32[1,80,128]{2,1,0:T(8,128)S(1)} %shard_map.130.refs_0_), channel_id=1, source_target_pairs={{0,6},{1,7},{2,4},{3,5},{4,2},{5,3},{6,0},{7,1},{8,14},{9,15},{10,... | collective-permute-start | bytes 122888 | tf_op jit(solution)/shard_map/ppermute | solution.py:62
  62.7 5.0 %collective-permute-start.25 = (f32[1,80,128]{2,1,0:T(8,128)S(1)}, f32[1,80,128]{2,1,0:T(8,128)S(1)}, u32[]{:S(2)}, u32[]{:S(2)}) collective-permute-start(f32[1,80,128]{2,1,0:T(8,128)S(1)} %shard_map.130.refs_0_), channel_id=1, source_target_pairs={{0,4},{1,5},{2,6},{3,7},{4,0},{5,1},{6,2},{7,3},{8,12},{9,13},{10,... | collective-permute-start | bytes 122888 | tf_op jit(solution)/shard_map/ppermute | solution.py:62
  63.5 4.4 %collective-permute-start.26 = (f32[1,80,128]{2,1,0:T(8,128)S(1)}, f32[1,80,128]{2,1,0:T(8,128)S(1)}, u32[]{:S(2)}, u32[]{:S(2)}) collective-permute-start(f32[1,80,128]{2,1,0:T(8,128)S(1)} %shard_map.130.refs_0_), channel_id=1, source_target_pairs={{0,2},{1,3},{2,0},{3,1},{4,6},{5,7},{6,4},{7,5},{8,10},{9,11},{10,... | collective-permute-start | bytes 122888 | tf_op jit(solution)/shard_map/ppermute | solution.py:62
  68.0 6.0 %collective-permute-start.27 = (f32[1,240,128]{2,1,0:T(8,128)S(1)}, f32[1,240,128]{2,1,0:T(8,128)S(1)}, u32[]{:S(2)}, u32[]{:S(2)}) collective-permute-start(f32[1,240,128]{2,1,0:T(8,128)S(1)} %shard_map.133.refs_0_), channel_id=1, source_target_pairs={{0,17},{1,16},{2,19},{3,18},{4,21},{5,20},{6,23},{7,22},{8,25},{9,... | collective-permute-start | bytes 368648 | tf_op jit(solution)/shard_map/ppermute | solution.py:62
  68.7 6.2 %collective-permute-start.28 = (f32[1,240,128]{2,1,0:T(8,128)S(1)}, f32[1,240,128]{2,1,0:T(8,128)S(1)}, u32[]{:S(2)}, u32[]{:S(2)}) collective-permute-start(f32[1,240,128]{2,1,0:T(8,128)S(1)} %shard_map.133.refs_0_), channel_id=1, source_target_pairs={{0,16},{1,17},{2,18},{3,19},{4,20},{5,21},{6,22},{7,23},{8,24},{9,... | collective-permute-start | bytes 368648 | tf_op jit(solution)/shard_map/ppermute | solution.py:62
  70.1 4.9 %collective-permute-start.29 = (f32[1,240,128]{2,1,0:T(8,128)S(1)}, f32[1,240,128]{2,1,0:T(8,128)S(1)}, u32[]{:S(2)}, u32[]{:S(2)}) collective-permute-start(f32[1,240,128]{2,1,0:T(8,128)S(1)} %shard_map.133.refs_0_), channel_id=1, source_target_pairs={{0,1},{1,0},{2,3},{3,2},{4,5},{5,4},{6,7},{7,6},{8,9},{9,8},{10,11... | collective-permute-start | bytes 368648 | tf_op jit(solution)/shard_map/ppermute | solution.py:62
  75.0 1.9 %collective-permute-start.30 = (f32[4,240,128]{2,1,0:T(8,128)S(1)}, f32[4,240,128]{2,1,0:T(8,128)S(1)}, u32[]{:S(2)}, u32[]{:S(2)}) collective-permute-start(f32[4,240,128]{2,1,0:T(8,128)S(1)} %shard_map.134.refs_0_), channel_id=1, source_target_pairs={{0,8},{1,9},{2,10},{3,11},{4,12},{5,13},{6,14},{7,15},{8,0},{9,1},... | collective-permute-start | bytes 1474568 | tf_op jit(solution)/shard_map/ppermute | solution.py:62
